TPU v7x, 32 devices: a whole 2x2x4 slice. The times are simulated.
32 devices in a mesh: grp: 4 (over y, x), seq: 8 (over z, core).
Axes of the slice: x: 2, y: 2, z: 4, core: 2. Of those that a mesh axis runs over, the one named last changes fastest.
Arguments:
- grad_output: bfloat16 [1024, 8192], P('seq', 'grp'), may hold values from -6 to 6
- hidden: bfloat16 [1024, 28672], P('seq', 'grp'), may hold values from -6 to 6
- down_weight: bfloat16 [28672, 8192], P('seq', 'grp'), may hold values from -0.0625 to 0.0625
- adapter_down: bfloat16 [16, 64, 28672], P(None, None, ('grp', 'seq')), may hold values from -0.03125 to 0.03125
- adapter_up: bfloat16 [16, 64, 8192], P(None, None, ('grp', 'seq')), may hold values from -0.0625 to 0.0625
- job_tenant: int32 [8, 4], replicated, may hold values from 0 to 15, all different within a row
- job_count: int32 [8, 4], replicated, may hold values from 1 to 64, 128 in all within a row
Outputs:
- grad_hidden: bfloat16 [1024, 28672], P('seq', 'grp')
- grad_adapter_down: float32 [16, 64, 28672], P(None, None, ('grp', 'seq'))
- grad_adapter_up: float32 [16, 64, 8192], P(None, None, ('grp', 'seq'))
Inputs may be any that keep to these rules, and one draw needn't show every extreme that they name: `job_tenant`: each row names 4 different tenants; every tenant is named by some row. `job_count`: each row sums to 128, and its largest entry is exactly 64.
All inputs are finite; a program needn't handle non-finite values.
Results may differ from a plain program's by a relative error of at most 0.015.
Values may be sent and summed in bfloat16 or wider, within the bound.
No kernel may reach another device: no remote copies, remote signals or barrier semaphores. Data moves between devices by JAX's collectives and lax.ppermute only.
A program may use at most 128 MiB of HBM per device.

v0:
```python
import functools

import jax
import jax.numpy as jnp
from jax import lax
from jax.experimental import pallas as pl
from jax.experimental.pallas import tpu as pltpu
from jax.sharding import PartitionSpec as P

ADAPTER_SCALE = 2.0
CONTRACT_LAST = (((1,), (1,)), ((), ()))
CONTRACT_ROWS = (((0,), (0,)), ((), ()))
CORES = 2
MOST_ROWS = 1024


def dot(left, right, dims):
    return lax.dot_general(left, right, dims, preferred_element_type=jnp.float32)


def pieces(total):
    step = min(total, MOST_ROWS)
    return [(at, min(step, total - at)) for at in range(0, total, step)]


def tile_of(width):
    return next(tile for tile in (512, 448, 384, 256, 128, width) if width % tile == 0 and tile % 128 == 0 or tile == width)


def chunk_kernel(groups, group_ref, near_ref, far_ref, weight_ref, *rest):
    outs, rows = rest[:groups], rest[groups]
    part = near_ref.shape[0] // groups

    @pl.when(pl.program_id(0) == 0)
    def _():
        for flip in range(groups):
            at = pl.multiple_of((group_ref[0] ^ flip) * part, part)
            low = flip * CORES * part
            rows[low : low + part] = near_ref[pl.ds(at, part)]
            rows[low + part : low + 2 * part] = far_ref[pl.ds(at, part)]

    full = dot(rows[...], weight_ref[...], CONTRACT_LAST).astype(jnp.bfloat16)
    for flip in range(groups):
        for core in range(CORES):
            low = (flip * CORES + core) * part
            outs[flip][core] = full[low : low + part]


def chunk_product(near, far, weight, group, groups):
    block, depth = near.shape
    width = weight.shape[0]
    tile = tile_of(width)
    part = block // groups
    return pl.pallas_call(
        functools.partial(chunk_kernel, groups),
        grid_spec=pltpu.PrefetchScalarGridSpec(
            num_scalar_prefetch=1,
            grid=(width // tile,),
            in_specs=[
                pl.BlockSpec((block, depth), lambda at, group: (0, 0)),
                pl.BlockSpec((block, depth), lambda at, group: (0, 0)),
                pl.BlockSpec((tile, depth), lambda at, group: (at, 0)),
            ],
            out_specs=[pl.BlockSpec((CORES, part, tile), lambda at, group: (0, 0, at))] * groups,
            scratch_shapes=[pltpu.VMEM((CORES * block, depth), jnp.bfloat16)],
        ),
        out_shape=[jax.ShapeDtypeStruct((CORES, part, width), jnp.bfloat16)] * groups,
        compiler_params=pltpu.CompilerParams(vmem_limit_bytes=24 << 20),
        cost_estimate=pl.CostEstimate(
            flops=2 * CORES * block * depth * width,
            bytes_accessed=2 * (width * depth + CORES * block * (depth + width)),
            transcendentals=0,
        ),
    )(group.reshape(1), near, far, weight)


def project(rows, adapter, mask):
    tenants, ranks, width = adapter.shape
    flat = adapter.reshape(tenants * ranks, width)
    parts = []
    for at, size in pieces(rows.shape[0]):
        full = dot(rows[at : at + size], flat, CONTRACT_LAST)
        chosen = full.reshape(size, tenants, ranks) * mask[at : at + size, :, None]
        parts.append(jnp.sum(chosen, axis=1))
    return jnp.concatenate(parts, axis=0).astype(jnp.bfloat16)


def spread(rank, mask):
    wide = rank[:, None, :] * mask.astype(jnp.bfloat16)[:, :, None]
    return wide.reshape(rank.shape[0], -1)


def adapter_grad(rank, mask, rows, weights):
    tenants, ranks = mask.shape[1], rank.shape[1]
    parts = []
    for at, size in pieces(tenants * ranks):
        low, high = at // ranks, (at + size) // ranks
        grad = dot(spread(rank, mask[:, low:high]), rows, CONTRACT_ROWS)
        parts.append(grad.reshape(high - low, ranks, -1) * weights[low:high, None, None])
    return jnp.concatenate(parts, axis=0)


def shards(grad_output, hidden, down_weight, adapter_down, adapter_up, job_tenant, job_count):
    index = lax.axis_index("seq")
    group = lax.axis_index("grp")
    count = lax.axis_size("seq")
    groups = lax.axis_size("grp")
    chips = count // CORES
    chip, core = index // CORES, index % CORES
    block = grad_output.shape[0]
    tenants, ranks, down_slab = adapter_down.shape
    up_slab = adapter_up.shape[2]
    width = down_weight.shape[0]
    part = block // groups

    named = (job_tenant[:, :, None] == jnp.arange(tenants, dtype=jnp.int32)).astype(jnp.float32)
    totals = jnp.sum(job_count.astype(jnp.float32)[:, :, None] * named, axis=(0, 1))
    weights = ADAPTER_SCALE / totals
    ends = jnp.cumsum(job_count, axis=1)
    places = jnp.arange(block, dtype=jnp.int32)[None, :, None]
    member = (places >= (ends - job_count)[:, None, :]) & (places < ends[:, None, :])
    owner = jnp.sum(jnp.where(member, job_tenant[:, None, :], 0), axis=2).reshape(count * block)
    mask = (owner[:, None] == jnp.arange(tenants, dtype=jnp.int32)).astype(jnp.float32)

    def seq_move(value, chips_back, flip):
        pairs = [
            (s, ((s // CORES - chips_back) % chips) * CORES + ((s % CORES) ^ flip))
            for s in range(count)
        ]
        return lax.ppermute(value, "seq", pairs)

    def grp_move(value, flip):
        return lax.ppermute(value, "grp", [(g, g ^ flip) for g in range(groups)])

    hidden_slab = lax.all_to_all(
        hidden.reshape(block, count, down_slab).transpose(1, 0, 2),
        "seq",
        split_axis=0,
        concat_axis=0,
        tiled=True,
    ).reshape(count * block, down_slab)

    held = grad_output
    grad_slab = jnp.zeros((count, block, up_slab), jnp.bfloat16)
    arrived = jnp.zeros((count, part, width), jnp.bfloat16)
    for step in range(chips):
        if step:
            held = seq_move(held, -1, 0)
        other = seq_move(held, 0, 1)
        back = ((chip - step) % chips) * CORES
        ahead = ((chip + step) % chips) * CORES
        for flip, rows in enumerate((held, other)):
            columns = lax.dynamic_slice_in_dim(rows, index * up_slab, up_slab, 1)
            grad_slab = lax.dynamic_update_index_in_dim(grad_slab, columns, back + (core ^ flip), 0)
        sent = chunk_product(held, other, down_weight, group, groups)
        total = sent[0].astype(jnp.float32)
        for flip in range(1, groups):
            total = total + grp_move(sent[flip], flip).astype(jnp.float32)
        total = total.astype(jnp.bfloat16)
        for flip in range(CORES):
            came = total[flip] if step == 0 and flip == 0 else seq_move(total[flip], step, flip)
            arrived = lax.dynamic_update_index_in_dim(arrived, came, ahead + (core ^ flip), 0)
    grad_slab = grad_slab.reshape(count * block, up_slab)

    each = count // groups
    columns_of = [
        lax.dynamic_slice_in_dim(arrived, (group ^ flip) * each, each, 0) for flip in range(groups)
    ]
    base = jnp.zeros((groups, part, each, width), jnp.bfloat16)
    for flip in range(groups):
        came = columns_of[flip] if flip == 0 else grp_move(columns_of[flip], flip)
        base = lax.dynamic_update_index_in_dim(base, came.transpose(1, 0, 2), group ^ flip, 0)
    base = base.reshape(block, -1)

    ranked = jnp.concatenate(
        [project(grad_slab, adapter_up, mask), project(hidden_slab, adapter_down, mask)], axis=1
    )
    devices = count * groups
    share = lax.all_to_all(
        ranked.reshape(devices, -1, 2 * ranks),
        ("grp", "seq"),
        split_axis=0,
        concat_axis=0,
        tiled=True,
    )
    share = jnp.sum(share.astype(jnp.float32), axis=0).astype(jnp.bfloat16)
    ranked = lax.all_to_all(
        jnp.broadcast_to(share[None], (devices,) + share.shape),
        ("grp", "seq"),
        split_axis=0,
        concat_axis=0,
        tiled=True,
    ).reshape(count * block, 2 * ranks)
    grad_rank, act_rank = ranked[:, :ranks], ranked[:, ranks:]

    flat_down = adapter_down.reshape(tenants * ranks, down_slab)
    term = jnp.concatenate(
        [
            jnp.dot(
                spread(grad_rank[at : at + size], mask[at : at + size]),
                flat_down,
                preferred_element_type=jnp.float32,
            )
            for at, size in pieces(count * block)
        ],
        axis=0,
    )
    term = (term * ADAPTER_SCALE).astype(jnp.bfloat16).reshape(count, block, down_slab)
    term = lax.all_to_all(term, "seq", split_axis=0, concat_axis=0, tiled=True)
    term = term.transpose(1, 0, 2).reshape(block, -1)
    grad_hidden = (base.astype(jnp.float32) + term.astype(jnp.float32)).astype(jnp.bfloat16)

    grad_down = adapter_grad(grad_rank, mask, hidden_slab, weights)
    grad_up = adapter_grad(act_rank, mask, grad_slab, weights)
    return grad_hidden, grad_down, grad_up


def solution(mesh):
    placed = (
        P("seq", "grp"),
        P("seq", "grp"),
        P("seq", "grp"),
        P(None, None, ("grp", "seq")),
        P(None, None, ("grp", "seq")),
        P(),
        P(),
    )
    return jax.shard_map(
        shards,
        mesh=mesh,
        in_specs=placed,
        out_specs=(P("seq", "grp"), P(None, None, ("grp", "seq")), P(None, None, ("grp", "seq"))),
        check_vma=False,
    )
```

profile of v0, /device:TPU:0, one launch (start us, length us, event | category | flops | bytes accessed | tf_op | source)
XLA Modules:
  0.0 259.4 jit_solution(3578025946869499862)
XLA Ops:
  6.8 4.5 %all-to-all-start = ((bf16[8,128,896]{2,1,0:T(8,128)(2,1)}), bf16[8,128,896]{2,1,0:T(8,128)(2,1)}, u32[]{:S(2)}, u32[]{:S(2)}) async-start(bf16[8,128,896]{2,1,0:T(8,128)(2,1)} %bitcast.115), calls=%async_computation | async-start | bytes 3670016 | tf_op jit(solution)/shard_map/all_to_all | solution.py:135
  12.3 5.2 %copy-done.2 = bf16[3584,2048]{1,0:T(8,128)(2,1)S(1)} copy-done((bf16[3584,2048]{1,0:T(8,128)(2,1)S(1)}, bf16[3584,2048]{1,0:T(8,128)(2,1)}, u32[]{:S(2)}) %copy-start.2) | copy-done | bytes 14680088
  17.5 6.1 %shard_map.94 = (bf16[2,32,3584]{2,1,0:T(8,128)(2,1)S(1)}, bf16[2,32,3584]{2,1,0:T(8,128)(2,1)}, bf16[2,32,3584]{2,1,0:T(8,128)(2,1)}, bf16[2,32,3584]{2,1,0:T(8,128)(2,1)}) custom-call(s32[1]{0:T(128)} %bitcast.group_ref, bf16[128,2048]{1,0:T(8,128)(2,1)S(1)} %copy-done.4, bf16[128,2048]{1,0:T(8,128)(2,1)S(1)} %collective-permute-done.far_ref, ...), custom_call_target="tpu_custom_call" | custom-call | flops 3758096384 | bytes 17563648 | tf_op jit(solution)/shard_map/pallas_call | solution.py:54
  31.0 7.8 %collective-permute-done.3 = bf16[2,32,3584]{2,1,0:T(8,128)(2,1)S(1)} collective-permute-done((bf16[2,32,3584]{2,1,0:T(8,128)(2,1)}, bf16[2,32,3584]{2,1,0:T(8,128)(2,1)S(1)}, u32[]{:S(2)}, u32[]{:S(2)}) %collective-permute-start.3) | collective-permute-done | bytes 458784 | tf_op jit(solution)/shard_map/ppermute | solution.py:133
  38.8 9.2 %collective-permute-done.2 = bf16[2,32,3584]{2,1,0:T(8,128)(2,1)} collective-permute-done((bf16[2,32,3584]{2,1,0:T(8,128)(2,1)}, bf16[2,32,3584]{2,1,0:T(8,128)(2,1)}, u32[]{:S(2)}, u32[]{:S(2)}) %collective-permute-start.2) | collective-permute-done | bytes 458784 | tf_op jit(solution)/shard_map/ppermute | solution.py:133
  51.8 5.2 %copy-done.3 = bf16[3584,2048]{1,0:T(8,128)(2,1)S(1)} copy-done((bf16[3584,2048]{1,0:T(8,128)(2,1)S(1)}, bf16[3584,2048]{1,0:T(8,128)(2,1)}, u32[]{:S(2)}) %copy-start.3) | copy-done | bytes 14680088
  56.9 5.4 %shard_map.95 = (bf16[2,32,3584]{2,1,0:T(8,128)(2,1)S(1)}, bf16[2,32,3584]{2,1,0:T(8,128)(2,1)S(1)}, bf16[2,32,3584]{2,1,0:T(8,128)(2,1)S(1)}, bf16[2,32,3584]{2,1,0:T(8,128)(2,1)S(1)}) custom-call(s32[1]{0:T(128)} %bitcast.group_ref, bf16[128,2048]{1,0:T(8,128)(2,1)S(1)} %collective-permute-done.5.near_ref, ...), custom_call_target="tpu_custom_call" | custom-call | flops 3758096384 | bytes 17563648 | tf_op jit(solution)/shard_map/pallas_call | solution.py:54
  68.8 7.9 %collective-permute-done.9 = bf16[2,32,3584]{2,1,0:T(8,128)(2,1)S(1)} collective-permute-done((bf16[2,32,3584]{2,1,0:T(8,128)(2,1)S(1)}, bf16[2,32,3584]{2,1,0:T(8,128)(2,1)S(1)}, u32[]{:S(2)}, u32[]{:S(2)}) %collective-permute-start.9) | collective-permute-done | bytes 458784 | tf_op jit(solution)/shard_map/ppermute | solution.py:133
  76.7 9.4 %collective-permute-done.8 = bf16[2,32,3584]{2,1,0:T(8,128)(2,1)S(1)} collective-permute-done((bf16[2,32,3584]{2,1,0:T(8,128)(2,1)S(1)}, bf16[2,32,3584]{2,1,0:T(8,128)(2,1)S(1)}, u32[]{:S(2)}, u32[]{:S(2)}) %collective-permute-start.8) | collective-permute-done | bytes 458784 | tf_op jit(solution)/shard_map/ppermute | solution.py:133
  89.9 5.4 %shard_map.96 = (bf16[2,32,3584]{2,1,0:T(8,128)(2,1)S(1)}, bf16[2,32,3584]{2,1,0:T(8,128)(2,1)S(1)}, bf16[2,32,3584]{2,1,0:T(8,128)(2,1)S(1)}, bf16[2,32,3584]{2,1,0:T(8,128)(2,1)S(1)}) custom-call(s32[1]{0:T(128)} %bitcast.group_ref, bf16[128,2048]{1,0:T(8,128)(2,1)S(1)} %collective-permute-done.12.near_ref, ...), custom_call_target="tpu_custom_call" | custom-call | flops 3758096384 | bytes 17563648 | tf_op jit(solution)/shard_map/pallas_call | solution.py:54
  100.6 9.2 %collective-permute-done.16 = bf16[2,32,3584]{2,1,0:T(8,128)(2,1)S(1)} collective-permute-done((bf16[2,32,3584]{2,1,0:T(8,128)(2,1)S(1)}, bf16[2,32,3584]{2,1,0:T(8,128)(2,1)S(1)}, u32[]{:S(2)}, u32[]{:S(2)}) %collective-permute-start.16) | collective-permute-done | bytes 458784 | tf_op jit(solution)/shard_map/ppermute | solution.py:133
  109.8 9.5 %collective-permute-done.15 = bf16[2,32,3584]{2,1,0:T(8,128)(2,1)S(1)} collective-permute-done((bf16[2,32,3584]{2,1,0:T(8,128)(2,1)S(1)}, bf16[2,32,3584]{2,1,0:T(8,128)(2,1)S(1)}, u32[]{:S(2)}, u32[]{:S(2)}) %collective-permute-start.15) | collective-permute-done | bytes 458784 | tf_op jit(solution)/shard_map/ppermute | solution.py:133
  122.6 6.1 %shard_map.97 = (bf16[2,32,3584]{2,1,0:T(8,128)(2,1)S(1)}, bf16[2,32,3584]{2,1,0:T(8,128)(2,1)}, bf16[2,32,3584]{2,1,0:T(8,128)(2,1)}, bf16[2,32,3584]{2,1,0:T(8,128)(2,1)}) custom-call(s32[1]{0:T(128)} %bitcast.group_ref, bf16[128,2048]{1,0:T(8,128)(2,1)S(1)} %collective-permute-done.19.near_ref, bf16[128,2048]{1,0:T(8,128)(2,1)S(1)} %collective-permute-done.20.far_ref, ...), custom_call_target="tpu_custom_call" | custom-call | flops 3758096384 | bytes 17563648 | tf_op jit(solution)/shard_map/pallas_call | solution.py:54
  133.9 5.9 %collective-permute-done.17 = bf16[32,3584]{1,0:T(8,128)(2,1)} collective-permute-done((bf16[32,3584]{1,0:T(8,128)(2,1)}, bf16[32,3584]{1,0:T(8,128)(2,1)}, u32[]{:S(2)}, u32[]{:S(2)}) %collective-permute-start.17) | collective-permute-done | bytes 229408 | tf_op jit(solution)/shard_map/ppermute | solution.py:130
  143.3 9.6 %collective-permute-done.22 = bf16[2,32,3584]{2,1,0:T(8,128)(2,1)} collective-permute-done((bf16[2,32,3584]{2,1,0:T(8,128)(2,1)}, bf16[2,32,3584]{2,1,0:T(8,128)(2,1)}, u32[]{:S(2)}, u32[]{:S(2)}) %collective-permute-start.22) | collective-permute-done | bytes 458784 | tf_op jit(solution)/shard_map/ppermute | solution.py:133
  157.6 7.1 %collective-permute-done.24 = bf16[32,3584]{1,0:T(8,128)(2,1)S(1)} collective-permute-done((bf16[32,3584]{1,0:T(8,128)(2,1)S(1)}, bf16[32,3584]{1,0:T(8,128)(2,1)S(1)}, u32[]{:S(2)}, u32[]{:S(2)}) %collective-permute-start.24) | collective-permute-done | bytes 229408 | tf_op jit(solution)/shard_map/ppermute | solution.py:130
  165.5 3.9 %multiply_reduce_fusion = bf16[1024,64]{0,1:T(8,128)(2,1)S(1)} fusion(f32[1024,16]{0,1:T(8,128)S(1)} %get-tuple-element.49, bf16[1024,896,1]{1,0,2:T(8,128)(2,1)} %bitcast.37, bf16[16,64,896]{2,1,0:T(8,128)(2,1)S(1)} %copy-done), kind=kOutput, calls=%fused_computation | convolution fusion | flops 1881079808 | bytes 3866624 | tf_op jit(solution)/shard_map/dot_general | solution.py:18
  179.7 3.7 %all-to-all-done.1 = bf16[32,32,128]{2,1,0:T(8,128)(2,1)S(1)} async-done(((bf16[32,32,128]{2,1,0:T(8,128)(2,1)}), bf16[32,32,128]{2,1,0:T(8,128)(2,1)S(1)}, u32[]{:S(2)}, u32[]{:S(2)}) %all-to-all-start.1) | async-done | bytes 262176 | tf_op jit(solution)/shard_map/all_to_all | solution.py:179
  190.3 13.6 %all-to-all-done.2 = bf16[32,32,128]{2,1,0:T(8,128)(2,1)S(1)} async-done(((bf16[32,32,128]{2,1,0:T(8,128)(2,1)}), bf16[32,32,128]{2,1,0:T(8,128)(2,1)S(1)}, u32[]{:S(2)}, u32[]{:S(2)}) %all-to-all-start.2) | async-done | bytes 262176 | tf_op jit(solution)/shard_map/all_to_all | solution.py:187
  204.2 3.6 %fusion = bf16[1024,896]{1,0:T(8,128)(2,1)} fusion(bf16[16,64,896]{2,1,0:T(8,128)(2,1)S(1)} %copy-done, bf16[1024,16]{0,1:T(8,128)(2,1)S(1)} %get-tuple-element.50, bf16[1024,64]{0,1:T(8,128)(2,1)S(1)} %copy.65), kind=kOutput, calls=%fused_computation.3 | convolution fusion | flops 1881931776 | bytes 3833856 | tf_op jit(solution)/shard_map/dot_general | solution.py:199
  207.8 3.9 %all-to-all-start.3 = ((bf16[8,128,896]{2,1,0:T(8,128)(2,1)}), bf16[8,128,896]{2,1,0:T(8,128)(2,1)S(1)}, u32[]{:S(2)}, u32[]{:S(2)}) async-start(bf16[8,128,896]{2,1,0:T(8,128)(2,1)} %bitcast.118), calls=%async_computation.3 | async-start | bytes 3670016 | tf_op jit(solution)/shard_map/all_to_all | solution.py:209
  218.5 3.8 %copy.70 = f32[16,8,2,3584]{3,1,2,0:T(8,128)} copy(bf16[16,8,2,3584]{3,2,1,0:T(2,128)(2,1)} %bitcast.103) | data formatting | bytes 5505024
  224.2 5.7 %fusion.7 = f32[16,64,896]{2,1,0:T(8,128)} fusion(bf16[1024,896,1]{1,0,2:T(8,128)(2,1)} %bitcast.37, f32[16]{0:T(128)S(1)} %broadcast_divide_fusion, bf16[1024,16]{0,1:T(8,128)(2,1)S(1)} %get-tuple-element.50, bf16[1024,64]{0,1:T(8,128)(2,1)S(1)} %copy.65), kind=kOutput, calls=%fused_computation.13 | convolution fusion | flops 1881014272 | bytes 5668928 | tf_op jit(solution)/shard_map/dot_general | solution.py:18
  229.9 25.3 %all-to-all-done.3 = bf16[8,128,896]{2,1,0:T(8,128)(2,1)S(1)} async-done(((bf16[8,128,896]{2,1,0:T(8,128)(2,1)}), bf16[8,128,896]{2,1,0:T(8,128)(2,1)S(1)}, u32[]{:S(2)}, u32[]{:S(2)}) %all-to-all-start.3) | async-done | bytes 1835040 | tf_op jit(solution)/shard_map/all_to_all | solution.py:209
  (129 shorter events, 81.4 us)
Async XLA Ops:
  1.2 26.7 %collective-permute-start.5 = (bf16[128,2048]{1,0:T(8,128)(2,1)}, bf16[128,2048]{1,0:T(8,128)(2,1)S(1)}, u32[]{:S(2)}, u32[]{:S(2)}) collective-permute-start(bf16[128,2048]{1,0:T(8,128)(2,1)} %near_ref.1), channel_id=1, source_target_pairs={{0,2},{1,3},{2,4},{3,5},{4,6},{5,7},{6,0},{7,1},{8,10},{9,11},{10,... | collective-permute-start | bytes 1572872 | tf_op jit(solution)/shard_map/ppermute | solution.py:130
  6.8 158.7 %all-to-all-start = ((bf16[8,128,896]{2,1,0:T(8,128)(2,1)}), bf16[8,128,896]{2,1,0:T(8,128)(2,1)}, u32[]{:S(2)}, u32[]{:S(2)}) async-start(bf16[8,128,896]{2,1,0:T(8,128)(2,1)} %bitcast.115), calls=%async_computation | async-start | bytes 3670016 | tf_op jit(solution)/shard_map/all_to_all | solution.py:135
  26.8 21.2 %collective-permute-start.2 = (bf16[2,32,3584]{2,1,0:T(8,128)(2,1)}, bf16[2,32,3584]{2,1,0:T(8,128)(2,1)}, u32[]{:S(2)}, u32[]{:S(2)}) collective-permute-start(bf16[2,32,3584]{2,1,0:T(8,128)(2,1)} %get-tuple-element.21), channel_id=1, source_target_pairs={{0,16},{8,24},{16,0},{24,8},{1,17},{9,25},{17,1},{25,9},{2,18},{10... | collective-permute-start | bytes 1376264 | tf_op jit(solution)/shard_map/ppermute | solution.py:133
  27.3 20.8 %collective-permute-start.1 = (bf16[2,32,3584]{2,1,0:T(8,128)(2,1)}, bf16[2,32,3584]{2,1,0:T(8,128)(2,1)}, u32[]{:S(2)}, u32[]{:S(2)}) collective-permute-start(bf16[2,32,3584]{2,1,0:T(8,128)(2,1)} %get-tuple-element.20), channel_id=1, source_target_pairs={{0,8},{8,0},{16,24},{24,16},{1,9},{9,1},{17,25},{25,17},{2,10},{10... | collective-permute-start | bytes 1376264 | tf_op jit(solution)/shard_map/ppermute | solution.py:133
  27.8 23.9 %collective-permute-start.6 = (bf16[128,2048]{1,0:T(8,128)(2,1)S(1)}, bf16[128,2048]{1,0:T(8,128)(2,1)S(1)}, u32[]{:S(2)}, u32[]{:S(2)}) collective-permute-start(bf16[128,2048]{1,0:T(8,128)(2,1)S(1)} %collective-permute-done.5.near_ref), channel_id=1, source_target_pairs={{0,1},{1,0},{2,3},{3,2},{4,5},{5,4},{6,7},{7,6},{8,9},{9,8},{10,11... | collective-permute-start | bytes 1572872 | tf_op jit(solution)/shard_map/ppermute | solution.py:130
  27.9 38.0 %collective-permute-start.12 = (bf16[128,2048]{1,0:T(8,128)(2,1)S(1)}, bf16[128,2048]{1,0:T(8,128)(2,1)S(1)}, u32[]{:S(2)}, u32[]{:S(2)}) collective-permute-start(bf16[128,2048]{1,0:T(8,128)(2,1)S(1)} %collective-permute-done.5.near_ref), channel_id=1, source_target_pairs={{0,2},{1,3},{2,4},{3,5},{4,6},{5,7},{6,0},{7,1},{8,10},{9,11},{10,... | collective-permute-start | bytes 1572872 | tf_op jit(solution)/shard_map/ppermute | solution.py:130
  64.1 22.0 %collective-permute-start.8 = (bf16[2,32,3584]{2,1,0:T(8,128)(2,1)S(1)}, bf16[2,32,3584]{2,1,0:T(8,128)(2,1)S(1)}, u32[]{:S(2)}, u32[]{:S(2)}) collective-permute-start(bf16[2,32,3584]{2,1,0:T(8,128)(2,1)S(1)} %get-tuple-element.25), channel_id=1, source_target_pairs={{0,16},{8,24},{16,0},{24,8},{1,17},{9,25},{17,1},{25,9},{2,18},{10... | collective-permute-start | bytes 1376264 | tf_op jit(solution)/shard_map/ppermute | solution.py:133
  65.4 20.7 %collective-permute-start.7 = (bf16[2,32,3584]{2,1,0:T(8,128)(2,1)S(1)}, bf16[2,32,3584]{2,1,0:T(8,128)(2,1)S(1)}, u32[]{:S(2)}, u32[]{:S(2)}) collective-permute-start(bf16[2,32,3584]{2,1,0:T(8,128)(2,1)S(1)} %get-tuple-element.24), channel_id=1, source_target_pairs={{0,8},{8,0},{16,24},{24,16},{1,9},{9,1},{17,25},{25,17},{2,10},{10... | collective-permute-start | bytes 1376264 | tf_op jit(solution)/shard_map/ppermute | solution.py:133
  65.9 24.0 %collective-permute-start.13 = (bf16[128,2048]{1,0:T(8,128)(2,1)S(1)}, bf16[128,2048]{1,0:T(8,128)(2,1)S(1)}, u32[]{:S(2)}, u32[]{:S(2)}) collective-permute-start(bf16[128,2048]{1,0:T(8,128)(2,1)S(1)} %collective-permute-done.12.near_ref), channel_id=1, source_target_pairs={{0,1},{1,0},{2,3},{3,2},{4,5},{5,4},{6,7},{7,6},{8,9},{9,8},{10,11... | collective-permute-start | bytes 1572872 | tf_op jit(solution)/shard_map/ppermute | solution.py:130
  66.0 32.4 %collective-permute-start.19 = (bf16[128,2048]{1,0:T(8,128)(2,1)S(1)}, bf16[128,2048]{1,0:T(8,128)(2,1)S(1)}, u32[]{:S(2)}, u32[]{:S(2)}) collective-permute-start(bf16[128,2048]{1,0:T(8,128)(2,1)S(1)} %collective-permute-done.12.near_ref), channel_id=1, source_target_pairs={{0,2},{1,3},{2,4},{3,5},{4,6},{5,7},{6,0},{7,1},{8,10},{9,11},{10,... | collective-permute-start | bytes 1572872 | tf_op jit(solution)/shard_map/ppermute | solution.py:130
  97.1 22.2 %collective-permute-start.15 = (bf16[2,32,3584]{2,1,0:T(8,128)(2,1)S(1)}, bf16[2,32,3584]{2,1,0:T(8,128)(2,1)S(1)}, u32[]{:S(2)}, u32[]{:S(2)}) collective-permute-start(bf16[2,32,3584]{2,1,0:T(8,128)(2,1)S(1)} %get-tuple-element.29), channel_id=1, source_target_pairs={{0,16},{8,24},{16,0},{24,8},{1,17},{9,25},{17,1},{25,9},{2,18},{10... | collective-permute-start | bytes 1376264 | tf_op jit(solution)/shard_map/ppermute | solution.py:133
  98.4 20.8 %collective-permute-start.14 = (bf16[2,32,3584]{2,1,0:T(8,128)(2,1)S(1)}, bf16[2,32,3584]{2,1,0:T(8,128)(2,1)S(1)}, u32[]{:S(2)}, u32[]{:S(2)}) collective-permute-start(bf16[2,32,3584]{2,1,0:T(8,128)(2,1)S(1)} %get-tuple-element.28), channel_id=1, source_target_pairs={{0,8},{8,0},{16,24},{24,16},{1,9},{9,1},{17,25},{25,17},{2,10},{10... | collective-permute-start | bytes 1376264 | tf_op jit(solution)/shard_map/ppermute | solution.py:133
  99.1 23.5 %collective-permute-start.20 = (bf16[128,2048]{1,0:T(8,128)(2,1)S(1)}, bf16[128,2048]{1,0:T(8,128)(2,1)S(1)}, u32[]{:S(2)}, u32[]{:S(2)}) collective-permute-start(bf16[128,2048]{1,0:T(8,128)(2,1)S(1)} %collective-permute-done.19.near_ref), channel_id=1, source_target_pairs={{0,1},{1,0},{2,3},{3,2},{4,5},{5,4},{6,7},{7,6},{8,9},{9,8},{10,11... | collective-permute-start | bytes 1572872 | tf_op jit(solution)/shard_map/ppermute | solution.py:130
  120.3 19.5 %collective-permute-start.17 = (bf16[32,3584]{1,0:T(8,128)(2,1)}, bf16[32,3584]{1,0:T(8,128)(2,1)}, u32[]{:S(2)}, u32[]{:S(2)}) collective-permute-start(bf16[32,3584]{1,0:T(8,128)(2,1)} %get-tuple-element.42), channel_id=1, source_target_pairs={{0,4},{1,5},{2,6},{3,7},{4,0},{5,1},{6,2},{7,3},{8,12},{9,13},{10,... | collective-permute-start | bytes 688136 | tf_op jit(solution)/shard_map/ppermute | solution.py:130
  120.3 35.7 %collective-permute-start.18 = (bf16[32,3584]{1,0:T(8,128)(2,1)}, bf16[32,3584]{1,0:T(8,128)(2,1)}, u32[]{:S(2)}, u32[]{:S(2)}) collective-permute-start(bf16[32,3584]{1,0:T(8,128)(2,1)} %get-tuple-element.41), channel_id=1, source_target_pairs={{0,5},{1,4},{2,7},{3,6},{4,1},{5,0},{6,3},{7,2},{8,13},{9,12},{10,... | collective-permute-start | bytes 688136 | tf_op jit(solution)/shard_map/ppermute | solution.py:130
  128.7 14.6 %collective-permute-start.23 = (bf16[2,32,3584]{2,1,0:T(8,128)(2,1)}, bf16[2,32,3584]{2,1,0:T(8,128)(2,1)}, u32[]{:S(2)}, u32[]{:S(2)}) collective-permute-start(bf16[2,32,3584]{2,1,0:T(8,128)(2,1)} %get-tuple-element.34), channel_id=1, source_target_pairs={{0,24},{8,16},{16,8},{24,0},{1,25},{9,17},{17,9},{25,1},{2,26},{10... | collective-permute-start | bytes 1376264 | tf_op jit(solution)/shard_map/ppermute | solution.py:133
  130.3 22.6 %collective-permute-start.22 = (bf16[2,32,3584]{2,1,0:T(8,128)(2,1)}, bf16[2,32,3584]{2,1,0:T(8,128)(2,1)}, u32[]{:S(2)}, u32[]{:S(2)}) collective-permute-start(bf16[2,32,3584]{2,1,0:T(8,128)(2,1)} %get-tuple-element.33), channel_id=1, source_target_pairs={{0,16},{8,24},{16,0},{24,8},{1,17},{9,25},{17,1},{25,9},{2,18},{10... | collective-permute-start | bytes 1376264 | tf_op jit(solution)/shard_map/ppermute | solution.py:133
  131.7 21.3 %collective-permute-start.21 = (bf16[2,32,3584]{2,1,0:T(8,128)(2,1)}, bf16[2,32,3584]{2,1,0:T(8,128)(2,1)}, u32[]{:S(2)}, u32[]{:S(2)}) collective-permute-start(bf16[2,32,3584]{2,1,0:T(8,128)(2,1)} %get-tuple-element.32), channel_id=1, source_target_pairs={{0,8},{8,0},{16,24},{24,16},{1,9},{9,1},{17,25},{25,17},{2,10},{10... | collective-permute-start | bytes 1376264 | tf_op jit(solution)/shard_map/ppermute | solution.py:133
  157.6 15.3 %collective-permute-start.25 = (bf16[32,3584]{1,0:T(8,128)(2,1)S(1)}, bf16[32,3584]{1,0:T(8,128)(2,1)S(1)}, u32[]{:S(2)}, u32[]{:S(2)}) collective-permute-start(bf16[32,3584]{1,0:T(8,128)(2,1)S(1)} %get-tuple-element.39), channel_id=1, source_target_pairs={{0,3},{1,2},{2,5},{3,4},{4,7},{5,6},{6,1},{7,0},{8,11},{9,10},{10,... | collective-permute-start | bytes 688136 | tf_op jit(solution)/shard_map/ppermute | solution.py:130
  176.2 35.6 %collective-permute-start.26 = (bf16[2,32,3584]{2,1,0:T(8,128)(2,1)}, bf16[2,32,3584]{2,1,0:T(8,128)(2,1)}, u32[]{:S(2)}, u32[]{:S(2)}) collective-permute-start(bf16[2,32,3584]{2,1,0:T(8,128)(2,1)} %get-tuple-element.37), channel_id=1, source_target_pairs={{0,8},{8,0},{16,24},{24,16},{1,9},{9,1},{17,25},{25,17},{2,10},{10... | collective-permute-start | bytes 1376264 | tf_op jit(solution)/shard_map/ppermute | solution.py:133
  177.8 36.2 %collective-permute-start.27 = (bf16[2,32,3584]{2,1,0:T(8,128)(2,1)}, bf16[2,32,3584]{2,1,0:T(8,128)(2,1)}, u32[]{:S(2)}, u32[]{:S(2)}) collective-permute-start(bf16[2,32,3584]{2,1,0:T(8,128)(2,1)} %get-tuple-element.36), channel_id=1, source_target_pairs={{0,16},{8,24},{16,0},{24,8},{1,17},{9,25},{17,1},{25,9},{2,18},{10... | collective-permute-start | bytes 1376264 | tf_op jit(solution)/shard_map/ppermute | solution.py:133
  179.3 37.0 %collective-permute-start.28 = (bf16[2,32,3584]{2,1,0:T(8,128)(2,1)S(1)}, bf16[2,32,3584]{2,1,0:T(8,128)(2,1)}, u32[]{:S(2)}, u32[]{:S(2)}) collective-permute-start(bf16[2,32,3584]{2,1,0:T(8,128)(2,1)S(1)} %get-tuple-element.35), channel_id=1, source_target_pairs={{0,24},{8,16},{16,8},{24,0},{1,25},{9,17},{17,9},{25,1},{2,26},{10... | collective-permute-start | bytes 1376264 | tf_op jit(solution)/shard_map/ppermute | solution.py:133
  184.2 19.8 %all-to-all-start.2 = ((bf16[32,32,128]{2,1,0:T(8,128)(2,1)}), bf16[32,32,128]{2,1,0:T(8,128)(2,1)S(1)}, u32[]{:S(2)}, u32[]{:S(2)}) async-start(bf16[32,32,128]{2,1,0:T(8,128)(2,1)} %broadcast_in_dim.130), calls=%async_computation.2 | async-start | bytes 524288 | tf_op jit(solution)/shard_map/all_to_all | solution.py:187
  207.8 47.4 %all-to-all-start.3 = ((bf16[8,128,896]{2,1,0:T(8,128)(2,1)}), bf16[8,128,896]{2,1,0:T(8,128)(2,1)S(1)}, u32[]{:S(2)}, u32[]{:S(2)}) async-start(bf16[8,128,896]{2,1,0:T(8,128)(2,1)} %bitcast.118), calls=%async_computation.3 | async-start | bytes 3670016 | tf_op jit(solution)/shard_map/all_to_all | solution.py:209
  (23 other events, 335.8 us)
where the time goes:
time: 260 us; the launch traced here: 259 us
  waiting for transfers between devices  120 us (46%)
  local copies, waits for them, and re-layouts  47 us (18%)
  starting transfers between devices  46 us (18%)
  Pallas kernels  23 us (9%)
  matrix products  15.6 us (6%)
  other arithmetic  6.48 us (2%)
    ppermute x15, waiting for transfers between devices, grp_move(): return lax.ppermute(value, 'grp', [(g, g ^ flip) for g in range(groups)])  64.5 us
    all_to_all x1, waiting for transfers between devices, shards(): term = lax.all_to_all(term, 'seq', split_axis=0, concat_axis=0, tiled=True)  25.3 us
    pallas_call x4, Pallas kernels, chunk_product(): pl.pallas_call(functools.partial(chunk_kernel, groups), grid_spec=pltpu.P...  23 us
    unnamed x29, local copies, waits for them, and re-layouts  18.3 us
    ppermute x15, starting transfers between devices, grp_move(): return lax.ppermute(value, 'grp', [(g, g ^ flip) for g in range(groups)])  17.7 us
    ppermute x14, starting transfers between devices, seq_move(): return lax.ppermute(value, 'seq', pairs)  14.6 us
    all_to_all x1, waiting for transfers between devices, shards(): lax.all_to_all(jnp.broadcast_to(share[None], (devices,) + share.shape), (...  13.6 us
    ppermute x14, waiting for transfers between devices, seq_move(): return lax.ppermute(value, 'seq', pairs)  13.1 us
  transfers between devices with their start and end apart: 33, of which 15 were waited for; matrix products, arithmetic and copies ran while one was open for 20% of the time, Pallas kernels for 9%

commit v1 on v0

--- a/solution.py
+++ b/solution.py
@@ -24,47 +24,49 @@
 
 
 def tile_of(width):
-    return next(tile for tile in (512, 448, 384, 256, 128, width) if width % tile == 0 and tile % 128 == 0 or tile == width)
-
-
-def chunk_kernel(groups, group_ref, near_ref, far_ref, weight_ref, *rest):
-    outs, rows = rest[:groups], rest[groups]
-    part = near_ref.shape[0] // groups
+    fits = [tile for tile in (512, 448, 384, 256, 128) if width % tile == 0 and tile % 128 == 0]
+    return fits[0] if fits else width
+
+
+def chunk_kernel(stages, place_ref, near_ref, far_ref, weight_ref, *rest):
+    outs, rows = rest[:-1], rest[-1]
+    part = near_ref.shape[0] // (2 * len(stages))
+    sides = [(ref, flips) for ref, order in zip((near_ref, far_ref), stages) for flips in order]
+    cuts = [(ref, flip) for ref, flips in sides for flip in flips]
 
     @pl.when(pl.program_id(0) == 0)
     def _():
-        for flip in range(groups):
-            at = pl.multiple_of((group_ref[0] ^ flip) * part, part)
-            low = flip * CORES * part
-            rows[low : low + part] = near_ref[pl.ds(at, part)]
-            rows[low + part : low + 2 * part] = far_ref[pl.ds(at, part)]
+        for at, (ref, flip) in enumerate(cuts):
+            low = pl.multiple_of((place_ref[0] ^ flip) * part, part)
+            rows[at * part : (at + 1) * part] = ref[pl.ds(low, part)]
 
     full = dot(rows[...], weight_ref[...], CONTRACT_LAST).astype(jnp.bfloat16)
-    for flip in range(groups):
-        for core in range(CORES):
-            low = (flip * CORES + core) * part
-            outs[flip][core] = full[low : low + part]
-
-
-def chunk_product(near, far, weight, group, groups):
+    for at in range(len(cuts)):
+        outs[at // 2][at % 2] = full[at * part : (at + 1) * part]
+
+
+STAGES = (((0, 2), (1, 3)), ((0, 1), (2, 3)))
+
+
+def chunk_product(near, far, weight, group):
     block, depth = near.shape
     width = weight.shape[0]
     tile = tile_of(width)
-    part = block // groups
+    part = block // (2 * len(STAGES))
     return pl.pallas_call(
-        functools.partial(chunk_kernel, groups),
+        functools.partial(chunk_kernel, STAGES),
         grid_spec=pltpu.PrefetchScalarGridSpec(
             num_scalar_prefetch=1,
             grid=(width // tile,),
             in_specs=[
-                pl.BlockSpec((block, depth), lambda at, group: (0, 0)),
-                pl.BlockSpec((block, depth), lambda at, group: (0, 0)),
-                pl.BlockSpec((tile, depth), lambda at, group: (at, 0)),
+                pl.BlockSpec((block, depth), lambda at, place: (0, 0)),
+                pl.BlockSpec((block, depth), lambda at, place: (0, 0)),
+                pl.BlockSpec((tile, depth), lambda at, place: (at, 0)),
             ],
-            out_specs=[pl.BlockSpec((CORES, part, tile), lambda at, group: (0, 0, at))] * groups,
+            out_specs=[pl.BlockSpec((2, part, tile), lambda at, place: (0, 0, at))] * 4,
             scratch_shapes=[pltpu.VMEM((CORES * block, depth), jnp.bfloat16)],
         ),
-        out_shape=[jax.ShapeDtypeStruct((CORES, part, width), jnp.bfloat16)] * groups,
+        out_shape=[jax.ShapeDtypeStruct((2, part, width), jnp.bfloat16)] * 4,
         compiler_params=pltpu.CompilerParams(vmem_limit_bytes=24 << 20),
         cost_estimate=pl.CostEstimate(
             flops=2 * CORES * block * depth * width,
@@ -72,6 +74,54 @@
             transcendentals=0,
         ),
     )(group.reshape(1), near, far, weight)
+
+
+def join_kernel(groups, slab, place_ref, *refs):
+    bases, term_ref, out_ref = refs[:groups], refs[groups], refs[groups + 1]
+    width = bases[0].shape[2]
+    for flip in range(groups):
+
+        @pl.when(pl.program_id(0) == flip)
+        def _():
+            for at in range(term_ref.shape[0]):
+                low = at * slab
+                base = bases[flip][low // width, :, low % width : low % width + slab]
+                total = base.astype(jnp.float32) + term_ref[at].astype(jnp.float32)
+                out_ref[:, low : low + slab] = total.astype(jnp.bfloat16)
+
+
+def join(bases, term, group):
+    groups = len(bases)
+    each, part, width = bases[0].shape
+    count, block, slab = term.shape
+    if slab % 128:
+        base = jnp.zeros((groups, part, each, width), jnp.bfloat16)
+        for flip, rows in enumerate(bases):
+            base = lax.dynamic_update_index_in_dim(base, rows.transpose(1, 0, 2), group ^ flip, 0)
+        total = base.reshape(block, -1).astype(jnp.float32)
+        return (total + term.transpose(1, 0, 2).reshape(block, -1)).astype(jnp.bfloat16)
+    return pl.pallas_call(
+        functools.partial(join_kernel, groups, slab),
+        grid_spec=pltpu.PrefetchScalarGridSpec(
+            num_scalar_prefetch=1,
+            grid=(groups,),
+            in_specs=[pl.BlockSpec((each, part, width), lambda at, place: (0, 0, 0))] * groups
+            + [pl.BlockSpec((count, part, slab), lambda at, place: (0, place[0] ^ at, 0))],
+            out_specs=pl.BlockSpec((part, each * width), lambda at, place: (place[0] ^ at, 0)),
+        ),
+        out_shape=jax.ShapeDtypeStruct((block, each * width), jnp.bfloat16),
+        cost_estimate=pl.CostEstimate(
+            flops=block * each * width, bytes_accessed=6 * block * each * width, transcendentals=0
+        ),
+    )(group.reshape(1), *bases, term)
+
+
+def add(*terms):
+    return sum(term.astype(jnp.float32) for term in terms).astype(jnp.bfloat16)
+
+
+def after(value, *others):
+    return lax.optimization_barrier((value,) + others)[0]
 
 
 def project(rows, adapter, mask):
@@ -132,6 +182,11 @@
     def grp_move(value, flip):
         return lax.ppermute(value, "grp", [(g, g ^ flip) for g in range(groups)])
 
+    held = [grad_output]
+    for step in range(1, chips):
+        held.append(seq_move(held[-1], -1, 0))
+    pairs = [(near, seq_move(near, 0, 1)) for near in held]
+
     hidden_slab = lax.all_to_all(
         hidden.reshape(block, count, down_slab).transpose(1, 0, 2),
         "seq",
@@ -140,40 +195,64 @@
         tiled=True,
     ).reshape(count * block, down_slab)
 
-    held = grad_output
+    last = chips - 1
+    products = [chunk_product(near, far, down_weight, group) for near, far in pairs]
+    firsts = [
+        (grp_move(near_sent, 1), grp_move(far_sent, 2)) for _, near_sent, _, far_sent in products
+    ]
     grad_slab = jnp.zeros((count, block, up_slab), jnp.bfloat16)
-    arrived = jnp.zeros((count, part, width), jnp.bfloat16)
-    for step in range(chips):
-        if step:
-            held = seq_move(held, -1, 0)
-        other = seq_move(held, 0, 1)
+    for step, pair in enumerate(pairs):
         back = ((chip - step) % chips) * CORES
-        ahead = ((chip + step) % chips) * CORES
-        for flip, rows in enumerate((held, other)):
+        for flip, rows in enumerate(pair):
             columns = lax.dynamic_slice_in_dim(rows, index * up_slab, up_slab, 1)
             grad_slab = lax.dynamic_update_index_in_dim(grad_slab, columns, back + (core ^ flip), 0)
-        sent = chunk_product(held, other, down_weight, group, groups)
-        total = sent[0].astype(jnp.float32)
-        for flip in range(1, groups):
-            total = total + grp_move(sent[flip], flip).astype(jnp.float32)
-        total = total.astype(jnp.bfloat16)
+    grad_slab = grad_slab.reshape(count * block, up_slab)
+
+    def second(step, *gates):
+        near_kept, _, far_kept, _ = products[step]
+        near_came, far_came = firsts[step]
+        near_came, far_came = lax.optimization_barrier((near_came, far_came) + gates)[:2]
+        near_sum = add(near_kept[1], near_came[1])
+        far_sum = add(far_kept[1], far_came[1])
+        return near_sum, (grp_move(near_sum, 2), grp_move(far_sum, 1))
+
+    def total(step, seconds, *gates):
+        near_kept, _, far_kept, _ = products[step]
+        near_came, far_came = firsts[step]
+        near_last, far_last = lax.optimization_barrier(seconds + gates)[:2]
+        return (
+            add(near_kept[0], near_came[0], near_last),
+            add(far_kept[0], far_came[0], far_last),
+        )
+
+    arrived = jnp.zeros((count, part, width), jnp.bfloat16)
+
+    def hop(step, sums):
+        return [
+            sums[flip] if step == 0 and flip == 0 else seq_move(sums[flip], step, flip)
+            for flip in range(CORES)
+        ]
+
+    def put(arrived, step, came, *gates):
+        ahead = ((chip + step) % chips) * CORES
+        came = lax.optimization_barrier(tuple(came) + gates)
         for flip in range(CORES):
-            came = total[flip] if step == 0 and flip == 0 else seq_move(total[flip], step, flip)
-            arrived = lax.dynamic_update_index_in_dim(arrived, came, ahead + (core ^ flip), 0)
-    grad_slab = grad_slab.reshape(count * block, up_slab)
-
-    each = count // groups
-    columns_of = [
-        lax.dynamic_slice_in_dim(arrived, (group ^ flip) * each, each, 0) for flip in range(groups)
-    ]
-    base = jnp.zeros((groups, part, each, width), jnp.bfloat16)
-    for flip in range(groups):
-        came = columns_of[flip] if flip == 0 else grp_move(columns_of[flip], flip)
-        base = lax.dynamic_update_index_in_dim(base, came.transpose(1, 0, 2), group ^ flip, 0)
-    base = base.reshape(block, -1)
-
+            arrived = lax.dynamic_update_index_in_dim(arrived, came[flip], ahead + (core ^ flip), 0)
+        return arrived
+
+    came = None
+    for step in range(last - 1):
+        _, seconds = second(step, products[step + 1][0])
+        sums = total(step, seconds)
+        if came is not None:
+            arrived = put(arrived, step - 1, came, sums[0])
+        came = hop(step, sums)
+
+    begun, seconds = second(last - 1, products[last][0])
+    rows_here = lax.optimization_barrier((grad_slab, hidden_slab, begun))
     ranked = jnp.concatenate(
-        [project(grad_slab, adapter_up, mask), project(hidden_slab, adapter_down, mask)], axis=1
+        [project(rows_here[0], adapter_up, mask), project(rows_here[1], adapter_down, mask)],
+        axis=1,
     )
     devices = count * groups
     share = lax.all_to_all(
@@ -183,6 +262,11 @@
         concat_axis=0,
         tiled=True,
     )
+    sums = total(last - 1, seconds, ranked)
+    arrived = put(arrived, last - 2, came, sums[0])
+    came = hop(last - 1, sums)
+    begun, seconds = second(last, sums[0])
+    share = after(share, begun)
     share = jnp.sum(share.astype(jnp.float32), axis=0).astype(jnp.bfloat16)
     ranked = lax.all_to_all(
         jnp.broadcast_to(share[None], (devices,) + share.shape),
@@ -191,7 +275,11 @@
         concat_axis=0,
         tiled=True,
     ).reshape(count * block, 2 * ranks)
-    grad_rank, act_rank = ranked[:, :ranks], ranked[:, ranks:]
+    sums = total(last, seconds, share)
+    arrived = put(arrived, last - 1, came, sums[0])
+    came = hop(last, sums)
+    ranked = after(ranked, *sums)
+    grad_rank = ranked[:, :ranks]
 
     flat_down = adapter_down.reshape(tenants * ranks, down_slab)
     term = jnp.concatenate(
@@ -206,12 +294,19 @@
         axis=0,
     )
     term = (term * ADAPTER_SCALE).astype(jnp.bfloat16).reshape(count, block, down_slab)
+    arrived = put(arrived, last, came, term)
+    rank_here = after(ranked, term)
     term = lax.all_to_all(term, "seq", split_axis=0, concat_axis=0, tiled=True)
-    term = term.transpose(1, 0, 2).reshape(block, -1)
-    grad_hidden = (base.astype(jnp.float32) + term.astype(jnp.float32)).astype(jnp.bfloat16)
-
-    grad_down = adapter_grad(grad_rank, mask, hidden_slab, weights)
-    grad_up = adapter_grad(act_rank, mask, grad_slab, weights)
+
+    each = count // groups
+    bases = []
+    for flip in range(groups):
+        sums = lax.dynamic_slice_in_dim(arrived, (group ^ flip) * each, each, 0)
+        bases.append(grp_move(sums, flip) if flip else sums)
+
+    grad_down = adapter_grad(rank_here[:, :ranks], mask, hidden_slab, weights)
+    grad_up = adapter_grad(rank_here[:, ranks:], mask, grad_slab, weights)
+    grad_hidden = join(bases, term, group)
     return grad_hidden, grad_down, grad_up
 
 

time: 260 us -> 217 us (0.83)
  waiting for transfers between devices: 120 us -> 82.4 us
  local copies, waits for them, and re-layouts: 47 us -> 19.2 us
  starting transfers between devices: 46 us -> 62.6 us
  Pallas kernels: 23 us -> 26.2 us
    ppermute x15 -> x19, waiting for transfers between devices: 64.5 us -> 27.7 us  [grp_move(): return lax.ppermute(value, 'grp', [(g, g ^ flip) for g in range(groups)])]
    unnamed x29 -> x24, local copies, waits for them, and re-layouts: 18.3 us -> 5.22 us
    ppermute x14, starting transfers between devices: 14.6 us -> 24.7 us  [seq_move(): return lax.ppermute(value, 'seq', pairs)]
    all_to_all x1, waiting for transfers between devices: 25.3 us -> 15.4 us  [shards(): term = lax.all_to_all(term, 'seq', split_axis=0, concat_axis=0, tiled=True)]
    dynamic_update_slice x11 -> x8, local copies, waits for them, and re-layouts: 14.8 us -> 6.41 us  [put(): lax.dynamic_update_index_in_dim(arrived, came[flip], ahead + (core ^ flip...]
    ppermute x14, waiting for transfers between devices: 13.1 us -> 20.3 us  [seq_move(): return lax.ppermute(value, 'seq', pairs)]
    all_to_all x1, waiting for transfers between devices: 3.71 us -> 8.74 us  [shards(): lax.all_to_all(ranked.reshape(devices, -1, 2 * ranks), ('grp', 'seq'), sp...]
    ppermute x15 -> x19, starting transfers between devices: 17.7 us -> 22.1 us  [grp_move(): return lax.ppermute(value, 'grp', [(g, g ^ flip) for g in range(groups)])]
  transfers between devices with their start and end apart: 33 -> 37, of which waited for: 15 -> 16; matrix products, arithmetic and copies ran while one was open for 20% -> 18% of each run, Pallas kernels for 9% -> 10%
where the time goes in v1:
time: 217 us; the launch traced here: 216 us
  waiting for transfers between devices  82.4 us (38%)
  starting transfers between devices  62.6 us (29%)
  Pallas kernels  26.2 us (12%)
  local copies, waits for them, and re-layouts  19.2 us (9%)
  matrix products  16.8 us (8%)
  other arithmetic  7.19 us (3%)
    ppermute x19, waiting for transfers between devices, grp_move(): return lax.ppermute(value, 'grp', [(g, g ^ flip) for g in range(groups)])  27.7 us
    ppermute x14, starting transfers between devices, seq_move(): return lax.ppermute(value, 'seq', pairs)  24.7 us
    ppermute x19, starting transfers between devices, grp_move(): return lax.ppermute(value, 'grp', [(g, g ^ flip) for g in range(groups)])  22.1 us
    pallas_call x4, Pallas kernels, chunk_product(): pl.pallas_call(functools.partial(chunk_kernel, STAGES), grid_spec=pltpu.P...  21.8 us
    ppermute x14, waiting for transfers between devices, seq_move(): return lax.ppermute(value, 'seq', pairs)  20.3 us
    all_to_all x1, waiting for transfers between devices, shards(): term = lax.all_to_all(term, 'seq', split_axis=0, concat_axis=0, tiled=True)  15.4 us
    dot_general x4, matrix products, dot(): lax.dot_general(left, right, dims, preferred_element_type=jnp.float32)  13.2 us
    all_to_all x1, waiting for transfers between devices, shards(): lax.all_to_all(jnp.broadcast_to(share[None], (devices,) + share.shape), (...  10.3 us
  transfers between devices with their start and end apart: 37, of which 16 were waited for; matrix products, arithmetic and copies ran while one was open for 18% of the time, Pallas kernels for 10%

profile of v1, /device:TPU:0, one launch (start us, length us, event | category | flops | bytes accessed | tf_op | source)
XLA Modules:
  0.0 215.8 jit_solution(17275307160153523413)
XLA Ops:
  3.8 3.0 %copy.53 = bf16[16,8,8,896]{3,2,0,1:T(8,128)(2,1)} copy(bf16[16,8,8,896]{3,2,1,0:T(8,128)(2,1)} %bitcast.136) | data formatting | bytes 3670016 | tf_op jit(solution)/shard_map/reshape | solution.py:191
  6.8 4.5 %all-to-all-start = ((bf16[8,128,896]{2,1,0:T(8,128)(2,1)}), bf16[8,128,896]{2,1,0:T(8,128)(2,1)}, u32[]{:S(2)}, u32[]{:S(2)}) async-start(bf16[8,128,896]{2,1,0:T(8,128)(2,1)} %bitcast.133), calls=%async_computation | async-start | bytes 3670016 | tf_op jit(solution)/shard_map/all_to_all | solution.py:190
  11.8 7.1 %collective-permute-done.3.near_ref = bf16[128,2048]{1,0:T(8,128)(2,1)S(1)} collective-permute-done((bf16[128,2048]{1,0:T(8,128)(2,1)}, bf16[128,2048]{1,0:T(8,128)(2,1)S(1)}, u32[]{:S(2)}, u32[]{:S(2)}) %collective-permute-start.3) | collective-permute-done | bytes 524320 | tf_op jit(solution)/shard_map/ppermute | solution.py:180
  19.0 5.2 %copy-done.1 = bf16[3584,2048]{1,0:T(8,128)(2,1)S(1)} copy-done((bf16[3584,2048]{1,0:T(8,128)(2,1)S(1)}, bf16[3584,2048]{1,0:T(8,128)(2,1)}, u32[]{:S(2)}) %copy-start.1) | copy-done | bytes 14680088
  24.2 5.4 %shard_map.94 = (bf16[2,32,3584]{2,1,0:T(8,128)(2,1)S(1)}, bf16[2,32,3584]{2,1,0:T(8,128)(2,1)S(1)}, bf16[2,32,3584]{2,1,0:T(8,128)(2,1)S(1)}, bf16[2,32,3584]{2,1,0:T(8,128)(2,1)S(1)}) custom-call(s32[1]{0:T(128)} %bitcast.place_ref, bf16[128,2048]{1,0:T(8,128)(2,1)S(1)} %copy-done.3, bf16[128,2048]{1,0:T(8,128)(2,1)S(1)} %collective-permute-done.far_ref, ...), custom_call_target="tpu_custom_call" | custom-call | flops 3758096384 | bytes 17563648 | tf_op jit(solution)/shard_map/pallas_call | solution.py:56
  32.9 4.3 %collective-permute-start.10 = (bf16[128,2048]{1,0:T(8,128)(2,1)S(1)}, bf16[128,2048]{1,0:T(8,128)(2,1)S(1)}, u32[]{:S(2)}, u32[]{:S(2)}) collective-permute-start(bf16[128,2048]{1,0:T(8,128)(2,1)S(1)} %collective-permute-done.3.near_ref), channel_id=1, source_target_pairs={{0,2},{1,3},{2,4},{3,5},{4,6},{5,7},{6,0},{7,1},{8,10},{9,11},{10,... | collective-permute-start | bytes 1572872 | tf_op jit(solution)/shard_map/ppermute | solution.py:180
  37.2 5.5 %shard_map.95 = (bf16[2,32,3584]{2,1,0:T(8,128)(2,1)S(1)}, bf16[2,32,3584]{2,1,0:T(8,128)(2,1)S(1)}, bf16[2,32,3584]{2,1,0:T(8,128)(2,1)S(1)}, bf16[2,32,3584]{2,1,0:T(8,128)(2,1)S(1)}) custom-call(s32[1]{0:T(128)} %bitcast.place_ref, bf16[128,2048]{1,0:T(8,128)(2,1)S(1)} %collective-permute-done.3.near_ref, ...), custom_call_target="tpu_custom_call" | custom-call | flops 3758096384 | bytes 17563648 | tf_op jit(solution)/shard_map/pallas_call | solution.py:56
  48.4 11.1 %collective-permute-done.10.near_ref = bf16[128,2048]{1,0:T(8,128)(2,1)S(1)} collective-permute-done((bf16[128,2048]{1,0:T(8,128)(2,1)S(1)}, bf16[128,2048]{1,0:T(8,128)(2,1)S(1)}, u32[]{:S(2)}, u32[]{:S(2)}) %collective-permute-start.10) | collective-permute-done | bytes 524320 | tf_op jit(solution)/shard_map/ppermute | solution.py:180
  59.5 8.6 %collective-permute-start.18 = (bf16[128,2048]{1,0:T(8,128)(2,1)S(1)}, bf16[128,2048]{1,0:T(8,128)(2,1)S(1)}, u32[]{:S(2)}, u32[]{:S(2)}) collective-permute-start(bf16[128,2048]{1,0:T(8,128)(2,1)S(1)} %collective-permute-done.10.near_ref), channel_id=1, source_target_pairs={{0,2},{1,3},{2,4},{3,5},{4,6},{5,7},{6,0},{7,1},{8,10},{9,11},{10,... | collective-permute-start | bytes 1572872 | tf_op jit(solution)/shard_map/ppermute | solution.py:180
  68.5 5.4 %shard_map.96 = (bf16[2,32,3584]{2,1,0:T(8,128)(2,1)S(1)}, bf16[2,32,3584]{2,1,0:T(8,128)(2,1)S(1)}, bf16[2,32,3584]{2,1,0:T(8,128)(2,1)S(1)}, bf16[2,32,3584]{2,1,0:T(8,128)(2,1)S(1)}) custom-call(s32[1]{0:T(128)} %bitcast.place_ref, bf16[128,2048]{1,0:T(8,128)(2,1)S(1)} %collective-permute-done.10.near_ref, ...), custom_call_target="tpu_custom_call" | custom-call | flops 3758096384 | bytes 17563648 | tf_op jit(solution)/shard_map/pallas_call | solution.py:56
  87.7 5.5 %shard_map.97 = (bf16[2,32,3584]{2,1,0:T(8,128)(2,1)S(1)}, bf16[2,32,3584]{2,1,0:T(8,128)(2,1)S(1)}, bf16[2,32,3584]{2,1,0:T(8,128)(2,1)S(1)}, bf16[2,32,3584]{2,1,0:T(8,128)(2,1)S(1)}) custom-call(s32[1]{0:T(128)} %bitcast.place_ref, bf16[128,2048]{1,0:T(8,128)(2,1)S(1)} %collective-permute-done.18.near_ref, ...), custom_call_target="tpu_custom_call" | custom-call | flops 3758096384 | bytes 17563648 | tf_op jit(solution)/shard_map/pallas_call | solution.py:56
  96.3 4.7 %collective-permute-done.20 = bf16[32,3584]{1,0:T(8,128)(2,1)S(1)} collective-permute-done((bf16[32,3584]{1,0:T(8,128)(2,1)S(1)}, bf16[32,3584]{1,0:T(8,128)(2,1)S(1)}, u32[]{:S(2)}, u32[]{:S(2)}) %collective-permute-start.20) | collective-permute-done | bytes 229408 | tf_op jit(solution)/shard_map/ppermute | solution.py:183
  103.0 4.6 %collective-permute-start.22 = (bf16[32,3584]{1,0:T(8,128)(2,1)}, bf16[32,3584]{1,0:T(8,128)(2,1)}, u32[]{:S(2)}, u32[]{:S(2)}) collective-permute-start(bf16[32,3584]{1,0:T(8,128)(2,1)} %fusion.28), channel_id=1, source_target_pairs={{0,4},{1,5},{2,6},{3,7},{4,0},{5,1},{6,2},{7,3},{8,12},{9,13},{10,... | collective-permute-start | bytes 688136 | tf_op jit(solution)/shard_map/ppermute | solution.py:180
  108.4 3.6 %collective-permute-done.24 = bf16[2,32,3584]{2,1,0:T(8,128)(2,1)S(1)} collective-permute-done((bf16[2,32,3584]{2,1,0:T(8,128)(2,1)S(1)}, bf16[2,32,3584]{2,1,0:T(8,128)(2,1)S(1)}, u32[]{:S(2)}, u32[]{:S(2)}) %collective-permute-start.24) | collective-permute-done | bytes 458784 | tf_op jit(solution)/shard_map/ppermute | solution.py:183
  118.1 3.9 %multiply_reduce_fusion = bf16[1024,64]{0,1:T(8,128)(2,1)S(1)} fusion(f32[1024,16]{0,1:T(8,128)S(1)} %get-tuple-element.100, bf16[16,64,896]{2,1,0:T(8,128)(2,1)S(1)} %copy-done, bf16[1024,896]{1,0:T(8,128)(2,1)} %bitcast.30), kind=kOutput, calls=%fused_computation | convolution fusion | flops 1881079808 | bytes 3866624 | tf_op jit(solution)/shard_map/dot_general | solution.py:18
  129.4 8.7 %all-to-all-done.1 = bf16[32,32,128]{2,1,0:T(8,128)(2,1)S(1)} async-done(((bf16[32,32,128]{2,1,0:T(8,128)(2,1)}), bf16[32,32,128]{2,1,0:T(8,128)(2,1)S(1)}, u32[]{:S(2)}, u32[]{:S(2)}) %all-to-all-start.1) | async-done | bytes 262176 | tf_op jit(solution)/shard_map/all_to_all | solution.py:258
  141.8 4.4 %all-to-all-start.2 = ((bf16[32,32,128]{2,1,0:T(8,128)(2,1)}), bf16[32,32,128]{2,1,0:T(8,128)(2,1)S(1)}, u32[]{:S(2)}, u32[]{:S(2)}) async-start(bf16[32,32,128]{2,1,0:T(8,128)(2,1)} %broadcast_in_dim.110), calls=%async_computation.2 | async-start | bytes 524288 | tf_op jit(solution)/shard_map/all_to_all | solution.py:271
  149.6 10.3 %all-to-all-done.2 = bf16[32,32,128]{2,1,0:T(8,128)(2,1)S(1)} async-done(((bf16[32,32,128]{2,1,0:T(8,128)(2,1)}), bf16[32,32,128]{2,1,0:T(8,128)(2,1)S(1)}, u32[]{:S(2)}, u32[]{:S(2)}) %all-to-all-start.2) | async-done | bytes 262176 | tf_op jit(solution)/shard_map/all_to_all | solution.py:271
  160.0 3.6 %fusion = bf16[1024,896]{1,0:T(8,128)(2,1)} fusion(bf16[16,64,896]{2,1,0:T(8,128)(2,1)S(1)} %copy-done, bf16[1024,16]{0,1:T(8,128)(2,1)S(1)} %get-tuple-element.99, bf16[1024,64]{0,1:T(8,128)(2,1)S(1)} %copy.48), kind=kOutput, calls=%fused_computation.3 | convolution fusion | flops 1881931776 | bytes 3833856 | tf_op jit(solution)/shard_map/dot_general | solution.py:287
  163.6 4.3 %all-to-all-start.3 = ((bf16[8,128,896]{2,1,0:T(8,128)(2,1)}), bf16[8,128,896]{2,1,0:T(8,128)(2,1)}, u32[]{:S(2)}, u32[]{:S(2)}) async-start(bf16[8,128,896]{2,1,0:T(8,128)(2,1)} %bitcast.137), calls=%async_computation.3 | async-start | bytes 3670016 | tf_op jit(solution)/shard_map/all_to_all | solution.py:299
  177.7 5.7 %fusion.9 = f32[16,64,896]{2,1,0:T(8,128)} fusion(bf16[1024,896,1]{1,0,2:T(8,128)(2,1)} %bitcast.47, f32[16]{0:T(128)S(1)} %broadcast_divide_fusion, bf16[1024,64]{0,1:T(8,128)(2,1)S(1)} %copy.49, bf16[1024,16]{0,1:T(8,128)(2,1)S(1)} %get-tuple-element.99), kind=kOutput, calls=%fused_computation.12 | convolution fusion | flops 1881014272 | bytes 5668928 | tf_op jit(solution)/shard_map/dot_general | solution.py:18
  185.8 8.7 %collective-permute-done.31.refs_2_ = bf16[2,32,3584]{2,1,0:T(8,128)(2,1)} collective-permute-done((bf16[2,32,3584]{2,1,0:T(8,128)(2,1)}, bf16[2,32,3584]{2,1,0:T(8,128)(2,1)}, u32[]{:S(2)}, u32[]{:S(2)}) %collective-permute-start.31) | collective-permute-done | bytes 458784 | tf_op jit(solution)/shard_map/ppermute | solution.py:183
  196.0 15.4 %all-to-all-done.3.refs_4_ = bf16[8,128,896]{2,1,0:T(8,128)(2,1)} async-done(((bf16[8,128,896]{2,1,0:T(8,128)(2,1)}), bf16[8,128,896]{2,1,0:T(8,128)(2,1)}, u32[]{:S(2)}, u32[]{:S(2)}) %all-to-all-start.3) | async-done | bytes 1835040 | tf_op jit(solution)/shard_map/all_to_all | solution.py:299
  211.4 4.4 %shard_map.98 = bf16[128,7168]{1,0:T(8,128)(2,1)} custom-call(s32[1]{0:T(128)} %bitcast.place_ref, bf16[2,32,3584]{2,1,0:T(8,128)(2,1)} %get-tuple-element.96.refs_0_, bf16[2,32,3584]{2,1,0:T(8,128)(2,1)} %collective-permute-done.30.refs_1_, bf16[2,32,3584]{2,1,0:T(8,128)(2,1)} %collective-permute-done.31.refs_2_, ...), custom_call_target="tpu_custom_call" | custom-call | flops 917504 | bytes 5505024 | tf_op jit(solution)/shard_map/pallas_call | solution.py:103
  (135 shorter events, 66.6 us)
Async XLA Ops:
  0.6 18.4 %collective-permute-start = (bf16[128,2048]{1,0:T(8,128)(2,1)}, bf16[128,2048]{1,0:T(8,128)(2,1)S(1)}, u32[]{:S(2)}, u32[]{:S(2)}) collective-permute-start(bf16[128,2048]{1,0:T(8,128)(2,1)} %near_ref.1), channel_id=1, source_target_pairs={{0,1},{1,0},{2,3},{3,2},{4,5},{5,4},{6,7},{7,6},{8,9},{9,8},{10,11... | collective-permute-start | bytes 1572872 | tf_op jit(solution)/shard_map/ppermute | solution.py:180
  1.2 17.8 %collective-permute-start.3 = (bf16[128,2048]{1,0:T(8,128)(2,1)}, bf16[128,2048]{1,0:T(8,128)(2,1)S(1)}, u32[]{:S(2)}, u32[]{:S(2)}) collective-permute-start(bf16[128,2048]{1,0:T(8,128)(2,1)} %near_ref.1), channel_id=1, source_target_pairs={{0,2},{1,3},{2,4},{3,5},{4,6},{5,7},{6,0},{7,1},{8,10},{9,11},{10,... | collective-permute-start | bytes 1572872 | tf_op jit(solution)/shard_map/ppermute | solution.py:180
  6.8 111.3 %all-to-all-start = ((bf16[8,128,896]{2,1,0:T(8,128)(2,1)}), bf16[8,128,896]{2,1,0:T(8,128)(2,1)}, u32[]{:S(2)}, u32[]{:S(2)}) async-start(bf16[8,128,896]{2,1,0:T(8,128)(2,1)} %bitcast.133), calls=%async_computation | async-start | bytes 3670016 | tf_op jit(solution)/shard_map/all_to_all | solution.py:190
  18.9 18.2 %collective-permute-start.4 = (bf16[128,2048]{1,0:T(8,128)(2,1)S(1)}, bf16[128,2048]{1,0:T(8,128)(2,1)S(1)}, u32[]{:S(2)}, u32[]{:S(2)}) collective-permute-start(bf16[128,2048]{1,0:T(8,128)(2,1)S(1)} %collective-permute-done.3.near_ref), channel_id=1, source_target_pairs={{0,1},{1,0},{2,3},{3,2},{4,5},{5,4},{6,7},{7,6},{8,9},{9,8},{10,11... | collective-permute-start | bytes 1572872 | tf_op jit(solution)/shard_map/ppermute | solution.py:180
  32.9 26.6 %collective-permute-start.10 = (bf16[128,2048]{1,0:T(8,128)(2,1)S(1)}, bf16[128,2048]{1,0:T(8,128)(2,1)S(1)}, u32[]{:S(2)}, u32[]{:S(2)}) collective-permute-start(bf16[128,2048]{1,0:T(8,128)(2,1)S(1)} %collective-permute-done.3.near_ref), channel_id=1, source_target_pairs={{0,2},{1,3},{2,4},{3,5},{4,6},{5,7},{6,0},{7,1},{8,10},{9,11},{10,... | collective-permute-start | bytes 1572872 | tf_op jit(solution)/shard_map/ppermute | solution.py:180
  45.7 22.4 %collective-permute-start.6 = (bf16[32,3584]{1,0:T(8,128)(2,1)S(1)}, bf16[32,3584]{1,0:T(8,128)(2,1)S(1)}, u32[]{:S(2)}, u32[]{:S(2)}) collective-permute-start(bf16[32,3584]{1,0:T(8,128)(2,1)S(1)} %fusion.34), channel_id=1, source_target_pairs={{0,8},{8,0},{16,24},{24,16},{1,9},{9,1},{17,25},{25,17},{2,10},{10... | collective-permute-start | bytes 688136 | tf_op jit(solution)/shard_map/ppermute | solution.py:183
  46.3 27.6 %collective-permute-start.8 = (bf16[2,32,3584]{2,1,0:T(8,128)(2,1)S(1)}, bf16[2,32,3584]{2,1,0:T(8,128)(2,1)S(1)}, u32[]{:S(2)}, u32[]{:S(2)}) collective-permute-start(bf16[2,32,3584]{2,1,0:T(8,128)(2,1)S(1)} %get-tuple-element.57), channel_id=1, source_target_pairs={{0,8},{8,0},{16,24},{24,16},{1,9},{9,1},{17,25},{25,17},{2,10},{10... | collective-permute-start | bytes 1376264 | tf_op jit(solution)/shard_map/ppermute | solution.py:183
  47.9 26.1 %collective-permute-start.9 = (bf16[2,32,3584]{2,1,0:T(8,128)(2,1)S(1)}, bf16[2,32,3584]{2,1,0:T(8,128)(2,1)S(1)}, u32[]{:S(2)}, u32[]{:S(2)}) collective-permute-start(bf16[2,32,3584]{2,1,0:T(8,128)(2,1)S(1)} %get-tuple-element.58), channel_id=1, source_target_pairs={{0,16},{8,24},{16,0},{24,8},{1,17},{9,25},{17,1},{25,9},{2,18},{10... | collective-permute-start | bytes 1376264 | tf_op jit(solution)/shard_map/ppermute | solution.py:183
  59.5 20.4 %collective-permute-start.18 = (bf16[128,2048]{1,0:T(8,128)(2,1)S(1)}, bf16[128,2048]{1,0:T(8,128)(2,1)S(1)}, u32[]{:S(2)}, u32[]{:S(2)}) collective-permute-start(bf16[128,2048]{1,0:T(8,128)(2,1)S(1)} %collective-permute-done.10.near_ref), channel_id=1, source_target_pairs={{0,2},{1,3},{2,4},{3,5},{4,6},{5,7},{6,0},{7,1},{8,10},{9,11},{10,... | collective-permute-start | bytes 1572872 | tf_op jit(solution)/shard_map/ppermute | solution.py:180
  68.2 17.7 %collective-permute-start.7 = (bf16[32,3584]{1,0:T(8,128)(2,1)S(1)}, bf16[32,3584]{1,0:T(8,128)(2,1)S(1)}, u32[]{:S(2)}, u32[]{:S(2)}) collective-permute-start(bf16[32,3584]{1,0:T(8,128)(2,1)S(1)} %fusion.31), channel_id=1, source_target_pairs={{0,1},{1,0},{2,3},{3,2},{4,5},{5,4},{6,7},{7,6},{8,9},{9,8},{10,11... | collective-permute-start | bytes 688136 | tf_op jit(solution)/shard_map/ppermute | solution.py:180
  77.3 15.9 %collective-permute-start.16 = (bf16[2,32,3584]{2,1,0:T(8,128)(2,1)S(1)}, bf16[2,32,3584]{2,1,0:T(8,128)(2,1)S(1)}, u32[]{:S(2)}, u32[]{:S(2)}) collective-permute-start(bf16[2,32,3584]{2,1,0:T(8,128)(2,1)S(1)} %get-tuple-element.67), channel_id=1, source_target_pairs={{0,8},{8,0},{16,24},{24,16},{1,9},{9,1},{17,25},{25,17},{2,10},{10... | collective-permute-start | bytes 1376264 | tf_op jit(solution)/shard_map/ppermute | solution.py:183
  84.3 23.3 %collective-permute-start.14 = (bf16[32,3584]{1,0:T(8,128)(2,1)S(1)}, bf16[32,3584]{1,0:T(8,128)(2,1)S(1)}, u32[]{:S(2)}, u32[]{:S(2)}) collective-permute-start(bf16[32,3584]{1,0:T(8,128)(2,1)S(1)} %fusion.30), channel_id=1, source_target_pairs={{0,6},{1,7},{2,0},{3,1},{4,2},{5,3},{6,4},{7,5},{8,14},{9,15},{10,... | collective-permute-start | bytes 688136 | tf_op jit(solution)/shard_map/ppermute | solution.py:180
  85.9 21.6 %collective-permute-start.15 = (bf16[32,3584]{1,0:T(8,128)(2,1)S(1)}, bf16[32,3584]{1,0:T(8,128)(2,1)S(1)}, u32[]{:S(2)}, u32[]{:S(2)}) collective-permute-start(bf16[32,3584]{1,0:T(8,128)(2,1)S(1)} %fusion.29), channel_id=1, source_target_pairs={{0,7},{1,6},{2,1},{3,0},{4,3},{5,2},{6,5},{7,4},{8,15},{9,14},{10,... | collective-permute-start | bytes 688136 | tf_op jit(solution)/shard_map/ppermute | solution.py:180
  95.6 16.4 %collective-permute-start.24 = (bf16[2,32,3584]{2,1,0:T(8,128)(2,1)S(1)}, bf16[2,32,3584]{2,1,0:T(8,128)(2,1)S(1)}, u32[]{:S(2)}, u32[]{:S(2)}) collective-permute-start(bf16[2,32,3584]{2,1,0:T(8,128)(2,1)S(1)} %get-tuple-element.77), channel_id=1, source_target_pairs={{0,8},{8,0},{16,24},{24,16},{1,9},{9,1},{17,25},{25,17},{2,10},{10... | collective-permute-start | bytes 1376264 | tf_op jit(solution)/shard_map/ppermute | solution.py:183
  103.0 36.9 %collective-permute-start.22 = (bf16[32,3584]{1,0:T(8,128)(2,1)}, bf16[32,3584]{1,0:T(8,128)(2,1)}, u32[]{:S(2)}, u32[]{:S(2)}) collective-permute-start(bf16[32,3584]{1,0:T(8,128)(2,1)} %fusion.28), channel_id=1, source_target_pairs={{0,4},{1,5},{2,6},{3,7},{4,0},{5,1},{6,2},{7,3},{8,12},{9,13},{10,... | collective-permute-start | bytes 688136 | tf_op jit(solution)/shard_map/ppermute | solution.py:180
  108.4 31.5 %collective-permute-start.23 = (bf16[32,3584]{1,0:T(8,128)(2,1)}, bf16[32,3584]{1,0:T(8,128)(2,1)}, u32[]{:S(2)}, u32[]{:S(2)}) collective-permute-start(bf16[32,3584]{1,0:T(8,128)(2,1)} %fusion.27), channel_id=1, source_target_pairs={{0,5},{1,4},{2,7},{3,6},{4,1},{5,0},{6,3},{7,2},{8,13},{9,12},{10,... | collective-permute-start | bytes 688136 | tf_op jit(solution)/shard_map/ppermute | solution.py:180
  115.1 23.1 %collective-permute-start.26 = (bf16[32,3584]{1,0:T(8,128)(2,1)}, bf16[32,3584]{1,0:T(8,128)(2,1)}, u32[]{:S(2)}, u32[]{:S(2)}) collective-permute-start(bf16[32,3584]{1,0:T(8,128)(2,1)} %fusion.39), channel_id=1, source_target_pairs={{0,16},{8,24},{16,0},{24,8},{1,17},{9,25},{17,1},{25,9},{2,18},{10... | collective-permute-start | bytes 688136 | tf_op jit(solution)/shard_map/ppermute | solution.py:183
  116.6 21.6 %collective-permute-start.27 = (bf16[32,3584]{1,0:T(8,128)(2,1)}, bf16[32,3584]{1,0:T(8,128)(2,1)}, u32[]{:S(2)}, u32[]{:S(2)}) collective-permute-start(bf16[32,3584]{1,0:T(8,128)(2,1)} %fusion.40), channel_id=1, source_target_pairs={{0,8},{8,0},{16,24},{24,16},{1,9},{9,1},{17,25},{25,17},{2,10},{10... | collective-permute-start | bytes 688136 | tf_op jit(solution)/shard_map/ppermute | solution.py:183
  139.4 28.6 %collective-permute-start.28 = (bf16[32,3584]{1,0:T(8,128)(2,1)S(1)}, bf16[32,3584]{1,0:T(8,128)(2,1)S(1)}, u32[]{:S(2)}, u32[]{:S(2)}) collective-permute-start(bf16[32,3584]{1,0:T(8,128)(2,1)S(1)} %fusion.26), channel_id=1, source_target_pairs={{0,2},{1,3},{2,4},{3,5},{4,6},{5,7},{6,0},{7,1},{8,10},{9,11},{10,... | collective-permute-start | bytes 688136 | tf_op jit(solution)/shard_map/ppermute | solution.py:180
  141.0 26.9 %collective-permute-start.29 = (bf16[32,3584]{1,0:T(8,128)(2,1)S(1)}, bf16[32,3584]{1,0:T(8,128)(2,1)S(1)}, u32[]{:S(2)}, u32[]{:S(2)}) collective-permute-start(bf16[32,3584]{1,0:T(8,128)(2,1)S(1)} %fusion.25), channel_id=1, source_target_pairs={{0,3},{1,2},{2,5},{3,4},{4,7},{5,6},{6,1},{7,0},{8,11},{9,10},{10,... | collective-permute-start | bytes 688136 | tf_op jit(solution)/shard_map/ppermute | solution.py:180
  141.8 18.0 %all-to-all-start.2 = ((bf16[32,32,128]{2,1,0:T(8,128)(2,1)}), bf16[32,32,128]{2,1,0:T(8,128)(2,1)S(1)}, u32[]{:S(2)}, u32[]{:S(2)}) async-start(bf16[32,32,128]{2,1,0:T(8,128)(2,1)} %broadcast_in_dim.110), calls=%async_computation.2 | async-start | bytes 524288 | tf_op jit(solution)/shard_map/all_to_all | solution.py:271
  163.6 47.8 %all-to-all-start.3 = ((bf16[8,128,896]{2,1,0:T(8,128)(2,1)}), bf16[8,128,896]{2,1,0:T(8,128)(2,1)}, u32[]{:S(2)}, u32[]{:S(2)}) async-start(bf16[8,128,896]{2,1,0:T(8,128)(2,1)} %bitcast.137), calls=%async_computation.3 | async-start | bytes 3670016 | tf_op jit(solution)/shard_map/all_to_all | solution.py:299
  173.4 21.1 %collective-permute-start.31 = (bf16[2,32,3584]{2,1,0:T(8,128)(2,1)}, bf16[2,32,3584]{2,1,0:T(8,128)(2,1)}, u32[]{:S(2)}, u32[]{:S(2)}) collective-permute-start(bf16[2,32,3584]{2,1,0:T(8,128)(2,1)} %get-tuple-element.94), channel_id=1, source_target_pairs={{0,16},{8,24},{16,0},{24,8},{1,17},{9,25},{17,1},{25,9},{2,18},{10... | collective-permute-start | bytes 1376264 | tf_op jit(solution)/shard_map/ppermute | solution.py:183
  174.2 21.8 %collective-permute-start.32 = (bf16[2,32,3584]{2,1,0:T(8,128)(2,1)}, bf16[2,32,3584]{2,1,0:T(8,128)(2,1)}, u32[]{:S(2)}, u32[]{:S(2)}) collective-permute-start(bf16[2,32,3584]{2,1,0:T(8,128)(2,1)} %get-tuple-element.93), channel_id=1, source_target_pairs={{0,24},{8,16},{16,8},{24,0},{1,25},{9,17},{17,9},{25,1},{2,26},{10... | collective-permute-start | bytes 1376264 | tf_op jit(solution)/shard_map/ppermute | solution.py:183
  (25 other events, 344.0 us)

commit v2 on v1

--- a/solution.py
+++ b/solution.py
@@ -12,6 +12,7 @@
 CONTRACT_ROWS = (((0,), (0,)), ((), ()))
 CORES = 2
 MOST_ROWS = 1024
+VMEM_GRANT = 56 << 20
 
 
 def dot(left, right, dims):
@@ -67,7 +68,7 @@
             scratch_shapes=[pltpu.VMEM((CORES * block, depth), jnp.bfloat16)],
         ),
         out_shape=[jax.ShapeDtypeStruct((2, part, width), jnp.bfloat16)] * 4,
-        compiler_params=pltpu.CompilerParams(vmem_limit_bytes=24 << 20),
+        compiler_params=pltpu.CompilerParams(vmem_limit_bytes=VMEM_GRANT),
         cost_estimate=pl.CostEstimate(
             flops=2 * CORES * block * depth * width,
             bytes_accessed=2 * (width * depth + CORES * block * (depth + width)),
@@ -116,12 +117,90 @@
     )(group.reshape(1), *bases, term)
 
 
+ANYWHERE = pl.BlockSpec(memory_space=pl.ANY)
+
+
+def touch_kernel(*refs):
+    pass
+
+
+def touch(value, *gates):
+    return pl.pallas_call(
+        touch_kernel,
+        in_specs=[ANYWHERE] * (1 + len(gates)),
+        out_specs=ANYWHERE,
+        out_shape=jax.ShapeDtypeStruct(value.shape, value.dtype),
+        input_output_aliases={0: 0},
+    )(value, *gates)
+
+
+def cut_kernel(rows_ref, out_ref):
+    out_ref[0] = rows_ref[...]
+
+
+def cut_columns(rows, count):
+    block, width = rows.shape
+    slab = width // count
+    if slab % 128:
+        return rows.reshape(block, count, slab).transpose(1, 0, 2)
+    return pl.pallas_call(
+        cut_kernel,
+        grid=(count,),
+        in_specs=[pl.BlockSpec((block, slab), lambda at: (0, at))],
+        out_specs=pl.BlockSpec((1, block, slab), lambda at: (at, 0, 0)),
+        out_shape=jax.ShapeDtypeStruct((count, block, slab), rows.dtype),
+        cost_estimate=pl.CostEstimate(flops=0, bytes_accessed=4 * rows.size, transcendentals=0),
+    )(rows)
+
+
 def add(*terms):
     return sum(term.astype(jnp.float32) for term in terms).astype(jnp.bfloat16)
 
 
-def after(value, *others):
-    return lax.optimization_barrier((value,) + others)[0]
+def half_kernel(near_kept, near_came, far_kept, far_came, *rest):
+    near_out, far_out = rest[-2:]
+    near_out[...] = add(near_kept[0], near_came[0])
+    far_out[...] = add(far_kept[0], far_came[0])
+
+
+def half_sums(near_kept, near_came, far_kept, far_came, *gates):
+    _, part, width = near_kept.shape
+    return pl.pallas_call(
+        half_kernel,
+        grid=(1,),
+        in_specs=[pl.BlockSpec((1, part, width), lambda at: (1, 0, 0))] * 4
+        + [ANYWHERE] * len(gates),
+        out_specs=[pl.BlockSpec((part, width), lambda at: (0, 0))] * 2,
+        out_shape=[jax.ShapeDtypeStruct((part, width), jnp.bfloat16)] * 2,
+    )(near_kept, near_came, far_kept, far_came, *gates)
+
+
+def full_kernel(place_ref, *refs):
+    out_ref = refs[-1]
+    for side in range(2):
+
+        @pl.when(pl.program_id(0) == side)
+        def _():
+            kept, came, last = refs[3 * side : 3 * side + 3]
+            out_ref[0] = add(kept[0], came[0], last[...])
+
+
+def full_sums(sides, places, filled, count):
+    part, width = sides[0][2].shape
+    first = pl.BlockSpec((1, part, width), lambda at, place: (0, 0, 0))
+    whole = pl.BlockSpec((part, width), lambda at, place: (0, 0))
+    extra = [] if filled is None else [filled]
+    return pl.pallas_call(
+        full_kernel,
+        grid_spec=pltpu.PrefetchScalarGridSpec(
+            num_scalar_prefetch=1,
+            grid=(2,),
+            in_specs=[first, first, whole] * 2 + [ANYWHERE] * len(extra),
+            out_specs=pl.BlockSpec((1, part, width), lambda at, place: (place[at], 0, 0)),
+        ),
+        out_shape=jax.ShapeDtypeStruct((count, part, width), jnp.bfloat16),
+        input_output_aliases={7: 0} if extra else {},
+    )(jnp.stack(places), *sides[0], *sides[1], *extra)
 
 
 def project(rows, adapter, mask):
@@ -187,99 +266,52 @@
         held.append(seq_move(held[-1], -1, 0))
     pairs = [(near, seq_move(near, 0, 1)) for near in held]
 
-    hidden_slab = lax.all_to_all(
-        hidden.reshape(block, count, down_slab).transpose(1, 0, 2),
-        "seq",
-        split_axis=0,
-        concat_axis=0,
-        tiled=True,
-    ).reshape(count * block, down_slab)
-
-    last = chips - 1
+    cut = touch(cut_columns(hidden, count), held[min(2, chips - 1)])
+    hidden_slab = lax.all_to_all(cut, "seq", split_axis=0, concat_axis=0, tiled=True)
+    hidden_slab = hidden_slab.reshape(count * block, down_slab)
+
     products = [chunk_product(near, far, down_weight, group) for near, far in pairs]
     firsts = [
         (grp_move(near_sent, 1), grp_move(far_sent, 2)) for _, near_sent, _, far_sent in products
     ]
+    summed = None
+    for step in range(chips):
+        near_kept, _, far_kept, _ = products[step]
+        near_came, far_came = firsts[step]
+        gates = [products[step + 1][0]] if step + 1 < chips else []
+        near_sum, far_sum = half_sums(near_kept, near_came, far_kept, far_came, *gates)
+        sides = (
+            (near_kept, near_came, grp_move(near_sum, 2)),
+            (far_kept, far_came, grp_move(far_sum, 1)),
+        )
+        back = ((chip - step) % chips) * CORES
+        summed = full_sums(sides, (back + core, back + 1 - core), summed, count)
+
+    arrived = lax.all_to_all(summed, "seq", split_axis=0, concat_axis=0, tiled=True)
+
     grad_slab = jnp.zeros((count, block, up_slab), jnp.bfloat16)
     for step, pair in enumerate(pairs):
         back = ((chip - step) % chips) * CORES
         for flip, rows in enumerate(pair):
             columns = lax.dynamic_slice_in_dim(rows, index * up_slab, up_slab, 1)
             grad_slab = lax.dynamic_update_index_in_dim(grad_slab, columns, back + (core ^ flip), 0)
-    grad_slab = grad_slab.reshape(count * block, up_slab)
-
-    def second(step, *gates):
-        near_kept, _, far_kept, _ = products[step]
-        near_came, far_came = firsts[step]
-        near_came, far_came = lax.optimization_barrier((near_came, far_came) + gates)[:2]
-        near_sum = add(near_kept[1], near_came[1])
-        far_sum = add(far_kept[1], far_came[1])
-        return near_sum, (grp_move(near_sum, 2), grp_move(far_sum, 1))
-
-    def total(step, seconds, *gates):
-        near_kept, _, far_kept, _ = products[step]
-        near_came, far_came = firsts[step]
-        near_last, far_last = lax.optimization_barrier(seconds + gates)[:2]
-        return (
-            add(near_kept[0], near_came[0], near_last),
-            add(far_kept[0], far_came[0], far_last),
-        )
-
-    arrived = jnp.zeros((count, part, width), jnp.bfloat16)
-
-    def hop(step, sums):
-        return [
-            sums[flip] if step == 0 and flip == 0 else seq_move(sums[flip], step, flip)
-            for flip in range(CORES)
-        ]
-
-    def put(arrived, step, came, *gates):
-        ahead = ((chip + step) % chips) * CORES
-        came = lax.optimization_barrier(tuple(came) + gates)
-        for flip in range(CORES):
-            arrived = lax.dynamic_update_index_in_dim(arrived, came[flip], ahead + (core ^ flip), 0)
-        return arrived
-
-    came = None
-    for step in range(last - 1):
-        _, seconds = second(step, products[step + 1][0])
-        sums = total(step, seconds)
-        if came is not None:
-            arrived = put(arrived, step - 1, came, sums[0])
-        came = hop(step, sums)
-
-    begun, seconds = second(last - 1, products[last][0])
-    rows_here = lax.optimization_barrier((grad_slab, hidden_slab, begun))
-    ranked = jnp.concatenate(
-        [project(rows_here[0], adapter_up, mask), project(rows_here[1], adapter_down, mask)],
-        axis=1,
-    )
-    devices = count * groups
-    share = lax.all_to_all(
-        ranked.reshape(devices, -1, 2 * ranks),
-        ("grp", "seq"),
-        split_axis=0,
-        concat_axis=0,
-        tiled=True,
-    )
-    sums = total(last - 1, seconds, ranked)
-    arrived = put(arrived, last - 2, came, sums[0])
-    came = hop(last - 1, sums)
-    begun, seconds = second(last, sums[0])
-    share = after(share, begun)
-    share = jnp.sum(share.astype(jnp.float32), axis=0).astype(jnp.bfloat16)
-    ranked = lax.all_to_all(
-        jnp.broadcast_to(share[None], (devices,) + share.shape),
-        ("grp", "seq"),
-        split_axis=0,
-        concat_axis=0,
-        tiled=True,
-    ).reshape(count * block, 2 * ranks)
-    sums = total(last, seconds, share)
-    arrived = put(arrived, last - 1, came, sums[0])
-    came = hop(last, sums)
-    ranked = after(ranked, *sums)
-    grad_rank = ranked[:, :ranks]
+    grad_slab = touch(grad_slab.reshape(count * block, up_slab), summed)
+    hidden_slab = touch(hidden_slab, summed)
+
+    def sum_ranks(parts):
+        rows = parts.shape[0] // 2
+        parts = jnp.concatenate([parts[:rows], parts[rows:]], axis=1)
+        for axis in ("seq", "grp"):
+            size = lax.axis_size(axis)
+            flip = 1
+            while flip < size:
+                pairs = [(at, at ^ flip) for at in range(size)]
+                parts = add(parts, lax.ppermute(parts, axis, pairs))
+                flip *= 2
+        return jnp.concatenate([parts[:, :ranks], parts[:, ranks:]], axis=0)
+
+    grad_rank = sum_ranks(project(grad_slab, adapter_up, mask))
+    act_rank = sum_ranks(project(hidden_slab, adapter_down, mask))
 
     flat_down = adapter_down.reshape(tenants * ranks, down_slab)
     term = jnp.concatenate(
@@ -294,8 +326,6 @@
         axis=0,
     )
     term = (term * ADAPTER_SCALE).astype(jnp.bfloat16).reshape(count, block, down_slab)
-    arrived = put(arrived, last, came, term)
-    rank_here = after(ranked, term)
     term = lax.all_to_all(term, "seq", split_axis=0, concat_axis=0, tiled=True)
 
     each = count // groups
@@ -304,8 +334,8 @@
         sums = lax.dynamic_slice_in_dim(arrived, (group ^ flip) * each, each, 0)
         bases.append(grp_move(sums, flip) if flip else sums)
 
-    grad_down = adapter_grad(rank_here[:, :ranks], mask, hidden_slab, weights)
-    grad_up = adapter_grad(rank_here[:, ranks:], mask, grad_slab, weights)
+    grad_down = adapter_grad(grad_rank, mask, hidden_slab, weights)
+    grad_up = adapter_grad(act_rank, mask, grad_slab, weights)
     grad_hidden = join(bases, term, group)
     return grad_hidden, grad_down, grad_up
 

time: 217 us -> 294 us (1.35)
  Pallas kernels: 26.2 us -> 72.9 us
  waiting for transfers between devices: 82.4 us -> 129 us
  starting transfers between devices: 62.6 us -> 51.8 us
  other arithmetic: 7.19 us -> 3.89 us
    ppermute x0 -> x10, waiting for transfers between devices: none -> 62.1 us  [sum_ranks(): parts = add(parts, lax.ppermute(parts, axis, pairs))]
    pallas_call x0 -> x12, Pallas kernels: none -> 26.1 us  [the longest x4 12 us: full_sums(): pl.pallas_call(full_kernel, grid_spec=pltpu.PrefetchScalarGridSpec(num_sc...]
    ppermute x14 -> x7, starting transfers between devices: 24.7 us -> 3.59 us  [seq_move(): return lax.ppermute(value, 'seq', pairs)]
    pallas_call x4, Pallas kernels: 21.8 us -> 42.4 us  [chunk_product(): pl.pallas_call(functools.partial(chunk_kernel, STAGES), grid_spec=pltpu.P...]
    all_to_all x1, waiting for transfers between devices: 15.4 us -> 0.01 us  [shards(): term = lax.all_to_all(term, 'seq', split_axis=0, concat_axis=0, tiled=True)]
    ppermute x0 -> x10, starting transfers between devices: none -> 13.4 us  [sum_ranks(): parts = add(parts, lax.ppermute(parts, axis, pairs))]
    dynamic_update_slice x8, local copies, waits for them, and re-layouts: 0.09 us -> 6.76 us  [shards(): lax.dynamic_update_index_in_dim(grad_slab, columns, back + (core ^ flip), 0)]
    dynamic_update_slice x8 -> x0, local copies, waits for them, and re-layouts: 6.41 us -> none  [put(): lax.dynamic_update_index_in_dim(arrived, came[flip], ahead + (core ^ flip...]
  transfers between devices with their start and end apart: 37 -> 39, of which waited for: 16 -> 15; matrix products, arithmetic and copies ran while one was open for 18% -> 10% of each run, Pallas kernels for 10% -> 23%
where the time goes in v2:
time: 294 us; the launch traced here: 292 us
  waiting for transfers between devices  129 us (44%)
  Pallas kernels  72.9 us (25%)
  starting transfers between devices  51.8 us (18%)
  matrix products  16.6 us (6%)
  local copies, waits for them, and re-layouts  16.3 us (6%)
  other arithmetic  3.89 us (1%)
    ppermute x10, waiting for transfers between devices, sum_ranks(): parts = add(parts, lax.ppermute(parts, axis, pairs))  62.1 us
    pallas_call x4, Pallas kernels, chunk_product(): pl.pallas_call(functools.partial(chunk_kernel, STAGES), grid_spec=pltpu.P...  42.4 us
    all_to_all x1, waiting for transfers between devices, shards(): lax.all_to_all(summed, 'seq', split_axis=0, concat_axis=0, tiled=True)  24.1 us
    ppermute x7, waiting for transfers between devices, seq_move(): return lax.ppermute(value, 'seq', pairs)  21.5 us
    ppermute x19, waiting for transfers between devices, grp_move(): return lax.ppermute(value, 'grp', [(g, g ^ flip) for g in range(groups)])  21.5 us
    ppermute x19, starting transfers between devices, grp_move(): return lax.ppermute(value, 'grp', [(g, g ^ flip) for g in range(groups)])  21 us
    ppermute x10, starting transfers between devices, sum_ranks(): parts = add(parts, lax.ppermute(parts, axis, pairs))  13.4 us
    dot_general x4, matrix products, dot(): lax.dot_general(left, right, dims, preferred_element_type=jnp.float32)  13 us
  transfers between devices with their start and end apart: 39, of which 15 were waited for; matrix products, arithmetic and copies ran while one was open for 10% of the time, Pallas kernels for 23%

profile of v2, /device:TPU:0, one launch (start us, length us, event | category | flops | bytes accessed | tf_op | source)
XLA Modules:
  0.0 291.8 jit_solution(2240955959590525408)
XLA Ops:
  3.7 5.6 %shard_map.108.refs_0_ = bf16[8,128,896]{2,1,0:T(8,128)(2,1)} custom-call(bf16[128,7168]{1,0:T(8,128)(2,1)} %rows_ref.1), custom_call_target="tpu_custom_call" | custom-call | bytes 3670016 | tf_op jit(solution)/shard_map/pallas_call | solution.py:146
  9.3 8.6 %collective-permute-done.near_ref = bf16[128,2048]{1,0:T(8,128)(2,1)} collective-permute-done((bf16[128,2048]{1,0:T(8,128)(2,1)}, bf16[128,2048]{1,0:T(8,128)(2,1)}, u32[]{:S(2)}, u32[]{:S(2)}) %collective-permute-start) | collective-permute-done | bytes 524320 | tf_op jit(solution)/shard_map/ppermute | solution.py:259
  20.2 12.9 %collective-permute-done.1.near_ref.refs_1_ = bf16[128,2048]{1,0:T(8,128)(2,1)S(1)} collective-permute-done((bf16[128,2048]{1,0:T(8,128)(2,1)}, bf16[128,2048]{1,0:T(8,128)(2,1)S(1)}, u32[]{:S(2)}, u32[]{:S(2)}) %collective-permute-start.1) | collective-permute-done | bytes 524320 | tf_op jit(solution)/shard_map/ppermute | solution.py:259
  34.6 10.6 %shard_map.100 = (bf16[2,32,3584]{2,1,0:T(8,128)(2,1)}, bf16[2,32,3584]{2,1,0:T(8,128)(2,1)}, bf16[2,32,3584]{2,1,0:T(8,128)(2,1)}, bf16[2,32,3584]{2,1,0:T(8,128)(2,1)}) custom-call(s32[1]{0:T(128)} %bitcast.place_ref, bf16[128,2048]{1,0:T(8,128)(2,1)} %near_ref.1, bf16[128,2048]{1,0:T(8,128)(2,1)} %copy-done.9, bf16[3584,2048]{1,0:T(8,128)(2,1)} %weight_ref.7), custom_call_target="tpu_custom_call" | custom-call | flops 3758096384 | bytes 17563648 | tf_op jit(solution)/shard_map/pallas_call | solution.py:57
  48.7 5.0 %all-to-all-start.2 = ((bf16[8,128,896]{2,1,0:T(8,128)(2,1)}), bf16[8,128,896]{2,1,0:T(8,128)(2,1)}, u32[]{:S(2)}, u32[]{:S(2)}) async-start(bf16[8,128,896]{2,1,0:T(8,128)(2,1)} %shard_map.109), calls=%async_computation.2 | async-start | bytes 3670016 | tf_op jit(solution)/shard_map/all_to_all | solution.py:270
  54.3 10.6 %shard_map.98 = (bf16[2,32,3584]{2,1,0:T(8,128)(2,1)}, bf16[2,32,3584]{2,1,0:T(8,128)(2,1)}, bf16[2,32,3584]{2,1,0:T(8,128)(2,1)}, bf16[2,32,3584]{2,1,0:T(8,128)(2,1)}) custom-call(s32[1]{0:T(128)} %bitcast.place_ref, bf16[128,2048]{1,0:T(8,128)(2,1)} %collective-permute-done.near_ref, bf16[128,2048]{1,0:T(8,128)(2,1)} %collective-permute-done.13.far_ref, ...), custom_call_target="tpu_custom_call" | custom-call | flops 3758096384 | bytes 17563648 | tf_op jit(solution)/shard_map/pallas_call | solution.py:57
  71.8 10.6 %shard_map.96 = (bf16[2,32,3584]{2,1,0:T(8,128)(2,1)}, bf16[2,32,3584]{2,1,0:T(8,128)(2,1)}, bf16[2,32,3584]{2,1,0:T(8,128)(2,1)}, bf16[2,32,3584]{2,1,0:T(8,128)(2,1)}) custom-call(s32[1]{0:T(128)} %bitcast.place_ref, bf16[128,2048]{1,0:T(8,128)(2,1)} %copy-done.1, bf16[128,2048]{1,0:T(8,128)(2,1)} %collective-permute-done.8.far_ref, ...), custom_call_target="tpu_custom_call" | custom-call | flops 3758096384 | bytes 17563648 | tf_op jit(solution)/shard_map/pallas_call | solution.py:57
  83.0 10.6 %shard_map.94 = (bf16[2,32,3584]{2,1,0:T(8,128)(2,1)}, bf16[2,32,3584]{2,1,0:T(8,128)(2,1)}, bf16[2,32,3584]{2,1,0:T(8,128)(2,1)}, bf16[2,32,3584]{2,1,0:T(8,128)(2,1)}) custom-call(s32[1]{0:T(128)} %bitcast.place_ref, bf16[128,2048]{1,0:T(8,128)(2,1)} %collective-permute-done.2.near_ref, bf16[128,2048]{1,0:T(8,128)(2,1)} %collective-permute-done.3.far_ref, ...), custom_call_target="tpu_custom_call" | custom-call | flops 3758096384 | bytes 17563648 | tf_op jit(solution)/shard_map/pallas_call | solution.py:57
  112.2 5.0 %collective-permute-done.4.near_came.refs_1_ = bf16[2,32,3584]{2,1,0:T(8,128)(2,1)S(1)} collective-permute-done((bf16[2,32,3584]{2,1,0:T(8,128)(2,1)}, bf16[2,32,3584]{2,1,0:T(8,128)(2,1)S(1)}, u32[]{:S(2)}, u32[]{:S(2)}) %collective-permute-start.4) | collective-permute-done | bytes 458784 | tf_op jit(solution)/shard_map/ppermute | solution.py:262
  143.4 3.9 %collective-permute-done.27 = bf16[512,128]{0,1:T(8,128)(2,1)S(1)} collective-permute-done((bf16[512,128]{0,1:T(8,128)(2,1)S(1)}, bf16[512,128]{0,1:T(8,128)(2,1)S(1)}, u32[]{:S(2)}, u32[]{:S(2)}) %collective-permute-start.27) | collective-permute-done | bytes 131104 | tf_op jit(solution)/shard_map/ppermute | solution.py:309
  150.0 4.5 %all-to-all-start = ((bf16[8,32,3584]{2,1,0:T(8,128)(2,1)}), bf16[8,32,3584]{2,1,0:T(8,128)(2,1)}, u32[]{:S(2)}, u32[]{:S(2)}) async-start(bf16[8,32,3584]{2,1,0:T(8,128)(2,1)} %shard_map.105.refs_1_), calls=%async_computation | async-start | bytes 3670016 | tf_op jit(solution)/shard_map/all_to_all | solution.py:290
  156.5 4.4 %collective-permute-done.29 = bf16[512,128]{0,1:T(8,128)(2,1)S(1)} collective-permute-done((bf16[512,128]{0,1:T(8,128)(2,1)S(1)}, bf16[512,128]{0,1:T(8,128)(2,1)S(1)}, u32[]{:S(2)}, u32[]{:S(2)}) %collective-permute-start.29) | collective-permute-done | bytes 131104 | tf_op jit(solution)/shard_map/ppermute | solution.py:309
  161.5 4.5 %collective-permute-done.30 = bf16[512,128]{0,1:T(8,128)(2,1)S(1)} collective-permute-done((bf16[512,128]{0,1:T(8,128)(2,1)S(1)}, bf16[512,128]{0,1:T(8,128)(2,1)S(1)}, u32[]{:S(2)}, u32[]{:S(2)}) %collective-permute-start.30) | collective-permute-done | bytes 131104 | tf_op jit(solution)/shard_map/ppermute | solution.py:309
  166.1 3.9 %multiply_reduce_fusion = bf16[1024,64]{0,1:T(8,128)(2,1)S(1)} fusion(f32[1024,16]{0,1:T(8,128)S(1)} %copy-done.17, bf16[16,64,896]{2,1,0:T(8,128)(2,1)S(1)} %copy-done, bf16[1024,896]{1,0:T(8,128)(2,1)} %shard_map.110), kind=kOutput, calls=%fused_computation | convolution fusion | flops 1881079808 | bytes 3866624 | tf_op jit(solution)/shard_map/dot_general | solution.py:19
  173.7 24.1 %all-to-all-done = bf16[8,32,3584]{2,1,0:T(8,128)(2,1)} async-done(((bf16[8,32,3584]{2,1,0:T(8,128)(2,1)}), bf16[8,32,3584]{2,1,0:T(8,128)(2,1)}, u32[]{:S(2)}, u32[]{:S(2)}) %all-to-all-start) | async-done | bytes 1835040 | tf_op jit(solution)/shard_map/all_to_all | solution.py:290
  197.8 4.3 %all-to-all-start.1 = ((bf16[8,128,896]{2,1,0:T(8,128)(2,1)}), bf16[8,128,896]{2,1,0:T(8,128)(2,1)}, u32[]{:S(2)}, u32[]{:S(2)}) async-start(bf16[8,128,896]{2,1,0:T(8,128)(2,1)} %bitcast.65), calls=%async_computation.1 | async-start | bytes 3670016 | tf_op jit(solution)/shard_map/all_to_all | solution.py:329
  204.1 31.4 %collective-permute-done.32 = bf16[512,128]{0,1:T(8,128)(2,1)S(1)} collective-permute-done((bf16[512,128]{0,1:T(8,128)(2,1)S(1)}, bf16[512,128]{0,1:T(8,128)(2,1)S(1)}, u32[]{:S(2)}, u32[]{:S(2)}) %collective-permute-start.32) | collective-permute-done | bytes 131104 | tf_op jit(solution)/shard_map/ppermute | solution.py:309
  235.5 4.6 %collective-permute-start.33 = (bf16[512,128]{0,1:T(8,128)(2,1)S(1)}, bf16[512,128]{0,1:T(8,128)(2,1)S(1)}, u32[]{:S(2)}, u32[]{:S(2)}) collective-permute-start(bf16[512,128]{0,1:T(8,128)(2,1)S(1)} %add_convert_fusion.3), channel_id=1, source_target_pairs={{0,4},{1,5},{2,6},{3,7},{4,0},{5,1},{6,2},{7,3},{8,12},{9,13},{10,... | collective-permute-start | bytes 393224 | tf_op jit(solution)/shard_map/ppermute | solution.py:309
  240.2 10.9 %collective-permute-done.33 = bf16[512,128]{0,1:T(8,128)(2,1)S(1)} collective-permute-done((bf16[512,128]{0,1:T(8,128)(2,1)S(1)}, bf16[512,128]{0,1:T(8,128)(2,1)S(1)}, u32[]{:S(2)}, u32[]{:S(2)}) %collective-permute-start.33) | collective-permute-done | bytes 131104 | tf_op jit(solution)/shard_map/ppermute | solution.py:309
  251.7 4.5 %collective-permute-done.34 = bf16[512,128]{0,1:T(8,128)(2,1)S(1)} collective-permute-done((bf16[512,128]{0,1:T(8,128)(2,1)S(1)}, bf16[512,128]{0,1:T(8,128)(2,1)S(1)}, u32[]{:S(2)}, u32[]{:S(2)}) %collective-permute-start.34) | collective-permute-done | bytes 131104 | tf_op jit(solution)/shard_map/ppermute | solution.py:309
  256.8 5.7 %fusion.7 = f32[16,64,896]{2,1,0:T(8,128)} fusion(bf16[1024,896]{1,0:T(8,128)(2,1)} %shard_map.110, f32[16]{0:T(128)S(1)} %broadcast_divide_fusion, bf16[1024,16]{0,1:T(8,128)(2,1)S(1)} %get-tuple-element.64, bf16[1024,64]{0,1:T(8,128)(2,1)S(1)} %pad_maximum_fusion.1), kind=kOutput, calls=%fused_computation.11 | convolution fusion | flops 1881014272 | bytes 5668928 | tf_op jit(solution)/shard_map/dot_general | solution.py:19
  270.1 8.2 %collective-permute-done.23.refs_1_ = bf16[2,32,3584]{2,1,0:T(8,128)(2,1)S(1)} collective-permute-done((bf16[2,32,3584]{2,1,0:T(8,128)(2,1)S(1)}, bf16[2,32,3584]{2,1,0:T(8,128)(2,1)S(1)}, u32[]{:S(2)}, u32[]{:S(2)}) %collective-permute-start.23) | collective-permute-done | bytes 458784 | tf_op jit(solution)/shard_map/ppermute | solution.py:262
  278.4 6.6 %collective-permute-done.24.refs_2_ = bf16[2,32,3584]{2,1,0:T(8,128)(2,1)S(1)} collective-permute-done((bf16[2,32,3584]{2,1,0:T(8,128)(2,1)S(1)}, bf16[2,32,3584]{2,1,0:T(8,128)(2,1)S(1)}, u32[]{:S(2)}, u32[]{:S(2)}) %collective-permute-start.24) | collective-permute-done | bytes 458784 | tf_op jit(solution)/shard_map/ppermute | solution.py:262
  287.4 4.4 %shard_map.107 = bf16[128,7168]{1,0:T(8,128)(2,1)} custom-call(s32[1]{0:T(128)} %bitcast.place_ref, bf16[2,32,3584]{2,1,0:T(8,128)(2,1)} %get-tuple-element.54.refs_0_, bf16[2,32,3584]{2,1,0:T(8,128)(2,1)} %copy-done.10, bf16[2,32,3584]{2,1,0:T(8,128)(2,1)} %copy-done.11, bf16[2,32,3584]{2,1,0:T(8,128)(2,1)} %copy-done.12, ...), custom_call_target="tpu_custom_call" | custom-call | flops 917504 | bytes 5505024 | tf_op jit(solution)/shard_map/pallas_call | solution.py:104
  (156 shorter events, 85.6 us)
Async XLA Ops:
  3.7 30.1 %collective-permute-start.18 = (bf16[128,2048]{1,0:T(8,128)(2,1)}, bf16[128,2048]{1,0:T(8,128)(2,1)S(1)}, u32[]{:S(2)}, u32[]{:S(2)}) collective-permute-start(bf16[128,2048]{1,0:T(8,128)(2,1)} %near_ref.1), channel_id=1, source_target_pairs={{0,1},{1,0},{2,3},{3,2},{4,5},{5,4},{6,7},{7,6},{8,9},{9,8},{10,11... | collective-permute-start | bytes 1572872 | tf_op jit(solution)/shard_map/ppermute | solution.py:259
  20.2 34.0 %collective-permute-start.13 = (bf16[128,2048]{1,0:T(8,128)(2,1)}, bf16[128,2048]{1,0:T(8,128)(2,1)}, u32[]{:S(2)}, u32[]{:S(2)}) collective-permute-start(bf16[128,2048]{1,0:T(8,128)(2,1)} %collective-permute-done.near_ref), channel_id=1, source_target_pairs={{0,1},{1,0},{2,3},{3,2},{4,5},{5,4},{6,7},{7,6},{8,9},{9,8},{10,11... | collective-permute-start | bytes 1572872 | tf_op jit(solution)/shard_map/ppermute | solution.py:259
  33.1 20.6 %collective-permute-start.2 = (bf16[128,2048]{1,0:T(8,128)(2,1)S(1)}, bf16[128,2048]{1,0:T(8,128)(2,1)}, u32[]{:S(2)}, u32[]{:S(2)}) collective-permute-start(bf16[128,2048]{1,0:T(8,128)(2,1)S(1)} %collective-permute-done.1.near_ref.refs_1_), channel_id=1, source_target_pairs={{0,2},{1,3},{2,4},{3,5},{4,6},{5,7},{6,0},{7,1},{8,10},{9,11},{10,... | collective-permute-start | bytes 1572872 | tf_op jit(solution)/shard_map/ppermute | solution.py:259
  33.8 36.5 %collective-permute-start.8 = (bf16[128,2048]{1,0:T(8,128)(2,1)S(1)}, bf16[128,2048]{1,0:T(8,128)(2,1)}, u32[]{:S(2)}, u32[]{:S(2)}) collective-permute-start(bf16[128,2048]{1,0:T(8,128)(2,1)S(1)} %collective-permute-done.1.near_ref.refs_1_), channel_id=1, source_target_pairs={{0,1},{1,0},{2,3},{3,2},{4,5},{5,4},{6,7},{7,6},{8,9},{9,8},{10,11... | collective-permute-start | bytes 1572872 | tf_op jit(solution)/shard_map/ppermute | solution.py:259
  45.2 19.6 %collective-permute-start.19 = (bf16[2,32,3584]{2,1,0:T(8,128)(2,1)}, bf16[2,32,3584]{2,1,0:T(8,128)(2,1)S(1)}, u32[]{:S(2)}, u32[]{:S(2)}) collective-permute-start(bf16[2,32,3584]{2,1,0:T(8,128)(2,1)} %get-tuple-element.46), channel_id=1, source_target_pairs={{0,8},{8,0},{16,24},{24,16},{1,9},{9,1},{17,25},{25,17},{2,10},{10... | collective-permute-start | bytes 1376264 | tf_op jit(solution)/shard_map/ppermute | solution.py:262
  46.5 18.3 %collective-permute-start.20 = (bf16[2,32,3584]{2,1,0:T(8,128)(2,1)}, bf16[2,32,3584]{2,1,0:T(8,128)(2,1)}, u32[]{:S(2)}, u32[]{:S(2)}) collective-permute-start(bf16[2,32,3584]{2,1,0:T(8,128)(2,1)} %get-tuple-element.48), channel_id=1, source_target_pairs={{0,16},{8,24},{16,0},{24,8},{1,17},{9,25},{17,1},{25,9},{2,18},{10... | collective-permute-start | bytes 1376264 | tf_op jit(solution)/shard_map/ppermute | solution.py:262
  48.7 101.3 %all-to-all-start.2 = ((bf16[8,128,896]{2,1,0:T(8,128)(2,1)}), bf16[8,128,896]{2,1,0:T(8,128)(2,1)}, u32[]{:S(2)}, u32[]{:S(2)}) async-start(bf16[8,128,896]{2,1,0:T(8,128)(2,1)} %shard_map.109), calls=%async_computation.2 | async-start | bytes 3670016 | tf_op jit(solution)/shard_map/all_to_all | solution.py:270
  53.7 28.7 %collective-permute-start.3 = (bf16[128,2048]{1,0:T(8,128)(2,1)}, bf16[128,2048]{1,0:T(8,128)(2,1)}, u32[]{:S(2)}, u32[]{:S(2)}) collective-permute-start(bf16[128,2048]{1,0:T(8,128)(2,1)} %collective-permute-done.2.near_ref), channel_id=1, source_target_pairs={{0,1},{1,0},{2,3},{3,2},{4,5},{5,4},{6,7},{7,6},{8,9},{9,8},{10,11... | collective-permute-start | bytes 1572872 | tf_op jit(solution)/shard_map/ppermute | solution.py:259
  67.8 25.9 %collective-permute-start.21 = (bf16[32,3584]{1,0:T(8,128)(2,1)}, bf16[32,3584]{1,0:T(8,128)(2,1)S(1)}, u32[]{:S(2)}, u32[]{:S(2)}) collective-permute-start(bf16[32,3584]{1,0:T(8,128)(2,1)} %get-tuple-element.49), channel_id=1, source_target_pairs={{0,16},{8,24},{16,0},{24,8},{1,17},{9,25},{17,1},{25,9},{2,18},{10... | collective-permute-start | bytes 688136 | tf_op jit(solution)/shard_map/ppermute | solution.py:262
  68.3 33.4 %collective-permute-start.22 = (bf16[32,3584]{1,0:T(8,128)(2,1)}, bf16[32,3584]{1,0:T(8,128)(2,1)}, u32[]{:S(2)}, u32[]{:S(2)}) collective-permute-start(bf16[32,3584]{1,0:T(8,128)(2,1)} %get-tuple-element.50), channel_id=1, source_target_pairs={{0,8},{8,0},{16,24},{24,16},{1,9},{9,1},{17,25},{25,17},{2,10},{10... | collective-permute-start | bytes 688136 | tf_op jit(solution)/shard_map/ppermute | solution.py:262
  69.1 25.4 %collective-permute-start.14 = (bf16[2,32,3584]{2,1,0:T(8,128)(2,1)}, bf16[2,32,3584]{2,1,0:T(8,128)(2,1)S(1)}, u32[]{:S(2)}, u32[]{:S(2)}) collective-permute-start(bf16[2,32,3584]{2,1,0:T(8,128)(2,1)} %get-tuple-element.40), channel_id=1, source_target_pairs={{0,8},{8,0},{16,24},{24,16},{1,9},{9,1},{17,25},{25,17},{2,10},{10... | collective-permute-start | bytes 1376264 | tf_op jit(solution)/shard_map/ppermute | solution.py:262
  70.3 25.4 %collective-permute-start.15 = (bf16[2,32,3584]{2,1,0:T(8,128)(2,1)}, bf16[2,32,3584]{2,1,0:T(8,128)(2,1)S(1)}, u32[]{:S(2)}, u32[]{:S(2)}) collective-permute-start(bf16[2,32,3584]{2,1,0:T(8,128)(2,1)} %get-tuple-element.42), channel_id=1, source_target_pairs={{0,16},{8,24},{16,0},{24,8},{1,17},{9,25},{17,1},{25,9},{2,18},{10... | collective-permute-start | bytes 1376264 | tf_op jit(solution)/shard_map/ppermute | solution.py:262
  82.4 21.4 %collective-permute-start.10 = (bf16[2,32,3584]{2,1,0:T(8,128)(2,1)}, bf16[2,32,3584]{2,1,0:T(8,128)(2,1)}, u32[]{:S(2)}, u32[]{:S(2)}) collective-permute-start(bf16[2,32,3584]{2,1,0:T(8,128)(2,1)} %get-tuple-element.36), channel_id=1, source_target_pairs={{0,16},{8,24},{16,0},{24,8},{1,17},{9,25},{17,1},{25,9},{2,18},{10... | collective-permute-start | bytes 1376264 | tf_op jit(solution)/shard_map/ppermute | solution.py:262
  94.5 22.7 %collective-permute-start.4 = (bf16[2,32,3584]{2,1,0:T(8,128)(2,1)}, bf16[2,32,3584]{2,1,0:T(8,128)(2,1)S(1)}, u32[]{:S(2)}, u32[]{:S(2)}) collective-permute-start(bf16[2,32,3584]{2,1,0:T(8,128)(2,1)} %get-tuple-element.28), channel_id=1, source_target_pairs={{0,8},{8,0},{16,24},{24,16},{1,9},{9,1},{17,25},{25,17},{2,10},{10... | collective-permute-start | bytes 1376264 | tf_op jit(solution)/shard_map/ppermute | solution.py:262
  96.5 21.4 %collective-permute-start.5 = (bf16[2,32,3584]{2,1,0:T(8,128)(2,1)}, bf16[2,32,3584]{2,1,0:T(8,128)(2,1)S(1)}, u32[]{:S(2)}, u32[]{:S(2)}) collective-permute-start(bf16[2,32,3584]{2,1,0:T(8,128)(2,1)} %get-tuple-element.30), channel_id=1, source_target_pairs={{0,16},{8,24},{16,0},{24,8},{1,17},{9,25},{17,1},{25,9},{2,18},{10... | collective-permute-start | bytes 1376264 | tf_op jit(solution)/shard_map/ppermute | solution.py:262
  101.7 20.5 %collective-permute-start.16 = (bf16[32,3584]{1,0:T(8,128)(2,1)}, bf16[32,3584]{1,0:T(8,128)(2,1)}, u32[]{:S(2)}, u32[]{:S(2)}) collective-permute-start(bf16[32,3584]{1,0:T(8,128)(2,1)} %get-tuple-element.43), channel_id=1, source_target_pairs={{0,16},{8,24},{16,0},{24,8},{1,17},{9,25},{17,1},{25,9},{2,18},{10... | collective-permute-start | bytes 688136 | tf_op jit(solution)/shard_map/ppermute | solution.py:262
  103.9 21.5 %collective-permute-start.17 = (bf16[32,3584]{1,0:T(8,128)(2,1)}, bf16[32,3584]{1,0:T(8,128)(2,1)}, u32[]{:S(2)}, u32[]{:S(2)}) collective-permute-start(bf16[32,3584]{1,0:T(8,128)(2,1)} %get-tuple-element.44), channel_id=1, source_target_pairs={{0,8},{8,0},{16,24},{24,16},{1,9},{9,1},{17,25},{25,17},{2,10},{10... | collective-permute-start | bytes 688136 | tf_op jit(solution)/shard_map/ppermute | solution.py:262
  110.7 18.5 %collective-permute-start.11 = (bf16[32,3584]{1,0:T(8,128)(2,1)}, bf16[32,3584]{1,0:T(8,128)(2,1)S(1)}, u32[]{:S(2)}, u32[]{:S(2)}) collective-permute-start(bf16[32,3584]{1,0:T(8,128)(2,1)} %get-tuple-element.37), channel_id=1, source_target_pairs={{0,16},{8,24},{16,0},{24,8},{1,17},{9,25},{17,1},{25,9},{2,18},{10... | collective-permute-start | bytes 688136 | tf_op jit(solution)/shard_map/ppermute | solution.py:262
  150.0 47.8 %all-to-all-start = ((bf16[8,32,3584]{2,1,0:T(8,128)(2,1)}), bf16[8,32,3584]{2,1,0:T(8,128)(2,1)}, u32[]{:S(2)}, u32[]{:S(2)}) async-start(bf16[8,32,3584]{2,1,0:T(8,128)(2,1)} %shard_map.105.refs_1_), calls=%async_computation | async-start | bytes 3670016 | tf_op jit(solution)/shard_map/all_to_all | solution.py:290
  170.0 32.1 %collective-permute-start.31 = (bf16[512,128]{0,1:T(8,128)(2,1)S(1)}, bf16[512,128]{0,1:T(8,128)(2,1)S(1)}, u32[]{:S(2)}, u32[]{:S(2)}) collective-permute-start(bf16[512,128]{0,1:T(8,128)(2,1)S(1)} %pad_maximum_fusion.2), channel_id=1, source_target_pairs={{0,1},{1,0},{2,3},{3,2},{4,5},{5,4},{6,7},{7,6},{8,9},{9,8},{10,11... | collective-permute-start | bytes 393224 | tf_op jit(solution)/shard_map/ppermute | solution.py:309
  197.8 88.8 %all-to-all-start.1 = ((bf16[8,128,896]{2,1,0:T(8,128)(2,1)}), bf16[8,128,896]{2,1,0:T(8,128)(2,1)}, u32[]{:S(2)}, u32[]{:S(2)}) async-start(bf16[8,128,896]{2,1,0:T(8,128)(2,1)} %bitcast.65), calls=%async_computation.1 | async-start | bytes 3670016 | tf_op jit(solution)/shard_map/all_to_all | solution.py:329
  202.2 33.3 %collective-permute-start.32 = (bf16[512,128]{0,1:T(8,128)(2,1)S(1)}, bf16[512,128]{0,1:T(8,128)(2,1)S(1)}, u32[]{:S(2)}, u32[]{:S(2)}) collective-permute-start(bf16[512,128]{0,1:T(8,128)(2,1)S(1)} %add_convert_fusion.4), channel_id=1, source_target_pairs={{0,2},{1,3},{2,0},{3,1},{4,6},{5,7},{6,4},{7,5},{8,10},{9,11},{10,... | collective-permute-start | bytes 393224 | tf_op jit(solution)/shard_map/ppermute | solution.py:309
  265.7 19.3 %collective-permute-start.24 = (bf16[2,32,3584]{2,1,0:T(8,128)(2,1)S(1)}, bf16[2,32,3584]{2,1,0:T(8,128)(2,1)S(1)}, u32[]{:S(2)}, u32[]{:S(2)}) collective-permute-start(bf16[2,32,3584]{2,1,0:T(8,128)(2,1)S(1)} %get-tuple-element.52), channel_id=1, source_target_pairs={{0,16},{8,24},{16,0},{24,8},{1,17},{9,25},{17,1},{25,9},{2,18},{10... | collective-permute-start | bytes 1376264 | tf_op jit(solution)/shard_map/ppermute | solution.py:262
  267.0 19.6 %collective-permute-start.25 = (bf16[2,32,3584]{2,1,0:T(8,128)(2,1)S(1)}, bf16[2,32,3584]{2,1,0:T(8,128)(2,1)S(1)}, u32[]{:S(2)}, u32[]{:S(2)}) collective-permute-start(bf16[2,32,3584]{2,1,0:T(8,128)(2,1)S(1)} %get-tuple-element.51), channel_id=1, source_target_pairs={{0,24},{8,16},{16,8},{24,0},{1,25},{9,17},{17,9},{25,1},{2,26},{10... | collective-permute-start | bytes 1376264 | tf_op jit(solution)/shard_map/ppermute | solution.py:262
  (36 other events, 388.5 us)

commit v3 on v1

--- a/solution.py
+++ b/solution.py
@@ -12,6 +12,7 @@
 CONTRACT_ROWS = (((0,), (0,)), ((), ()))
 CORES = 2
 MOST_ROWS = 1024
+ANYWHERE = pl.BlockSpec(memory_space=pl.ANY)
 
 
 def dot(left, right, dims):
@@ -29,7 +30,7 @@
 
 
 def chunk_kernel(stages, place_ref, near_ref, far_ref, weight_ref, *rest):
-    outs, rows = rest[:-1], rest[-1]
+    outs, rows = rest[-5:-1], rest[-1]
     part = near_ref.shape[0] // (2 * len(stages))
     sides = [(ref, flips) for ref, order in zip((near_ref, far_ref), stages) for flips in order]
     cuts = [(ref, flip) for ref, flips in sides for flip in flips]
@@ -48,7 +49,7 @@
 STAGES = (((0, 2), (1, 3)), ((0, 1), (2, 3)))
 
 
-def chunk_product(near, far, weight, group):
+def chunk_product(near, far, weight, group, *gates):
     block, depth = near.shape
     width = weight.shape[0]
     tile = tile_of(width)
@@ -62,7 +63,8 @@
                 pl.BlockSpec((block, depth), lambda at, place: (0, 0)),
                 pl.BlockSpec((block, depth), lambda at, place: (0, 0)),
                 pl.BlockSpec((tile, depth), lambda at, place: (at, 0)),
-            ],
+            ]
+            + [ANYWHERE] * len(gates),
             out_specs=[pl.BlockSpec((2, part, tile), lambda at, place: (0, 0, at))] * 4,
             scratch_shapes=[pltpu.VMEM((CORES * block, depth), jnp.bfloat16)],
         ),
@@ -73,7 +75,7 @@
             bytes_accessed=2 * (width * depth + CORES * block * (depth + width)),
             transcendentals=0,
         ),
-    )(group.reshape(1), near, far, weight)
+    )(group.reshape(1), near, far, weight, *gates)
 
 
 def join_kernel(groups, slab, place_ref, *refs):
@@ -120,8 +122,18 @@
     return sum(term.astype(jnp.float32) for term in terms).astype(jnp.bfloat16)
 
 
-def after(value, *others):
-    return lax.optimization_barrier((value,) + others)[0]
+def touch_kernel(*refs):
+    pass
+
+
+def touch(values, *gates):
+    return pl.pallas_call(
+        touch_kernel,
+        in_specs=[ANYWHERE] * (len(values) + len(gates)),
+        out_specs=[ANYWHERE] * len(values),
+        out_shape=[jax.ShapeDtypeStruct(value.shape, value.dtype) for value in values],
+        input_output_aliases={at: at for at in range(len(values))},
+    )(*values, *gates)
 
 
 def project(rows, adapter, mask):
@@ -196,10 +208,12 @@
     ).reshape(count * block, down_slab)
 
     last = chips - 1
-    products = [chunk_product(near, far, down_weight, group) for near, far in pairs]
-    firsts = [
-        (grp_move(near_sent, 1), grp_move(far_sent, 2)) for _, near_sent, _, far_sent in products
-    ]
+
+    def product(step, *gates):
+        return chunk_product(*pairs[step], down_weight, group, *gates)
+
+    products = [product(step) for step in range(last - 1)]
+    (hidden_slab,) = touch([hidden_slab], products[-1][0])
     grad_slab = jnp.zeros((count, block, up_slab), jnp.bfloat16)
     for step, pair in enumerate(pairs):
         back = ((chip - step) % chips) * CORES
@@ -207,19 +221,27 @@
             columns = lax.dynamic_slice_in_dim(rows, index * up_slab, up_slab, 1)
             grad_slab = lax.dynamic_update_index_in_dim(grad_slab, columns, back + (core ^ flip), 0)
     grad_slab = grad_slab.reshape(count * block, up_slab)
+    act_part = project(hidden_slab, adapter_down, mask)
+    grad_part = project(grad_slab, adapter_up, mask)
+    ranked = jnp.concatenate([grad_part, act_part], axis=1)
+
+    products += [product(last - 1, act_part), product(last, ranked)]
+
+    firsts = [
+        (grp_move(near_sent, 1), grp_move(far_sent, 2)) for _, near_sent, _, far_sent in products
+    ]
 
     def second(step, *gates):
         near_kept, _, far_kept, _ = products[step]
-        near_came, far_came = firsts[step]
-        near_came, far_came = lax.optimization_barrier((near_came, far_came) + gates)[:2]
+        near_came, far_came = firsts[step] = touch(firsts[step], *gates)
         near_sum = add(near_kept[1], near_came[1])
         far_sum = add(far_kept[1], far_came[1])
-        return near_sum, (grp_move(near_sum, 2), grp_move(far_sum, 1))
+        return near_sum, [grp_move(near_sum, 2), grp_move(far_sum, 1)]
 
     def total(step, seconds, *gates):
         near_kept, _, far_kept, _ = products[step]
         near_came, far_came = firsts[step]
-        near_last, far_last = lax.optimization_barrier(seconds + gates)[:2]
+        near_last, far_last = touch(seconds, *gates) if gates else seconds
         return (
             add(near_kept[0], near_came[0], near_last),
             add(far_kept[0], far_came[0], far_last),
@@ -235,7 +257,7 @@
 
     def put(arrived, step, came, *gates):
         ahead = ((chip + step) % chips) * CORES
-        came = lax.optimization_barrier(tuple(came) + gates)
+        came = touch(came, *gates)
         for flip in range(CORES):
             arrived = lax.dynamic_update_index_in_dim(arrived, came[flip], ahead + (core ^ flip), 0)
         return arrived
@@ -248,12 +270,6 @@
             arrived = put(arrived, step - 1, came, sums[0])
         came = hop(step, sums)
 
-    begun, seconds = second(last - 1, products[last][0])
-    rows_here = lax.optimization_barrier((grad_slab, hidden_slab, begun))
-    ranked = jnp.concatenate(
-        [project(rows_here[0], adapter_up, mask), project(rows_here[1], adapter_down, mask)],
-        axis=1,
-    )
     devices = count * groups
     share = lax.all_to_all(
         ranked.reshape(devices, -1, 2 * ranks),
@@ -262,11 +278,8 @@
         concat_axis=0,
         tiled=True,
     )
-    sums = total(last - 1, seconds, ranked)
-    arrived = put(arrived, last - 2, came, sums[0])
-    came = hop(last - 1, sums)
-    begun, seconds = second(last, sums[0])
-    share = after(share, begun)
+    begun, seconds = second(last - 1, products[last][0])
+    (share,) = touch([share], begun)
     share = jnp.sum(share.astype(jnp.float32), axis=0).astype(jnp.bfloat16)
     ranked = lax.all_to_all(
         jnp.broadcast_to(share[None], (devices,) + share.shape),
@@ -275,10 +288,14 @@
         concat_axis=0,
         tiled=True,
     ).reshape(count * block, 2 * ranks)
-    sums = total(last, seconds, share)
+    sums = total(last - 1, seconds, share)
+    arrived = put(arrived, last - 2, came, sums[0])
+    came = hop(last - 1, sums)
+    _, seconds = second(last, sums[0])
+    sums = total(last, seconds)
     arrived = put(arrived, last - 1, came, sums[0])
     came = hop(last, sums)
-    ranked = after(ranked, *sums)
+    (ranked,) = touch([ranked], *sums)
     grad_rank = ranked[:, :ranks]
 
     flat_down = adapter_down.reshape(tenants * ranks, down_slab)
@@ -295,7 +312,7 @@
     )
     term = (term * ADAPTER_SCALE).astype(jnp.bfloat16).reshape(count, block, down_slab)
     arrived = put(arrived, last, came, term)
-    rank_here = after(ranked, term)
+    (rank_here,) = touch([ranked], term)
     term = lax.all_to_all(term, "seq", split_axis=0, concat_axis=0, tiled=True)
 
     each = count // groups

time: 217 us -> 264 us (1.22)
  local copies, waits for them, and re-layouts: 19.2 us -> 54.7 us
  other arithmetic: 7.19 us -> 29 us
  waiting for transfers between devices: 82.4 us -> 60.6 us
  starting transfers between devices: 62.6 us -> 73.3 us
    unnamed x24 -> x108, local copies, waits for them, and re-layouts: 5.22 us -> 29.3 us
    convert_element_type x16, other arithmetic: 6.04 us -> 24.9 us  [add(): sum((term.astype(jnp.float32) for term in terms)).astype(jnp.bfloat16)]
    ppermute x14, waiting for transfers between devices: 20.3 us -> 34.7 us  [seq_move(): return lax.ppermute(value, 'seq', pairs)]
    ppermute x19, waiting for transfers between devices: 27.7 us -> 16.7 us  [grp_move(): return lax.ppermute(value, 'grp', [(g, g ^ flip) for g in range(groups)])]
    all_to_all x1, waiting for transfers between devices: 10.3 us -> 0.01 us  [shards(): lax.all_to_all(jnp.broadcast_to(share[None], (devices,) + share.shape), (...]
    all_to_all x1, waiting for transfers between devices: 8.74 us -> 0.01 us  [shards(): lax.all_to_all(ranked.reshape(devices, -1, 2 * ranks), ('grp', 'seq'), sp...]
    ppermute x14, starting transfers between devices: 24.7 us -> 32.1 us  [seq_move(): return lax.ppermute(value, 'seq', pairs)]
    all_to_all x1, waiting for transfers between devices: 15.4 us -> 9.15 us  [shards(): term = lax.all_to_all(term, 'seq', split_axis=0, concat_axis=0, tiled=True)]
  transfers between devices with their start and end apart: 37 -> 37, of which waited for: 16 -> 11; matrix products, arithmetic and copies ran while one was open for 18% -> 27% of each run, Pallas kernels for 10% -> 9%
where the time goes in v3:
time: 264 us; the launch traced here: 263 us
  starting transfers between devices  73.3 us (28%)
  waiting for transfers between devices  60.6 us (23%)
  local copies, waits for them, and re-layouts  54.7 us (21%)
  other arithmetic  29 us (11%)
  Pallas kernels  26.8 us (10%)
  matrix products  16.7 us (6%)
    ppermute x14, waiting for transfers between devices, seq_move(): return lax.ppermute(value, 'seq', pairs)  34.7 us
    ppermute x14, starting transfers between devices, seq_move(): return lax.ppermute(value, 'seq', pairs)  32.1 us
    unnamed x108, local copies, waits for them, and re-layouts  29.3 us
    convert_element_type x16, other arithmetic, add(): sum((term.astype(jnp.float32) for term in terms)).astype(jnp.bfloat16)  24.9 us
    pallas_call x4, Pallas kernels, chunk_product(): pl.pallas_call(functools.partial(chunk_kernel, STAGES), grid_spec=pltpu.P...  22.4 us
    ppermute x19, starting transfers between devices, grp_move(): return lax.ppermute(value, 'grp', [(g, g ^ flip) for g in range(groups)])  22.4 us
    ppermute x19, waiting for transfers between devices, grp_move(): return lax.ppermute(value, 'grp', [(g, g ^ flip) for g in range(groups)])  16.7 us
    dot_general x4, matrix products, dot(): lax.dot_general(left, right, dims, preferred_element_type=jnp.float32)  13.1 us
  transfers between devices with their start and end apart: 37, of which 11 were waited for; matrix products, arithmetic and copies ran while one was open for 27% of the time, Pallas kernels for 9%

profile of v3, /device:TPU:0, one launch (start us, length us, event | category | flops | bytes accessed | tf_op | source)
XLA Modules:
  0.0 262.6 jit_solution(13467323010813798485)
XLA Ops:
  6.8 4.5 %all-to-all-start = ((bf16[8,128,896]{2,1,0:T(8,128)(2,1)}), bf16[8,128,896]{2,1,0:T(8,128)(2,1)}, u32[]{:S(2)}, u32[]{:S(2)}) async-start(bf16[8,128,896]{2,1,0:T(8,128)(2,1)} %bitcast.134), calls=%async_computation | async-start | bytes 3670016 | tf_op jit(solution)/shard_map/all_to_all | solution.py:202
  11.9 7.0 %collective-permute-done.3.near_ref = bf16[128,2048]{1,0:T(8,128)(2,1)S(1)} collective-permute-done((bf16[128,2048]{1,0:T(8,128)(2,1)}, bf16[128,2048]{1,0:T(8,128)(2,1)S(1)}, u32[]{:S(2)}, u32[]{:S(2)}) %collective-permute-start.3) | collective-permute-done | bytes 524320 | tf_op jit(solution)/shard_map/ppermute | solution.py:192
  18.9 5.2 %copy-done.1 = bf16[3584,2048]{1,0:T(8,128)(2,1)S(1)} copy-done((bf16[3584,2048]{1,0:T(8,128)(2,1)S(1)}, bf16[3584,2048]{1,0:T(8,128)(2,1)}, u32[]{:S(2)}) %copy-start.1) | copy-done | bytes 14680088
  24.1 5.4 %shard_map.94 = (bf16[2,32,3584]{2,1,0:T(8,128)(2,1)S(1)}, bf16[2,32,3584]{2,1,0:T(8,128)(2,1)S(1)}, bf16[2,32,3584]{2,1,0:T(8,128)(2,1)S(1)}, bf16[2,32,3584]{2,1,0:T(8,128)(2,1)S(1)}) custom-call(s32[1]{0:T(128)} %bitcast.place_ref, bf16[128,2048]{1,0:T(8,128)(2,1)S(1)} %copy-done.11, bf16[128,2048]{1,0:T(8,128)(2,1)S(1)} %collective-permute-done.far_ref, ...), custom_call_target="tpu_custom_call" | custom-call | flops 3758096384 | bytes 17563648 | tf_op jit(solution)/shard_map/pallas_call | solution.py:57
  32.8 4.3 %collective-permute-start.10 = (bf16[128,2048]{1,0:T(8,128)(2,1)S(1)}, bf16[128,2048]{1,0:T(8,128)(2,1)S(1)}, u32[]{:S(2)}, u32[]{:S(2)}) collective-permute-start(bf16[128,2048]{1,0:T(8,128)(2,1)S(1)} %collective-permute-done.3.near_ref), channel_id=1, source_target_pairs={{0,2},{1,3},{2,4},{3,5},{4,6},{5,7},{6,0},{7,1},{8,10},{9,11},{10,... | collective-permute-start | bytes 1572872 | tf_op jit(solution)/shard_map/ppermute | solution.py:192
  37.2 5.5 %shard_map.95 = (bf16[2,32,3584]{2,1,0:T(8,128)(2,1)S(1)}, bf16[2,32,3584]{2,1,0:T(8,128)(2,1)S(1)}, bf16[2,32,3584]{2,1,0:T(8,128)(2,1)S(1)}, bf16[2,32,3584]{2,1,0:T(8,128)(2,1)S(1)}) custom-call(s32[1]{0:T(128)} %bitcast.place_ref, bf16[128,2048]{1,0:T(8,128)(2,1)S(1)} %collective-permute-done.3.near_ref, ...), custom_call_target="tpu_custom_call" | custom-call | flops 3758096384 | bytes 17563648 | tf_op jit(solution)/shard_map/pallas_call | solution.py:57
  53.9 5.6 %collective-permute-done.10.near_ref = bf16[128,2048]{1,0:T(8,128)(2,1)S(1)} collective-permute-done((bf16[128,2048]{1,0:T(8,128)(2,1)S(1)}, bf16[128,2048]{1,0:T(8,128)(2,1)S(1)}, u32[]{:S(2)}, u32[]{:S(2)}) %collective-permute-start.10) | collective-permute-done | bytes 524320 | tf_op jit(solution)/shard_map/ppermute | solution.py:192
  61.6 8.5 %collective-permute-start.18 = (bf16[128,2048]{1,0:T(8,128)(2,1)S(1)}, bf16[128,2048]{1,0:T(8,128)(2,1)S(1)}, u32[]{:S(2)}, u32[]{:S(2)}) collective-permute-start(bf16[128,2048]{1,0:T(8,128)(2,1)S(1)} %collective-permute-done.10.near_ref), channel_id=1, source_target_pairs={{0,2},{1,3},{2,4},{3,5},{4,6},{5,7},{6,0},{7,1},{8,10},{9,11},{10,... | collective-permute-start | bytes 1572872 | tf_op jit(solution)/shard_map/ppermute | solution.py:192
  72.2 9.8 %collective-permute-done.18.near_ref = bf16[128,2048]{1,0:T(8,128)(2,1)S(1)} collective-permute-done((bf16[128,2048]{1,0:T(8,128)(2,1)S(1)}, bf16[128,2048]{1,0:T(8,128)(2,1)S(1)}, u32[]{:S(2)}, u32[]{:S(2)}) %collective-permute-start.18) | collective-permute-done | bytes 524320 | tf_op jit(solution)/shard_map/ppermute | solution.py:192
  87.1 3.9 %multiply_reduce_fusion.1 = bf16[1024,64]{0,1:T(8,128)(2,1)S(1)} fusion(f32[1024,16]{0,1:T(8,128)S(1)} %get-tuple-element.78, bf16[16,64,896]{2,1,0:T(8,128)(2,1)S(1)} %copy-done, bf16[1024,896]{1,0:T(8,128)(2,1)} %shard_map.97), kind=kOutput, calls=%fused_computation.1 | convolution fusion | flops 1881079808 | bytes 3866624 | tf_op jit(solution)/shard_map/dot_general | solution.py:19
  91.2 5.2 %copy-done.3 = bf16[3584,2048]{1,0:T(8,128)(2,1)S(1)} copy-done((bf16[3584,2048]{1,0:T(8,128)(2,1)S(1)}, bf16[3584,2048]{1,0:T(8,128)(2,1)}, u32[]{:S(2)}) %copy-start.3) | copy-done | bytes 14680088
  97.4 5.4 %shard_map.98 = (bf16[2,32,3584]{2,1,0:T(8,128)(2,1)S(1)}, bf16[2,32,3584]{2,1,0:T(8,128)(2,1)S(1)}, bf16[2,32,3584]{2,1,0:T(8,128)(2,1)S(1)}, bf16[2,32,3584]{2,1,0:T(8,128)(2,1)S(1)}) custom-call(s32[1]{0:T(128)} %bitcast.place_ref, bf16[128,2048]{1,0:T(8,128)(2,1)S(1)} %copy-done.13, bf16[128,2048]{1,0:T(8,128)(2,1)S(1)} %copy-done.20, ...), custom_call_target="tpu_custom_call" | custom-call | flops 3758096384 | bytes 17563648 | tf_op jit(solution)/shard_map/pallas_call | solution.py:57
  116.5 6.8 %all-to-all-start.1 = ((bf16[32,32,128]{2,1,0:T(8,128)(2,1)}), bf16[32,32,128]{2,1,0:T(8,128)(2,1)}, u32[]{:S(2)}, u32[]{:S(2)}) async-start(bf16[32,32,128]{2,1,0:T(8,128)(2,1)} %pad_maximum_fusion.1), calls=%async_computation.1 | async-start | bytes 524288 | tf_op jit(solution)/shard_map/all_to_all | solution.py:274
  123.3 5.2 %copy-done.4 = bf16[3584,2048]{1,0:T(8,128)(2,1)S(1)} copy-done((bf16[3584,2048]{1,0:T(8,128)(2,1)S(1)}, bf16[3584,2048]{1,0:T(8,128)(2,1)}, u32[]{:S(2)}) %copy-start.4) | copy-done | bytes 14680088
  129.5 6.1 %shard_map.101 = (bf16[2,32,3584]{2,1,0:T(8,128)(2,1)S(1)}, bf16[2,32,3584]{2,1,0:T(8,128)(2,1)}, bf16[2,32,3584]{2,1,0:T(8,128)(2,1)S(1)}, bf16[2,32,3584]{2,1,0:T(8,128)(2,1)}) custom-call(s32[1]{0:T(128)} %bitcast.place_ref, bf16[128,2048]{1,0:T(8,128)(2,1)S(1)} %copy-done.15, bf16[128,2048]{1,0:T(8,128)(2,1)S(1)} %copy-done.17, ...), custom_call_target="tpu_custom_call" | custom-call | flops 3758096384 | bytes 17563648 | tf_op jit(solution)/shard_map/pallas_call | solution.py:57
  183.7 6.6 %collective-permute-start.29 = (bf16[32,3584]{1,0:T(8,128)(2,1)}, bf16[32,3584]{1,0:T(8,128)(2,1)S(1)}, u32[]{:S(2)}, u32[]{:S(2)}) collective-permute-start(bf16[32,3584]{1,0:T(8,128)(2,1)} %fusion.25.refs_2_), channel_id=1, source_target_pairs={{0,3},{1,2},{2,5},{3,4},{4,7},{5,6},{6,1},{7,0},{8,11},{9,10},{10,... | collective-permute-start | bytes 688136 | tf_op jit(solution)/shard_map/ppermute | solution.py:192
  190.3 8.0 %collective-permute-done.22.refs_0_ = bf16[32,3584]{1,0:T(8,128)(2,1)S(1)} collective-permute-done((bf16[32,3584]{1,0:T(8,128)(2,1)}, bf16[32,3584]{1,0:T(8,128)(2,1)S(1)}, u32[]{:S(2)}, u32[]{:S(2)}) %collective-permute-start.22) | collective-permute-done | bytes 229408 | tf_op jit(solution)/shard_map/ppermute | solution.py:192
  198.3 4.1 %collective-permute-done.23.refs_1_ = bf16[32,3584]{1,0:T(8,128)(2,1)} collective-permute-done((bf16[32,3584]{1,0:T(8,128)(2,1)}, bf16[32,3584]{1,0:T(8,128)(2,1)}, u32[]{:S(2)}, u32[]{:S(2)}) %collective-permute-start.23) | collective-permute-done | bytes 229408 | tf_op jit(solution)/shard_map/ppermute | solution.py:192
  210.4 4.3 %all-to-all-start.3 = ((bf16[8,128,896]{2,1,0:T(8,128)(2,1)}), bf16[8,128,896]{2,1,0:T(8,128)(2,1)}, u32[]{:S(2)}, u32[]{:S(2)}) async-start(bf16[8,128,896]{2,1,0:T(8,128)(2,1)} %bitcast.131), calls=%async_computation.3 | async-start | bytes 3670016 | tf_op jit(solution)/shard_map/all_to_all | solution.py:316
  228.7 5.7 %fusion.9 = f32[16,64,896]{2,1,0:T(8,128)} fusion(bf16[1024,896]{1,0:T(8,128)(2,1)} %shard_map.97, f32[16]{0:T(128)S(1)} %broadcast_divide_fusion, bf16[1024,64]{0,1:T(8,128)(2,1)S(1)} %copy.56, bf16[1024,16]{0,1:T(8,128)(2,1)S(1)} %get-tuple-element.77), kind=kOutput, calls=%fused_computation.12 | convolution fusion | flops 1881014272 | bytes 5668928 | tf_op jit(solution)/shard_map/dot_general | solution.py:19
  234.4 4.2 %collective-permute-done.30.refs_1_ = bf16[2,32,3584]{2,1,0:T(8,128)(2,1)S(1)} collective-permute-done((bf16[2,32,3584]{2,1,0:T(8,128)(2,1)S(1)}, bf16[2,32,3584]{2,1,0:T(8,128)(2,1)S(1)}, u32[]{:S(2)}, u32[]{:S(2)}) %collective-permute-start.30) | collective-permute-done | bytes 458784 | tf_op jit(solution)/shard_map/ppermute | solution.py:195
  238.6 10.5 %collective-permute-done.31.refs_2_ = bf16[2,32,3584]{2,1,0:T(8,128)(2,1)S(1)} collective-permute-done((bf16[2,32,3584]{2,1,0:T(8,128)(2,1)S(1)}, bf16[2,32,3584]{2,1,0:T(8,128)(2,1)S(1)}, u32[]{:S(2)}, u32[]{:S(2)}) %collective-permute-start.31) | collective-permute-done | bytes 458784 | tf_op jit(solution)/shard_map/ppermute | solution.py:195
  249.0 9.2 %all-to-all-done.3.refs_4_ = bf16[8,128,896]{2,1,0:T(8,128)(2,1)} async-done(((bf16[8,128,896]{2,1,0:T(8,128)(2,1)}), bf16[8,128,896]{2,1,0:T(8,128)(2,1)}, u32[]{:S(2)}, u32[]{:S(2)}) %all-to-all-start.3) | async-done | bytes 1835040 | tf_op jit(solution)/shard_map/all_to_all | solution.py:316
  258.2 4.4 %shard_map.110 = bf16[128,7168]{1,0:T(8,128)(2,1)} custom-call(s32[1]{0:T(128)} %bitcast.place_ref, bf16[2,32,3584]{2,1,0:T(8,128)(2,1)} %get-tuple-element.74.refs_0_, bf16[2,32,3584]{2,1,0:T(8,128)(2,1)} %copy-done.47, bf16[2,32,3584]{2,1,0:T(8,128)(2,1)} %copy-done.48, bf16[2,32,3584]{2,1,0:T(8,128)(2,1)} %copy-done.49, ...), custom_call_target="tpu_custom_call" | custom-call | flops 917504 | bytes 5505024 | tf_op jit(solution)/shard_map/pallas_call | solution.py:105
  (233 shorter events, 116.0 us)
Async XLA Ops:
  6.8 80.3 %all-to-all-start = ((bf16[8,128,896]{2,1,0:T(8,128)(2,1)}), bf16[8,128,896]{2,1,0:T(8,128)(2,1)}, u32[]{:S(2)}, u32[]{:S(2)}) async-start(bf16[8,128,896]{2,1,0:T(8,128)(2,1)} %bitcast.134), calls=%async_computation | async-start | bytes 3670016 | tf_op jit(solution)/shard_map/all_to_all | solution.py:202
  32.8 26.7 %collective-permute-start.10 = (bf16[128,2048]{1,0:T(8,128)(2,1)S(1)}, bf16[128,2048]{1,0:T(8,128)(2,1)S(1)}, u32[]{:S(2)}, u32[]{:S(2)}) collective-permute-start(bf16[128,2048]{1,0:T(8,128)(2,1)S(1)} %collective-permute-done.3.near_ref), channel_id=1, source_target_pairs={{0,2},{1,3},{2,4},{3,5},{4,6},{5,7},{6,0},{7,1},{8,10},{9,11},{10,... | collective-permute-start | bytes 1572872 | tf_op jit(solution)/shard_map/ppermute | solution.py:192
  50.3 21.7 %collective-permute-start.5 = (bf16[32,3584]{1,0:T(8,128)(2,1)S(1)}, bf16[32,3584]{1,0:T(8,128)(2,1)S(1)}, u32[]{:S(2)}, u32[]{:S(2)}) collective-permute-start(bf16[32,3584]{1,0:T(8,128)(2,1)S(1)} %fusion.33), channel_id=1, source_target_pairs={{0,16},{8,24},{16,0},{24,8},{1,17},{9,25},{17,1},{25,9},{2,18},{10... | collective-permute-start | bytes 688136 | tf_op jit(solution)/shard_map/ppermute | solution.py:195
  50.9 55.1 %collective-permute-start.8 = (bf16[2,32,3584]{2,1,0:T(8,128)(2,1)}, bf16[2,32,3584]{2,1,0:T(8,128)(2,1)}, u32[]{:S(2)}, u32[]{:S(2)}) collective-permute-start(bf16[2,32,3584]{2,1,0:T(8,128)(2,1)} %copy-done.32), channel_id=1, source_target_pairs={{0,8},{8,0},{16,24},{24,16},{1,9},{9,1},{17,25},{25,17},{2,10},{10... | collective-permute-start | bytes 1376264 | tf_op jit(solution)/shard_map/ppermute | solution.py:195
  52.4 53.6 %collective-permute-start.9 = (bf16[2,32,3584]{2,1,0:T(8,128)(2,1)}, bf16[2,32,3584]{2,1,0:T(8,128)(2,1)}, u32[]{:S(2)}, u32[]{:S(2)}) collective-permute-start(bf16[2,32,3584]{2,1,0:T(8,128)(2,1)} %copy-done.31), channel_id=1, source_target_pairs={{0,16},{8,24},{16,0},{24,8},{1,17},{9,25},{17,1},{25,9},{2,18},{10... | collective-permute-start | bytes 1376264 | tf_op jit(solution)/shard_map/ppermute | solution.py:195
  59.5 23.4 %collective-permute-start.11 = (bf16[128,2048]{1,0:T(8,128)(2,1)S(1)}, bf16[128,2048]{1,0:T(8,128)(2,1)S(1)}, u32[]{:S(2)}, u32[]{:S(2)}) collective-permute-start(bf16[128,2048]{1,0:T(8,128)(2,1)S(1)} %collective-permute-done.10.near_ref), channel_id=1, source_target_pairs={{0,1},{1,0},{2,3},{3,2},{4,5},{5,4},{6,7},{7,6},{8,9},{9,8},{10,11... | collective-permute-start | bytes 1572872 | tf_op jit(solution)/shard_map/ppermute | solution.py:192
  61.6 20.3 %collective-permute-start.18 = (bf16[128,2048]{1,0:T(8,128)(2,1)S(1)}, bf16[128,2048]{1,0:T(8,128)(2,1)S(1)}, u32[]{:S(2)}, u32[]{:S(2)}) collective-permute-start(bf16[128,2048]{1,0:T(8,128)(2,1)S(1)} %collective-permute-done.10.near_ref), channel_id=1, source_target_pairs={{0,2},{1,3},{2,4},{3,5},{4,6},{5,7},{6,0},{7,1},{8,10},{9,11},{10,... | collective-permute-start | bytes 1572872 | tf_op jit(solution)/shard_map/ppermute | solution.py:192
  72.0 70.5 %collective-permute-start.7 = (bf16[32,3584]{1,0:T(8,128)(2,1)}, bf16[32,3584]{1,0:T(8,128)(2,1)}, u32[]{:S(2)}, u32[]{:S(2)}) collective-permute-start(bf16[32,3584]{1,0:T(8,128)(2,1)} %fusion.31), channel_id=1, source_target_pairs={{0,1},{1,0},{2,3},{3,2},{4,5},{5,4},{6,7},{7,6},{8,9},{9,8},{10,11... | collective-permute-start | bytes 688136 | tf_op jit(solution)/shard_map/ppermute | solution.py:192
  107.7 27.8 %collective-permute-start.12 = (bf16[32,3584]{1,0:T(8,128)(2,1)}, bf16[32,3584]{1,0:T(8,128)(2,1)}, u32[]{:S(2)}, u32[]{:S(2)}) collective-permute-start(bf16[32,3584]{1,0:T(8,128)(2,1)} %fusion.35), channel_id=1, source_target_pairs={{0,16},{8,24},{16,0},{24,8},{1,17},{9,25},{17,1},{25,9},{2,18},{10... | collective-permute-start | bytes 688136 | tf_op jit(solution)/shard_map/ppermute | solution.py:195
  111.0 28.1 %collective-permute-start.14 = (bf16[32,3584]{1,0:T(8,128)(2,1)}, bf16[32,3584]{1,0:T(8,128)(2,1)}, u32[]{:S(2)}, u32[]{:S(2)}) collective-permute-start(bf16[32,3584]{1,0:T(8,128)(2,1)} %fusion.36), channel_id=1, source_target_pairs={{0,8},{8,0},{16,24},{24,16},{1,9},{9,1},{17,25},{25,17},{2,10},{10... | collective-permute-start | bytes 688136 | tf_op jit(solution)/shard_map/ppermute | solution.py:195
  112.5 35.4 %collective-permute-start.16 = (bf16[2,32,3584]{2,1,0:T(8,128)(2,1)}, bf16[2,32,3584]{2,1,0:T(8,128)(2,1)}, u32[]{:S(2)}, u32[]{:S(2)}) collective-permute-start(bf16[2,32,3584]{2,1,0:T(8,128)(2,1)} %copy-done.34), channel_id=1, source_target_pairs={{0,8},{8,0},{16,24},{24,16},{1,9},{9,1},{17,25},{25,17},{2,10},{10... | collective-permute-start | bytes 1376264 | tf_op jit(solution)/shard_map/ppermute | solution.py:195
  113.1 34.9 %collective-permute-start.17 = (bf16[2,32,3584]{2,1,0:T(8,128)(2,1)}, bf16[2,32,3584]{2,1,0:T(8,128)(2,1)}, u32[]{:S(2)}, u32[]{:S(2)}) collective-permute-start(bf16[2,32,3584]{2,1,0:T(8,128)(2,1)} %copy-done.33), channel_id=1, source_target_pairs={{0,16},{8,24},{16,0},{24,8},{1,17},{9,25},{17,1},{25,9},{2,18},{10... | collective-permute-start | bytes 1376264 | tf_op jit(solution)/shard_map/ppermute | solution.py:195
  116.5 37.6 %all-to-all-start.1 = ((bf16[32,32,128]{2,1,0:T(8,128)(2,1)}), bf16[32,32,128]{2,1,0:T(8,128)(2,1)}, u32[]{:S(2)}, u32[]{:S(2)}) async-start(bf16[32,32,128]{2,1,0:T(8,128)(2,1)} %pad_maximum_fusion.1), calls=%async_computation.1 | async-start | bytes 524288 | tf_op jit(solution)/shard_map/all_to_all | solution.py:274
  135.5 31.5 %collective-permute-start.24 = (bf16[2,32,3584]{2,1,0:T(8,128)(2,1)}, bf16[2,32,3584]{2,1,0:T(8,128)(2,1)}, u32[]{:S(2)}, u32[]{:S(2)}) collective-permute-start(bf16[2,32,3584]{2,1,0:T(8,128)(2,1)} %get-tuple-element.62), channel_id=1, source_target_pairs={{0,8},{8,0},{16,24},{24,16},{1,9},{9,1},{17,25},{25,17},{2,10},{10... | collective-permute-start | bytes 1376264 | tf_op jit(solution)/shard_map/ppermute | solution.py:195
  139.1 30.5 %collective-permute-start.25 = (bf16[2,32,3584]{2,1,0:T(8,128)(2,1)}, bf16[2,32,3584]{2,1,0:T(8,128)(2,1)}, u32[]{:S(2)}, u32[]{:S(2)}) collective-permute-start(bf16[2,32,3584]{2,1,0:T(8,128)(2,1)} %get-tuple-element.63), channel_id=1, source_target_pairs={{0,16},{8,24},{16,0},{24,8},{1,17},{9,25},{17,1},{25,9},{2,18},{10... | collective-permute-start | bytes 1376264 | tf_op jit(solution)/shard_map/ppermute | solution.py:195
  142.5 31.4 %collective-permute-start.13 = (bf16[32,3584]{1,0:T(8,128)(2,1)}, bf16[32,3584]{1,0:T(8,128)(2,1)}, u32[]{:S(2)}, u32[]{:S(2)}) collective-permute-start(bf16[32,3584]{1,0:T(8,128)(2,1)} %fusion.30.refs_2_), channel_id=1, source_target_pairs={{0,6},{1,7},{2,0},{3,1},{4,2},{5,3},{6,4},{7,5},{8,14},{9,15},{10,... | collective-permute-start | bytes 688136 | tf_op jit(solution)/shard_map/ppermute | solution.py:192
  155.8 49.9 %all-to-all-start.2 = ((bf16[32,32,128]{2,1,0:T(8,128)(2,1)}), bf16[32,32,128]{2,1,0:T(8,128)(2,1)}, u32[]{:S(2)}, u32[]{:S(2)}) async-start(bf16[32,32,128]{2,1,0:T(8,128)(2,1)} %broadcast_in_dim.110), calls=%async_computation.2 | async-start | bytes 524288 | tf_op jit(solution)/shard_map/all_to_all | solution.py:284
  165.1 33.2 %collective-permute-start.22 = (bf16[32,3584]{1,0:T(8,128)(2,1)}, bf16[32,3584]{1,0:T(8,128)(2,1)S(1)}, u32[]{:S(2)}, u32[]{:S(2)}) collective-permute-start(bf16[32,3584]{1,0:T(8,128)(2,1)} %fusion.28.refs_2_), channel_id=1, source_target_pairs={{0,4},{1,5},{2,6},{3,7},{4,0},{5,1},{6,2},{7,3},{8,12},{9,13},{10,... | collective-permute-start | bytes 688136 | tf_op jit(solution)/shard_map/ppermute | solution.py:192
  167.0 35.3 %collective-permute-start.23 = (bf16[32,3584]{1,0:T(8,128)(2,1)}, bf16[32,3584]{1,0:T(8,128)(2,1)}, u32[]{:S(2)}, u32[]{:S(2)}) collective-permute-start(bf16[32,3584]{1,0:T(8,128)(2,1)} %fusion.27), channel_id=1, source_target_pairs={{0,5},{1,4},{2,7},{3,6},{4,1},{5,0},{6,3},{7,2},{8,13},{9,12},{10,... | collective-permute-start | bytes 688136 | tf_op jit(solution)/shard_map/ppermute | solution.py:192
  179.9 39.0 %collective-permute-start.27 = (bf16[32,3584]{1,0:T(8,128)(2,1)S(1)}, bf16[32,3584]{1,0:T(8,128)(2,1)}, u32[]{:S(2)}, u32[]{:S(2)}) collective-permute-start(bf16[32,3584]{1,0:T(8,128)(2,1)S(1)} %fusion.26.refs_2_.refs_1_), channel_id=1, source_target_pairs={{0,2},{1,3},{2,4},{3,5},{4,6},{5,7},{6,0},{7,1},{8,10},{9,11},{10,... | collective-permute-start | bytes 688136 | tf_op jit(solution)/shard_map/ppermute | solution.py:192
  183.7 35.2 %collective-permute-start.29 = (bf16[32,3584]{1,0:T(8,128)(2,1)}, bf16[32,3584]{1,0:T(8,128)(2,1)S(1)}, u32[]{:S(2)}, u32[]{:S(2)}) collective-permute-start(bf16[32,3584]{1,0:T(8,128)(2,1)} %fusion.25.refs_2_), channel_id=1, source_target_pairs={{0,3},{1,2},{2,5},{3,4},{4,7},{5,6},{6,1},{7,0},{8,11},{9,10},{10,... | collective-permute-start | bytes 688136 | tf_op jit(solution)/shard_map/ppermute | solution.py:192
  210.4 47.8 %all-to-all-start.3 = ((bf16[8,128,896]{2,1,0:T(8,128)(2,1)}), bf16[8,128,896]{2,1,0:T(8,128)(2,1)}, u32[]{:S(2)}, u32[]{:S(2)}) async-start(bf16[8,128,896]{2,1,0:T(8,128)(2,1)} %bitcast.131), calls=%async_computation.3 | async-start | bytes 3670016 | tf_op jit(solution)/shard_map/all_to_all | solution.py:316
  226.7 22.3 %collective-permute-start.31 = (bf16[2,32,3584]{2,1,0:T(8,128)(2,1)S(1)}, bf16[2,32,3584]{2,1,0:T(8,128)(2,1)S(1)}, u32[]{:S(2)}, u32[]{:S(2)}) collective-permute-start(bf16[2,32,3584]{2,1,0:T(8,128)(2,1)S(1)} %get-tuple-element.72), channel_id=1, source_target_pairs={{0,16},{8,24},{16,0},{24,8},{1,17},{9,25},{17,1},{25,9},{2,18},{10... | collective-permute-start | bytes 1376264 | tf_op jit(solution)/shard_map/ppermute | solution.py:195
  228.2 20.8 %collective-permute-start.32 = (bf16[2,32,3584]{2,1,0:T(8,128)(2,1)S(1)}, bf16[2,32,3584]{2,1,0:T(8,128)(2,1)S(1)}, u32[]{:S(2)}, u32[]{:S(2)}) collective-permute-start(bf16[2,32,3584]{2,1,0:T(8,128)(2,1)S(1)} %get-tuple-element.71), channel_id=1, source_target_pairs={{0,24},{8,16},{16,8},{24,0},{1,25},{9,17},{17,9},{25,1},{2,26},{10... | collective-permute-start | bytes 1376264 | tf_op jit(solution)/shard_map/ppermute | solution.py:195
  (67 other events, 655.8 us)

commit v4 on v1

--- a/solution.py
+++ b/solution.py
@@ -12,6 +12,8 @@
 CONTRACT_ROWS = (((0,), (0,)), ((), ()))
 CORES = 2
 MOST_ROWS = 1024
+STREAMS = 2
+ANYWHERE = pl.BlockSpec(memory_space=pl.ANY)
 
 
 def dot(left, right, dims):
@@ -28,8 +30,8 @@
     return fits[0] if fits else width
 
 
-def chunk_kernel(stages, place_ref, near_ref, far_ref, weight_ref, *rest):
-    outs, rows = rest[:-1], rest[-1]
+def chunk_kernel(stages, streams, place_ref, near_ref, far_ref, *rest):
+    weights, outs, rows = rest[: 2 * streams], rest[-5:-1], rest[-1]
     part = near_ref.shape[0] // (2 * len(stages))
     sides = [(ref, flips) for ref, order in zip((near_ref, far_ref), stages) for flips in order]
     cuts = [(ref, flip) for ref, flips in sides for flip in flips]
@@ -40,40 +42,92 @@
             low = pl.multiple_of((place_ref[0] ^ flip) * part, part)
             rows[at * part : (at + 1) * part] = ref[pl.ds(low, part)]
 
-    full = dot(rows[...], weight_ref[...], CONTRACT_LAST).astype(jnp.bfloat16)
-    for at in range(len(cuts)):
-        outs[at // 2][at % 2] = full[at * part : (at + 1) * part]
+    size, depth = weights[0].shape
+    for stream in range(streams):
+        full = sum(
+            dot(rows[:, half * depth : (half + 1) * depth], weights[2 * stream + half][...], CONTRACT_LAST)
+            for half in range(2)
+        ).astype(jnp.bfloat16)
+        for at in range(len(cuts)):
+            outs[at // 2][at % 2, :, stream * size : (stream + 1) * size] = full[
+                at * part : (at + 1) * part
+            ]
 
 
 STAGES = (((0, 2), (1, 3)), ((0, 1), (2, 3)))
 
 
-def chunk_product(near, far, weight, group):
+def chunk_product(near, far, weight, group, *gates):
     block, depth = near.shape
     width = weight.shape[0]
     tile = tile_of(width)
     part = block // (2 * len(STAGES))
+    streams = STREAMS if tile % (128 * STREAMS) == 0 else 1
+
+    def piece(stream, half):
+        return lambda at, place: (at * streams + stream, half)
+
     return pl.pallas_call(
-        functools.partial(chunk_kernel, STAGES),
+        functools.partial(chunk_kernel, STAGES, streams),
         grid_spec=pltpu.PrefetchScalarGridSpec(
             num_scalar_prefetch=1,
             grid=(width // tile,),
             in_specs=[
                 pl.BlockSpec((block, depth), lambda at, place: (0, 0)),
                 pl.BlockSpec((block, depth), lambda at, place: (0, 0)),
-                pl.BlockSpec((tile, depth), lambda at, place: (at, 0)),
-            ],
+            ]
+            + [
+                pl.BlockSpec((tile // streams, depth // 2), piece(stream, half))
+                for stream in range(streams)
+                for half in range(2)
+            ]
+            + [ANYWHERE] * len(gates),
             out_specs=[pl.BlockSpec((2, part, tile), lambda at, place: (0, 0, at))] * 4,
             scratch_shapes=[pltpu.VMEM((CORES * block, depth), jnp.bfloat16)],
         ),
         out_shape=[jax.ShapeDtypeStruct((2, part, width), jnp.bfloat16)] * 4,
-        compiler_params=pltpu.CompilerParams(vmem_limit_bytes=24 << 20),
+        compiler_params=pltpu.CompilerParams(vmem_limit_bytes=52 << 20),
         cost_estimate=pl.CostEstimate(
             flops=2 * CORES * block * depth * width,
             bytes_accessed=2 * (width * depth + CORES * block * (depth + width)),
             transcendentals=0,
         ),
-    )(group.reshape(1), near, far, weight)
+    )(group.reshape(1), near, far, *[weight] * (2 * streams), *gates)
+
+
+def cut_kernel(rows_ref, out_ref):
+    out_ref[0] = rows_ref[...]
+
+
+def cut_columns(rows, count):
+    block, width = rows.shape
+    slab = width // count
+    if slab % 128:
+        return rows.reshape(block, count, slab).transpose(1, 0, 2)
+    return pl.pallas_call(
+        cut_kernel,
+        grid=(count,),
+        in_specs=[pl.BlockSpec((block, slab), lambda at: (0, at))],
+        out_specs=pl.BlockSpec((1, block, slab), lambda at: (at, 0, 0)),
+        out_shape=jax.ShapeDtypeStruct((count, block, slab), rows.dtype),
+        compiler_params=pltpu.CompilerParams(vmem_limit_bytes=4 << 20),
+        cost_estimate=pl.CostEstimate(flops=0, bytes_accessed=4 * rows.size, transcendentals=0),
+    )(rows)
+
+
+def touch_kernel(*refs):
+    pass
+
+
+def touch(value, *gates):
+    return pl.pallas_call(
+        touch_kernel,
+        in_specs=[ANYWHERE] * (1 + len(gates)),
+        out_specs=ANYWHERE,
+        out_shape=jax.ShapeDtypeStruct(value.shape, value.dtype),
+        input_output_aliases={0: 0},
+        compiler_params=pltpu.CompilerParams(vmem_limit_bytes=1 << 20),
+    )(value, *gates)
 
 
 def join_kernel(groups, slab, place_ref, *refs):
@@ -110,6 +164,7 @@
             out_specs=pl.BlockSpec((part, each * width), lambda at, place: (place[0] ^ at, 0)),
         ),
         out_shape=jax.ShapeDtypeStruct((block, each * width), jnp.bfloat16),
+        compiler_params=pltpu.CompilerParams(vmem_limit_bytes=24 << 20),
         cost_estimate=pl.CostEstimate(
             flops=block * each * width, bytes_accessed=6 * block * each * width, transcendentals=0
         ),
@@ -182,24 +237,20 @@
     def grp_move(value, flip):
         return lax.ppermute(value, "grp", [(g, g ^ flip) for g in range(groups)])
 
-    held = [grad_output]
-    for step in range(1, chips):
-        held.append(seq_move(held[-1], -1, 0))
-    pairs = [(near, seq_move(near, 0, 1)) for near in held]
-
-    hidden_slab = lax.all_to_all(
-        hidden.reshape(block, count, down_slab).transpose(1, 0, 2),
-        "seq",
-        split_axis=0,
-        concat_axis=0,
-        tiled=True,
-    ).reshape(count * block, down_slab)
-
     last = chips - 1
-    products = [chunk_product(near, far, down_weight, group) for near, far in pairs]
-    firsts = [
-        (grp_move(near_sent, 1), grp_move(far_sent, 2)) for _, near_sent, _, far_sent in products
-    ]
+    held, pairs, products = [grad_output], [], []
+    for step in range(chips):
+        if step:
+            came = seq_move(held[-1], -1, 0)
+            held.append(touch(came, products[step - 2][0]) if step > 1 else came)
+        pairs.append((held[step], seq_move(held[step], 0, 1)))
+        if step < last:
+            products.append(chunk_product(*pairs[step], down_weight, group))
+
+    cut = touch(cut_columns(hidden, count), held[1])
+    hidden_slab = lax.all_to_all(cut, "seq", split_axis=0, concat_axis=0, tiled=True)
+    hidden_slab = touch(hidden_slab.reshape(count * block, down_slab), products[last - 1][0])
+
     grad_slab = jnp.zeros((count, block, up_slab), jnp.bfloat16)
     for step, pair in enumerate(pairs):
         back = ((chip - step) % chips) * CORES
@@ -207,6 +258,14 @@
             columns = lax.dynamic_slice_in_dim(rows, index * up_slab, up_slab, 1)
             grad_slab = lax.dynamic_update_index_in_dim(grad_slab, columns, back + (core ^ flip), 0)
     grad_slab = grad_slab.reshape(count * block, up_slab)
+    ranked = jnp.concatenate(
+        [project(grad_slab, adapter_up, mask), project(hidden_slab, adapter_down, mask)], axis=1
+    )
+    products.append(chunk_product(*pairs[last], down_weight, group, ranked))
+
+    firsts = [
+        (grp_move(near_sent, 1), grp_move(far_sent, 2)) for _, near_sent, _, far_sent in products
+    ]
 
     def second(step, *gates):
         near_kept, _, far_kept, _ = products[step]
@@ -249,11 +308,6 @@
         came = hop(step, sums)
 
     begun, seconds = second(last - 1, products[last][0])
-    rows_here = lax.optimization_barrier((grad_slab, hidden_slab, begun))
-    ranked = jnp.concatenate(
-        [project(rows_here[0], adapter_up, mask), project(rows_here[1], adapter_down, mask)],
-        axis=1,
-    )
     devices = count * groups
     share = lax.all_to_all(
         ranked.reshape(devices, -1, 2 * ranks),

time: 217 us -> 259 us (1.19)
  Pallas kernels: 26.2 us -> 46.3 us
  other arithmetic: 7.19 us -> 21.5 us
  local copies, waits for them, and re-layouts: 19.2 us -> 32.3 us
  starting transfers between devices: 62.6 us -> 58.2 us
    pallas_call x4 -> x9, Pallas kernels: 21.8 us -> 42.3 us  [the longest x4 41.8 us: chunk_product(): pl.pallas_call(functools.partial(chunk_kernel, STAGES, streams), grid_spe...]
    ppermute x14, waiting for transfers between devices: 20.3 us -> 37.7 us  [seq_move(): return lax.ppermute(value, 'seq', pairs)]
    ppermute x19, waiting for transfers between devices: 27.7 us -> 14.3 us  [grp_move(): return lax.ppermute(value, 'grp', [(g, g ^ flip) for g in range(groups)])]
    convert_element_type x16, other arithmetic: 6.04 us -> 18.2 us  [add(): sum((term.astype(jnp.float32) for term in terms)).astype(jnp.bfloat16)]
    all_to_all x1, waiting for transfers between devices: 8.74 us -> 0.01 us  [shards(): lax.all_to_all(ranked.reshape(devices, -1, 2 * ranks), ('grp', 'seq'), sp...]
    ppermute x14, starting transfers between devices: 24.7 us -> 19.4 us  [seq_move(): return lax.ppermute(value, 'seq', pairs)]
    dynamic_update_slice x8, local copies, waits for them, and re-layouts: 0.09 us -> 5.05 us  [shards(): lax.dynamic_update_index_in_dim(grad_slab, columns, back + (core ^ flip), 0)]
    unnamed x24 -> x60, local copies, waits for them, and re-layouts: 5.22 us -> 9.61 us
  transfers between devices with their start and end apart: 37 -> 37, of which waited for: 16 -> 9; matrix products, arithmetic and copies ran while one was open for 18% -> 24% of each run, Pallas kernels for 10% -> 16%
where the time goes in v4:
time: 259 us; the launch traced here: 257 us
  waiting for transfers between devices  80.5 us (31%)
  starting transfers between devices  58.2 us (22%)
  Pallas kernels  46.3 us (18%)
  local copies, waits for them, and re-layouts  32.3 us (12%)
  other arithmetic  21.5 us (8%)
  matrix products  16.6 us (6%)
    pallas_call x4, Pallas kernels, chunk_product(): pl.pallas_call(functools.partial(chunk_kernel, STAGES, streams), grid_spe...  41.8 us
    ppermute x14, waiting for transfers between devices, seq_move(): return lax.ppermute(value, 'seq', pairs)  37.7 us
    ppermute x19, starting transfers between devices, grp_move(): return lax.ppermute(value, 'grp', [(g, g ^ flip) for g in range(groups)])  21.2 us
    ppermute x14, starting transfers between devices, seq_move(): return lax.ppermute(value, 'seq', pairs)  19.4 us
    all_to_all x1, waiting for transfers between devices, shards(): term = lax.all_to_all(term, 'seq', split_axis=0, concat_axis=0, tiled=True)  18.8 us
    convert_element_type x16, other arithmetic, add(): sum((term.astype(jnp.float32) for term in terms)).astype(jnp.bfloat16)  18.2 us
    ppermute x19, waiting for transfers between devices, grp_move(): return lax.ppermute(value, 'grp', [(g, g ^ flip) for g in range(groups)])  14.3 us
    dot_general x4, matrix products, dot(): lax.dot_general(left, right, dims, preferred_element_type=jnp.float32)  13 us
  transfers between devices with their start and end apart: 37, of which 9 were waited for; matrix products, arithmetic and copies ran while one was open for 24% of the time, Pallas kernels for 16%

profile of v4, /device:TPU:0, one launch (start us, length us, event | category | flops | bytes accessed | tf_op | source)
XLA Modules:
  0.0 256.6 jit_solution(9204451078312183580)
XLA Ops:
  1.2 2.6 %collective-permute-start.3 = (bf16[128,2048]{1,0:T(8,128)(2,1)}, bf16[128,2048]{1,0:T(8,128)(2,1)S(1)}, u32[]{:S(2)}, u32[]{:S(2)}) collective-permute-start(bf16[128,2048]{1,0:T(8,128)(2,1)} %near_ref.1), channel_id=1, source_target_pairs={{0,2},{1,3},{2,4},{3,5},{4,6},{5,7},{6,0},{7,1},{8,10},{9,11},{10,... | collective-permute-start | bytes 1572872 | tf_op jit(solution)/shard_map/ppermute | solution.py:235
  9.4 9.2 %collective-permute-done.3.near_ref.refs_1_ = bf16[128,2048]{1,0:T(8,128)(2,1)S(1)} collective-permute-done((bf16[128,2048]{1,0:T(8,128)(2,1)}, bf16[128,2048]{1,0:T(8,128)(2,1)S(1)}, u32[]{:S(2)}, u32[]{:S(2)}) %collective-permute-start.3) | collective-permute-done | bytes 524320 | tf_op jit(solution)/shard_map/ppermute | solution.py:235
  21.1 10.7 %shard_map.94 = (bf16[2,32,3584]{2,1,0:T(8,128)(2,1)S(1)}, bf16[2,32,3584]{2,1,0:T(8,128)(2,1)}, bf16[2,32,3584]{2,1,0:T(8,128)(2,1)S(1)}, bf16[2,32,3584]{2,1,0:T(8,128)(2,1)}) custom-call(s32[1]{0:T(128)} %bitcast.place_ref, bf16[128,2048]{1,0:T(8,128)(2,1)} %near_ref.1, bf16[128,2048]{1,0:T(8,128)(2,1)} %copy-done.15, bf16[3584,2048]{1,0:T(8,128)(2,1)} %rest_3_.7, ...), custom_call_target="tpu_custom_call" | custom-call | flops 3758096384 | bytes 17563648 | tf_op jit(solution)/shard_map/pallas_call | solution.py:70
  36.1 4.3 %all-to-all-start = ((bf16[8,128,896]{2,1,0:T(8,128)(2,1)}), bf16[8,128,896]{2,1,0:T(8,128)(2,1)}, u32[]{:S(2)}, u32[]{:S(2)}) async-start(bf16[8,128,896]{2,1,0:T(8,128)(2,1)} %copy-done.3), calls=%async_computation | async-start | bytes 3670016 | tf_op jit(solution)/shard_map/all_to_all | solution.py:251
  43.8 9.9 %shard_map.95 = (bf16[2,32,3584]{2,1,0:T(8,128)(2,1)S(1)}, bf16[2,32,3584]{2,1,0:T(8,128)(2,1)S(1)}, bf16[2,32,3584]{2,1,0:T(8,128)(2,1)S(1)}, bf16[2,32,3584]{2,1,0:T(8,128)(2,1)S(1)}) custom-call(s32[1]{0:T(128)} %bitcast.place_ref, bf16[128,2048]{1,0:T(8,128)(2,1)} %copy-done.6, bf16[128,2048]{1,0:T(8,128)(2,1)} %collective-permute-done.4.far_ref, ...), custom_call_target="tpu_custom_call" | custom-call | flops 3758096384 | bytes 17563648 | tf_op jit(solution)/shard_map/pallas_call | solution.py:70
  57.7 28.5 %collective-permute-done.10.refs_0_ = bf16[128,2048]{1,0:T(8,128)(2,1)S(1)} collective-permute-done((bf16[128,2048]{1,0:T(8,128)(2,1)S(1)}, bf16[128,2048]{1,0:T(8,128)(2,1)S(1)}, u32[]{:S(2)}, u32[]{:S(2)}) %collective-permute-start.10) | collective-permute-done | bytes 524320 | tf_op jit(solution)/shard_map/ppermute | solution.py:235
  86.2 7.3 %collective-permute-start.18 = (bf16[128,2048]{1,0:T(8,128)(2,1)S(1)}, bf16[128,2048]{1,0:T(8,128)(2,1)S(1)}, u32[]{:S(2)}, u32[]{:S(2)}) collective-permute-start(bf16[128,2048]{1,0:T(8,128)(2,1)S(1)} %shard_map.96.near_ref), channel_id=1, source_target_pairs={{0,2},{1,3},{2,4},{3,5},{4,6},{5,7},{6,0},{7,1},{8,10},{9,11},{10,... | collective-permute-start | bytes 1572872 | tf_op jit(solution)/shard_map/ppermute | solution.py:235
  97.4 10.6 %shard_map.97 = (bf16[2,32,3584]{2,1,0:T(8,128)(2,1)S(1)}, bf16[2,32,3584]{2,1,0:T(8,128)(2,1)}, bf16[2,32,3584]{2,1,0:T(8,128)(2,1)S(1)}, bf16[2,32,3584]{2,1,0:T(8,128)(2,1)}) custom-call(s32[1]{0:T(128)} %bitcast.place_ref, bf16[128,2048]{1,0:T(8,128)(2,1)} %copy-done.5, bf16[128,2048]{1,0:T(8,128)(2,1)} %copy-done.16, bf16[3584,2048]{1,0:T(8,128)(2,1)} %rest_3_.7, ...), custom_call_target="tpu_custom_call" | custom-call | flops 3758096384 | bytes 17563648 | tf_op jit(solution)/shard_map/pallas_call | solution.py:70
  126.2 3.9 %multiply_reduce_fusion = bf16[1024,64]{0,1:T(8,128)(2,1)S(1)} fusion(f32[1024,16]{0,1:T(8,128)S(1)} %copy-done.26, bf16[16,64,896]{2,1,0:T(8,128)(2,1)S(1)} %copy-done, bf16[1024,896]{1,0:T(8,128)(2,1)} %shard_map.101), kind=kOutput, calls=%fused_computation | convolution fusion | flops 1881079808 | bytes 3866624 | tf_op jit(solution)/shard_map/dot_general | solution.py:20
  131.1 10.6 %shard_map.102 = (bf16[2,32,3584]{2,1,0:T(8,128)(2,1)S(1)}, bf16[2,32,3584]{2,1,0:T(8,128)(2,1)}, bf16[2,32,3584]{2,1,0:T(8,128)(2,1)S(1)}, bf16[2,32,3584]{2,1,0:T(8,128)(2,1)}) custom-call(s32[1]{0:T(128)} %bitcast.place_ref, bf16[128,2048]{1,0:T(8,128)(2,1)} %copy-done.4, bf16[128,2048]{1,0:T(8,128)(2,1)} %copy-done.17, bf16[3584,2048]{1,0:T(8,128)(2,1)} %rest_3_.7, ...), custom_call_target="tpu_custom_call" | custom-call | flops 3758096384 | bytes 17563648 | tf_op jit(solution)/shard_map/pallas_call | solution.py:70
  150.0 5.0 %all-to-all-start.1 = ((bf16[32,32,128]{2,1,0:T(8,128)(2,1)}), bf16[32,32,128]{2,1,0:T(8,128)(2,1)S(1)}, u32[]{:S(2)}, u32[]{:S(2)}) async-start(bf16[32,32,128]{2,1,0:T(8,128)(2,1)} %pad_maximum_fusion.1), calls=%async_computation.1 | async-start | bytes 524288 | tf_op jit(solution)/shard_map/all_to_all | solution.py:312
  158.7 2.4 collective-permute-start.22
  166.3 4.1 %collective-permute-done.25 = bf16[2,32,3584]{2,1,0:T(8,128)(2,1)S(1)} collective-permute-done((bf16[2,32,3584]{2,1,0:T(8,128)(2,1)}, bf16[2,32,3584]{2,1,0:T(8,128)(2,1)S(1)}, u32[]{:S(2)}, u32[]{:S(2)}) %collective-permute-start.25) | collective-permute-done | bytes 458784 | tf_op jit(solution)/shard_map/ppermute | solution.py:238
  178.3 4.0 %all-to-all-start.2 = ((bf16[32,32,128]{2,1,0:T(8,128)(2,1)}), bf16[32,32,128]{2,1,0:T(8,128)(2,1)S(1)}, u32[]{:S(2)}, u32[]{:S(2)}) async-start(bf16[32,32,128]{2,1,0:T(8,128)(2,1)} %broadcast_in_dim.110), calls=%async_computation.2 | async-start | bytes 524288 | tf_op jit(solution)/shard_map/all_to_all | solution.py:325
  191.4 9.7 %all-to-all-done.2 = bf16[32,32,128]{2,1,0:T(8,128)(2,1)S(1)} async-done(((bf16[32,32,128]{2,1,0:T(8,128)(2,1)}), bf16[32,32,128]{2,1,0:T(8,128)(2,1)S(1)}, u32[]{:S(2)}, u32[]{:S(2)}) %all-to-all-start.2) | async-done | bytes 262176 | tf_op jit(solution)/shard_map/all_to_all | solution.py:325
  201.2 3.6 %fusion = bf16[1024,896]{1,0:T(8,128)(2,1)} fusion(bf16[16,64,896]{2,1,0:T(8,128)(2,1)S(1)} %copy-done, bf16[1024,16]{0,1:T(8,128)(2,1)S(1)} %copy-done.27, bf16[1024,64]{0,1:T(8,128)(2,1)S(1)} %copy.39), kind=kOutput, calls=%fused_computation.3 | convolution fusion | flops 1881931776 | bytes 3833856 | tf_op jit(solution)/shard_map/dot_general | solution.py:341
  204.9 4.3 %all-to-all-start.3 = ((bf16[8,128,896]{2,1,0:T(8,128)(2,1)}), bf16[8,128,896]{2,1,0:T(8,128)(2,1)}, u32[]{:S(2)}, u32[]{:S(2)}) async-start(bf16[8,128,896]{2,1,0:T(8,128)(2,1)} %bitcast.127), calls=%async_computation.3 | async-start | bytes 3670016 | tf_op jit(solution)/shard_map/all_to_all | solution.py:353
  210.6 2.6 %constant_dynamic-slice_fusion = (bf16[2,32,3584]{2,1,0:T(8,128)(2,1)}, bf16[2,32,3584]{2,1,0:T(8,128)(2,1)}, bf16[2,32,3584]{2,1,0:T(8,128)(2,1)}, bf16[2,32,3584]{2,1,0:T(8,128)(2,1)S(1)}) fusion(bf16[8,32,3584]{2,1,0:T(8,128)(2,1)} %bitcast_dynamic-update-slice_fusion, s32[]{:T(128)S(6)} %select_n.141, s32[]{:T(128)S(6)} %select_n.140, s32[]{:T(128)S(6)} %select_n.139, ...), kind=kLoop, calls=%fused_computation.81 | loop fusion | bytes 3670032 | tf_op jit(solution)/shard_map/dynamic_slice | solution.py:358
  213.4 3.3 %collective-permute-start.32 = (bf16[2,32,3584]{2,1,0:T(8,128)(2,1)}, bf16[2,32,3584]{2,1,0:T(8,128)(2,1)}, u32[]{:S(2)}, u32[]{:S(2)}) collective-permute-start(bf16[2,32,3584]{2,1,0:T(8,128)(2,1)} %get-tuple-element.89), channel_id=1, source_target_pairs={{0,24},{8,16},{16,8},{24,0},{1,25},{9,17},{17,9},{25,1},{2,26},{10... | collective-permute-start | bytes 1376264 | tf_op jit(solution)/shard_map/ppermute | solution.py:238
  219.7 2.7 %fusion.16 = f32[16,64,256]{2,1,0:T(8,128)} fusion(bf16[1024,256,1]{1,0,2:T(8,128)(2,1)} %bitcast.129, bf16[1024,64]{0,1:T(8,128)(2,1)S(1)} %copy.41, bf16[1024,16]{0,1:T(8,128)(2,1)S(1)} %copy-done.27, f32[16]{0:T(128)S(1)} %broadcast_divide_fusion), kind=kOutput, calls=%fused_computation.15 | convolution fusion | flops 538181632 | bytes 1736768 | tf_op jit(solution)/shard_map/dot_general | solution.py:20
  222.5 5.7 %fusion.9 = f32[16,64,896]{2,1,0:T(8,128)} fusion(bf16[1024,896]{1,0:T(8,128)(2,1)} %shard_map.101, f32[16]{0:T(128)S(1)} %broadcast_divide_fusion, bf16[1024,64]{0,1:T(8,128)(2,1)S(1)} %copy.40, bf16[1024,16]{0,1:T(8,128)(2,1)S(1)} %copy-done.27), kind=kOutput, calls=%fused_computation.12 | convolution fusion | flops 1881014272 | bytes 5668928 | tf_op jit(solution)/shard_map/dot_general | solution.py:20
  228.1 5.6 %collective-permute-done.32.refs_3_ = bf16[2,32,3584]{2,1,0:T(8,128)(2,1)} collective-permute-done((bf16[2,32,3584]{2,1,0:T(8,128)(2,1)}, bf16[2,32,3584]{2,1,0:T(8,128)(2,1)}, u32[]{:S(2)}, u32[]{:S(2)}) %collective-permute-start.32) | collective-permute-done | bytes 458784 | tf_op jit(solution)/shard_map/ppermute | solution.py:238
  233.8 18.8 %all-to-all-done.3.refs_4_ = bf16[8,128,896]{2,1,0:T(8,128)(2,1)} async-done(((bf16[8,128,896]{2,1,0:T(8,128)(2,1)}), bf16[8,128,896]{2,1,0:T(8,128)(2,1)}, u32[]{:S(2)}, u32[]{:S(2)}) %all-to-all-start.3) | async-done | bytes 1835040 | tf_op jit(solution)/shard_map/all_to_all | solution.py:353
  252.6 4.0 %shard_map.103 = bf16[128,7168]{1,0:T(8,128)(2,1)} custom-call(s32[1]{0:T(128)} %bitcast.place_ref, bf16[2,32,3584]{2,1,0:T(8,128)(2,1)S(1)} %get-tuple-element.92.refs_0_, bf16[2,32,3584]{2,1,0:T(8,128)(2,1)S(1)} %collective-permute-done.30.refs_1_, bf16[2,32,3584]{2,1,0:T(8,128)(2,1)S(1)} %collective-permute-done.31.refs_2_, ...), custom_call_target="tpu_custom_call" | custom-call | flops 917504 | bytes 5505024 | tf_op jit(solution)/shard_map/pallas_call | solution.py:157
  (176 shorter events, 81.9 us)
Async XLA Ops:
  0.6 18.9 %collective-permute-start = (bf16[128,2048]{1,0:T(8,128)(2,1)}, bf16[128,2048]{1,0:T(8,128)(2,1)S(1)}, u32[]{:S(2)}, u32[]{:S(2)}) collective-permute-start(bf16[128,2048]{1,0:T(8,128)(2,1)} %near_ref.1), channel_id=1, source_target_pairs={{0,1},{1,0},{2,3},{3,2},{4,5},{5,4},{6,7},{7,6},{8,9},{9,8},{10,11... | collective-permute-start | bytes 1572872 | tf_op jit(solution)/shard_map/ppermute | solution.py:235
  1.2 17.4 %collective-permute-start.3 = (bf16[128,2048]{1,0:T(8,128)(2,1)}, bf16[128,2048]{1,0:T(8,128)(2,1)S(1)}, u32[]{:S(2)}, u32[]{:S(2)}) collective-permute-start(bf16[128,2048]{1,0:T(8,128)(2,1)} %near_ref.1), channel_id=1, source_target_pairs={{0,2},{1,3},{2,4},{3,5},{4,6},{5,7},{6,0},{7,1},{8,10},{9,11},{10,... | collective-permute-start | bytes 1572872 | tf_op jit(solution)/shard_map/ppermute | solution.py:235
  18.6 25.2 %collective-permute-start.4 = (bf16[128,2048]{1,0:T(8,128)(2,1)S(1)}, bf16[128,2048]{1,0:T(8,128)(2,1)}, u32[]{:S(2)}, u32[]{:S(2)}) collective-permute-start(bf16[128,2048]{1,0:T(8,128)(2,1)S(1)} %collective-permute-done.3.near_ref.refs_1_), channel_id=1, source_target_pairs={{0,1},{1,0},{2,3},{3,2},{4,5},{5,4},{6,7},{7,6},{8,9},{9,8},{10,11... | collective-permute-start | bytes 1572872 | tf_op jit(solution)/shard_map/ppermute | solution.py:235
  31.8 21.9 %collective-permute-start.1 = (bf16[2,32,3584]{2,1,0:T(8,128)(2,1)}, bf16[2,32,3584]{2,1,0:T(8,128)(2,1)}, u32[]{:S(2)}, u32[]{:S(2)}) collective-permute-start(bf16[2,32,3584]{2,1,0:T(8,128)(2,1)} %get-tuple-element.47), channel_id=1, source_target_pairs={{0,8},{8,0},{16,24},{24,16},{1,9},{9,1},{17,25},{25,17},{2,10},{10... | collective-permute-start | bytes 1376264 | tf_op jit(solution)/shard_map/ppermute | solution.py:238
  33.3 20.4 %collective-permute-start.2 = (bf16[2,32,3584]{2,1,0:T(8,128)(2,1)}, bf16[2,32,3584]{2,1,0:T(8,128)(2,1)}, u32[]{:S(2)}, u32[]{:S(2)}) collective-permute-start(bf16[2,32,3584]{2,1,0:T(8,128)(2,1)} %get-tuple-element.48), channel_id=1, source_target_pairs={{0,16},{8,24},{16,0},{24,8},{1,17},{9,25},{17,1},{25,9},{2,18},{10... | collective-permute-start | bytes 1376264 | tf_op jit(solution)/shard_map/ppermute | solution.py:238
  36.1 89.3 %all-to-all-start = ((bf16[8,128,896]{2,1,0:T(8,128)(2,1)}), bf16[8,128,896]{2,1,0:T(8,128)(2,1)}, u32[]{:S(2)}, u32[]{:S(2)}) async-start(bf16[8,128,896]{2,1,0:T(8,128)(2,1)} %copy-done.3), calls=%async_computation | async-start | bytes 3670016 | tf_op jit(solution)/shard_map/all_to_all | solution.py:251
  40.4 45.8 %collective-permute-start.10 = (bf16[128,2048]{1,0:T(8,128)(2,1)S(1)}, bf16[128,2048]{1,0:T(8,128)(2,1)S(1)}, u32[]{:S(2)}, u32[]{:S(2)}) collective-permute-start(bf16[128,2048]{1,0:T(8,128)(2,1)S(1)} %collective-permute-done.3.near_ref.refs_1_), channel_id=1, source_target_pairs={{0,2},{1,3},{2,4},{3,5},{4,6},{5,7},{6,0},{7,1},{8,10},{9,11},{10,... | collective-permute-start | bytes 1572872 | tf_op jit(solution)/shard_map/ppermute | solution.py:235
  54.7 40.2 %collective-permute-start.5 = (bf16[32,3584]{1,0:T(8,128)(2,1)S(1)}, bf16[32,3584]{1,0:T(8,128)(2,1)S(1)}, u32[]{:S(2)}, u32[]{:S(2)}) collective-permute-start(bf16[32,3584]{1,0:T(8,128)(2,1)S(1)} %fusion.33), channel_id=1, source_target_pairs={{0,16},{8,24},{16,0},{24,8},{1,17},{9,25},{17,1},{25,9},{2,18},{10... | collective-permute-start | bytes 688136 | tf_op jit(solution)/shard_map/ppermute | solution.py:238
  56.3 39.2 %collective-permute-start.6 = (bf16[32,3584]{1,0:T(8,128)(2,1)S(1)}, bf16[32,3584]{1,0:T(8,128)(2,1)S(1)}, u32[]{:S(2)}, u32[]{:S(2)}) collective-permute-start(bf16[32,3584]{1,0:T(8,128)(2,1)S(1)} %fusion.34), channel_id=1, source_target_pairs={{0,8},{8,0},{16,24},{24,16},{1,9},{9,1},{17,25},{25,17},{2,10},{10... | collective-permute-start | bytes 688136 | tf_op jit(solution)/shard_map/ppermute | solution.py:238
  86.2 26.7 %collective-permute-start.18 = (bf16[128,2048]{1,0:T(8,128)(2,1)S(1)}, bf16[128,2048]{1,0:T(8,128)(2,1)S(1)}, u32[]{:S(2)}, u32[]{:S(2)}) collective-permute-start(bf16[128,2048]{1,0:T(8,128)(2,1)S(1)} %shard_map.96.near_ref), channel_id=1, source_target_pairs={{0,2},{1,3},{2,4},{3,5},{4,6},{5,7},{6,0},{7,1},{8,10},{9,11},{10,... | collective-permute-start | bytes 1572872 | tf_op jit(solution)/shard_map/ppermute | solution.py:235
  96.5 22.5 %collective-permute-start.7 = (bf16[32,3584]{1,0:T(8,128)(2,1)S(1)}, bf16[32,3584]{1,0:T(8,128)(2,1)S(1)}, u32[]{:S(2)}, u32[]{:S(2)}) collective-permute-start(bf16[32,3584]{1,0:T(8,128)(2,1)S(1)} %fusion.31), channel_id=1, source_target_pairs={{0,1},{1,0},{2,3},{3,2},{4,5},{5,4},{6,7},{7,6},{8,9},{9,8},{10,11... | collective-permute-start | bytes 688136 | tf_op jit(solution)/shard_map/ppermute | solution.py:235
  112.3 30.2 %collective-permute-start.16 = (bf16[2,32,3584]{2,1,0:T(8,128)(2,1)}, bf16[2,32,3584]{2,1,0:T(8,128)(2,1)}, u32[]{:S(2)}, u32[]{:S(2)}) collective-permute-start(bf16[2,32,3584]{2,1,0:T(8,128)(2,1)} %get-tuple-element.65), channel_id=1, source_target_pairs={{0,8},{8,0},{16,24},{24,16},{1,9},{9,1},{17,25},{25,17},{2,10},{10... | collective-permute-start | bytes 1376264 | tf_op jit(solution)/shard_map/ppermute | solution.py:238
  116.1 26.4 %collective-permute-start.17 = (bf16[2,32,3584]{2,1,0:T(8,128)(2,1)}, bf16[2,32,3584]{2,1,0:T(8,128)(2,1)}, u32[]{:S(2)}, u32[]{:S(2)}) collective-permute-start(bf16[2,32,3584]{2,1,0:T(8,128)(2,1)} %get-tuple-element.66), channel_id=1, source_target_pairs={{0,16},{8,24},{16,0},{24,8},{1,17},{9,25},{17,1},{25,9},{2,18},{10... | collective-permute-start | bytes 1376264 | tf_op jit(solution)/shard_map/ppermute | solution.py:238
  119.0 42.1 %collective-permute-start.14 = (bf16[32,3584]{1,0:T(8,128)(2,1)}, bf16[32,3584]{1,0:T(8,128)(2,1)}, u32[]{:S(2)}, u32[]{:S(2)}) collective-permute-start(bf16[32,3584]{1,0:T(8,128)(2,1)} %fusion.30), channel_id=1, source_target_pairs={{0,6},{1,7},{2,0},{3,1},{4,2},{5,3},{6,4},{7,5},{8,14},{9,15},{10,... | collective-permute-start | bytes 688136 | tf_op jit(solution)/shard_map/ppermute | solution.py:235
  119.8 41.4 %collective-permute-start.15 = (bf16[32,3584]{1,0:T(8,128)(2,1)}, bf16[32,3584]{1,0:T(8,128)(2,1)}, u32[]{:S(2)}, u32[]{:S(2)}) collective-permute-start(bf16[32,3584]{1,0:T(8,128)(2,1)} %fusion.29), channel_id=1, source_target_pairs={{0,7},{1,6},{2,1},{3,0},{4,3},{5,2},{6,5},{7,4},{8,15},{9,14},{10,... | collective-permute-start | bytes 688136 | tf_op jit(solution)/shard_map/ppermute | solution.py:235
  148.6 17.7 %collective-permute-start.24 = (bf16[2,32,3584]{2,1,0:T(8,128)(2,1)}, bf16[2,32,3584]{2,1,0:T(8,128)(2,1)}, u32[]{:S(2)}, u32[]{:S(2)}) collective-permute-start(bf16[2,32,3584]{2,1,0:T(8,128)(2,1)} %get-tuple-element.75), channel_id=1, source_target_pairs={{0,8},{8,0},{16,24},{24,16},{1,9},{9,1},{17,25},{25,17},{2,10},{10... | collective-permute-start | bytes 1376264 | tf_op jit(solution)/shard_map/ppermute | solution.py:238
  150.0 27.5 %all-to-all-start.1 = ((bf16[32,32,128]{2,1,0:T(8,128)(2,1)}), bf16[32,32,128]{2,1,0:T(8,128)(2,1)S(1)}, u32[]{:S(2)}, u32[]{:S(2)}) async-start(bf16[32,32,128]{2,1,0:T(8,128)(2,1)} %pad_maximum_fusion.1), calls=%async_computation.1 | async-start | bytes 524288 | tf_op jit(solution)/shard_map/all_to_all | solution.py:312
  158.7 27.2 %collective-permute-start.22 = (bf16[32,3584]{1,0:T(8,128)(2,1)}, bf16[32,3584]{1,0:T(8,128)(2,1)}, u32[]{:S(2)}, u32[]{:S(2)}) collective-permute-start(bf16[32,3584]{1,0:T(8,128)(2,1)} %fusion.28), channel_id=1, source_target_pairs={{0,4},{1,5},{2,6},{3,7},{4,0},{5,1},{6,2},{7,3},{8,12},{9,13},{10,... | collective-permute-start | bytes 688136 | tf_op jit(solution)/shard_map/ppermute | solution.py:235
  162.9 23.0 %collective-permute-start.23 = (bf16[32,3584]{1,0:T(8,128)(2,1)}, bf16[32,3584]{1,0:T(8,128)(2,1)}, u32[]{:S(2)}, u32[]{:S(2)}) collective-permute-start(bf16[32,3584]{1,0:T(8,128)(2,1)} %fusion.27), channel_id=1, source_target_pairs={{0,5},{1,4},{2,7},{3,6},{4,1},{5,0},{6,3},{7,2},{8,13},{9,12},{10,... | collective-permute-start | bytes 688136 | tf_op jit(solution)/shard_map/ppermute | solution.py:235
  178.3 22.8 %all-to-all-start.2 = ((bf16[32,32,128]{2,1,0:T(8,128)(2,1)}), bf16[32,32,128]{2,1,0:T(8,128)(2,1)S(1)}, u32[]{:S(2)}, u32[]{:S(2)}) async-start(bf16[32,32,128]{2,1,0:T(8,128)(2,1)} %broadcast_in_dim.110), calls=%async_computation.2 | async-start | bytes 524288 | tf_op jit(solution)/shard_map/all_to_all | solution.py:325
  184.1 25.0 %collective-permute-start.28 = (bf16[32,3584]{1,0:T(8,128)(2,1)}, bf16[32,3584]{1,0:T(8,128)(2,1)S(1)}, u32[]{:S(2)}, u32[]{:S(2)}) collective-permute-start(bf16[32,3584]{1,0:T(8,128)(2,1)} %fusion.26), channel_id=1, source_target_pairs={{0,2},{1,3},{2,4},{3,5},{4,6},{5,7},{6,0},{7,1},{8,10},{9,11},{10,... | collective-permute-start | bytes 688136 | tf_op jit(solution)/shard_map/ppermute | solution.py:235
  187.0 22.2 %collective-permute-start.29 = (bf16[32,3584]{1,0:T(8,128)(2,1)S(1)}, bf16[32,3584]{1,0:T(8,128)(2,1)S(1)}, u32[]{:S(2)}, u32[]{:S(2)}) collective-permute-start(bf16[32,3584]{1,0:T(8,128)(2,1)S(1)} %fusion.25), channel_id=1, source_target_pairs={{0,3},{1,2},{2,5},{3,4},{4,7},{5,6},{6,1},{7,0},{8,11},{9,10},{10,... | collective-permute-start | bytes 688136 | tf_op jit(solution)/shard_map/ppermute | solution.py:235
  204.9 47.8 %all-to-all-start.3 = ((bf16[8,128,896]{2,1,0:T(8,128)(2,1)}), bf16[8,128,896]{2,1,0:T(8,128)(2,1)}, u32[]{:S(2)}, u32[]{:S(2)}) async-start(bf16[8,128,896]{2,1,0:T(8,128)(2,1)} %bitcast.127), calls=%async_computation.3 | async-start | bytes 3670016 | tf_op jit(solution)/shard_map/all_to_all | solution.py:353
  213.4 20.4 %collective-permute-start.32 = (bf16[2,32,3584]{2,1,0:T(8,128)(2,1)}, bf16[2,32,3584]{2,1,0:T(8,128)(2,1)}, u32[]{:S(2)}, u32[]{:S(2)}) collective-permute-start(bf16[2,32,3584]{2,1,0:T(8,128)(2,1)} %get-tuple-element.89), channel_id=1, source_target_pairs={{0,24},{8,16},{16,8},{24,0},{1,25},{9,17},{17,9},{25,1},{2,26},{10... | collective-permute-start | bytes 1376264 | tf_op jit(solution)/shard_map/ppermute | solution.py:238
  (43 other events, 592.6 us)

commit v5 on v3

--- a/solution.py
+++ b/solution.py
@@ -112,6 +112,7 @@
             out_specs=pl.BlockSpec((part, each * width), lambda at, place: (place[0] ^ at, 0)),
         ),
         out_shape=jax.ShapeDtypeStruct((block, each * width), jnp.bfloat16),
+        compiler_params=pltpu.CompilerParams(vmem_limit_bytes=24 << 20),
         cost_estimate=pl.CostEstimate(
             flops=block * each * width, bytes_accessed=6 * block * each * width, transcendentals=0
         ),
@@ -133,7 +134,12 @@
         out_specs=[ANYWHERE] * len(values),
         out_shape=[jax.ShapeDtypeStruct(value.shape, value.dtype) for value in values],
         input_output_aliases={at: at for at in range(len(values))},
+        compiler_params=pltpu.CompilerParams(vmem_limit_bytes=1 << 20),
     )(*values, *gates)
+
+
+def after(value, *others):
+    return lax.optimization_barrier((value,) + others)[0]
 
 
 def project(rows, adapter, mask):
@@ -208,12 +214,6 @@
     ).reshape(count * block, down_slab)
 
     last = chips - 1
-
-    def product(step, *gates):
-        return chunk_product(*pairs[step], down_weight, group, *gates)
-
-    products = [product(step) for step in range(last - 1)]
-    (hidden_slab,) = touch([hidden_slab], products[-1][0])
     grad_slab = jnp.zeros((count, block, up_slab), jnp.bfloat16)
     for step, pair in enumerate(pairs):
         back = ((chip - step) % chips) * CORES
@@ -221,27 +221,30 @@
             columns = lax.dynamic_slice_in_dim(rows, index * up_slab, up_slab, 1)
             grad_slab = lax.dynamic_update_index_in_dim(grad_slab, columns, back + (core ^ flip), 0)
     grad_slab = grad_slab.reshape(count * block, up_slab)
-    act_part = project(hidden_slab, adapter_down, mask)
-    grad_part = project(grad_slab, adapter_up, mask)
-    ranked = jnp.concatenate([grad_part, act_part], axis=1)
-
-    products += [product(last - 1, act_part), product(last, ranked)]
-
+    ranked = jnp.concatenate(
+        [project(grad_slab, adapter_up, mask), project(hidden_slab, adapter_down, mask)], axis=1
+    )
+
+    products = [
+        chunk_product(near, far, down_weight, group, *([ranked] if step == last else []))
+        for step, (near, far) in enumerate(pairs)
+    ]
     firsts = [
         (grp_move(near_sent, 1), grp_move(far_sent, 2)) for _, near_sent, _, far_sent in products
     ]
 
     def second(step, *gates):
         near_kept, _, far_kept, _ = products[step]
-        near_came, far_came = firsts[step] = touch(firsts[step], *gates)
+        near_came, far_came = firsts[step]
+        near_came, far_came = lax.optimization_barrier((near_came, far_came) + gates)[:2]
         near_sum = add(near_kept[1], near_came[1])
         far_sum = add(far_kept[1], far_came[1])
-        return near_sum, [grp_move(near_sum, 2), grp_move(far_sum, 1)]
+        return near_sum, (grp_move(near_sum, 2), grp_move(far_sum, 1))
 
     def total(step, seconds, *gates):
         near_kept, _, far_kept, _ = products[step]
         near_came, far_came = firsts[step]
-        near_last, far_last = touch(seconds, *gates) if gates else seconds
+        near_last, far_last = lax.optimization_barrier(seconds + gates)[:2]
         return (
             add(near_kept[0], near_came[0], near_last),
             add(far_kept[0], far_came[0], far_last),
@@ -257,7 +260,7 @@
 
     def put(arrived, step, came, *gates):
         ahead = ((chip + step) % chips) * CORES
-        came = touch(came, *gates)
+        came = lax.optimization_barrier(tuple(came) + gates)
         for flip in range(CORES):
             arrived = lax.dynamic_update_index_in_dim(arrived, came[flip], ahead + (core ^ flip), 0)
         return arrived
@@ -278,8 +281,12 @@
         concat_axis=0,
         tiled=True,
     )
-    begun, seconds = second(last - 1, products[last][0])
-    (share,) = touch([share], begun)
+    firsts[last - 1] = touch(firsts[last - 1], share)
+    _, seconds = second(last - 1, products[last][0])
+    sums = total(last - 1, seconds)
+    arrived = put(arrived, last - 2, came, sums[0])
+    came = hop(last - 1, sums)
+    _, seconds = second(last, sums[0])
     share = jnp.sum(share.astype(jnp.float32), axis=0).astype(jnp.bfloat16)
     ranked = lax.all_to_all(
         jnp.broadcast_to(share[None], (devices,) + share.shape),
@@ -288,14 +295,10 @@
         concat_axis=0,
         tiled=True,
     ).reshape(count * block, 2 * ranks)
-    sums = total(last - 1, seconds, share)
-    arrived = put(arrived, last - 2, came, sums[0])
-    came = hop(last - 1, sums)
-    _, seconds = second(last, sums[0])
-    sums = total(last, seconds)
+    sums = total(last, seconds, share)
     arrived = put(arrived, last - 1, came, sums[0])
     came = hop(last, sums)
-    (ranked,) = touch([ranked], *sums)
+    ranked = after(ranked, *sums)
     grad_rank = ranked[:, :ranks]
 
     flat_down = adapter_down.reshape(tenants * ranks, down_slab)
@@ -312,7 +315,7 @@
     )
     term = (term * ADAPTER_SCALE).astype(jnp.bfloat16).reshape(count, block, down_slab)
     arrived = put(arrived, last, came, term)
-    (rank_here,) = touch([ranked], term)
+    rank_here = after(ranked, term)
     term = lax.all_to_all(term, "seq", split_axis=0, concat_axis=0, tiled=True)
 
     each = count // groups

time: 264 us -> 226 us (0.86); the launches traced: 263 us -> 221 us
  local copies, waits for them, and re-layouts: 54.7 us -> 36.2 us
  other arithmetic: 29 us -> 13 us
  waiting for transfers between devices: 60.6 us -> 56.8 us
  starting transfers between devices: 73.3 us -> 70 us
    ppermute x14, waiting for transfers between devices: 34.7 us -> 19.3 us  [seq_move(): return lax.ppermute(value, 'seq', pairs)]
    convert_element_type x16, other arithmetic: 24.9 us -> 10.1 us  [add(): sum((term.astype(jnp.float32) for term in terms)).astype(jnp.bfloat16)]
    ppermute x19, waiting for transfers between devices: 16.7 us -> 30.9 us  [grp_move(): return lax.ppermute(value, 'grp', [(g, g ^ flip) for g in range(groups)])]
    unnamed x108 -> x60, local copies, waits for them, and re-layouts: 29.3 us -> 16.8 us
    ppermute x14, starting transfers between devices: 32.1 us -> 22.9 us  [seq_move(): return lax.ppermute(value, 'seq', pairs)]
    ppermute x19, starting transfers between devices: 22.4 us -> 29.1 us  [grp_move(): return lax.ppermute(value, 'grp', [(g, g ^ flip) for g in range(groups)])]
    all_to_all x1, starting transfers between devices: 6.78 us -> 3.97 us  [shards(): lax.all_to_all(ranked.reshape(devices, -1, 2 * ranks), ('grp', 'seq'), sp...]
    dynamic_update_slice x8, local copies, waits for them, and re-layouts: 12.2 us -> 9.38 us  [put(): lax.dynamic_update_index_in_dim(arrived, came[flip], ahead + (core ^ flip...]
  transfers between devices with their start and end apart: 37 -> 37, of which waited for: 11 -> 14; matrix products, arithmetic and copies ran while one was open for 27% -> 22% of each run, Pallas kernels for 9% -> 10%
where the time goes in v5:
time: 226 us; the launch traced here: 221 us
  starting transfers between devices  70 us (31%)
  waiting for transfers between devices  56.8 us (25%)
  local copies, waits for them, and re-layouts  36.2 us (16%)
  Pallas kernels  26.9 us (12%)
  matrix products  17 us (8%)
  other arithmetic  13 us (6%)
    ppermute x19, waiting for transfers between devices, grp_move(): return lax.ppermute(value, 'grp', [(g, g ^ flip) for g in range(groups)])  30.9 us
    ppermute x19, starting transfers between devices, grp_move(): return lax.ppermute(value, 'grp', [(g, g ^ flip) for g in range(groups)])  29.1 us
    pallas_call x4, Pallas kernels, chunk_product(): pl.pallas_call(functools.partial(chunk_kernel, STAGES), grid_spec=pltpu.P...  23 us
    ppermute x14, starting transfers between devices, seq_move(): return lax.ppermute(value, 'seq', pairs)  22.9 us
    ppermute x14, waiting for transfers between devices, seq_move(): return lax.ppermute(value, 'seq', pairs)  19.3 us
    unnamed x60, local copies, waits for them, and re-layouts  16.8 us
    dot_general x4, matrix products, dot(): lax.dot_general(left, right, dims, preferred_element_type=jnp.float32)  13.4 us
    convert_element_type x16, other arithmetic, add(): sum((term.astype(jnp.float32) for term in terms)).astype(jnp.bfloat16)  10.1 us
  transfers between devices with their start and end apart: 37, of which 14 were waited for; matrix products, arithmetic and copies ran while one was open for 22% of the time, Pallas kernels for 10%

profile of v5, /device:TPU:0, one launch (start us, length us, event | category | flops | bytes accessed | tf_op | source)
XLA Modules:
  0.0 221.4 jit_solution(15899854034856255552)
XLA Ops:
  3.8 3.0 %copy.46 = bf16[16,8,8,896]{3,2,0,1:T(8,128)(2,1)} copy(bf16[16,8,8,896]{3,2,1,0:T(8,128)(2,1)} %bitcast.134) | data formatting | bytes 3670016 | tf_op jit(solution)/shard_map/reshape | solution.py:209
  6.8 4.5 %all-to-all-start = ((bf16[8,128,896]{2,1,0:T(8,128)(2,1)}), bf16[8,128,896]{2,1,0:T(8,128)(2,1)}, u32[]{:S(2)}, u32[]{:S(2)}) async-start(bf16[8,128,896]{2,1,0:T(8,128)(2,1)} %bitcast.129), calls=%async_computation | async-start | bytes 3670016 | tf_op jit(solution)/shard_map/all_to_all | solution.py:208
  12.4 6.5 %collective-permute-done.3.near_ref = bf16[128,2048]{1,0:T(8,128)(2,1)S(1)} collective-permute-done((bf16[128,2048]{1,0:T(8,128)(2,1)}, bf16[128,2048]{1,0:T(8,128)(2,1)S(1)}, u32[]{:S(2)}, u32[]{:S(2)}) %collective-permute-start.3) | collective-permute-done | bytes 524320 | tf_op jit(solution)/shard_map/ppermute | solution.py:198
  19.0 5.2 %copy-done.1 = bf16[3584,2048]{1,0:T(8,128)(2,1)S(1)} copy-done((bf16[3584,2048]{1,0:T(8,128)(2,1)S(1)}, bf16[3584,2048]{1,0:T(8,128)(2,1)}, u32[]{:S(2)}) %copy-start.1) | copy-done | bytes 14680088
  24.2 5.4 %shard_map.94 = (bf16[2,32,3584]{2,1,0:T(8,128)(2,1)S(1)}, bf16[2,32,3584]{2,1,0:T(8,128)(2,1)S(1)}, bf16[2,32,3584]{2,1,0:T(8,128)(2,1)S(1)}, bf16[2,32,3584]{2,1,0:T(8,128)(2,1)S(1)}) custom-call(s32[1]{0:T(128)} %bitcast.place_ref, bf16[128,2048]{1,0:T(8,128)(2,1)S(1)} %copy-done.4, bf16[128,2048]{1,0:T(8,128)(2,1)S(1)} %collective-permute-done.far_ref, ...), custom_call_target="tpu_custom_call" | custom-call | flops 3758096384 | bytes 17563648 | tf_op jit(solution)/shard_map/pallas_call | solution.py:57
  32.9 4.3 %collective-permute-start.10 = (bf16[128,2048]{1,0:T(8,128)(2,1)S(1)}, bf16[128,2048]{1,0:T(8,128)(2,1)S(1)}, u32[]{:S(2)}, u32[]{:S(2)}) collective-permute-start(bf16[128,2048]{1,0:T(8,128)(2,1)S(1)} %collective-permute-done.3.near_ref), channel_id=1, source_target_pairs={{0,2},{1,3},{2,4},{3,5},{4,6},{5,7},{6,0},{7,1},{8,10},{9,11},{10,... | collective-permute-start | bytes 1572872 | tf_op jit(solution)/shard_map/ppermute | solution.py:198
  37.2 5.5 %shard_map.95 = (bf16[2,32,3584]{2,1,0:T(8,128)(2,1)S(1)}, bf16[2,32,3584]{2,1,0:T(8,128)(2,1)S(1)}, bf16[2,32,3584]{2,1,0:T(8,128)(2,1)S(1)}, bf16[2,32,3584]{2,1,0:T(8,128)(2,1)S(1)}) custom-call(s32[1]{0:T(128)} %bitcast.place_ref, bf16[128,2048]{1,0:T(8,128)(2,1)S(1)} %collective-permute-done.3.near_ref, ...), custom_call_target="tpu_custom_call" | custom-call | flops 3758096384 | bytes 17563648 | tf_op jit(solution)/shard_map/pallas_call | solution.py:57
  48.4 11.1 %collective-permute-done.10.near_ref = bf16[128,2048]{1,0:T(8,128)(2,1)S(1)} collective-permute-done((bf16[128,2048]{1,0:T(8,128)(2,1)S(1)}, bf16[128,2048]{1,0:T(8,128)(2,1)S(1)}, u32[]{:S(2)}, u32[]{:S(2)}) %collective-permute-start.10) | collective-permute-done | bytes 524320 | tf_op jit(solution)/shard_map/ppermute | solution.py:198
  59.5 8.6 %collective-permute-start.18 = (bf16[128,2048]{1,0:T(8,128)(2,1)S(1)}, bf16[128,2048]{1,0:T(8,128)(2,1)S(1)}, u32[]{:S(2)}, u32[]{:S(2)}) collective-permute-start(bf16[128,2048]{1,0:T(8,128)(2,1)S(1)} %collective-permute-done.10.near_ref), channel_id=1, source_target_pairs={{0,2},{1,3},{2,4},{3,5},{4,6},{5,7},{6,0},{7,1},{8,10},{9,11},{10,... | collective-permute-start | bytes 1572872 | tf_op jit(solution)/shard_map/ppermute | solution.py:198
  68.5 6.1 %shard_map.96 = (bf16[2,32,3584]{2,1,0:T(8,128)(2,1)S(1)}, bf16[2,32,3584]{2,1,0:T(8,128)(2,1)}, bf16[2,32,3584]{2,1,0:T(8,128)(2,1)S(1)}, bf16[2,32,3584]{2,1,0:T(8,128)(2,1)}) custom-call(s32[1]{0:T(128)} %bitcast.place_ref, bf16[128,2048]{1,0:T(8,128)(2,1)S(1)} %collective-permute-done.10.near_ref, bf16[128,2048]{1,0:T(8,128)(2,1)S(1)} %collective-permute-done.11.far_ref, ...), custom_call_target="tpu_custom_call" | custom-call | flops 3758096384 | bytes 17563648 | tf_op jit(solution)/shard_map/pallas_call | solution.py:57
  92.9 4.6 %multiply_reduce_fusion = bf16[1024,64]{0,1:T(8,128)(2,1)} fusion(f32[1024,16]{0,1:T(8,128)} %copy-done.25, bf16[1024,896,1]{1,0,2:T(8,128)(2,1)} %bitcast.25, bf16[16,64,896]{2,1,0:T(8,128)(2,1)S(1)} %copy-done), kind=kOutput, calls=%fused_computation | convolution fusion | flops 1881079808 | bytes 3866624 | tf_op jit(solution)/shard_map/dot_general | solution.py:19
  101.1 4.0 %all-to-all-start.1 = ((bf16[32,32,128]{2,1,0:T(8,128)(2,1)}), bf16[32,32,128]{2,1,0:T(8,128)(2,1)S(1)}, u32[]{:S(2)}, u32[]{:S(2)}) async-start(bf16[32,32,128]{2,1,0:T(8,128)(2,1)} %pad_maximum_fusion), calls=%async_computation.1 | async-start | bytes 524288 | tf_op jit(solution)/shard_map/all_to_all | solution.py:277
  107.4 5.2 %copy-done.3 = bf16[3584,2048]{1,0:T(8,128)(2,1)S(1)} copy-done((bf16[3584,2048]{1,0:T(8,128)(2,1)S(1)}, bf16[3584,2048]{1,0:T(8,128)(2,1)}, u32[]{:S(2)}) %copy-start.3) | copy-done | bytes 14680088
  112.6 6.0 %shard_map.98 = (bf16[2,32,3584]{2,1,0:T(8,128)(2,1)S(1)}, bf16[2,32,3584]{2,1,0:T(8,128)(2,1)}, bf16[2,32,3584]{2,1,0:T(8,128)(2,1)S(1)}, bf16[2,32,3584]{2,1,0:T(8,128)(2,1)S(1)}) custom-call(s32[1]{0:T(128)} %bitcast.place_ref, bf16[128,2048]{1,0:T(8,128)(2,1)S(1)} %collective-permute-done.18.near_ref, bf16[128,2048]{1,0:T(8,128)(2,1)S(1)} %copy-done.6, ...), custom_call_target="tpu_custom_call" | custom-call | flops 3758096384 | bytes 17563648 | tf_op jit(solution)/shard_map/pallas_call | solution.py:57
  128.7 4.6 %all-to-all-start.2 = ((bf16[32,32,128]{2,1,0:T(8,128)(2,1)}), bf16[32,32,128]{2,1,0:T(8,128)(2,1)S(1)}, u32[]{:S(2)}, u32[]{:S(2)}) async-start(bf16[32,32,128]{2,1,0:T(8,128)(2,1)} %broadcast_in_dim.110), calls=%async_computation.2 | async-start | bytes 524288 | tf_op jit(solution)/shard_map/all_to_all | solution.py:291
  140.0 5.1 %collective-permute-done.24 = bf16[2,32,3584]{2,1,0:T(8,128)(2,1)} collective-permute-done((bf16[2,32,3584]{2,1,0:T(8,128)(2,1)}, bf16[2,32,3584]{2,1,0:T(8,128)(2,1)}, u32[]{:S(2)}, u32[]{:S(2)}) %collective-permute-start.24) | collective-permute-done | bytes 458784 | tf_op jit(solution)/shard_map/ppermute | solution.py:201
  145.0 3.8 %collective-permute-done.25 = bf16[2,32,3584]{2,1,0:T(8,128)(2,1)S(1)} collective-permute-done((bf16[2,32,3584]{2,1,0:T(8,128)(2,1)}, bf16[2,32,3584]{2,1,0:T(8,128)(2,1)S(1)}, u32[]{:S(2)}, u32[]{:S(2)}) %collective-permute-start.25) | collective-permute-done | bytes 458784 | tf_op jit(solution)/shard_map/ppermute | solution.py:201
  164.3 3.7 %fusion = bf16[1024,896]{1,0:T(8,128)(2,1)} fusion(bf16[16,64,896]{2,1,0:T(8,128)(2,1)S(1)} %copy-done, bf16[1024,16]{0,1:T(8,128)(2,1)S(1)} %copy-done.26, bf16[1024,64]{0,1:T(8,128)(2,1)S(1)} %copy.41), kind=kOutput, calls=%fused_computation.3 | convolution fusion | flops 1881931776 | bytes 3833856 | tf_op jit(solution)/shard_map/dot_general | solution.py:307
  168.0 5.0 %all-to-all-start.3 = ((bf16[8,128,896]{2,1,0:T(8,128)(2,1)}), bf16[8,128,896]{2,1,0:T(8,128)(2,1)}, u32[]{:S(2)}, u32[]{:S(2)}) async-start(bf16[8,128,896]{2,1,0:T(8,128)(2,1)} %bitcast.135), calls=%async_computation.3 | async-start | bytes 3670016 | tf_op jit(solution)/shard_map/all_to_all | solution.py:319
  182.1 6.4 %collective-permute-start.31 = (bf16[2,32,3584]{2,1,0:T(8,128)(2,1)S(1)}, bf16[2,32,3584]{2,1,0:T(8,128)(2,1)S(1)}, u32[]{:S(2)}, u32[]{:S(2)}) collective-permute-start(bf16[2,32,3584]{2,1,0:T(8,128)(2,1)S(1)} %get-tuple-element.92), channel_id=1, source_target_pairs={{0,16},{8,24},{16,0},{24,8},{1,17},{9,25},{17,1},{25,9},{2,18},{10... | collective-permute-start | bytes 1376264 | tf_op jit(solution)/shard_map/ppermute | solution.py:201
  188.5 5.7 %fusion.9 = f32[16,64,896]{2,1,0:T(8,128)} fusion(bf16[1024,896,1]{1,0,2:T(8,128)(2,1)} %bitcast.25, f32[16]{0:T(128)S(1)} %broadcast_divide_fusion, bf16[1024,64]{0,1:T(8,128)(2,1)S(1)} %copy.42, bf16[1024,16]{0,1:T(8,128)(2,1)S(1)} %copy-done.26), kind=kOutput, calls=%fused_computation.12 | convolution fusion | flops 1881014272 | bytes 5668928 | tf_op jit(solution)/shard_map/dot_general | solution.py:19
  194.1 14.3 %collective-permute-done.31.refs_2_ = bf16[2,32,3584]{2,1,0:T(8,128)(2,1)S(1)} collective-permute-done((bf16[2,32,3584]{2,1,0:T(8,128)(2,1)S(1)}, bf16[2,32,3584]{2,1,0:T(8,128)(2,1)S(1)}, u32[]{:S(2)}, u32[]{:S(2)}) %collective-permute-start.31) | collective-permute-done | bytes 458784 | tf_op jit(solution)/shard_map/ppermute | solution.py:201
  210.0 6.5 %all-to-all-done.3.refs_4_ = bf16[8,128,896]{2,1,0:T(8,128)(2,1)} async-done(((bf16[8,128,896]{2,1,0:T(8,128)(2,1)}), bf16[8,128,896]{2,1,0:T(8,128)(2,1)}, u32[]{:S(2)}, u32[]{:S(2)}) %all-to-all-start.3) | async-done | bytes 1835040 | tf_op jit(solution)/shard_map/all_to_all | solution.py:319
  217.5 3.8 %shard_map.99 = bf16[128,7168]{1,0:T(8,128)(2,1)} custom-call(s32[1]{0:T(128)} %bitcast.place_ref, bf16[2,32,3584]{2,1,0:T(8,128)(2,1)S(1)} %get-tuple-element.94.refs_0_, bf16[2,32,3584]{2,1,0:T(8,128)(2,1)S(1)} %collective-permute-done.30.refs_1_, bf16[2,32,3584]{2,1,0:T(8,128)(2,1)S(1)} %collective-permute-done.31.refs_2_, ...), custom_call_target="tpu_custom_call" | custom-call | flops 917504 | bytes 5505024 | tf_op jit(solution)/shard_map/pallas_call | solution.py:105
  (173 shorter events, 81.2 us)
Async XLA Ops:
  0.6 18.4 %collective-permute-start = (bf16[128,2048]{1,0:T(8,128)(2,1)}, bf16[128,2048]{1,0:T(8,128)(2,1)S(1)}, u32[]{:S(2)}, u32[]{:S(2)}) collective-permute-start(bf16[128,2048]{1,0:T(8,128)(2,1)} %near_ref.1), channel_id=1, source_target_pairs={{0,1},{1,0},{2,3},{3,2},{4,5},{5,4},{6,7},{7,6},{8,9},{9,8},{10,11... | collective-permute-start | bytes 1572872 | tf_op jit(solution)/shard_map/ppermute | solution.py:198
  1.2 17.8 %collective-permute-start.3 = (bf16[128,2048]{1,0:T(8,128)(2,1)}, bf16[128,2048]{1,0:T(8,128)(2,1)S(1)}, u32[]{:S(2)}, u32[]{:S(2)}) collective-permute-start(bf16[128,2048]{1,0:T(8,128)(2,1)} %near_ref.1), channel_id=1, source_target_pairs={{0,2},{1,3},{2,4},{3,5},{4,6},{5,7},{6,0},{7,1},{8,10},{9,11},{10,... | collective-permute-start | bytes 1572872 | tf_op jit(solution)/shard_map/ppermute | solution.py:198
  6.8 86.1 %all-to-all-start = ((bf16[8,128,896]{2,1,0:T(8,128)(2,1)}), bf16[8,128,896]{2,1,0:T(8,128)(2,1)}, u32[]{:S(2)}, u32[]{:S(2)}) async-start(bf16[8,128,896]{2,1,0:T(8,128)(2,1)} %bitcast.129), calls=%async_computation | async-start | bytes 3670016 | tf_op jit(solution)/shard_map/all_to_all | solution.py:208
  18.9 18.2 %collective-permute-start.4 = (bf16[128,2048]{1,0:T(8,128)(2,1)S(1)}, bf16[128,2048]{1,0:T(8,128)(2,1)S(1)}, u32[]{:S(2)}, u32[]{:S(2)}) collective-permute-start(bf16[128,2048]{1,0:T(8,128)(2,1)S(1)} %collective-permute-done.3.near_ref), channel_id=1, source_target_pairs={{0,1},{1,0},{2,3},{3,2},{4,5},{5,4},{6,7},{7,6},{8,9},{9,8},{10,11... | collective-permute-start | bytes 1572872 | tf_op jit(solution)/shard_map/ppermute | solution.py:198
  32.9 26.6 %collective-permute-start.10 = (bf16[128,2048]{1,0:T(8,128)(2,1)S(1)}, bf16[128,2048]{1,0:T(8,128)(2,1)S(1)}, u32[]{:S(2)}, u32[]{:S(2)}) collective-permute-start(bf16[128,2048]{1,0:T(8,128)(2,1)S(1)} %collective-permute-done.3.near_ref), channel_id=1, source_target_pairs={{0,2},{1,3},{2,4},{3,5},{4,6},{5,7},{6,0},{7,1},{8,10},{9,11},{10,... | collective-permute-start | bytes 1572872 | tf_op jit(solution)/shard_map/ppermute | solution.py:198
  44.1 15.4 %collective-permute-start.5 = (bf16[32,3584]{1,0:T(8,128)(2,1)S(1)}, bf16[32,3584]{1,0:T(8,128)(2,1)S(1)}, u32[]{:S(2)}, u32[]{:S(2)}) collective-permute-start(bf16[32,3584]{1,0:T(8,128)(2,1)S(1)} %fusion.31), channel_id=1, source_target_pairs={{0,16},{8,24},{16,0},{24,8},{1,17},{9,25},{17,1},{25,9},{2,18},{10... | collective-permute-start | bytes 688136 | tf_op jit(solution)/shard_map/ppermute | solution.py:201
  45.7 22.4 %collective-permute-start.6 = (bf16[32,3584]{1,0:T(8,128)(2,1)S(1)}, bf16[32,3584]{1,0:T(8,128)(2,1)S(1)}, u32[]{:S(2)}, u32[]{:S(2)}) collective-permute-start(bf16[32,3584]{1,0:T(8,128)(2,1)S(1)} %fusion.32), channel_id=1, source_target_pairs={{0,8},{8,0},{16,24},{24,16},{1,9},{9,1},{17,25},{25,17},{2,10},{10... | collective-permute-start | bytes 688136 | tf_op jit(solution)/shard_map/ppermute | solution.py:201
  46.3 28.2 %collective-permute-start.8 = (bf16[2,32,3584]{2,1,0:T(8,128)(2,1)S(1)}, bf16[2,32,3584]{2,1,0:T(8,128)(2,1)S(1)}, u32[]{:S(2)}, u32[]{:S(2)}) collective-permute-start(bf16[2,32,3584]{2,1,0:T(8,128)(2,1)S(1)} %get-tuple-element.56), channel_id=1, source_target_pairs={{0,8},{8,0},{16,24},{24,16},{1,9},{9,1},{17,25},{25,17},{2,10},{10... | collective-permute-start | bytes 1376264 | tf_op jit(solution)/shard_map/ppermute | solution.py:201
  47.9 26.7 %collective-permute-start.9 = (bf16[2,32,3584]{2,1,0:T(8,128)(2,1)S(1)}, bf16[2,32,3584]{2,1,0:T(8,128)(2,1)S(1)}, u32[]{:S(2)}, u32[]{:S(2)}) collective-permute-start(bf16[2,32,3584]{2,1,0:T(8,128)(2,1)S(1)} %get-tuple-element.57), channel_id=1, source_target_pairs={{0,16},{8,24},{16,0},{24,8},{1,17},{9,25},{17,1},{25,9},{2,18},{10... | collective-permute-start | bytes 1376264 | tf_op jit(solution)/shard_map/ppermute | solution.py:201
  59.5 20.4 %collective-permute-start.18 = (bf16[128,2048]{1,0:T(8,128)(2,1)S(1)}, bf16[128,2048]{1,0:T(8,128)(2,1)S(1)}, u32[]{:S(2)}, u32[]{:S(2)}) collective-permute-start(bf16[128,2048]{1,0:T(8,128)(2,1)S(1)} %collective-permute-done.10.near_ref), channel_id=1, source_target_pairs={{0,2},{1,3},{2,4},{3,5},{4,6},{5,7},{6,0},{7,1},{8,10},{9,11},{10,... | collective-permute-start | bytes 1572872 | tf_op jit(solution)/shard_map/ppermute | solution.py:198
  68.2 18.3 %collective-permute-start.7 = (bf16[32,3584]{1,0:T(8,128)(2,1)S(1)}, bf16[32,3584]{1,0:T(8,128)(2,1)S(1)}, u32[]{:S(2)}, u32[]{:S(2)}) collective-permute-start(bf16[32,3584]{1,0:T(8,128)(2,1)S(1)} %fusion.29), channel_id=1, source_target_pairs={{0,1},{1,0},{2,3},{3,2},{4,5},{5,4},{6,7},{7,6},{8,9},{9,8},{10,11... | collective-permute-start | bytes 688136 | tf_op jit(solution)/shard_map/ppermute | solution.py:198
  78.6 41.6 %collective-permute-start.16 = (bf16[2,32,3584]{2,1,0:T(8,128)(2,1)}, bf16[2,32,3584]{2,1,0:T(8,128)(2,1)S(1)}, u32[]{:S(2)}, u32[]{:S(2)}) collective-permute-start(bf16[2,32,3584]{2,1,0:T(8,128)(2,1)} %get-tuple-element.66), channel_id=1, source_target_pairs={{0,8},{8,0},{16,24},{24,16},{1,9},{9,1},{17,25},{25,17},{2,10},{10... | collective-permute-start | bytes 1376264 | tf_op jit(solution)/shard_map/ppermute | solution.py:201
  79.9 41.0 %collective-permute-start.17 = (bf16[2,32,3584]{2,1,0:T(8,128)(2,1)}, bf16[2,32,3584]{2,1,0:T(8,128)(2,1)S(1)}, u32[]{:S(2)}, u32[]{:S(2)}) collective-permute-start(bf16[2,32,3584]{2,1,0:T(8,128)(2,1)} %get-tuple-element.67), channel_id=1, source_target_pairs={{0,16},{8,24},{16,0},{24,8},{1,17},{9,25},{17,1},{25,9},{2,18},{10... | collective-permute-start | bytes 1376264 | tf_op jit(solution)/shard_map/ppermute | solution.py:201
  85.6 54.3 %collective-permute-start.14 = (bf16[32,3584]{1,0:T(8,128)(2,1)}, bf16[32,3584]{1,0:T(8,128)(2,1)}, u32[]{:S(2)}, u32[]{:S(2)}) collective-permute-start(bf16[32,3584]{1,0:T(8,128)(2,1)} %fusion.28), channel_id=1, source_target_pairs={{0,6},{1,7},{2,0},{3,1},{4,2},{5,3},{6,4},{7,5},{8,14},{9,15},{10,... | collective-permute-start | bytes 688136 | tf_op jit(solution)/shard_map/ppermute | solution.py:198
  87.3 52.6 %collective-permute-start.15 = (bf16[32,3584]{1,0:T(8,128)(2,1)}, bf16[32,3584]{1,0:T(8,128)(2,1)}, u32[]{:S(2)}, u32[]{:S(2)}) collective-permute-start(bf16[32,3584]{1,0:T(8,128)(2,1)} %fusion.27), channel_id=1, source_target_pairs={{0,7},{1,6},{2,1},{3,0},{4,3},{5,2},{6,5},{7,4},{8,15},{9,14},{10,... | collective-permute-start | bytes 688136 | tf_op jit(solution)/shard_map/ppermute | solution.py:198
  101.1 19.9 %all-to-all-start.1 = ((bf16[32,32,128]{2,1,0:T(8,128)(2,1)}), bf16[32,32,128]{2,1,0:T(8,128)(2,1)S(1)}, u32[]{:S(2)}, u32[]{:S(2)}) async-start(bf16[32,32,128]{2,1,0:T(8,128)(2,1)} %pad_maximum_fusion), calls=%async_computation.1 | async-start | bytes 524288 | tf_op jit(solution)/shard_map/all_to_all | solution.py:277
  127.4 17.6 %collective-permute-start.24 = (bf16[2,32,3584]{2,1,0:T(8,128)(2,1)}, bf16[2,32,3584]{2,1,0:T(8,128)(2,1)}, u32[]{:S(2)}, u32[]{:S(2)}) collective-permute-start(bf16[2,32,3584]{2,1,0:T(8,128)(2,1)} %get-tuple-element.78), channel_id=1, source_target_pairs={{0,8},{8,0},{16,24},{24,16},{1,9},{9,1},{17,25},{25,17},{2,10},{10... | collective-permute-start | bytes 1376264 | tf_op jit(solution)/shard_map/ppermute | solution.py:201
  128.7 35.4 %all-to-all-start.2 = ((bf16[32,32,128]{2,1,0:T(8,128)(2,1)}), bf16[32,32,128]{2,1,0:T(8,128)(2,1)S(1)}, u32[]{:S(2)}, u32[]{:S(2)}) async-start(bf16[32,32,128]{2,1,0:T(8,128)(2,1)} %broadcast_in_dim.110), calls=%async_computation.2 | async-start | bytes 524288 | tf_op jit(solution)/shard_map/all_to_all | solution.py:291
  136.4 24.6 %collective-permute-start.22 = (bf16[32,3584]{1,0:T(8,128)(2,1)S(1)}, bf16[32,3584]{1,0:T(8,128)(2,1)S(1)}, u32[]{:S(2)}, u32[]{:S(2)}) collective-permute-start(bf16[32,3584]{1,0:T(8,128)(2,1)S(1)} %fusion.26), channel_id=1, source_target_pairs={{0,4},{1,5},{2,6},{3,7},{4,0},{5,1},{6,2},{7,3},{8,12},{9,13},{10,... | collective-permute-start | bytes 688136 | tf_op jit(solution)/shard_map/ppermute | solution.py:198
  139.9 22.1 %collective-permute-start.23 = (bf16[32,3584]{1,0:T(8,128)(2,1)S(1)}, bf16[32,3584]{1,0:T(8,128)(2,1)S(1)}, u32[]{:S(2)}, u32[]{:S(2)}) collective-permute-start(bf16[32,3584]{1,0:T(8,128)(2,1)S(1)} %fusion.25), channel_id=1, source_target_pairs={{0,5},{1,4},{2,7},{3,6},{4,1},{5,0},{6,3},{7,2},{8,13},{9,12},{10,... | collective-permute-start | bytes 688136 | tf_op jit(solution)/shard_map/ppermute | solution.py:198
  159.5 16.2 %collective-permute-start.28 = (bf16[32,3584]{1,0:T(8,128)(2,1)S(1)}, bf16[32,3584]{1,0:T(8,128)(2,1)}, u32[]{:S(2)}, u32[]{:S(2)}) collective-permute-start(bf16[32,3584]{1,0:T(8,128)(2,1)S(1)} %fusion.24), channel_id=1, source_target_pairs={{0,2},{1,3},{2,4},{3,5},{4,6},{5,7},{6,0},{7,1},{8,10},{9,11},{10,... | collective-permute-start | bytes 688136 | tf_op jit(solution)/shard_map/ppermute | solution.py:198
  168.0 48.6 %all-to-all-start.3 = ((bf16[8,128,896]{2,1,0:T(8,128)(2,1)}), bf16[8,128,896]{2,1,0:T(8,128)(2,1)}, u32[]{:S(2)}, u32[]{:S(2)}) async-start(bf16[8,128,896]{2,1,0:T(8,128)(2,1)} %bitcast.135), calls=%async_computation.3 | async-start | bytes 3670016 | tf_op jit(solution)/shard_map/all_to_all | solution.py:319
  182.1 26.4 %collective-permute-start.31 = (bf16[2,32,3584]{2,1,0:T(8,128)(2,1)S(1)}, bf16[2,32,3584]{2,1,0:T(8,128)(2,1)S(1)}, u32[]{:S(2)}, u32[]{:S(2)}) collective-permute-start(bf16[2,32,3584]{2,1,0:T(8,128)(2,1)S(1)} %get-tuple-element.92), channel_id=1, source_target_pairs={{0,16},{8,24},{16,0},{24,8},{1,17},{9,25},{17,1},{25,9},{2,18},{10... | collective-permute-start | bytes 1376264 | tf_op jit(solution)/shard_map/ppermute | solution.py:201
  188.5 20.7 %collective-permute-start.32 = (bf16[2,32,3584]{2,1,0:T(8,128)(2,1)S(1)}, bf16[2,32,3584]{2,1,0:T(8,128)(2,1)S(1)}, u32[]{:S(2)}, u32[]{:S(2)}) collective-permute-start(bf16[2,32,3584]{2,1,0:T(8,128)(2,1)S(1)} %get-tuple-element.91), channel_id=1, source_target_pairs={{0,24},{8,16},{16,8},{24,0},{1,25},{9,17},{17,9},{25,1},{2,26},{10... | collective-permute-start | bytes 1376264 | tf_op jit(solution)/shard_map/ppermute | solution.py:201
  (43 other events, 457.5 us)

commit v6 on v5

--- a/solution.py
+++ b/solution.py
@@ -29,33 +29,32 @@
     return fits[0] if fits else width
 
 
-def chunk_kernel(stages, place_ref, near_ref, far_ref, weight_ref, *rest):
-    outs, rows = rest[-5:-1], rest[-1]
-    part = near_ref.shape[0] // (2 * len(stages))
-    sides = [(ref, flips) for ref, order in zip((near_ref, far_ref), stages) for flips in order]
-    cuts = [(ref, flip) for ref, flips in sides for flip in flips]
+def chunk_kernel(groups, place_ref, near_ref, far_ref, weight_ref, *rest):
+    outs, rows = rest[-groups - 1 : -1], rest[-1]
+    part = near_ref.shape[0] // groups
 
     @pl.when(pl.program_id(0) == 0)
     def _():
-        for at, (ref, flip) in enumerate(cuts):
-            low = pl.multiple_of((place_ref[0] ^ flip) * part, part)
-            rows[at * part : (at + 1) * part] = ref[pl.ds(low, part)]
+        for flip in range(groups):
+            at = pl.multiple_of((place_ref[0] ^ flip) * part, part)
+            low = flip * CORES * part
+            rows[low : low + part] = near_ref[pl.ds(at, part)]
+            rows[low + part : low + 2 * part] = far_ref[pl.ds(at, part)]
 
     full = dot(rows[...], weight_ref[...], CONTRACT_LAST).astype(jnp.bfloat16)
-    for at in range(len(cuts)):
-        outs[at // 2][at % 2] = full[at * part : (at + 1) * part]
-
-
-STAGES = (((0, 2), (1, 3)), ((0, 1), (2, 3)))
-
-
-def chunk_product(near, far, weight, group, *gates):
+    for flip in range(groups):
+        for core in range(CORES):
+            low = (flip * CORES + core) * part
+            outs[flip][core] = full[low : low + part]
+
+
+def chunk_product(near, far, weight, group, groups, *gates):
     block, depth = near.shape
     width = weight.shape[0]
     tile = tile_of(width)
-    part = block // (2 * len(STAGES))
+    part = block // groups
     return pl.pallas_call(
-        functools.partial(chunk_kernel, STAGES),
+        functools.partial(chunk_kernel, groups),
         grid_spec=pltpu.PrefetchScalarGridSpec(
             num_scalar_prefetch=1,
             grid=(width // tile,),
@@ -65,10 +64,10 @@
                 pl.BlockSpec((tile, depth), lambda at, place: (at, 0)),
             ]
             + [ANYWHERE] * len(gates),
-            out_specs=[pl.BlockSpec((2, part, tile), lambda at, place: (0, 0, at))] * 4,
+            out_specs=[pl.BlockSpec((CORES, part, tile), lambda at, place: (0, 0, at))] * groups,
             scratch_shapes=[pltpu.VMEM((CORES * block, depth), jnp.bfloat16)],
         ),
-        out_shape=[jax.ShapeDtypeStruct((2, part, width), jnp.bfloat16)] * 4,
+        out_shape=[jax.ShapeDtypeStruct((CORES, part, width), jnp.bfloat16)] * groups,
         compiler_params=pltpu.CompilerParams(vmem_limit_bytes=24 << 20),
         cost_estimate=pl.CostEstimate(
             flops=2 * CORES * block * depth * width,
@@ -153,6 +152,61 @@
     return jnp.concatenate(parts, axis=0).astype(jnp.bfloat16)
 
 
+def project_kernel(owner_ref, grad_ref, act_ref, up_ref, down_ref, out_ref):
+    rows, lanes = out_ref.shape
+    owner = owner_ref[...]
+    lane = lax.broadcasted_iota(jnp.int32, (rows, lanes), 1)
+    high = (lane >= lanes // 2).astype(jnp.int32)
+
+    def pick(left, adapter):
+        full = dot(left, adapter, CONTRACT_LAST)
+        total = jnp.zeros((rows, lanes), jnp.float32)
+        for pair in range(full.shape[1] // lanes):
+            mine = owner == 2 * pair + high
+            total += jnp.where(mine, full[:, pair * lanes : (pair + 1) * lanes], 0.0)
+        return total + pltpu.roll(total, lanes // 2, 1)
+
+    grad = pick(grad_ref[...], up_ref[...])
+    act = pick(act_ref[...], down_ref[...])
+    out_ref[...] = jnp.where(high == 0, grad, act).astype(jnp.bfloat16)
+
+
+def project_both(grad_slab, hidden_slab, adapter_up, adapter_down, owner, mask):
+    tenants, ranks, up_slab = adapter_up.shape
+    down_slab = adapter_down.shape[2]
+    tokens = grad_slab.shape[0]
+    rows = 256
+    if up_slab % 128 or down_slab % 128 or ranks != 64 or tenants % 2 or tokens % rows:
+        return jnp.concatenate(
+            [project(grad_slab, adapter_up, mask), project(hidden_slab, adapter_down, mask)], axis=1
+        )
+    return pl.pallas_call(
+        project_kernel,
+        grid=(tokens // rows,),
+        in_specs=[
+            pl.BlockSpec((rows, 1), lambda at: (at, 0)),
+            pl.BlockSpec((rows, up_slab), lambda at: (at, 0)),
+            pl.BlockSpec((rows, down_slab), lambda at: (at, 0)),
+            pl.BlockSpec((tenants * ranks, up_slab), lambda at: (0, 0)),
+            pl.BlockSpec((tenants * ranks, down_slab), lambda at: (0, 0)),
+        ],
+        out_specs=pl.BlockSpec((rows, 2 * ranks), lambda at: (at, 0)),
+        out_shape=jax.ShapeDtypeStruct((tokens, 2 * ranks), jnp.bfloat16),
+        compiler_params=pltpu.CompilerParams(vmem_limit_bytes=24 << 20),
+        cost_estimate=pl.CostEstimate(
+            flops=2 * tokens * tenants * ranks * (up_slab + down_slab),
+            bytes_accessed=2 * (tokens + tenants * ranks) * (up_slab + down_slab),
+            transcendentals=0,
+        ),
+    )(
+        owner.reshape(tokens, 1),
+        grad_slab,
+        hidden_slab,
+        adapter_up.reshape(tenants * ranks, up_slab),
+        adapter_down.reshape(tenants * ranks, down_slab),
+    )
+
+
 def spread(rank, mask):
     wide = rank[:, None, :] * mask.astype(jnp.bfloat16)[:, :, None]
     return wide.reshape(rank.shape[0], -1)
@@ -221,57 +275,22 @@
             columns = lax.dynamic_slice_in_dim(rows, index * up_slab, up_slab, 1)
             grad_slab = lax.dynamic_update_index_in_dim(grad_slab, columns, back + (core ^ flip), 0)
     grad_slab = grad_slab.reshape(count * block, up_slab)
-    ranked = jnp.concatenate(
-        [project(grad_slab, adapter_up, mask), project(hidden_slab, adapter_down, mask)], axis=1
-    )
+    ranked = project_both(grad_slab, hidden_slab, adapter_up, adapter_down, owner, mask)
 
     products = [
-        chunk_product(near, far, down_weight, group, *([ranked] if step == last else []))
-        for step, (near, far) in enumerate(pairs)
+        chunk_product(near, far, down_weight, group, groups) for near, far in pairs
     ]
-    firsts = [
-        (grp_move(near_sent, 1), grp_move(far_sent, 2)) for _, near_sent, _, far_sent in products
-    ]
-
-    def second(step, *gates):
-        near_kept, _, far_kept, _ = products[step]
-        near_came, far_came = firsts[step]
-        near_came, far_came = lax.optimization_barrier((near_came, far_came) + gates)[:2]
-        near_sum = add(near_kept[1], near_came[1])
-        far_sum = add(far_kept[1], far_came[1])
-        return near_sum, (grp_move(near_sum, 2), grp_move(far_sum, 1))
-
-    def total(step, seconds, *gates):
-        near_kept, _, far_kept, _ = products[step]
-        near_came, far_came = firsts[step]
-        near_last, far_last = lax.optimization_barrier(seconds + gates)[:2]
-        return (
-            add(near_kept[0], near_came[0], near_last),
-            add(far_kept[0], far_came[0], far_last),
-        )
-
-    arrived = jnp.zeros((count, part, width), jnp.bfloat16)
-
-    def hop(step, sums):
-        return [
-            sums[flip] if step == 0 and flip == 0 else seq_move(sums[flip], step, flip)
-            for flip in range(CORES)
-        ]
-
-    def put(arrived, step, came, *gates):
-        ahead = ((chip + step) % chips) * CORES
-        came = lax.optimization_barrier(tuple(came) + gates)
-        for flip in range(CORES):
-            arrived = lax.dynamic_update_index_in_dim(arrived, came[flip], ahead + (core ^ flip), 0)
-        return arrived
-
-    came = None
-    for step in range(last - 1):
-        _, seconds = second(step, products[step + 1][0])
-        sums = total(step, seconds)
-        if came is not None:
-            arrived = put(arrived, step - 1, came, sums[0])
-        came = hop(step, sums)
+    came = []
+    for step in range(chips):
+        kept = products[step][0]
+        others = [grp_move(products[step][flip], flip) for flip in range(1, groups)]
+        gates = [products[step + 1][0]] if step < last else []
+        if step == last - 1:
+            gates.append(ranked)
+        if gates:
+            (others[0],) = touch([others[0]], *gates)
+        sums = add(kept, *others)
+        came.append(seq_move(sums, step, 0) if step else sums)
 
     devices = count * groups
     share = lax.all_to_all(
@@ -281,12 +300,6 @@
         concat_axis=0,
         tiled=True,
     )
-    firsts[last - 1] = touch(firsts[last - 1], share)
-    _, seconds = second(last - 1, products[last][0])
-    sums = total(last - 1, seconds)
-    arrived = put(arrived, last - 2, came, sums[0])
-    came = hop(last - 1, sums)
-    _, seconds = second(last, sums[0])
     share = jnp.sum(share.astype(jnp.float32), axis=0).astype(jnp.bfloat16)
     ranked = lax.all_to_all(
         jnp.broadcast_to(share[None], (devices,) + share.shape),
@@ -295,10 +308,7 @@
         concat_axis=0,
         tiled=True,
     ).reshape(count * block, 2 * ranks)
-    sums = total(last, seconds, share)
-    arrived = put(arrived, last - 1, came, sums[0])
-    came = hop(last, sums)
-    ranked = after(ranked, *sums)
+    (ranked,) = touch([ranked], sums)
     grad_rank = ranked[:, :ranks]
 
     flat_down = adapter_down.reshape(tenants * ranks, down_slab)
@@ -314,14 +324,24 @@
         axis=0,
     )
     term = (term * ADAPTER_SCALE).astype(jnp.bfloat16).reshape(count, block, down_slab)
-    arrived = put(arrived, last, came, term)
     rank_here = after(ranked, term)
     term = lax.all_to_all(term, "seq", split_axis=0, concat_axis=0, tiled=True)
+
+    mine = jnp.stack([sums[0] for sums in came])
+    theirs = seq_move(jnp.stack([sums[1] for sums in came]), 0, 1)
+    halves = jnp.stack([mine, theirs], axis=1).reshape(count, part, width)
 
     each = count // groups
     bases = []
     for flip in range(groups):
-        sums = lax.dynamic_slice_in_dim(arrived, (group ^ flip) * each, each, 0)
+        wanted = []
+        for at in range(each):
+            owner_at = (group ^ flip) * each + at
+            ahead = (owner_at // CORES - chip) % chips
+            wanted.append(
+                lax.dynamic_slice_in_dim(halves, ahead * CORES + (owner_at % CORES ^ core), 1, 0)
+            )
+        sums = jnp.concatenate(wanted, axis=0)
         bases.append(grp_move(sums, flip) if flip else sums)
 
     grad_down = adapter_grad(rank_here[:, :ranks], mask, hidden_slab, weights)

time: 226 us -> 234 us (1.035); the launches traced: 221 us -> 233 us
  waiting for transfers between devices: 56.8 us -> 92 us
  local copies, waits for them, and re-layouts: 36.2 us -> 22.6 us
  matrix products: 17 us -> 11.9 us
  other arithmetic: 13 us -> 8.32 us
  starting transfers between devices: 70 us -> 67.6 us
    ppermute x19 -> x15, waiting for transfers between devices: 30.9 us -> 50.1 us  [grp_move(): return lax.ppermute(value, 'grp', [(g, g ^ flip) for g in range(groups)])]
    all_to_all x1, waiting for transfers between devices: 0.01 us -> 9.83 us  [shards(): lax.all_to_all(ranked.reshape(devices, -1, 2 * ranks), ('grp', 'seq'), sp...]
    dynamic_update_slice x8 -> x0, local copies, waits for them, and re-layouts: 9.38 us -> none  [put(): lax.dynamic_update_index_in_dim(arrived, came[flip], ahead + (core ^ flip...]
    convert_element_type x16 -> x4, other arithmetic: 10.1 us -> 2.06 us  [add(): sum((term.astype(jnp.float32) for term in terms)).astype(jnp.bfloat16)]
    ppermute x19 -> x15, starting transfers between devices: 29.1 us -> 22.8 us  [grp_move(): return lax.ppermute(value, 'grp', [(g, g ^ flip) for g in range(groups)])]
    all_to_all x1, starting transfers between devices: 3.97 us -> 10 us  [shards(): lax.all_to_all(ranked.reshape(devices, -1, 2 * ranks), ('grp', 'seq'), sp...]
    another operation x0 -> x3, other arithmetic: none -> 5.8 us  [the longest x2 3.46 us: shards(): halves = jnp.stack([mine, theirs], axis=1).reshape(count, part, width)]
    all_to_all x1, waiting for transfers between devices: 0.01 us -> 5.66 us  [shards(): lax.all_to_all(jnp.broadcast_to(share[None], (devices,) + share.shape), (...]
  transfers between devices with their start and end apart: 37 -> 30, of which waited for: 14 -> 14; matrix products, arithmetic and copies ran while one was open for 22% -> 13% of each run, Pallas kernels for 10% -> 12%
where the time goes in v6:
time: 234 us; the launch traced here: 233 us
  waiting for transfers between devices  92 us (39%)
  starting transfers between devices  67.6 us (29%)
  Pallas kernels  29.2 us (12%)
  local copies, waits for them, and re-layouts  22.6 us (10%)
  matrix products  11.9 us (5%)
  other arithmetic  8.32 us (4%)
    ppermute x15, waiting for transfers between devices, grp_move(): return lax.ppermute(value, 'grp', [(g, g ^ flip) for g in range(groups)])  50.1 us
    ppermute x11, starting transfers between devices, seq_move(): return lax.ppermute(value, 'seq', pairs)  22.9 us
    ppermute x15, starting transfers between devices, grp_move(): return lax.ppermute(value, 'grp', [(g, g ^ flip) for g in range(groups)])  22.8 us
    pallas_call x4, Pallas kernels, chunk_product(): pl.pallas_call(functools.partial(chunk_kernel, groups), grid_spec=pltpu.P...  22.5 us
    ppermute x11, waiting for transfers between devices, seq_move(): return lax.ppermute(value, 'seq', pairs)  18.4 us
    unnamed x50, local copies, waits for them, and re-layouts  12.1 us
    all_to_all x1, starting transfers between devices, shards(): lax.all_to_all(ranked.reshape(devices, -1, 2 * ranks), ('grp', 'seq'), sp...  10 us
    all_to_all x1, waiting for transfers between devices, shards(): lax.all_to_all(ranked.reshape(devices, -1, 2 * ranks), ('grp', 'seq'), sp...  9.83 us
  transfers between devices with their start and end apart: 30, of which 14 were waited for; matrix products, arithmetic and copies ran while one was open for 13% of the time, Pallas kernels for 12%

profile of v6, /device:TPU:0, one launch (start us, length us, event | category | flops | bytes accessed | tf_op | source)
XLA Modules:
  0.0 232.9 jit_solution(9250832158754622608)
XLA Ops:
  6.8 4.0 %all-to-all-start = ((bf16[8,128,896]{2,1,0:T(8,128)(2,1)}), bf16[8,128,896]{2,1,0:T(8,128)(2,1)S(1)}, u32[]{:S(2)}, u32[]{:S(2)}) async-start(bf16[8,128,896]{2,1,0:T(8,128)(2,1)} %bitcast.77), calls=%async_computation | async-start | bytes 3670016 | tf_op jit(solution)/shard_map/all_to_all | solution.py:262
  12.4 6.5 %collective-permute-done.2.near_ref = bf16[128,2048]{1,0:T(8,128)(2,1)S(1)} collective-permute-done((bf16[128,2048]{1,0:T(8,128)(2,1)}, bf16[128,2048]{1,0:T(8,128)(2,1)S(1)}, u32[]{:S(2)}, u32[]{:S(2)}) %collective-permute-start.2) | collective-permute-done | bytes 524320 | tf_op jit(solution)/shard_map/ppermute | solution.py:252
  18.9 5.2 %copy-done = bf16[3584,2048]{1,0:T(8,128)(2,1)S(1)} copy-done((bf16[3584,2048]{1,0:T(8,128)(2,1)S(1)}, bf16[3584,2048]{1,0:T(8,128)(2,1)}, u32[]{:S(2)}) %copy-start) | copy-done | bytes 14680088
  24.1 5.4 %shard_map.94 = (bf16[2,32,3584]{2,1,0:T(8,128)(2,1)S(1)}, bf16[2,32,3584]{2,1,0:T(8,128)(2,1)S(1)}, bf16[2,32,3584]{2,1,0:T(8,128)(2,1)S(1)}, bf16[2,32,3584]{2,1,0:T(8,128)(2,1)S(1)}) custom-call(s32[1]{0:T(128)} %bitcast.place_ref, bf16[128,2048]{1,0:T(8,128)(2,1)S(1)} %copy-done.4, bf16[128,2048]{1,0:T(8,128)(2,1)S(1)} %collective-permute-done.far_ref, ...), custom_call_target="tpu_custom_call" | custom-call | flops 3758096384 | bytes 17563648 | tf_op jit(solution)/shard_map/pallas_call | solution.py:56
  33.1 4.4 %collective-permute-start.7 = (bf16[128,2048]{1,0:T(8,128)(2,1)S(1)}, bf16[128,2048]{1,0:T(8,128)(2,1)S(1)}, u32[]{:S(2)}, u32[]{:S(2)}) collective-permute-start(bf16[128,2048]{1,0:T(8,128)(2,1)S(1)} %collective-permute-done.2.near_ref), channel_id=1, source_target_pairs={{0,2},{1,3},{2,4},{3,5},{4,6},{5,7},{6,0},{7,1},{8,10},{9,11},{10,... | collective-permute-start | bytes 1572872 | tf_op jit(solution)/shard_map/ppermute | solution.py:252
  37.6 5.5 %shard_map.95 = (bf16[2,32,3584]{2,1,0:T(8,128)(2,1)S(1)}, bf16[2,32,3584]{2,1,0:T(8,128)(2,1)S(1)}, bf16[2,32,3584]{2,1,0:T(8,128)(2,1)S(1)}, bf16[2,32,3584]{2,1,0:T(8,128)(2,1)S(1)}) custom-call(s32[1]{0:T(128)} %bitcast.place_ref, bf16[128,2048]{1,0:T(8,128)(2,1)S(1)} %collective-permute-done.2.near_ref, ...), custom_call_target="tpu_custom_call" | custom-call | flops 3758096384 | bytes 17563648 | tf_op jit(solution)/shard_map/pallas_call | solution.py:56
  46.2 7.6 %collective-permute-done.4 = bf16[2,32,3584]{2,1,0:T(8,128)(2,1)S(1)} collective-permute-done((bf16[2,32,3584]{2,1,0:T(8,128)(2,1)S(1)}, bf16[2,32,3584]{2,1,0:T(8,128)(2,1)S(1)}, u32[]{:S(2)}, u32[]{:S(2)}) %collective-permute-start.4) | collective-permute-done | bytes 458784 | tf_op jit(solution)/shard_map/ppermute | solution.py:255
  55.3 4.1 %collective-permute-done.7.near_ref = bf16[128,2048]{1,0:T(8,128)(2,1)S(1)} collective-permute-done((bf16[128,2048]{1,0:T(8,128)(2,1)S(1)}, bf16[128,2048]{1,0:T(8,128)(2,1)S(1)}, u32[]{:S(2)}, u32[]{:S(2)}) %collective-permute-start.7) | collective-permute-done | bytes 524320 | tf_op jit(solution)/shard_map/ppermute | solution.py:252
  60.4 8.5 %collective-permute-start.13 = (bf16[128,2048]{1,0:T(8,128)(2,1)S(1)}, bf16[128,2048]{1,0:T(8,128)(2,1)S(1)}, u32[]{:S(2)}, u32[]{:S(2)}) collective-permute-start(bf16[128,2048]{1,0:T(8,128)(2,1)S(1)} %collective-permute-done.7.near_ref), channel_id=1, source_target_pairs={{0,2},{1,3},{2,4},{3,5},{4,6},{5,7},{6,0},{7,1},{8,10},{9,11},{10,... | collective-permute-start | bytes 1572872 | tf_op jit(solution)/shard_map/ppermute | solution.py:252
  69.0 6.1 %shard_map.97 = (bf16[2,32,3584]{2,1,0:T(8,128)(2,1)S(1)}, bf16[2,32,3584]{2,1,0:T(8,128)(2,1)}, bf16[2,32,3584]{2,1,0:T(8,128)(2,1)}, bf16[2,32,3584]{2,1,0:T(8,128)(2,1)}) custom-call(s32[1]{0:T(128)} %bitcast.place_ref, bf16[128,2048]{1,0:T(8,128)(2,1)S(1)} %collective-permute-done.7.near_ref, bf16[128,2048]{1,0:T(8,128)(2,1)S(1)} %collective-permute-done.8.far_ref, ...), custom_call_target="tpu_custom_call" | custom-call | flops 3758096384 | bytes 17563648 | tf_op jit(solution)/shard_map/pallas_call | solution.py:56
  81.0 4.2 %collective-permute-start.11 = (bf16[2,32,3584]{2,1,0:T(8,128)(2,1)S(1)}, bf16[2,32,3584]{2,1,0:T(8,128)(2,1)S(1)}, u32[]{:S(2)}, u32[]{:S(2)}) collective-permute-start(bf16[2,32,3584]{2,1,0:T(8,128)(2,1)S(1)} %add_convert_fusion.2), channel_id=1, source_target_pairs={{0,6},{1,7},{2,0},{3,1},{4,2},{5,3},{6,4},{7,5},{8,14},{9,15},{10,... | collective-permute-start | bytes 1376264 | tf_op jit(solution)/shard_map/ppermute | solution.py:252
  85.3 5.5 %shard_map.99 = (bf16[2,32,3584]{2,1,0:T(8,128)(2,1)S(1)}, bf16[2,32,3584]{2,1,0:T(8,128)(2,1)S(1)}, bf16[2,32,3584]{2,1,0:T(8,128)(2,1)S(1)}, bf16[2,32,3584]{2,1,0:T(8,128)(2,1)S(1)}) custom-call(s32[1]{0:T(128)} %bitcast.place_ref, bf16[128,2048]{1,0:T(8,128)(2,1)S(1)} %collective-permute-done.13.near_ref, ...), custom_call_target="tpu_custom_call" | custom-call | flops 3758096384 | bytes 17563648 | tf_op jit(solution)/shard_map/pallas_call | solution.py:56
  98.9 5.3 %collective-permute-done.18 = bf16[2,32,3584]{2,1,0:T(8,128)(2,1)S(1)} collective-permute-done((bf16[2,32,3584]{2,1,0:T(8,128)(2,1)S(1)}, bf16[2,32,3584]{2,1,0:T(8,128)(2,1)S(1)}, u32[]{:S(2)}, u32[]{:S(2)}) %collective-permute-start.18) | collective-permute-done | bytes 458784 | tf_op jit(solution)/shard_map/ppermute | solution.py:255
  106.7 17.7 %collective-permute-done.19 = bf16[2,32,3584]{2,1,0:T(8,128)(2,1)S(1)} collective-permute-done((bf16[2,32,3584]{2,1,0:T(8,128)(2,1)S(1)}, bf16[2,32,3584]{2,1,0:T(8,128)(2,1)S(1)}, u32[]{:S(2)}, u32[]{:S(2)}) %collective-permute-start.19) | collective-permute-done | bytes 458784 | tf_op jit(solution)/shard_map/ppermute | solution.py:255
  129.7 4.6 %shard_map.100.refs_2_ = bf16[1024,128]{1,0:T(8,128)(2,1)} custom-call(s32[1024,1]{1,0:T(8,128)S(1)} %copy-done.8, bf16[1024,256]{1,0:T(8,128)(2,1)S(1)} %bitcast.73, bf16[1024,896]{1,0:T(8,128)(2,1)S(1)} %bitcast.71, bf16[1024,256]{1,0:T(8,128)(2,1)S(1)} %bitcast.76, bf16[1024,896]{1,0:T(8,128)(2,1)S(1)} %bitcast.75), custom_call_target="tpu_custom_call" | custom-call | flops 2415919104 | bytes 4718592 | tf_op jit(solution)/shard_map/pallas_call | solution.py:183
  141.9 10.0 %all-to-all-start.1 = ((bf16[32,32,128]{2,1,0:T(8,128)(2,1)}), bf16[32,32,128]{2,1,0:T(8,128)(2,1)S(1)}, u32[]{:S(2)}, u32[]{:S(2)}) async-start(bf16[32,32,128]{2,1,0:T(8,128)(2,1)} %bitcast.18), calls=%async_computation.1 | async-start | bytes 524288 | tf_op jit(solution)/shard_map/all_to_all | solution.py:296
  154.1 9.8 %all-to-all-done.1 = bf16[32,32,128]{2,1,0:T(8,128)(2,1)S(1)} async-done(((bf16[32,32,128]{2,1,0:T(8,128)(2,1)}), bf16[32,32,128]{2,1,0:T(8,128)(2,1)S(1)}, u32[]{:S(2)}, u32[]{:S(2)}) %all-to-all-start.1) | async-done | bytes 262176 | tf_op jit(solution)/shard_map/all_to_all | solution.py:296
  164.7 3.9 %all-to-all-start.2 = ((bf16[32,32,128]{2,1,0:T(8,128)(2,1)}), bf16[32,32,128]{2,1,0:T(8,128)(2,1)S(1)}, u32[]{:S(2)}, u32[]{:S(2)}) async-start(bf16[32,32,128]{2,1,0:T(8,128)(2,1)} %broadcast_in_dim.73), calls=%async_computation.2 | async-start | bytes 524288 | tf_op jit(solution)/shard_map/all_to_all | solution.py:304
  173.3 5.7 %all-to-all-done.2 = bf16[32,32,128]{2,1,0:T(8,128)(2,1)S(1)} async-done(((bf16[32,32,128]{2,1,0:T(8,128)(2,1)}), bf16[32,32,128]{2,1,0:T(8,128)(2,1)S(1)}, u32[]{:S(2)}, u32[]{:S(2)}) %all-to-all-start.2) | async-done | bytes 262176 | tf_op jit(solution)/shard_map/all_to_all | solution.py:304
  182.7 3.9 %all-to-all-start.3 = ((bf16[8,128,896]{2,1,0:T(8,128)(2,1)}), bf16[8,128,896]{2,1,0:T(8,128)(2,1)S(1)}, u32[]{:S(2)}, u32[]{:S(2)}) async-start(bf16[8,128,896]{2,1,0:T(8,128)(2,1)} %bitcast.80), calls=%async_computation.3 | async-start | bytes 3670016 | tf_op jit(solution)/shard_map/all_to_all | solution.py:328
  187.0 5.7 %fusion.9 = f32[16,64,896]{2,1,0:T(8,128)} fusion(bf16[1024,896,1]{1,0,2:T(8,128)(2,1)} %bitcast.72, f32[16]{0:T(128)S(1)} %broadcast_divide_fusion, bf16[1024,64]{0,1:T(8,128)(2,1)S(1)} %copy.39, bf16[1024,16]{0,1:T(8,128)(2,1)S(1)} %copy-done.18), kind=kOutput, calls=%fused_computation.10 | convolution fusion | flops 1881014272 | bytes 5668928 | tf_op jit(solution)/shard_map/dot_general | solution.py:19
  201.6 9.6 %collective-permute-done.23.refs_1_ = bf16[2,32,3584]{2,1,0:T(8,128)(2,1)S(1)} collective-permute-done((bf16[2,32,3584]{2,1,0:T(8,128)(2,1)S(1)}, bf16[2,32,3584]{2,1,0:T(8,128)(2,1)S(1)}, u32[]{:S(2)}, u32[]{:S(2)}) %collective-permute-start.23) | collective-permute-done | bytes 458784 | tf_op jit(solution)/shard_map/ppermute | solution.py:255
  211.1 9.9 %collective-permute-done.24.refs_2_ = bf16[2,32,3584]{2,1,0:T(8,128)(2,1)S(1)} collective-permute-done((bf16[2,32,3584]{2,1,0:T(8,128)(2,1)S(1)}, bf16[2,32,3584]{2,1,0:T(8,128)(2,1)S(1)}, u32[]{:S(2)}, u32[]{:S(2)}) %collective-permute-start.24) | collective-permute-done | bytes 458784 | tf_op jit(solution)/shard_map/ppermute | solution.py:255
  221.8 8.0 %all-to-all-done.3.refs_4_ = bf16[8,128,896]{2,1,0:T(8,128)(2,1)S(1)} async-done(((bf16[8,128,896]{2,1,0:T(8,128)(2,1)}), bf16[8,128,896]{2,1,0:T(8,128)(2,1)S(1)}, u32[]{:S(2)}, u32[]{:S(2)}) %all-to-all-start.3) | async-done | bytes 1835040 | tf_op jit(solution)/shard_map/all_to_all | solution.py:328
  (140 shorter events, 70.4 us)
Async XLA Ops:
  0.6 18.3 %collective-permute-start = (bf16[128,2048]{1,0:T(8,128)(2,1)}, bf16[128,2048]{1,0:T(8,128)(2,1)S(1)}, u32[]{:S(2)}, u32[]{:S(2)}) collective-permute-start(bf16[128,2048]{1,0:T(8,128)(2,1)} %near_ref.1), channel_id=1, source_target_pairs={{0,1},{1,0},{2,3},{3,2},{4,5},{5,4},{6,7},{7,6},{8,9},{9,8},{10,11... | collective-permute-start | bytes 1572872 | tf_op jit(solution)/shard_map/ppermute | solution.py:252
  1.1 17.8 %collective-permute-start.2 = (bf16[128,2048]{1,0:T(8,128)(2,1)}, bf16[128,2048]{1,0:T(8,128)(2,1)S(1)}, u32[]{:S(2)}, u32[]{:S(2)}) collective-permute-start(bf16[128,2048]{1,0:T(8,128)(2,1)} %near_ref.1), channel_id=1, source_target_pairs={{0,2},{1,3},{2,4},{3,5},{4,6},{5,7},{6,0},{7,1},{8,10},{9,11},{10,... | collective-permute-start | bytes 1572872 | tf_op jit(solution)/shard_map/ppermute | solution.py:252
  6.8 117.9 %all-to-all-start = ((bf16[8,128,896]{2,1,0:T(8,128)(2,1)}), bf16[8,128,896]{2,1,0:T(8,128)(2,1)S(1)}, u32[]{:S(2)}, u32[]{:S(2)}) async-start(bf16[8,128,896]{2,1,0:T(8,128)(2,1)} %bitcast.77), calls=%async_computation | async-start | bytes 3670016 | tf_op jit(solution)/shard_map/all_to_all | solution.py:262
  18.9 18.6 %collective-permute-start.3 = (bf16[128,2048]{1,0:T(8,128)(2,1)S(1)}, bf16[128,2048]{1,0:T(8,128)(2,1)S(1)}, u32[]{:S(2)}, u32[]{:S(2)}) collective-permute-start(bf16[128,2048]{1,0:T(8,128)(2,1)S(1)} %collective-permute-done.2.near_ref), channel_id=1, source_target_pairs={{0,1},{1,0},{2,3},{3,2},{4,5},{5,4},{6,7},{7,6},{8,9},{9,8},{10,11... | collective-permute-start | bytes 1572872 | tf_op jit(solution)/shard_map/ppermute | solution.py:252
  29.5 15.1 %collective-permute-start.1 = (bf16[2,32,3584]{2,1,0:T(8,128)(2,1)S(1)}, bf16[2,32,3584]{2,1,0:T(8,128)(2,1)S(1)}, u32[]{:S(2)}, u32[]{:S(2)}) collective-permute-start(bf16[2,32,3584]{2,1,0:T(8,128)(2,1)S(1)} %get-tuple-element.21), channel_id=1, source_target_pairs={{0,8},{8,0},{16,24},{24,16},{1,9},{9,1},{17,25},{25,17},{2,10},{10... | collective-permute-start | bytes 1376264 | tf_op jit(solution)/shard_map/ppermute | solution.py:255
  31.2 22.5 %collective-permute-start.4 = (bf16[2,32,3584]{2,1,0:T(8,128)(2,1)S(1)}, bf16[2,32,3584]{2,1,0:T(8,128)(2,1)S(1)}, u32[]{:S(2)}, u32[]{:S(2)}) collective-permute-start(bf16[2,32,3584]{2,1,0:T(8,128)(2,1)S(1)} %get-tuple-element.23), channel_id=1, source_target_pairs={{0,16},{8,24},{16,0},{24,8},{1,17},{9,25},{17,1},{25,9},{2,18},{10... | collective-permute-start | bytes 1376264 | tf_op jit(solution)/shard_map/ppermute | solution.py:255
  32.8 26.7 %collective-permute-start.5 = (bf16[2,32,3584]{2,1,0:T(8,128)(2,1)S(1)}, bf16[2,32,3584]{2,1,0:T(8,128)(2,1)S(1)}, u32[]{:S(2)}, u32[]{:S(2)}) collective-permute-start(bf16[2,32,3584]{2,1,0:T(8,128)(2,1)S(1)} %get-tuple-element.24), channel_id=1, source_target_pairs={{0,24},{8,16},{16,8},{24,0},{1,25},{9,17},{17,9},{25,1},{2,26},{10... | collective-permute-start | bytes 1376264 | tf_op jit(solution)/shard_map/ppermute | solution.py:255
  33.1 26.3 %collective-permute-start.7 = (bf16[128,2048]{1,0:T(8,128)(2,1)S(1)}, bf16[128,2048]{1,0:T(8,128)(2,1)S(1)}, u32[]{:S(2)}, u32[]{:S(2)}) collective-permute-start(bf16[128,2048]{1,0:T(8,128)(2,1)S(1)} %collective-permute-done.2.near_ref), channel_id=1, source_target_pairs={{0,2},{1,3},{2,4},{3,5},{4,6},{5,7},{6,0},{7,1},{8,10},{9,11},{10,... | collective-permute-start | bytes 1572872 | tf_op jit(solution)/shard_map/ppermute | solution.py:252
  43.1 33.5 %collective-permute-start.6 = (bf16[2,32,3584]{2,1,0:T(8,128)(2,1)S(1)}, bf16[2,32,3584]{2,1,0:T(8,128)(2,1)S(1)}, u32[]{:S(2)}, u32[]{:S(2)}) collective-permute-start(bf16[2,32,3584]{2,1,0:T(8,128)(2,1)S(1)} %get-tuple-element.25), channel_id=1, source_target_pairs={{0,8},{8,0},{16,24},{24,16},{1,9},{9,1},{17,25},{25,17},{2,10},{10... | collective-permute-start | bytes 1376264 | tf_op jit(solution)/shard_map/ppermute | solution.py:255
  44.6 36.2 %collective-permute-start.9 = (bf16[2,32,3584]{2,1,0:T(8,128)(2,1)S(1)}, bf16[2,32,3584]{2,1,0:T(8,128)(2,1)S(1)}, u32[]{:S(2)}, u32[]{:S(2)}) collective-permute-start(bf16[2,32,3584]{2,1,0:T(8,128)(2,1)S(1)} %get-tuple-element.27), channel_id=1, source_target_pairs={{0,16},{8,24},{16,0},{24,8},{1,17},{9,25},{17,1},{25,9},{2,18},{10... | collective-permute-start | bytes 1376264 | tf_op jit(solution)/shard_map/ppermute | solution.py:255
  53.7 27.1 %collective-permute-start.10 = (bf16[2,32,3584]{2,1,0:T(8,128)(2,1)S(1)}, bf16[2,32,3584]{2,1,0:T(8,128)(2,1)S(1)}, u32[]{:S(2)}, u32[]{:S(2)}) collective-permute-start(bf16[2,32,3584]{2,1,0:T(8,128)(2,1)S(1)} %get-tuple-element.28), channel_id=1, source_target_pairs={{0,24},{8,16},{16,8},{24,0},{1,25},{9,17},{17,9},{25,1},{2,26},{10... | collective-permute-start | bytes 1376264 | tf_op jit(solution)/shard_map/ppermute | solution.py:255
  60.4 20.4 %collective-permute-start.13 = (bf16[128,2048]{1,0:T(8,128)(2,1)S(1)}, bf16[128,2048]{1,0:T(8,128)(2,1)S(1)}, u32[]{:S(2)}, u32[]{:S(2)}) collective-permute-start(bf16[128,2048]{1,0:T(8,128)(2,1)S(1)} %collective-permute-done.7.near_ref), channel_id=1, source_target_pairs={{0,2},{1,3},{2,4},{3,5},{4,6},{5,7},{6,0},{7,1},{8,10},{9,11},{10,... | collective-permute-start | bytes 1572872 | tf_op jit(solution)/shard_map/ppermute | solution.py:252
  75.1 59.2 %collective-permute-start.12 = (bf16[2,32,3584]{2,1,0:T(8,128)(2,1)}, bf16[2,32,3584]{2,1,0:T(8,128)(2,1)S(1)}, u32[]{:S(2)}, u32[]{:S(2)}) collective-permute-start(bf16[2,32,3584]{2,1,0:T(8,128)(2,1)} %get-tuple-element.29), channel_id=1, source_target_pairs={{0,8},{8,0},{16,24},{24,16},{1,9},{9,1},{17,25},{25,17},{2,10},{10... | collective-permute-start | bytes 1376264 | tf_op jit(solution)/shard_map/ppermute | solution.py:255
  76.6 57.8 %collective-permute-start.15 = (bf16[2,32,3584]{2,1,0:T(8,128)(2,1)}, bf16[2,32,3584]{2,1,0:T(8,128)(2,1)}, u32[]{:S(2)}, u32[]{:S(2)}) collective-permute-start(bf16[2,32,3584]{2,1,0:T(8,128)(2,1)} %get-tuple-element.31), channel_id=1, source_target_pairs={{0,16},{8,24},{16,0},{24,8},{1,17},{9,25},{17,1},{25,9},{2,18},{10... | collective-permute-start | bytes 1376264 | tf_op jit(solution)/shard_map/ppermute | solution.py:255
  92.4 32.0 %collective-permute-start.19 = (bf16[2,32,3584]{2,1,0:T(8,128)(2,1)S(1)}, bf16[2,32,3584]{2,1,0:T(8,128)(2,1)S(1)}, u32[]{:S(2)}, u32[]{:S(2)}) collective-permute-start(bf16[2,32,3584]{2,1,0:T(8,128)(2,1)S(1)} %get-tuple-element.34), channel_id=1, source_target_pairs={{0,16},{8,24},{16,0},{24,8},{1,17},{9,25},{17,1},{25,9},{2,18},{10... | collective-permute-start | bytes 1376264 | tf_op jit(solution)/shard_map/ppermute | solution.py:255
  95.7 28.7 %collective-permute-start.20 = (bf16[2,32,3584]{2,1,0:T(8,128)(2,1)S(1)}, bf16[2,32,3584]{2,1,0:T(8,128)(2,1)S(1)}, u32[]{:S(2)}, u32[]{:S(2)}) collective-permute-start(bf16[2,32,3584]{2,1,0:T(8,128)(2,1)S(1)} %get-tuple-element.35), channel_id=1, source_target_pairs={{0,24},{8,16},{16,8},{24,0},{1,25},{9,17},{17,9},{25,1},{2,26},{10... | collective-permute-start | bytes 1376264 | tf_op jit(solution)/shard_map/ppermute | solution.py:255
  104.2 30.1 %collective-permute-start.16 = (bf16[2,32,3584]{2,1,0:T(8,128)(2,1)}, bf16[2,32,3584]{2,1,0:T(8,128)(2,1)}, u32[]{:S(2)}, u32[]{:S(2)}) collective-permute-start(bf16[2,32,3584]{2,1,0:T(8,128)(2,1)} %get-tuple-element.32), channel_id=1, source_target_pairs={{0,24},{8,16},{16,8},{24,0},{1,25},{9,17},{17,9},{25,1},{2,26},{10... | collective-permute-start | bytes 1376264 | tf_op jit(solution)/shard_map/ppermute | solution.py:255
  124.6 15.4 %collective-permute-start.21 = (bf16[2,32,3584]{2,1,0:T(8,128)(2,1)S(1)}, bf16[2,32,3584]{2,1,0:T(8,128)(2,1)}, u32[]{:S(2)}, u32[]{:S(2)}) collective-permute-start(bf16[2,32,3584]{2,1,0:T(8,128)(2,1)S(1)} %add_convert_fusion.refs_1_), channel_id=1, source_target_pairs={{0,2},{1,3},{2,4},{3,5},{4,6},{5,7},{6,0},{7,1},{8,10},{9,11},{10,... | collective-permute-start | bytes 1376264 | tf_op jit(solution)/shard_map/ppermute | solution.py:252
  135.8 17.5 %collective-permute-start.17 = (bf16[2,32,3584]{2,1,0:T(8,128)(2,1)S(1)}, bf16[2,32,3584]{2,1,0:T(8,128)(2,1)S(1)}, u32[]{:S(2)}, u32[]{:S(2)}) collective-permute-start(bf16[2,32,3584]{2,1,0:T(8,128)(2,1)S(1)} %add_convert_fusion.1), channel_id=1, source_target_pairs={{0,4},{1,5},{2,6},{3,7},{4,0},{5,1},{6,2},{7,3},{8,12},{9,13},{10,... | collective-permute-start | bytes 1376264 | tf_op jit(solution)/shard_map/ppermute | solution.py:252
  141.9 22.0 %all-to-all-start.1 = ((bf16[32,32,128]{2,1,0:T(8,128)(2,1)}), bf16[32,32,128]{2,1,0:T(8,128)(2,1)S(1)}, u32[]{:S(2)}, u32[]{:S(2)}) async-start(bf16[32,32,128]{2,1,0:T(8,128)(2,1)} %bitcast.18), calls=%async_computation.1 | async-start | bytes 524288 | tf_op jit(solution)/shard_map/all_to_all | solution.py:296
  170.9 25.1 %collective-permute-start.22 = (bf16[4,32,3584]{2,1,0:T(8,128)(2,1)}, bf16[4,32,3584]{2,1,0:T(8,128)(2,1)}, u32[]{:S(2)}, u32[]{:S(2)}) collective-permute-start(bf16[4,32,3584]{2,1,0:T(8,128)(2,1)} %pad_maximum_fusion.1), channel_id=1, source_target_pairs={{0,1},{1,0},{2,3},{3,2},{4,5},{5,4},{6,7},{7,6},{8,9},{9,8},{10,11... | collective-permute-start | bytes 2752520 | tf_op jit(solution)/shard_map/ppermute | solution.py:252
  182.7 47.1 %all-to-all-start.3 = ((bf16[8,128,896]{2,1,0:T(8,128)(2,1)}), bf16[8,128,896]{2,1,0:T(8,128)(2,1)S(1)}, u32[]{:S(2)}, u32[]{:S(2)}) async-start(bf16[8,128,896]{2,1,0:T(8,128)(2,1)} %bitcast.80), calls=%async_computation.3 | async-start | bytes 3670016 | tf_op jit(solution)/shard_map/all_to_all | solution.py:328
  198.3 22.7 %collective-permute-start.24 = (bf16[2,32,3584]{2,1,0:T(8,128)(2,1)S(1)}, bf16[2,32,3584]{2,1,0:T(8,128)(2,1)S(1)}, u32[]{:S(2)}, u32[]{:S(2)}) collective-permute-start(bf16[2,32,3584]{2,1,0:T(8,128)(2,1)S(1)} %pad_maximum_fusion.4), channel_id=1, source_target_pairs={{0,16},{8,24},{16,0},{24,8},{1,17},{9,25},{17,1},{25,9},{2,18},{10... | collective-permute-start | bytes 1376264 | tf_op jit(solution)/shard_map/ppermute | solution.py:255
  199.3 21.7 %collective-permute-start.25 = (bf16[2,32,3584]{2,1,0:T(8,128)(2,1)S(1)}, bf16[2,32,3584]{2,1,0:T(8,128)(2,1)S(1)}, u32[]{:S(2)}, u32[]{:S(2)}) collective-permute-start(bf16[2,32,3584]{2,1,0:T(8,128)(2,1)S(1)} %pad_maximum_fusion.5), channel_id=1, source_target_pairs={{0,24},{8,16},{16,8},{24,0},{1,25},{9,17},{17,9},{25,1},{2,26},{10... | collective-permute-start | bytes 1376264 | tf_op jit(solution)/shard_map/ppermute | solution.py:255
  (31 other events, 542.4 us)

commit v7 on v6

--- a/solution.py
+++ b/solution.py
@@ -278,15 +278,14 @@
     ranked = project_both(grad_slab, hidden_slab, adapter_up, adapter_down, owner, mask)
 
     products = [
-        chunk_product(near, far, down_weight, group, groups) for near, far in pairs
+        chunk_product(near, far, down_weight, group, groups, *([ranked] if step == last else []))
+        for step, (near, far) in enumerate(pairs)
     ]
     came = []
     for step in range(chips):
         kept = products[step][0]
         others = [grp_move(products[step][flip], flip) for flip in range(1, groups)]
         gates = [products[step + 1][0]] if step < last else []
-        if step == last - 1:
-            gates.append(ranked)
         if gates:
             (others[0],) = touch([others[0]], *gates)
         sums = add(kept, *others)

time: 234 us -> 228 us (0.974)
  waiting for transfers between devices: 92 us -> 83.2 us
  local copies, waits for them, and re-layouts: 22.6 us -> 28.4 us
  other arithmetic: 8.32 us -> 5.05 us
    all_to_all x1, waiting for transfers between devices: 9.83 us -> 0.01 us  [shards(): lax.all_to_all(ranked.reshape(devices, -1, 2 * ranks), ('grp', 'seq'), sp...]
    all_to_all x1, starting transfers between devices: 3.89 us -> 12.8 us  [shards(): lax.all_to_all(jnp.broadcast_to(share[None], (devices,) + share.shape), (...]
    unnamed x50 -> x40, local copies, waits for them, and re-layouts: 12.1 us -> 19.8 us
    ppermute x15, waiting for transfers between devices: 50.1 us -> 43.3 us  [grp_move(): return lax.ppermute(value, 'grp', [(g, g ^ flip) for g in range(groups)])]
    ppermute x11, waiting for transfers between devices: 18.4 us -> 23.7 us  [seq_move(): return lax.ppermute(value, 'seq', pairs)]
    ppermute x15, starting transfers between devices: 22.8 us -> 19 us  [grp_move(): return lax.ppermute(value, 'grp', [(g, g ^ flip) for g in range(groups)])]
    all_to_all x1, starting transfers between devices: 10 us -> 6.36 us  [shards(): lax.all_to_all(ranked.reshape(devices, -1, 2 * ranks), ('grp', 'seq'), sp...]
    all_to_all x1, waiting for transfers between devices: 5.66 us -> 8.88 us  [shards(): lax.all_to_all(jnp.broadcast_to(share[None], (devices,) + share.shape), (...]
  transfers between devices with their start and end apart: 30 -> 30, of which waited for: 14 -> 12; matrix products, arithmetic and copies ran while one was open for 13% -> 12% of each run, Pallas kernels for 12% -> 12%
where the time goes in v7:
time: 228 us; the launch traced here: 227 us
  waiting for transfers between devices  83.2 us (36%)
  starting transfers between devices  66.6 us (29%)
  Pallas kernels  29.1 us (13%)
  local copies, waits for them, and re-layouts  28.4 us (12%)
  matrix products  13.5 us (6%)
  other arithmetic  5.05 us (2%)
    ppermute x15, waiting for transfers between devices, grp_move(): return lax.ppermute(value, 'grp', [(g, g ^ flip) for g in range(groups)])  43.3 us
    ppermute x11, waiting for transfers between devices, seq_move(): return lax.ppermute(value, 'seq', pairs)  23.7 us
    pallas_call x4, Pallas kernels, chunk_product(): pl.pallas_call(functools.partial(chunk_kernel, groups), grid_spec=pltpu.P...  22.4 us
    ppermute x11, starting transfers between devices, seq_move(): return lax.ppermute(value, 'seq', pairs)  20.7 us
    unnamed x40, local copies, waits for them, and re-layouts  19.8 us
    ppermute x15, starting transfers between devices, grp_move(): return lax.ppermute(value, 'grp', [(g, g ^ flip) for g in range(groups)])  19 us
    all_to_all x1, starting transfers between devices, shards(): lax.all_to_all(jnp.broadcast_to(share[None], (devices,) + share.shape), (...  12.8 us
    all_to_all x1, waiting for transfers between devices, shards(): lax.all_to_all(jnp.broadcast_to(share[None], (devices,) + share.shape), (...  8.88 us
  transfers between devices with their start and end apart: 30, of which 12 were waited for; matrix products, arithmetic and copies ran while one was open for 12% of the time, Pallas kernels for 12%

profile of v7, /device:TPU:0, one launch (start us, length us, event | category | flops | bytes accessed | tf_op | source)
XLA Modules:
  0.0 227.2 jit_solution(8145371096337875402)
XLA Ops:
  6.8 4.0 %all-to-all-start = ((bf16[8,128,896]{2,1,0:T(8,128)(2,1)}), bf16[8,128,896]{2,1,0:T(8,128)(2,1)S(1)}, u32[]{:S(2)}, u32[]{:S(2)}) async-start(bf16[8,128,896]{2,1,0:T(8,128)(2,1)} %bitcast.75), calls=%async_computation | async-start | bytes 3670016 | tf_op jit(solution)/shard_map/all_to_all | solution.py:262
  12.4 6.5 %collective-permute-done.2.near_ref = bf16[128,2048]{1,0:T(8,128)(2,1)S(1)} collective-permute-done((bf16[128,2048]{1,0:T(8,128)(2,1)}, bf16[128,2048]{1,0:T(8,128)(2,1)S(1)}, u32[]{:S(2)}, u32[]{:S(2)}) %collective-permute-start.2) | collective-permute-done | bytes 524320 | tf_op jit(solution)/shard_map/ppermute | solution.py:252
  18.9 5.2 %copy-done = bf16[3584,2048]{1,0:T(8,128)(2,1)S(1)} copy-done((bf16[3584,2048]{1,0:T(8,128)(2,1)S(1)}, bf16[3584,2048]{1,0:T(8,128)(2,1)}, u32[]{:S(2)}) %copy-start) | copy-done | bytes 14680088
  24.1 5.4 %shard_map.94 = (bf16[2,32,3584]{2,1,0:T(8,128)(2,1)S(1)}, bf16[2,32,3584]{2,1,0:T(8,128)(2,1)S(1)}, bf16[2,32,3584]{2,1,0:T(8,128)(2,1)S(1)}, bf16[2,32,3584]{2,1,0:T(8,128)(2,1)S(1)}) custom-call(s32[1]{0:T(128)} %bitcast.place_ref, bf16[128,2048]{1,0:T(8,128)(2,1)S(1)} %copy-done.3, bf16[128,2048]{1,0:T(8,128)(2,1)S(1)} %collective-permute-done.far_ref, ...), custom_call_target="tpu_custom_call" | custom-call | flops 3758096384 | bytes 17563648 | tf_op jit(solution)/shard_map/pallas_call | solution.py:56
  33.1 4.4 %collective-permute-start.7 = (bf16[128,2048]{1,0:T(8,128)(2,1)S(1)}, bf16[128,2048]{1,0:T(8,128)(2,1)S(1)}, u32[]{:S(2)}, u32[]{:S(2)}) collective-permute-start(bf16[128,2048]{1,0:T(8,128)(2,1)S(1)} %collective-permute-done.2.near_ref), channel_id=1, source_target_pairs={{0,2},{1,3},{2,4},{3,5},{4,6},{5,7},{6,0},{7,1},{8,10},{9,11},{10,... | collective-permute-start | bytes 1572872 | tf_op jit(solution)/shard_map/ppermute | solution.py:252
  37.6 5.5 %shard_map.95 = (bf16[2,32,3584]{2,1,0:T(8,128)(2,1)S(1)}, bf16[2,32,3584]{2,1,0:T(8,128)(2,1)S(1)}, bf16[2,32,3584]{2,1,0:T(8,128)(2,1)S(1)}, bf16[2,32,3584]{2,1,0:T(8,128)(2,1)S(1)}) custom-call(s32[1]{0:T(128)} %bitcast.place_ref, bf16[128,2048]{1,0:T(8,128)(2,1)S(1)} %collective-permute-done.2.near_ref, ...), custom_call_target="tpu_custom_call" | custom-call | flops 3758096384 | bytes 17563648 | tf_op jit(solution)/shard_map/pallas_call | solution.py:56
  46.1 7.6 %collective-permute-done.4 = bf16[2,32,3584]{2,1,0:T(8,128)(2,1)S(1)} collective-permute-done((bf16[2,32,3584]{2,1,0:T(8,128)(2,1)S(1)}, bf16[2,32,3584]{2,1,0:T(8,128)(2,1)S(1)}, u32[]{:S(2)}, u32[]{:S(2)}) %collective-permute-start.4) | collective-permute-done | bytes 458784 | tf_op jit(solution)/shard_map/ppermute | solution.py:255
  55.3 4.1 %collective-permute-done.7.near_ref = bf16[128,2048]{1,0:T(8,128)(2,1)S(1)} collective-permute-done((bf16[128,2048]{1,0:T(8,128)(2,1)S(1)}, bf16[128,2048]{1,0:T(8,128)(2,1)S(1)}, u32[]{:S(2)}, u32[]{:S(2)}) %collective-permute-start.7) | collective-permute-done | bytes 524320 | tf_op jit(solution)/shard_map/ppermute | solution.py:252
  59.4 8.5 %collective-permute-start.13 = (bf16[128,2048]{1,0:T(8,128)(2,1)S(1)}, bf16[128,2048]{1,0:T(8,128)(2,1)S(1)}, u32[]{:S(2)}, u32[]{:S(2)}) collective-permute-start(bf16[128,2048]{1,0:T(8,128)(2,1)S(1)} %collective-permute-done.7.near_ref), channel_id=1, source_target_pairs={{0,2},{1,3},{2,4},{3,5},{4,6},{5,7},{6,0},{7,1},{8,10},{9,11},{10,... | collective-permute-start | bytes 1572872 | tf_op jit(solution)/shard_map/ppermute | solution.py:252
  69.9 6.1 %shard_map.97 = (bf16[2,32,3584]{2,1,0:T(8,128)(2,1)S(1)}, bf16[2,32,3584]{2,1,0:T(8,128)(2,1)}, bf16[2,32,3584]{2,1,0:T(8,128)(2,1)}, bf16[2,32,3584]{2,1,0:T(8,128)(2,1)}) custom-call(s32[1]{0:T(128)} %bitcast.place_ref, bf16[128,2048]{1,0:T(8,128)(2,1)S(1)} %collective-permute-done.7.near_ref, bf16[128,2048]{1,0:T(8,128)(2,1)S(1)} %collective-permute-done.8.far_ref, ...), custom_call_target="tpu_custom_call" | custom-call | flops 3758096384 | bytes 17563648 | tf_op jit(solution)/shard_map/pallas_call | solution.py:56
  80.7 9.5 %collective-permute-done.11 = bf16[2,32,3584]{2,1,0:T(8,128)(2,1)S(1)} collective-permute-done((bf16[2,32,3584]{2,1,0:T(8,128)(2,1)S(1)}, bf16[2,32,3584]{2,1,0:T(8,128)(2,1)S(1)}, u32[]{:S(2)}, u32[]{:S(2)}) %collective-permute-start.11) | collective-permute-done | bytes 458784 | tf_op jit(solution)/shard_map/ppermute | solution.py:252
  97.6 4.6 %shard_map.99.rest_0_ = bf16[1024,128]{1,0:T(8,128)(2,1)} custom-call(s32[1024,1]{1,0:T(8,128)S(1)} %copy-done.9, bf16[1024,256]{1,0:T(8,128)(2,1)S(1)} %bitcast.71, bf16[1024,896]{1,0:T(8,128)(2,1)S(1)} %bitcast.69, bf16[1024,256]{1,0:T(8,128)(2,1)S(1)} %bitcast.74, bf16[1024,896]{1,0:T(8,128)(2,1)S(1)} %bitcast.73), custom_call_target="tpu_custom_call" | custom-call | flops 2415919104 | bytes 4718592 | tf_op jit(solution)/shard_map/pallas_call | solution.py:183
  102.2 6.4 %all-to-all-start.1 = ((bf16[32,32,128]{2,1,0:T(8,128)(2,1)}), bf16[32,32,128]{2,1,0:T(8,128)(2,1)S(1)}, u32[]{:S(2)}, u32[]{:S(2)}) async-start(bf16[32,32,128]{2,1,0:T(8,128)(2,1)} %bitcast.18), calls=%async_computation.1 | async-start | bytes 524288 | tf_op jit(solution)/shard_map/all_to_all | solution.py:295
  108.6 5.2 %copy-done.1 = bf16[3584,2048]{1,0:T(8,128)(2,1)S(1)} copy-done((bf16[3584,2048]{1,0:T(8,128)(2,1)S(1)}, bf16[3584,2048]{1,0:T(8,128)(2,1)}, u32[]{:S(2)}) %copy-start.1) | copy-done | bytes 14680088
  114.8 5.4 %shard_map.100 = (bf16[2,32,3584]{2,1,0:T(8,128)(2,1)S(1)}, bf16[2,32,3584]{2,1,0:T(8,128)(2,1)S(1)}, bf16[2,32,3584]{2,1,0:T(8,128)(2,1)S(1)}, bf16[2,32,3584]{2,1,0:T(8,128)(2,1)S(1)}) custom-call(s32[1]{0:T(128)} %bitcast.place_ref, bf16[128,2048]{1,0:T(8,128)(2,1)S(1)} %collective-permute-done.13.near_ref, bf16[128,2048]{1,0:T(8,128)(2,1)S(1)} %copy-done.5, ...), custom_call_target="tpu_custom_call" | custom-call | flops 3758096384 | bytes 17563648 | tf_op jit(solution)/shard_map/pallas_call | solution.py:56
  128.0 5.7 %collective-permute-done.18 = bf16[2,32,3584]{2,1,0:T(8,128)(2,1)S(1)} collective-permute-done((bf16[2,32,3584]{2,1,0:T(8,128)(2,1)S(1)}, bf16[2,32,3584]{2,1,0:T(8,128)(2,1)S(1)}, u32[]{:S(2)}, u32[]{:S(2)}) %collective-permute-start.18) | collective-permute-done | bytes 458784 | tf_op jit(solution)/shard_map/ppermute | solution.py:255
  133.7 10.5 %collective-permute-done.19 = bf16[2,32,3584]{2,1,0:T(8,128)(2,1)S(1)} collective-permute-done((bf16[2,32,3584]{2,1,0:T(8,128)(2,1)S(1)}, bf16[2,32,3584]{2,1,0:T(8,128)(2,1)S(1)}, u32[]{:S(2)}, u32[]{:S(2)}) %collective-permute-start.19) | collective-permute-done | bytes 458784 | tf_op jit(solution)/shard_map/ppermute | solution.py:255
  148.7 12.8 %all-to-all-start.2 = ((bf16[32,32,128]{2,1,0:T(8,128)(2,1)}), bf16[32,32,128]{2,1,0:T(8,128)(2,1)S(1)}, u32[]{:S(2)}, u32[]{:S(2)}) async-start(bf16[32,32,128]{2,1,0:T(8,128)(2,1)} %broadcast_in_dim.73), calls=%async_computation.2 | async-start | bytes 524288 | tf_op jit(solution)/shard_map/all_to_all | solution.py:303
  163.0 8.9 %all-to-all-done.2 = bf16[32,32,128]{2,1,0:T(8,128)(2,1)S(1)} async-done(((bf16[32,32,128]{2,1,0:T(8,128)(2,1)}), bf16[32,32,128]{2,1,0:T(8,128)(2,1)S(1)}, u32[]{:S(2)}, u32[]{:S(2)}) %all-to-all-start.2) | async-done | bytes 262176 | tf_op jit(solution)/shard_map/all_to_all | solution.py:303
  172.0 5.1 %fusion = bf16[1024,896]{1,0:T(8,128)(2,1)} fusion(bf16[16,64,896]{2,1,0:T(8,128)(2,1)} %param.10, bf16[1024,16]{0,1:T(8,128)(2,1)S(1)} %convert_convert_fusion, bf16[1024,64]{0,1:T(8,128)(2,1)S(1)} %copy.38), kind=kOutput, calls=%fused_computation.1 | convolution fusion | flops 1881931776 | bytes 3833856 | tf_op jit(solution)/shard_map/dot_general | solution.py:316
  181.8 5.8 %fusion.9 = f32[16,64,896]{2,1,0:T(8,128)} fusion(bf16[1024,896,1]{1,0,2:T(8,128)(2,1)} %bitcast.70, f32[16]{0:T(128)S(1)} %broadcast_divide_fusion, bf16[1024,64]{0,1:T(8,128)(2,1)} %copy.39, bf16[1024,16]{0,1:T(8,128)(2,1)} %copy-done.17), kind=kOutput, calls=%fused_computation.10 | convolution fusion | flops 1881014272 | bytes 5668928 | tf_op jit(solution)/shard_map/dot_general | solution.py:19
  196.5 9.6 %collective-permute-done.23.refs_1_ = bf16[2,32,3584]{2,1,0:T(8,128)(2,1)S(1)} collective-permute-done((bf16[2,32,3584]{2,1,0:T(8,128)(2,1)S(1)}, bf16[2,32,3584]{2,1,0:T(8,128)(2,1)S(1)}, u32[]{:S(2)}, u32[]{:S(2)}) %collective-permute-start.23) | collective-permute-done | bytes 458784 | tf_op jit(solution)/shard_map/ppermute | solution.py:255
  206.1 9.9 %collective-permute-done.24.refs_2_ = bf16[2,32,3584]{2,1,0:T(8,128)(2,1)S(1)} collective-permute-done((bf16[2,32,3584]{2,1,0:T(8,128)(2,1)S(1)}, bf16[2,32,3584]{2,1,0:T(8,128)(2,1)S(1)}, u32[]{:S(2)}, u32[]{:S(2)}) %collective-permute-start.24) | collective-permute-done | bytes 458784 | tf_op jit(solution)/shard_map/ppermute | solution.py:255
  216.8 7.3 %all-to-all-done.3.refs_4_ = bf16[8,128,896]{2,1,0:T(8,128)(2,1)S(1)} async-done(((bf16[8,128,896]{2,1,0:T(8,128)(2,1)}), bf16[8,128,896]{2,1,0:T(8,128)(2,1)S(1)}, u32[]{:S(2)}, u32[]{:S(2)}) %all-to-all-start.3) | async-done | bytes 1835040 | tf_op jit(solution)/shard_map/all_to_all | solution.py:327
  (129 shorter events, 61.9 us)
Async XLA Ops:
  0.6 18.3 %collective-permute-start = (bf16[128,2048]{1,0:T(8,128)(2,1)}, bf16[128,2048]{1,0:T(8,128)(2,1)S(1)}, u32[]{:S(2)}, u32[]{:S(2)}) collective-permute-start(bf16[128,2048]{1,0:T(8,128)(2,1)} %near_ref.1), channel_id=1, source_target_pairs={{0,1},{1,0},{2,3},{3,2},{4,5},{5,4},{6,7},{7,6},{8,9},{9,8},{10,11... | collective-permute-start | bytes 1572872 | tf_op jit(solution)/shard_map/ppermute | solution.py:252
  1.1 17.8 %collective-permute-start.2 = (bf16[128,2048]{1,0:T(8,128)(2,1)}, bf16[128,2048]{1,0:T(8,128)(2,1)S(1)}, u32[]{:S(2)}, u32[]{:S(2)}) collective-permute-start(bf16[128,2048]{1,0:T(8,128)(2,1)} %near_ref.1), channel_id=1, source_target_pairs={{0,2},{1,3},{2,4},{3,5},{4,6},{5,7},{6,0},{7,1},{8,10},{9,11},{10,... | collective-permute-start | bytes 1572872 | tf_op jit(solution)/shard_map/ppermute | solution.py:252
  6.8 85.9 %all-to-all-start = ((bf16[8,128,896]{2,1,0:T(8,128)(2,1)}), bf16[8,128,896]{2,1,0:T(8,128)(2,1)S(1)}, u32[]{:S(2)}, u32[]{:S(2)}) async-start(bf16[8,128,896]{2,1,0:T(8,128)(2,1)} %bitcast.75), calls=%async_computation | async-start | bytes 3670016 | tf_op jit(solution)/shard_map/all_to_all | solution.py:262
  18.9 18.6 %collective-permute-start.3 = (bf16[128,2048]{1,0:T(8,128)(2,1)S(1)}, bf16[128,2048]{1,0:T(8,128)(2,1)S(1)}, u32[]{:S(2)}, u32[]{:S(2)}) collective-permute-start(bf16[128,2048]{1,0:T(8,128)(2,1)S(1)} %collective-permute-done.2.near_ref), channel_id=1, source_target_pairs={{0,1},{1,0},{2,3},{3,2},{4,5},{5,4},{6,7},{7,6},{8,9},{9,8},{10,11... | collective-permute-start | bytes 1572872 | tf_op jit(solution)/shard_map/ppermute | solution.py:252
  31.2 22.5 %collective-permute-start.4 = (bf16[2,32,3584]{2,1,0:T(8,128)(2,1)S(1)}, bf16[2,32,3584]{2,1,0:T(8,128)(2,1)S(1)}, u32[]{:S(2)}, u32[]{:S(2)}) collective-permute-start(bf16[2,32,3584]{2,1,0:T(8,128)(2,1)S(1)} %get-tuple-element.23), channel_id=1, source_target_pairs={{0,16},{8,24},{16,0},{24,8},{1,17},{9,25},{17,1},{25,9},{2,18},{10... | collective-permute-start | bytes 1376264 | tf_op jit(solution)/shard_map/ppermute | solution.py:255
  32.8 35.2 %collective-permute-start.5 = (bf16[2,32,3584]{2,1,0:T(8,128)(2,1)S(1)}, bf16[2,32,3584]{2,1,0:T(8,128)(2,1)S(1)}, u32[]{:S(2)}, u32[]{:S(2)}) collective-permute-start(bf16[2,32,3584]{2,1,0:T(8,128)(2,1)S(1)} %get-tuple-element.24), channel_id=1, source_target_pairs={{0,24},{8,16},{16,8},{24,0},{1,25},{9,17},{17,9},{25,1},{2,26},{10... | collective-permute-start | bytes 1376264 | tf_op jit(solution)/shard_map/ppermute | solution.py:255
  33.1 26.3 %collective-permute-start.7 = (bf16[128,2048]{1,0:T(8,128)(2,1)S(1)}, bf16[128,2048]{1,0:T(8,128)(2,1)S(1)}, u32[]{:S(2)}, u32[]{:S(2)}) collective-permute-start(bf16[128,2048]{1,0:T(8,128)(2,1)S(1)} %collective-permute-done.2.near_ref), channel_id=1, source_target_pairs={{0,2},{1,3},{2,4},{3,5},{4,6},{5,7},{6,0},{7,1},{8,10},{9,11},{10,... | collective-permute-start | bytes 1572872 | tf_op jit(solution)/shard_map/ppermute | solution.py:252
  43.0 32.9 %collective-permute-start.6 = (bf16[2,32,3584]{2,1,0:T(8,128)(2,1)S(1)}, bf16[2,32,3584]{2,1,0:T(8,128)(2,1)S(1)}, u32[]{:S(2)}, u32[]{:S(2)}) collective-permute-start(bf16[2,32,3584]{2,1,0:T(8,128)(2,1)S(1)} %get-tuple-element.25), channel_id=1, source_target_pairs={{0,8},{8,0},{16,24},{24,16},{1,9},{9,1},{17,25},{25,17},{2,10},{10... | collective-permute-start | bytes 1376264 | tf_op jit(solution)/shard_map/ppermute | solution.py:255
  44.6 31.4 %collective-permute-start.9 = (bf16[2,32,3584]{2,1,0:T(8,128)(2,1)S(1)}, bf16[2,32,3584]{2,1,0:T(8,128)(2,1)S(1)}, u32[]{:S(2)}, u32[]{:S(2)}) collective-permute-start(bf16[2,32,3584]{2,1,0:T(8,128)(2,1)S(1)} %get-tuple-element.27), channel_id=1, source_target_pairs={{0,16},{8,24},{16,0},{24,8},{1,17},{9,25},{17,1},{25,9},{2,18},{10... | collective-permute-start | bytes 1376264 | tf_op jit(solution)/shard_map/ppermute | solution.py:255
  53.7 22.3 %collective-permute-start.10 = (bf16[2,32,3584]{2,1,0:T(8,128)(2,1)S(1)}, bf16[2,32,3584]{2,1,0:T(8,128)(2,1)S(1)}, u32[]{:S(2)}, u32[]{:S(2)}) collective-permute-start(bf16[2,32,3584]{2,1,0:T(8,128)(2,1)S(1)} %get-tuple-element.28), channel_id=1, source_target_pairs={{0,24},{8,16},{16,8},{24,0},{1,25},{9,17},{17,9},{25,1},{2,26},{10... | collective-permute-start | bytes 1376264 | tf_op jit(solution)/shard_map/ppermute | solution.py:255
  59.4 21.2 %collective-permute-start.13 = (bf16[128,2048]{1,0:T(8,128)(2,1)S(1)}, bf16[128,2048]{1,0:T(8,128)(2,1)S(1)}, u32[]{:S(2)}, u32[]{:S(2)}) collective-permute-start(bf16[128,2048]{1,0:T(8,128)(2,1)S(1)} %collective-permute-done.7.near_ref), channel_id=1, source_target_pairs={{0,2},{1,3},{2,4},{3,5},{4,6},{5,7},{6,0},{7,1},{8,10},{9,11},{10,... | collective-permute-start | bytes 1572872 | tf_op jit(solution)/shard_map/ppermute | solution.py:252
  77.1 46.5 %collective-permute-start.12 = (bf16[2,32,3584]{2,1,0:T(8,128)(2,1)}, bf16[2,32,3584]{2,1,0:T(8,128)(2,1)S(1)}, u32[]{:S(2)}, u32[]{:S(2)}) collective-permute-start(bf16[2,32,3584]{2,1,0:T(8,128)(2,1)} %get-tuple-element.29), channel_id=1, source_target_pairs={{0,8},{8,0},{16,24},{24,16},{1,9},{9,1},{17,25},{25,17},{2,10},{10... | collective-permute-start | bytes 1376264 | tf_op jit(solution)/shard_map/ppermute | solution.py:255
  78.6 45.2 %collective-permute-start.15 = (bf16[2,32,3584]{2,1,0:T(8,128)(2,1)}, bf16[2,32,3584]{2,1,0:T(8,128)(2,1)}, u32[]{:S(2)}, u32[]{:S(2)}) collective-permute-start(bf16[2,32,3584]{2,1,0:T(8,128)(2,1)} %get-tuple-element.31), channel_id=1, source_target_pairs={{0,16},{8,24},{16,0},{24,8},{1,17},{9,25},{17,1},{25,9},{2,18},{10... | collective-permute-start | bytes 1376264 | tf_op jit(solution)/shard_map/ppermute | solution.py:255
  80.2 43.7 %collective-permute-start.16 = (bf16[2,32,3584]{2,1,0:T(8,128)(2,1)}, bf16[2,32,3584]{2,1,0:T(8,128)(2,1)}, u32[]{:S(2)}, u32[]{:S(2)}) collective-permute-start(bf16[2,32,3584]{2,1,0:T(8,128)(2,1)} %get-tuple-element.32), channel_id=1, source_target_pairs={{0,24},{8,16},{16,8},{24,0},{1,25},{9,17},{17,9},{25,1},{2,26},{10... | collective-permute-start | bytes 1376264 | tf_op jit(solution)/shard_map/ppermute | solution.py:255
  102.2 45.7 %all-to-all-start.1 = ((bf16[32,32,128]{2,1,0:T(8,128)(2,1)}), bf16[32,32,128]{2,1,0:T(8,128)(2,1)S(1)}, u32[]{:S(2)}, u32[]{:S(2)}) async-start(bf16[32,32,128]{2,1,0:T(8,128)(2,1)} %bitcast.18), calls=%async_computation.1 | async-start | bytes 524288 | tf_op jit(solution)/shard_map/all_to_all | solution.py:295
  122.1 22.1 %collective-permute-start.19 = (bf16[2,32,3584]{2,1,0:T(8,128)(2,1)S(1)}, bf16[2,32,3584]{2,1,0:T(8,128)(2,1)S(1)}, u32[]{:S(2)}, u32[]{:S(2)}) collective-permute-start(bf16[2,32,3584]{2,1,0:T(8,128)(2,1)S(1)} %get-tuple-element.34), channel_id=1, source_target_pairs={{0,16},{8,24},{16,0},{24,8},{1,17},{9,25},{17,1},{25,9},{2,18},{10... | collective-permute-start | bytes 1376264 | tf_op jit(solution)/shard_map/ppermute | solution.py:255
  123.6 20.7 %collective-permute-start.20 = (bf16[2,32,3584]{2,1,0:T(8,128)(2,1)S(1)}, bf16[2,32,3584]{2,1,0:T(8,128)(2,1)S(1)}, u32[]{:S(2)}, u32[]{:S(2)}) collective-permute-start(bf16[2,32,3584]{2,1,0:T(8,128)(2,1)S(1)} %get-tuple-element.35), channel_id=1, source_target_pairs={{0,24},{8,16},{16,8},{24,0},{1,25},{9,17},{17,9},{25,1},{2,26},{10... | collective-permute-start | bytes 1376264 | tf_op jit(solution)/shard_map/ppermute | solution.py:255
  125.2 22.6 %collective-permute-start.17 = (bf16[2,32,3584]{2,1,0:T(8,128)(2,1)S(1)}, bf16[2,32,3584]{2,1,0:T(8,128)(2,1)S(1)}, u32[]{:S(2)}, u32[]{:S(2)}) collective-permute-start(bf16[2,32,3584]{2,1,0:T(8,128)(2,1)S(1)} %add_convert_fusion.1), channel_id=1, source_target_pairs={{0,4},{1,5},{2,6},{3,7},{4,0},{5,1},{6,2},{7,3},{8,12},{9,13},{10,... | collective-permute-start | bytes 1376264 | tf_op jit(solution)/shard_map/ppermute | solution.py:252
  144.5 17.0 %collective-permute-start.21 = (bf16[2,32,3584]{2,1,0:T(8,128)(2,1)S(1)}, bf16[2,32,3584]{2,1,0:T(8,128)(2,1)S(1)}, u32[]{:S(2)}, u32[]{:S(2)}) collective-permute-start(bf16[2,32,3584]{2,1,0:T(8,128)(2,1)S(1)} %add_convert_fusion.refs_1_), channel_id=1, source_target_pairs={{0,2},{1,3},{2,4},{3,5},{4,6},{5,7},{6,0},{7,1},{8,10},{9,11},{10,... | collective-permute-start | bytes 1376264 | tf_op jit(solution)/shard_map/ppermute | solution.py:252
  148.7 23.2 %all-to-all-start.2 = ((bf16[32,32,128]{2,1,0:T(8,128)(2,1)}), bf16[32,32,128]{2,1,0:T(8,128)(2,1)S(1)}, u32[]{:S(2)}, u32[]{:S(2)}) async-start(bf16[32,32,128]{2,1,0:T(8,128)(2,1)} %broadcast_in_dim.73), calls=%async_computation.2 | async-start | bytes 524288 | tf_op jit(solution)/shard_map/all_to_all | solution.py:303
  162.6 28.4 %collective-permute-start.22 = (bf16[4,32,3584]{2,1,0:T(8,128)(2,1)}, bf16[4,32,3584]{2,1,0:T(8,128)(2,1)}, u32[]{:S(2)}, u32[]{:S(2)}) collective-permute-start(bf16[4,32,3584]{2,1,0:T(8,128)(2,1)} %pad_maximum_fusion.1), channel_id=1, source_target_pairs={{0,1},{1,0},{2,3},{3,2},{4,5},{5,4},{6,7},{7,6},{8,9},{9,8},{10,11... | collective-permute-start | bytes 2752520 | tf_op jit(solution)/shard_map/ppermute | solution.py:252
  177.1 47.0 %all-to-all-start.3 = ((bf16[8,128,896]{2,1,0:T(8,128)(2,1)}), bf16[8,128,896]{2,1,0:T(8,128)(2,1)S(1)}, u32[]{:S(2)}, u32[]{:S(2)}) async-start(bf16[8,128,896]{2,1,0:T(8,128)(2,1)} %bitcast.78), calls=%async_computation.3 | async-start | bytes 3670016 | tf_op jit(solution)/shard_map/all_to_all | solution.py:327
  193.3 22.7 %collective-permute-start.24 = (bf16[2,32,3584]{2,1,0:T(8,128)(2,1)S(1)}, bf16[2,32,3584]{2,1,0:T(8,128)(2,1)S(1)}, u32[]{:S(2)}, u32[]{:S(2)}) collective-permute-start(bf16[2,32,3584]{2,1,0:T(8,128)(2,1)S(1)} %pad_maximum_fusion.4), channel_id=1, source_target_pairs={{0,16},{8,24},{16,0},{24,8},{1,17},{9,25},{17,1},{25,9},{2,18},{10... | collective-permute-start | bytes 1376264 | tf_op jit(solution)/shard_map/ppermute | solution.py:255
  194.3 21.7 %collective-permute-start.25 = (bf16[2,32,3584]{2,1,0:T(8,128)(2,1)S(1)}, bf16[2,32,3584]{2,1,0:T(8,128)(2,1)S(1)}, u32[]{:S(2)}, u32[]{:S(2)}) collective-permute-start(bf16[2,32,3584]{2,1,0:T(8,128)(2,1)S(1)} %pad_maximum_fusion.5), channel_id=1, source_target_pairs={{0,24},{8,16},{16,8},{24,0},{1,25},{9,17},{17,9},{25,1},{2,26},{10... | collective-permute-start | bytes 1376264 | tf_op jit(solution)/shard_map/ppermute | solution.py:255
  (26 other events, 365.4 us)

commit v8 on v7

--- a/solution.py
+++ b/solution.py
@@ -192,7 +192,7 @@
         ],
         out_specs=pl.BlockSpec((rows, 2 * ranks), lambda at: (at, 0)),
         out_shape=jax.ShapeDtypeStruct((tokens, 2 * ranks), jnp.bfloat16),
-        compiler_params=pltpu.CompilerParams(vmem_limit_bytes=24 << 20),
+        compiler_params=pltpu.CompilerParams(vmem_limit_bytes=56 << 20),
         cost_estimate=pl.CostEstimate(
             flops=2 * tokens * tenants * ranks * (up_slab + down_slab),
             bytes_accessed=2 * (tokens + tenants * ranks) * (up_slab + down_slab),
@@ -275,21 +275,9 @@
             columns = lax.dynamic_slice_in_dim(rows, index * up_slab, up_slab, 1)
             grad_slab = lax.dynamic_update_index_in_dim(grad_slab, columns, back + (core ^ flip), 0)
     grad_slab = grad_slab.reshape(count * block, up_slab)
+    products = [chunk_product(near, far, down_weight, group, groups) for near, far in pairs]
+    (hidden_slab,) = touch([hidden_slab], products[last][0])
     ranked = project_both(grad_slab, hidden_slab, adapter_up, adapter_down, owner, mask)
-
-    products = [
-        chunk_product(near, far, down_weight, group, groups, *([ranked] if step == last else []))
-        for step, (near, far) in enumerate(pairs)
-    ]
-    came = []
-    for step in range(chips):
-        kept = products[step][0]
-        others = [grp_move(products[step][flip], flip) for flip in range(1, groups)]
-        gates = [products[step + 1][0]] if step < last else []
-        if gates:
-            (others[0],) = touch([others[0]], *gates)
-        sums = add(kept, *others)
-        came.append(seq_move(sums, step, 0) if step else sums)
 
     devices = count * groups
     share = lax.all_to_all(
@@ -300,14 +288,28 @@
         tiled=True,
     )
     share = jnp.sum(share.astype(jnp.float32), axis=0).astype(jnp.bfloat16)
-    ranked = lax.all_to_all(
+    rank_sums = lax.all_to_all(
         jnp.broadcast_to(share[None], (devices,) + share.shape),
         ("grp", "seq"),
         split_axis=0,
         concat_axis=0,
         tiled=True,
     ).reshape(count * block, 2 * ranks)
-    (ranked,) = touch([ranked], sums)
+
+    came = []
+    for step in range(chips):
+        kept, *sent = products[step]
+        if step == last:
+            sent = touch(sent, ranked)
+        others = [grp_move(rows, flip + 1) for flip, rows in enumerate(sent)]
+        if step < last - 1:
+            gate = products[step + 1][0]
+        else:
+            gate = rank_sums if step == last else share
+        (others[0],) = touch([others[0]], gate)
+        sums = add(kept, *others)
+        came.append(seq_move(sums, step, 0) if step else sums)
+    (ranked,) = touch([rank_sums], sums)
     grad_rank = ranked[:, :ranks]
 
     flat_down = adapter_down.reshape(tenants * ranks, down_slab)
@@ -324,8 +326,10 @@
     )
     term = (term * ADAPTER_SCALE).astype(jnp.bfloat16).reshape(count, block, down_slab)
     rank_here = after(ranked, term)
+    term_here = term
     term = lax.all_to_all(term, "seq", split_axis=0, concat_axis=0, tiled=True)
 
+    came = touch(came, term_here)
     mine = jnp.stack([sums[0] for sums in came])
     theirs = seq_move(jnp.stack([sums[1] for sums in came]), 0, 1)
     halves = jnp.stack([mine, theirs], axis=1).reshape(count, part, width)

time: 228 us -> 225 us (0.987)
  waiting for transfers between devices: 83.2 us -> 67.9 us
  Pallas kernels: 29.1 us -> 33.9 us
  starting transfers between devices: 66.6 us -> 70.1 us
  other arithmetic: 5.05 us -> 8.53 us
    all_to_all x1, waiting for transfers between devices: 8.88 us -> 2.57 us  [shards(): lax.all_to_all(jnp.broadcast_to(share[None], (devices,) + share.shape), (...]
    ppermute x11, waiting for transfers between devices: 23.7 us -> 17.7 us  [seq_move(): return lax.ppermute(value, 'seq', pairs)]
    dynamic_update_slice x8, local copies, waits for them, and re-layouts: 0.11 us -> 5.99 us  [shards(): lax.dynamic_update_index_in_dim(grad_slab, columns, back + (core ^ flip), 0)]
    unnamed x40 -> x44, local copies, waits for them, and re-layouts: 19.8 us -> 14.1 us
    convert_element_type x4, other arithmetic: 2.06 us -> 6.71 us  [add(): sum((term.astype(jnp.float32) for term in terms)).astype(jnp.bfloat16)]
    ppermute x11, starting transfers between devices: 20.7 us -> 24.2 us  [seq_move(): return lax.ppermute(value, 'seq', pairs)]
    ppermute x15, waiting for transfers between devices: 43.3 us -> 39.9 us  [grp_move(): return lax.ppermute(value, 'grp', [(g, g ^ flip) for g in range(groups)])]
    pallas_call x4, Pallas kernels: 22.4 us -> 25 us  [chunk_product(): pl.pallas_call(functools.partial(chunk_kernel, groups), grid_spec=pltpu.P...]
  transfers between devices with their start and end apart: 30 -> 30, of which waited for: 12 -> 10; matrix products, arithmetic and copies ran while one was open for 12% -> 16% of each run, Pallas kernels for 12% -> 14%
where the time goes in v8:
time: 225 us; the launch traced here: 224 us
  starting transfers between devices  70.1 us (31%)
  waiting for transfers between devices  67.9 us (30%)
  Pallas kernels  33.9 us (15%)
  local copies, waits for them, and re-layouts  30.4 us (14%)
  matrix products  12.1 us (5%)
  other arithmetic  8.53 us (4%)
    ppermute x15, waiting for transfers between devices, grp_move(): return lax.ppermute(value, 'grp', [(g, g ^ flip) for g in range(groups)])  39.9 us
    pallas_call x4, Pallas kernels, chunk_product(): pl.pallas_call(functools.partial(chunk_kernel, groups), grid_spec=pltpu.P...  25 us
    ppermute x11, starting transfers between devices, seq_move(): return lax.ppermute(value, 'seq', pairs)  24.2 us
    ppermute x15, starting transfers between devices, grp_move(): return lax.ppermute(value, 'grp', [(g, g ^ flip) for g in range(groups)])  20.1 us
    ppermute x11, waiting for transfers between devices, seq_move(): return lax.ppermute(value, 'seq', pairs)  17.7 us
    unnamed x44, local copies, waits for them, and re-layouts  14.1 us
    all_to_all x1, starting transfers between devices, shards(): lax.all_to_all(jnp.broadcast_to(share[None], (devices,) + share.shape), (...  11.2 us
    dot_general x2, matrix products, dot(): lax.dot_general(left, right, dims, preferred_element_type=jnp.float32)  6.89 us
  transfers between devices with their start and end apart: 30, of which 10 were waited for; matrix products, arithmetic and copies ran while one was open for 16% of the time, Pallas kernels for 14%

profile of v8, /device:TPU:0, one launch (start us, length us, event | category | flops | bytes accessed | tf_op | source)
XLA Modules:
  0.0 223.9 jit_solution(1244242496284579887)
XLA Ops:
  3.8 3.0 %copy.52 = bf16[16,8,8,896]{3,2,0,1:T(8,128)(2,1)} copy(bf16[16,8,8,896]{3,2,1,0:T(8,128)(2,1)} %bitcast.74) | data formatting | bytes 3670016 | tf_op jit(solution)/shard_map/reshape | solution.py:263
  6.8 4.0 %all-to-all-start = ((bf16[8,128,896]{2,1,0:T(8,128)(2,1)}), bf16[8,128,896]{2,1,0:T(8,128)(2,1)S(1)}, u32[]{:S(2)}, u32[]{:S(2)}) async-start(bf16[8,128,896]{2,1,0:T(8,128)(2,1)} %bitcast.72), calls=%async_computation | async-start | bytes 3670016 | tf_op jit(solution)/shard_map/all_to_all | solution.py:262
  13.6 5.3 %collective-permute-done.2.near_ref = bf16[128,2048]{1,0:T(8,128)(2,1)S(1)} collective-permute-done((bf16[128,2048]{1,0:T(8,128)(2,1)}, bf16[128,2048]{1,0:T(8,128)(2,1)S(1)}, u32[]{:S(2)}, u32[]{:S(2)}) %collective-permute-start.2) | collective-permute-done | bytes 524320 | tf_op jit(solution)/shard_map/ppermute | solution.py:252
  18.9 5.2 %copy-done = bf16[3584,2048]{1,0:T(8,128)(2,1)S(1)} copy-done((bf16[3584,2048]{1,0:T(8,128)(2,1)S(1)}, bf16[3584,2048]{1,0:T(8,128)(2,1)}, u32[]{:S(2)}) %copy-start) | copy-done | bytes 14680088
  24.1 6.7 %shard_map.94 = (bf16[2,32,3584]{2,1,0:T(8,128)(2,1)S(1)}, bf16[2,32,3584]{2,1,0:T(8,128)(2,1)S(1)}, bf16[2,32,3584]{2,1,0:T(8,128)(2,1)S(1)}, bf16[2,32,3584]{2,1,0:T(8,128)(2,1)S(1)}) custom-call(s32[1]{0:T(128)} %bitcast.place_ref, bf16[128,2048]{1,0:T(8,128)(2,1)S(1)} %copy-done.12, bf16[128,2048]{1,0:T(8,128)(2,1)} %collective-permute-done.far_ref, ...), custom_call_target="tpu_custom_call" | custom-call | flops 3758096384 | bytes 17563648 | tf_op jit(solution)/shard_map/pallas_call | solution.py:56
  34.3 4.4 %collective-permute-start.7 = (bf16[128,2048]{1,0:T(8,128)(2,1)S(1)}, bf16[128,2048]{1,0:T(8,128)(2,1)S(1)}, u32[]{:S(2)}, u32[]{:S(2)}) collective-permute-start(bf16[128,2048]{1,0:T(8,128)(2,1)S(1)} %collective-permute-done.2.near_ref), channel_id=1, source_target_pairs={{0,2},{1,3},{2,4},{3,5},{4,6},{5,7},{6,0},{7,1},{8,10},{9,11},{10,... | collective-permute-start | bytes 1572872 | tf_op jit(solution)/shard_map/ppermute | solution.py:252
  40.9 6.1 %shard_map.95 = (bf16[2,32,3584]{2,1,0:T(8,128)(2,1)S(1)}, bf16[2,32,3584]{2,1,0:T(8,128)(2,1)S(1)}, bf16[2,32,3584]{2,1,0:T(8,128)(2,1)}, bf16[2,32,3584]{2,1,0:T(8,128)(2,1)}) custom-call(s32[1]{0:T(128)} %bitcast.place_ref, bf16[128,2048]{1,0:T(8,128)(2,1)S(1)} %collective-permute-done.2.near_ref, bf16[128,2048]{1,0:T(8,128)(2,1)S(1)} %collective-permute-done.3.far_ref, ...), custom_call_target="tpu_custom_call" | custom-call | flops 3758096384 | bytes 17563648 | tf_op jit(solution)/shard_map/pallas_call | solution.py:56
  50.0 4.9 %collective-permute-done.4 = bf16[2,32,3584]{2,1,0:T(8,128)(2,1)S(1)} collective-permute-done((bf16[2,32,3584]{2,1,0:T(8,128)(2,1)S(1)}, bf16[2,32,3584]{2,1,0:T(8,128)(2,1)S(1)}, u32[]{:S(2)}, u32[]{:S(2)}) %collective-permute-start.4) | collective-permute-done | bytes 458784 | tf_op jit(solution)/shard_map/ppermute | solution.py:255
  56.6 2.9 %collective-permute-done.7.near_ref = bf16[128,2048]{1,0:T(8,128)(2,1)S(1)} collective-permute-done((bf16[128,2048]{1,0:T(8,128)(2,1)S(1)}, bf16[128,2048]{1,0:T(8,128)(2,1)S(1)}, u32[]{:S(2)}, u32[]{:S(2)}) %collective-permute-start.7) | collective-permute-done | bytes 524320 | tf_op jit(solution)/shard_map/ppermute | solution.py:252
  59.4 8.5 %collective-permute-start.13 = (bf16[128,2048]{1,0:T(8,128)(2,1)S(1)}, bf16[128,2048]{1,0:T(8,128)(2,1)S(1)}, u32[]{:S(2)}, u32[]{:S(2)}) collective-permute-start(bf16[128,2048]{1,0:T(8,128)(2,1)S(1)} %collective-permute-done.7.near_ref), channel_id=1, source_target_pairs={{0,2},{1,3},{2,4},{3,5},{4,6},{5,7},{6,0},{7,1},{8,10},{9,11},{10,... | collective-permute-start | bytes 1572872 | tf_op jit(solution)/shard_map/ppermute | solution.py:252
  69.5 9.5 %collective-permute-done.13.near_ref = bf16[128,2048]{1,0:T(8,128)(2,1)S(1)} collective-permute-done((bf16[128,2048]{1,0:T(8,128)(2,1)S(1)}, bf16[128,2048]{1,0:T(8,128)(2,1)S(1)}, u32[]{:S(2)}, u32[]{:S(2)}) %collective-permute-start.13) | collective-permute-done | bytes 524320 | tf_op jit(solution)/shard_map/ppermute | solution.py:252
  79.0 6.1 %shard_map.97 = (bf16[2,32,3584]{2,1,0:T(8,128)(2,1)S(1)}, bf16[2,32,3584]{2,1,0:T(8,128)(2,1)}, bf16[2,32,3584]{2,1,0:T(8,128)(2,1)}, bf16[2,32,3584]{2,1,0:T(8,128)(2,1)}) custom-call(s32[1]{0:T(128)} %bitcast.place_ref, bf16[128,2048]{1,0:T(8,128)(2,1)S(1)} %collective-permute-done.7.near_ref, bf16[128,2048]{1,0:T(8,128)(2,1)S(1)} %collective-permute-done.8.far_ref, ...), custom_call_target="tpu_custom_call" | custom-call | flops 3758096384 | bytes 17563648 | tf_op jit(solution)/shard_map/pallas_call | solution.py:56
  90.7 6.0 %shard_map.99 = (bf16[2,32,3584]{2,1,0:T(8,128)(2,1)S(1)}, bf16[2,32,3584]{2,1,0:T(8,128)(2,1)S(1)}, bf16[2,32,3584]{2,1,0:T(8,128)(2,1)}, bf16[2,32,3584]{2,1,0:T(8,128)(2,1)S(1)}) custom-call(s32[1]{0:T(128)} %bitcast.place_ref, bf16[128,2048]{1,0:T(8,128)(2,1)S(1)} %collective-permute-done.13.near_ref, ...), custom_call_target="tpu_custom_call" | custom-call | flops 3758096384 | bytes 17563648 | tf_op jit(solution)/shard_map/pallas_call | solution.py:56
  102.0 6.9 %shard_map.101.refs_3_ = bf16[1024,128]{1,0:T(8,128)(2,1)} custom-call(s32[1024,1]{1,0:T(8,128)} %copy.45.owner_ref, bf16[1024,256]{1,0:T(8,128)(2,1)} %bitcast.10.grad_ref, bf16[1024,896]{1,0:T(8,128)(2,1)} %copy-done.2, bf16[1024,256]{1,0:T(8,128)(2,1)} %bitcast.79, bf16[1024,896]{1,0:T(8,128)(2,1)} %bitcast.78), custom_call_target="tpu_custom_call" | custom-call | flops 2415919104 | bytes 4718592 | tf_op jit(solution)/shard_map/pallas_call | solution.py:183
  108.8 6.9 %all-to-all-start.1 = ((bf16[32,32,128]{2,1,0:T(8,128)(2,1)}), bf16[32,32,128]{2,1,0:T(8,128)(2,1)}, u32[]{:S(2)}, u32[]{:S(2)}) async-start(bf16[32,32,128]{2,1,0:T(8,128)(2,1)} %bitcast.71), calls=%async_computation.1 | async-start | bytes 524288 | tf_op jit(solution)/shard_map/all_to_all | solution.py:283
  117.9 3.5 %collective-permute-start.11 = (bf16[2,32,3584]{2,1,0:T(8,128)(2,1)}, bf16[2,32,3584]{2,1,0:T(8,128)(2,1)S(1)}, u32[]{:S(2)}, u32[]{:S(2)}) collective-permute-start(bf16[2,32,3584]{2,1,0:T(8,128)(2,1)} %add_convert_fusion.2), channel_id=1, source_target_pairs={{0,6},{1,7},{2,0},{3,1},{4,2},{5,3},{6,4},{7,5},{8,14},{9,15},{10,... | collective-permute-start | bytes 1376264 | tf_op jit(solution)/shard_map/ppermute | solution.py:252
  127.8 11.2 %all-to-all-start.2 = ((bf16[32,32,128]{2,1,0:T(8,128)(2,1)}), bf16[32,32,128]{2,1,0:T(8,128)(2,1)S(1)}, u32[]{:S(2)}, u32[]{:S(2)}) async-start(bf16[32,32,128]{2,1,0:T(8,128)(2,1)} %broadcast_in_dim.73), calls=%async_computation.2 | async-start | bytes 524288 | tf_op jit(solution)/shard_map/all_to_all | solution.py:291
  149.4 15.1 %collective-permute-done.19 = bf16[2,32,3584]{2,1,0:T(8,128)(2,1)} collective-permute-done((bf16[2,32,3584]{2,1,0:T(8,128)(2,1)}, bf16[2,32,3584]{2,1,0:T(8,128)(2,1)}, u32[]{:S(2)}, u32[]{:S(2)}) %collective-permute-start.19) | collective-permute-done | bytes 458784 | tf_op jit(solution)/shard_map/ppermute | solution.py:255
  168.5 5.2 %fusion = bf16[1024,896]{1,0:T(8,128)(2,1)} fusion(bf16[16,64,896]{2,1,0:T(8,128)(2,1)} %param.10, bf16[1024,16]{0,1:T(8,128)(2,1)S(1)} %convert_convert_fusion, bf16[1024,64]{0,1:T(8,128)(2,1)S(1)} %copy.46), kind=kOutput, calls=%fused_computation.1 | convolution fusion | flops 1881931776 | bytes 3833856 | tf_op jit(solution)/shard_map/dot_general | solution.py:318
  173.7 3.8 %all-to-all-start.3 = ((bf16[8,128,896]{2,1,0:T(8,128)(2,1)}), bf16[8,128,896]{2,1,0:T(8,128)(2,1)S(1)}, u32[]{:S(2)}, u32[]{:S(2)}) async-start(bf16[8,128,896]{2,1,0:T(8,128)(2,1)} %bitcast.19.refs_4_), calls=%async_computation.3 | async-start | bytes 3670016 | tf_op jit(solution)/shard_map/all_to_all | solution.py:330
  185.1 4.2 %fusion.9 = f32[16,64,896]{2,1,0:T(8,128)} fusion(bf16[1024,896]{1,0:T(8,128)(2,1)S(1)} %copy-done.3, f32[16]{0:T(128)S(1)} %broadcast_divide_fusion, bf16[1024,64]{0,1:T(8,128)(2,1)S(1)} %copy.48, bf16[1024,16]{0,1:T(8,128)(2,1)S(1)} %convert_convert_fusion), kind=kOutput, calls=%fused_computation.10 | convolution fusion | flops 1881014272 | bytes 5668928 | tf_op jit(solution)/shard_map/dot_general | solution.py:19
  193.8 9.6 %collective-permute-done.23.refs_1_ = bf16[2,32,3584]{2,1,0:T(8,128)(2,1)S(1)} collective-permute-done((bf16[2,32,3584]{2,1,0:T(8,128)(2,1)S(1)}, bf16[2,32,3584]{2,1,0:T(8,128)(2,1)S(1)}, u32[]{:S(2)}, u32[]{:S(2)}) %collective-permute-start.23) | collective-permute-done | bytes 458784 | tf_op jit(solution)/shard_map/ppermute | solution.py:255
  203.4 10.3 %collective-permute-done.24.refs_2_ = bf16[2,32,3584]{2,1,0:T(8,128)(2,1)S(1)} collective-permute-done((bf16[2,32,3584]{2,1,0:T(8,128)(2,1)S(1)}, bf16[2,32,3584]{2,1,0:T(8,128)(2,1)S(1)}, u32[]{:S(2)}, u32[]{:S(2)}) %collective-permute-start.24) | collective-permute-done | bytes 458784 | tf_op jit(solution)/shard_map/ppermute | solution.py:255
  214.4 6.4 %all-to-all-done.3.refs_4_ = bf16[8,128,896]{2,1,0:T(8,128)(2,1)S(1)} async-done(((bf16[8,128,896]{2,1,0:T(8,128)(2,1)}), bf16[8,128,896]{2,1,0:T(8,128)(2,1)S(1)}, u32[]{:S(2)}, u32[]{:S(2)}) %all-to-all-start.3) | async-done | bytes 1835040 | tf_op jit(solution)/shard_map/all_to_all | solution.py:330
  (135 shorter events, 67.4 us)
Async XLA Ops:
  0.6 18.3 %collective-permute-start = (bf16[128,2048]{1,0:T(8,128)(2,1)}, bf16[128,2048]{1,0:T(8,128)(2,1)}, u32[]{:S(2)}, u32[]{:S(2)}) collective-permute-start(bf16[128,2048]{1,0:T(8,128)(2,1)} %near_ref.1), channel_id=1, source_target_pairs={{0,1},{1,0},{2,3},{3,2},{4,5},{5,4},{6,7},{7,6},{8,9},{9,8},{10,11... | collective-permute-start | bytes 1572872 | tf_op jit(solution)/shard_map/ppermute | solution.py:252
  1.1 17.8 %collective-permute-start.2 = (bf16[128,2048]{1,0:T(8,128)(2,1)}, bf16[128,2048]{1,0:T(8,128)(2,1)S(1)}, u32[]{:S(2)}, u32[]{:S(2)}) collective-permute-start(bf16[128,2048]{1,0:T(8,128)(2,1)} %near_ref.1), channel_id=1, source_target_pairs={{0,2},{1,3},{2,4},{3,5},{4,6},{5,7},{6,0},{7,1},{8,10},{9,11},{10,... | collective-permute-start | bytes 1572872 | tf_op jit(solution)/shard_map/ppermute | solution.py:252
  6.8 92.9 %all-to-all-start = ((bf16[8,128,896]{2,1,0:T(8,128)(2,1)}), bf16[8,128,896]{2,1,0:T(8,128)(2,1)S(1)}, u32[]{:S(2)}, u32[]{:S(2)}) async-start(bf16[8,128,896]{2,1,0:T(8,128)(2,1)} %bitcast.72), calls=%async_computation | async-start | bytes 3670016 | tf_op jit(solution)/shard_map/all_to_all | solution.py:262
  18.9 21.9 %collective-permute-start.3 = (bf16[128,2048]{1,0:T(8,128)(2,1)S(1)}, bf16[128,2048]{1,0:T(8,128)(2,1)S(1)}, u32[]{:S(2)}, u32[]{:S(2)}) collective-permute-start(bf16[128,2048]{1,0:T(8,128)(2,1)S(1)} %collective-permute-done.2.near_ref), channel_id=1, source_target_pairs={{0,1},{1,0},{2,3},{3,2},{4,5},{5,4},{6,7},{7,6},{8,9},{9,8},{10,11... | collective-permute-start | bytes 1572872 | tf_op jit(solution)/shard_map/ppermute | solution.py:252
  30.8 17.7 %collective-permute-start.1 = (bf16[2,32,3584]{2,1,0:T(8,128)(2,1)S(1)}, bf16[2,32,3584]{2,1,0:T(8,128)(2,1)S(1)}, u32[]{:S(2)}, u32[]{:S(2)}) collective-permute-start(bf16[2,32,3584]{2,1,0:T(8,128)(2,1)S(1)} %get-tuple-element.28), channel_id=1, source_target_pairs={{0,8},{8,0},{16,24},{24,16},{1,9},{9,1},{17,25},{25,17},{2,10},{10... | collective-permute-start | bytes 1376264 | tf_op jit(solution)/shard_map/ppermute | solution.py:255
  32.5 22.5 %collective-permute-start.4 = (bf16[2,32,3584]{2,1,0:T(8,128)(2,1)S(1)}, bf16[2,32,3584]{2,1,0:T(8,128)(2,1)S(1)}, u32[]{:S(2)}, u32[]{:S(2)}) collective-permute-start(bf16[2,32,3584]{2,1,0:T(8,128)(2,1)S(1)} %get-tuple-element.30), channel_id=1, source_target_pairs={{0,16},{8,24},{16,0},{24,8},{1,17},{9,25},{17,1},{25,9},{2,18},{10... | collective-permute-start | bytes 1376264 | tf_op jit(solution)/shard_map/ppermute | solution.py:255
  34.0 34.0 %collective-permute-start.5 = (bf16[2,32,3584]{2,1,0:T(8,128)(2,1)S(1)}, bf16[2,32,3584]{2,1,0:T(8,128)(2,1)S(1)}, u32[]{:S(2)}, u32[]{:S(2)}) collective-permute-start(bf16[2,32,3584]{2,1,0:T(8,128)(2,1)S(1)} %get-tuple-element.31), channel_id=1, source_target_pairs={{0,24},{8,16},{16,8},{24,0},{1,25},{9,17},{17,9},{25,1},{2,26},{10... | collective-permute-start | bytes 1376264 | tf_op jit(solution)/shard_map/ppermute | solution.py:255
  34.3 25.1 %collective-permute-start.7 = (bf16[128,2048]{1,0:T(8,128)(2,1)S(1)}, bf16[128,2048]{1,0:T(8,128)(2,1)S(1)}, u32[]{:S(2)}, u32[]{:S(2)}) collective-permute-start(bf16[128,2048]{1,0:T(8,128)(2,1)S(1)} %collective-permute-done.2.near_ref), channel_id=1, source_target_pairs={{0,2},{1,3},{2,4},{3,5},{4,6},{5,7},{6,0},{7,1},{8,10},{9,11},{10,... | collective-permute-start | bytes 1572872 | tf_op jit(solution)/shard_map/ppermute | solution.py:252
  47.0 39.6 %collective-permute-start.6 = (bf16[2,32,3584]{2,1,0:T(8,128)(2,1)S(1)}, bf16[2,32,3584]{2,1,0:T(8,128)(2,1)S(1)}, u32[]{:S(2)}, u32[]{:S(2)}) collective-permute-start(bf16[2,32,3584]{2,1,0:T(8,128)(2,1)S(1)} %get-tuple-element.32), channel_id=1, source_target_pairs={{0,8},{8,0},{16,24},{24,16},{1,9},{9,1},{17,25},{25,17},{2,10},{10... | collective-permute-start | bytes 1376264 | tf_op jit(solution)/shard_map/ppermute | solution.py:255
  48.5 67.2 %collective-permute-start.9 = (bf16[2,32,3584]{2,1,0:T(8,128)(2,1)}, bf16[2,32,3584]{2,1,0:T(8,128)(2,1)}, u32[]{:S(2)}, u32[]{:S(2)}) collective-permute-start(bf16[2,32,3584]{2,1,0:T(8,128)(2,1)} %get-tuple-element.34), channel_id=1, source_target_pairs={{0,16},{8,24},{16,0},{24,8},{1,17},{9,25},{17,1},{25,9},{2,18},{10... | collective-permute-start | bytes 1376264 | tf_op jit(solution)/shard_map/ppermute | solution.py:255
  54.9 60.8 %collective-permute-start.10 = (bf16[2,32,3584]{2,1,0:T(8,128)(2,1)}, bf16[2,32,3584]{2,1,0:T(8,128)(2,1)}, u32[]{:S(2)}, u32[]{:S(2)}) collective-permute-start(bf16[2,32,3584]{2,1,0:T(8,128)(2,1)} %get-tuple-element.35), channel_id=1, source_target_pairs={{0,24},{8,16},{16,8},{24,0},{1,25},{9,17},{17,9},{25,1},{2,26},{10... | collective-permute-start | bytes 1376264 | tf_op jit(solution)/shard_map/ppermute | solution.py:255
  59.4 19.5 %collective-permute-start.13 = (bf16[128,2048]{1,0:T(8,128)(2,1)S(1)}, bf16[128,2048]{1,0:T(8,128)(2,1)S(1)}, u32[]{:S(2)}, u32[]{:S(2)}) collective-permute-start(bf16[128,2048]{1,0:T(8,128)(2,1)S(1)} %collective-permute-done.7.near_ref), channel_id=1, source_target_pairs={{0,2},{1,3},{2,4},{3,5},{4,6},{5,7},{6,0},{7,1},{8,10},{9,11},{10,... | collective-permute-start | bytes 1572872 | tf_op jit(solution)/shard_map/ppermute | solution.py:252
  85.1 53.9 %collective-permute-start.12 = (bf16[2,32,3584]{2,1,0:T(8,128)(2,1)}, bf16[2,32,3584]{2,1,0:T(8,128)(2,1)S(1)}, u32[]{:S(2)}, u32[]{:S(2)}) collective-permute-start(bf16[2,32,3584]{2,1,0:T(8,128)(2,1)} %get-tuple-element.36), channel_id=1, source_target_pairs={{0,8},{8,0},{16,24},{24,16},{1,9},{9,1},{17,25},{25,17},{2,10},{10... | collective-permute-start | bytes 1376264 | tf_op jit(solution)/shard_map/ppermute | solution.py:255
  86.6 54.3 %collective-permute-start.15 = (bf16[2,32,3584]{2,1,0:T(8,128)(2,1)}, bf16[2,32,3584]{2,1,0:T(8,128)(2,1)}, u32[]{:S(2)}, u32[]{:S(2)}) collective-permute-start(bf16[2,32,3584]{2,1,0:T(8,128)(2,1)} %get-tuple-element.38), channel_id=1, source_target_pairs={{0,16},{8,24},{16,0},{24,8},{1,17},{9,25},{17,1},{25,9},{2,18},{10... | collective-permute-start | bytes 1376264 | tf_op jit(solution)/shard_map/ppermute | solution.py:255
  90.2 52.1 %collective-permute-start.16 = (bf16[2,32,3584]{2,1,0:T(8,128)(2,1)}, bf16[2,32,3584]{2,1,0:T(8,128)(2,1)}, u32[]{:S(2)}, u32[]{:S(2)}) collective-permute-start(bf16[2,32,3584]{2,1,0:T(8,128)(2,1)} %get-tuple-element.39), channel_id=1, source_target_pairs={{0,24},{8,16},{16,8},{24,0},{1,25},{9,17},{17,9},{25,1},{2,26},{10... | collective-permute-start | bytes 1376264 | tf_op jit(solution)/shard_map/ppermute | solution.py:255
  117.9 65.3 %collective-permute-start.11 = (bf16[2,32,3584]{2,1,0:T(8,128)(2,1)}, bf16[2,32,3584]{2,1,0:T(8,128)(2,1)S(1)}, u32[]{:S(2)}, u32[]{:S(2)}) collective-permute-start(bf16[2,32,3584]{2,1,0:T(8,128)(2,1)} %add_convert_fusion.2), channel_id=1, source_target_pairs={{0,6},{1,7},{2,0},{3,1},{4,2},{5,3},{6,4},{7,5},{8,14},{9,15},{10,... | collective-permute-start | bytes 1376264 | tf_op jit(solution)/shard_map/ppermute | solution.py:252
  123.3 23.6 %collective-permute-start.18 = (bf16[2,32,3584]{2,1,0:T(8,128)(2,1)}, bf16[2,32,3584]{2,1,0:T(8,128)(2,1)S(1)}, u32[]{:S(2)}, u32[]{:S(2)}) collective-permute-start(bf16[2,32,3584]{2,1,0:T(8,128)(2,1)} %copy-done.17), channel_id=1, source_target_pairs={{0,8},{8,0},{16,24},{24,16},{1,9},{9,1},{17,25},{25,17},{2,10},{10... | collective-permute-start | bytes 1376264 | tf_op jit(solution)/shard_map/ppermute | solution.py:255
  127.8 21.6 %all-to-all-start.2 = ((bf16[32,32,128]{2,1,0:T(8,128)(2,1)}), bf16[32,32,128]{2,1,0:T(8,128)(2,1)S(1)}, u32[]{:S(2)}, u32[]{:S(2)}) async-start(bf16[32,32,128]{2,1,0:T(8,128)(2,1)} %broadcast_in_dim.73), calls=%async_computation.2 | async-start | bytes 524288 | tf_op jit(solution)/shard_map/all_to_all | solution.py:291
  139.0 25.5 %collective-permute-start.19 = (bf16[2,32,3584]{2,1,0:T(8,128)(2,1)}, bf16[2,32,3584]{2,1,0:T(8,128)(2,1)}, u32[]{:S(2)}, u32[]{:S(2)}) collective-permute-start(bf16[2,32,3584]{2,1,0:T(8,128)(2,1)} %get-tuple-element.44), channel_id=1, source_target_pairs={{0,16},{8,24},{16,0},{24,8},{1,17},{9,25},{17,1},{25,9},{2,18},{10... | collective-permute-start | bytes 1376264 | tf_op jit(solution)/shard_map/ppermute | solution.py:255
  140.8 23.7 %collective-permute-start.20 = (bf16[2,32,3584]{2,1,0:T(8,128)(2,1)S(1)}, bf16[2,32,3584]{2,1,0:T(8,128)(2,1)}, u32[]{:S(2)}, u32[]{:S(2)}) collective-permute-start(bf16[2,32,3584]{2,1,0:T(8,128)(2,1)S(1)} %get-tuple-element.45), channel_id=1, source_target_pairs={{0,24},{8,16},{16,8},{24,0},{1,25},{9,17},{17,9},{25,1},{2,26},{10... | collective-permute-start | bytes 1376264 | tf_op jit(solution)/shard_map/ppermute | solution.py:255
  144.5 38.7 %collective-permute-start.17 = (bf16[2,32,3584]{2,1,0:T(8,128)(2,1)}, bf16[2,32,3584]{2,1,0:T(8,128)(2,1)S(1)}, u32[]{:S(2)}, u32[]{:S(2)}) collective-permute-start(bf16[2,32,3584]{2,1,0:T(8,128)(2,1)} %add_convert_fusion.1), channel_id=1, source_target_pairs={{0,4},{1,5},{2,6},{3,7},{4,0},{5,1},{6,2},{7,3},{8,12},{9,13},{10,... | collective-permute-start | bytes 1376264 | tf_op jit(solution)/shard_map/ppermute | solution.py:252
  173.7 47.1 %all-to-all-start.3 = ((bf16[8,128,896]{2,1,0:T(8,128)(2,1)}), bf16[8,128,896]{2,1,0:T(8,128)(2,1)S(1)}, u32[]{:S(2)}, u32[]{:S(2)}) async-start(bf16[8,128,896]{2,1,0:T(8,128)(2,1)} %bitcast.19.refs_4_), calls=%async_computation.3 | async-start | bytes 3670016 | tf_op jit(solution)/shard_map/all_to_all | solution.py:330
  191.3 22.3 %collective-permute-start.24 = (bf16[2,32,3584]{2,1,0:T(8,128)(2,1)S(1)}, bf16[2,32,3584]{2,1,0:T(8,128)(2,1)S(1)}, u32[]{:S(2)}, u32[]{:S(2)}) collective-permute-start(bf16[2,32,3584]{2,1,0:T(8,128)(2,1)S(1)} %pad_maximum_fusion.4), channel_id=1, source_target_pairs={{0,16},{8,24},{16,0},{24,8},{1,17},{9,25},{17,1},{25,9},{2,18},{10... | collective-permute-start | bytes 1376264 | tf_op jit(solution)/shard_map/ppermute | solution.py:255
  192.4 21.3 %collective-permute-start.25 = (bf16[2,32,3584]{2,1,0:T(8,128)(2,1)S(1)}, bf16[2,32,3584]{2,1,0:T(8,128)(2,1)S(1)}, u32[]{:S(2)}, u32[]{:S(2)}) collective-permute-start(bf16[2,32,3584]{2,1,0:T(8,128)(2,1)S(1)} %pad_maximum_fusion.5), channel_id=1, source_target_pairs={{0,24},{8,16},{16,8},{24,0},{1,25},{9,17},{17,9},{25,1},{2,26},{10... | collective-permute-start | bytes 1376264 | tf_op jit(solution)/shard_map/ppermute | solution.py:255
  (28 other events, 215.1 us)

commit v9 on v8

--- a/solution.py
+++ b/solution.py
@@ -254,10 +254,20 @@
     def grp_move(value, flip):
         return lax.ppermute(value, "grp", [(g, g ^ flip) for g in range(groups)])
 
-    held = [grad_output]
-    for step in range(1, chips):
-        held.append(seq_move(held[-1], -1, 0))
-    pairs = [(near, seq_move(near, 0, 1)) for near in held]
+    last = chips - 1
+
+    def product(step, *gates):
+        return chunk_product(*pairs[step], down_weight, group, groups, *gates)
+
+    held, pairs, products = [grad_output], [], []
+    for step in range(chips):
+        if step:
+            held.append(seq_move(held[-1], -1, 0))
+        if step == last:
+            held[-1:] = touch(held[-1:], products[-1][0])
+        pairs.append((held[step], seq_move(held[step], 0, 1)))
+        if step < last:
+            products.append(product(step))
 
     hidden_slab = lax.all_to_all(
         hidden.reshape(block, count, down_slab).transpose(1, 0, 2),
@@ -267,7 +277,19 @@
         tiled=True,
     ).reshape(count * block, down_slab)
 
-    last = chips - 1
+    came = []
+
+    def sum_up(step, gate, sent):
+        others = [grp_move(rows, flip + 1) for flip, rows in enumerate(sent)]
+        (others[0],) = touch([others[0]], gate)
+        sums = add(products[step][0], *others)
+        came.append(seq_move(sums, step, 0) if step else sums)
+        return sums
+
+    for step in range(last - 1):
+        sums = sum_up(step, products[step + 1][0], products[step][1:])
+    products.append(product(last, sums))
+
     grad_slab = jnp.zeros((count, block, up_slab), jnp.bfloat16)
     for step, pair in enumerate(pairs):
         back = ((chip - step) % chips) * CORES
@@ -275,7 +297,6 @@
             columns = lax.dynamic_slice_in_dim(rows, index * up_slab, up_slab, 1)
             grad_slab = lax.dynamic_update_index_in_dim(grad_slab, columns, back + (core ^ flip), 0)
     grad_slab = grad_slab.reshape(count * block, up_slab)
-    products = [chunk_product(near, far, down_weight, group, groups) for near, far in pairs]
     (hidden_slab,) = touch([hidden_slab], products[last][0])
     ranked = project_both(grad_slab, hidden_slab, adapter_up, adapter_down, owner, mask)
 
@@ -296,19 +317,8 @@
         tiled=True,
     ).reshape(count * block, 2 * ranks)
 
-    came = []
-    for step in range(chips):
-        kept, *sent = products[step]
-        if step == last:
-            sent = touch(sent, ranked)
-        others = [grp_move(rows, flip + 1) for flip, rows in enumerate(sent)]
-        if step < last - 1:
-            gate = products[step + 1][0]
-        else:
-            gate = rank_sums if step == last else share
-        (others[0],) = touch([others[0]], gate)
-        sums = add(kept, *others)
-        came.append(seq_move(sums, step, 0) if step else sums)
+    sum_up(last - 1, ranked, products[last - 1][1:])
+    sums = sum_up(last, rank_sums, touch(products[last][1:], ranked))
     (ranked,) = touch([rank_sums], sums)
     grad_rank = ranked[:, :ranks]
 

time: 225 us -> 240 us (1.067)
  starting transfers between devices: 70.1 us -> 89.4 us
  local copies, waits for them, and re-layouts: 30.4 us -> 27.2 us
    ppermute x15, waiting for transfers between devices: 39.9 us -> 26.5 us  [grp_move(): return lax.ppermute(value, 'grp', [(g, g ^ flip) for g in range(groups)])]
    ppermute x11, waiting for transfers between devices: 17.7 us -> 31 us  [seq_move(): return lax.ppermute(value, 'seq', pairs)]
    all_to_all x1, starting transfers between devices: 6.89 us -> 20.2 us  [shards(): lax.all_to_all(ranked.reshape(devices, -1, 2 * ranks), ('grp', 'seq'), sp...]
    all_to_all x1, starting transfers between devices: 3.77 us -> 7.34 us  [shards(): term = lax.all_to_all(term, 'seq', split_axis=0, concat_axis=0, tiled=True)]
    unnamed x44 -> x40, local copies, waits for them, and re-layouts: 14.1 us -> 10.9 us
  transfers between devices with their start and end apart: 30 -> 30, of which waited for: 10 -> 10; matrix products, arithmetic and copies ran while one was open for 16% -> 15% of each run, Pallas kernels for 14% -> 13%
where the time goes in v9:
time: 240 us; the launch traced here: 239 us
  starting transfers between devices  89.4 us (37%)
  waiting for transfers between devices  67.4 us (28%)
  Pallas kernels  33.7 us (14%)
  local copies, waits for them, and re-layouts  27.2 us (11%)
  matrix products  12.1 us (5%)
  other arithmetic  8.3 us (3%)
    ppermute x11, waiting for transfers between devices, seq_move(): return lax.ppermute(value, 'seq', pairs)  31 us
    ppermute x15, waiting for transfers between devices, grp_move(): return lax.ppermute(value, 'grp', [(g, g ^ flip) for g in range(groups)])  26.5 us
    pallas_call x4, Pallas kernels, chunk_product(): pl.pallas_call(functools.partial(chunk_kernel, groups), grid_spec=pltpu.P...  24.8 us
    ppermute x11, starting transfers between devices, seq_move(): return lax.ppermute(value, 'seq', pairs)  23.8 us
    ppermute x15, starting transfers between devices, grp_move(): return lax.ppermute(value, 'grp', [(g, g ^ flip) for g in range(groups)])  22 us
    all_to_all x1, starting transfers between devices, shards(): lax.all_to_all(ranked.reshape(devices, -1, 2 * ranks), ('grp', 'seq'), sp...  20.2 us
    all_to_all x1, starting transfers between devices, shards(): lax.all_to_all(jnp.broadcast_to(share[None], (devices,) + share.shape), (...  12.2 us
    unnamed x40, local copies, waits for them, and re-layouts  10.9 us
  transfers between devices with their start and end apart: 30, of which 10 were waited for; matrix products, arithmetic and copies ran while one was open for 15% of the time, Pallas kernels for 13%

profile of v9, /device:TPU:0, one launch (start us, length us, event | category | flops | bytes accessed | tf_op | source)
XLA Modules:
  0.0 239.0 jit_solution(14313254987830177598)
XLA Ops:
  3.8 3.0 %copy.53 = bf16[16,8,8,896]{3,2,0,1:T(8,128)(2,1)} copy(bf16[16,8,8,896]{3,2,1,0:T(8,128)(2,1)} %bitcast.74) | data formatting | bytes 3670016 | tf_op jit(solution)/shard_map/reshape | solution.py:273
  6.8 4.0 %all-to-all-start = ((bf16[8,128,896]{2,1,0:T(8,128)(2,1)}), bf16[8,128,896]{2,1,0:T(8,128)(2,1)S(1)}, u32[]{:S(2)}, u32[]{:S(2)}) async-start(bf16[8,128,896]{2,1,0:T(8,128)(2,1)} %bitcast.72), calls=%async_computation | async-start | bytes 3670016 | tf_op jit(solution)/shard_map/all_to_all | solution.py:272
  14.2 4.9 %collective-permute-done.2.near_ref = bf16[128,2048]{1,0:T(8,128)(2,1)} collective-permute-done((bf16[128,2048]{1,0:T(8,128)(2,1)}, bf16[128,2048]{1,0:T(8,128)(2,1)}, u32[]{:S(2)}, u32[]{:S(2)}) %collective-permute-start.2) | collective-permute-done | bytes 524320 | tf_op jit(solution)/shard_map/ppermute | solution.py:252
  19.0 4.3 %collective-permute-start.7 = (bf16[128,2048]{1,0:T(8,128)(2,1)}, bf16[128,2048]{1,0:T(8,128)(2,1)S(1)}, u32[]{:S(2)}, u32[]{:S(2)}) collective-permute-start(bf16[128,2048]{1,0:T(8,128)(2,1)} %collective-permute-done.2.near_ref), channel_id=1, source_target_pairs={{0,2},{1,3},{2,4},{3,5},{4,6},{5,7},{6,0},{7,1},{8,10},{9,11},{10,... | collective-permute-start | bytes 1572872 | tf_op jit(solution)/shard_map/ppermute | solution.py:252
  23.4 5.2 %copy-done = bf16[3584,2048]{1,0:T(8,128)(2,1)S(1)} copy-done((bf16[3584,2048]{1,0:T(8,128)(2,1)S(1)}, bf16[3584,2048]{1,0:T(8,128)(2,1)}, u32[]{:S(2)}) %copy-start) | copy-done | bytes 14680088
  28.5 6.1 %shard_map.94 = (bf16[2,32,3584]{2,1,0:T(8,128)(2,1)S(1)}, bf16[2,32,3584]{2,1,0:T(8,128)(2,1)S(1)}, bf16[2,32,3584]{2,1,0:T(8,128)(2,1)}, bf16[2,32,3584]{2,1,0:T(8,128)(2,1)}) custom-call(s32[1]{0:T(128)} %bitcast.place_ref, bf16[128,2048]{1,0:T(8,128)(2,1)S(1)} %copy-done.7, bf16[128,2048]{1,0:T(8,128)(2,1)S(1)} %collective-permute-done.far_ref, ...), custom_call_target="tpu_custom_call" | custom-call | flops 3758096384 | bytes 17563648 | tf_op jit(solution)/shard_map/pallas_call | solution.py:56
  38.2 21.2 %collective-permute-done.7.near_ref = bf16[128,2048]{1,0:T(8,128)(2,1)S(1)} collective-permute-done((bf16[128,2048]{1,0:T(8,128)(2,1)}, bf16[128,2048]{1,0:T(8,128)(2,1)S(1)}, u32[]{:S(2)}, u32[]{:S(2)}) %collective-permute-start.7) | collective-permute-done | bytes 524320 | tf_op jit(solution)/shard_map/ppermute | solution.py:252
  59.4 6.5 %shard_map.95 = (bf16[2,32,3584]{2,1,0:T(8,128)(2,1)S(1)}, bf16[2,32,3584]{2,1,0:T(8,128)(2,1)S(1)}, bf16[2,32,3584]{2,1,0:T(8,128)(2,1)S(1)}, bf16[2,32,3584]{2,1,0:T(8,128)(2,1)S(1)}) custom-call(s32[1]{0:T(128)} %bitcast.place_ref, bf16[128,2048]{1,0:T(8,128)(2,1)} %collective-permute-done.2.near_ref, ...), custom_call_target="tpu_custom_call" | custom-call | flops 3758096384 | bytes 17563648 | tf_op jit(solution)/shard_map/pallas_call | solution.py:56
  69.6 8.6 %collective-permute-start.13 = (bf16[128,2048]{1,0:T(8,128)(2,1)S(1)}, bf16[128,2048]{1,0:T(8,128)(2,1)S(1)}, u32[]{:S(2)}, u32[]{:S(2)}) collective-permute-start(bf16[128,2048]{1,0:T(8,128)(2,1)S(1)} %collective-permute-done.7.near_ref), channel_id=1, source_target_pairs={{0,2},{1,3},{2,4},{3,5},{4,6},{5,7},{6,0},{7,1},{8,10},{9,11},{10,... | collective-permute-start | bytes 1572872 | tf_op jit(solution)/shard_map/ppermute | solution.py:252
  81.0 6.1 %shard_map.97 = (bf16[2,32,3584]{2,1,0:T(8,128)(2,1)S(1)}, bf16[2,32,3584]{2,1,0:T(8,128)(2,1)}, bf16[2,32,3584]{2,1,0:T(8,128)(2,1)}, bf16[2,32,3584]{2,1,0:T(8,128)(2,1)}) custom-call(s32[1]{0:T(128)} %bitcast.place_ref, bf16[128,2048]{1,0:T(8,128)(2,1)S(1)} %collective-permute-done.7.near_ref, bf16[128,2048]{1,0:T(8,128)(2,1)S(1)} %collective-permute-done.8.far_ref, ...), custom_call_target="tpu_custom_call" | custom-call | flops 3758096384 | bytes 17563648 | tf_op jit(solution)/shard_map/pallas_call | solution.py:56
  97.4 6.1 %shard_map.100 = (bf16[2,32,3584]{2,1,0:T(8,128)(2,1)S(1)}, bf16[2,32,3584]{2,1,0:T(8,128)(2,1)S(1)}, bf16[2,32,3584]{2,1,0:T(8,128)(2,1)}, bf16[2,32,3584]{2,1,0:T(8,128)(2,1)S(1)}) custom-call(s32[1]{0:T(128)} %bitcast.place_ref, bf16[128,2048]{1,0:T(8,128)(2,1)S(1)} %shard_map.99.near_ref, bf16[128,2048]{1,0:T(8,128)(2,1)S(1)} %collective-permute-done.14.far_ref, ...), custom_call_target="tpu_custom_call" | custom-call | flops 3758096384 | bytes 17563648 | tf_op jit(solution)/shard_map/pallas_call | solution.py:56
  107.1 6.9 %shard_map.102.refs_1_.refs_3_ = bf16[1024,128]{1,0:T(8,128)(2,1)} custom-call(s32[1024,1]{1,0:T(8,128)} %copy.46.owner_ref, bf16[1024,256]{1,0:T(8,128)(2,1)} %bitcast.10.grad_ref, bf16[1024,896]{1,0:T(8,128)(2,1)} %copy-done.2, bf16[1024,256]{1,0:T(8,128)(2,1)} %bitcast.79, bf16[1024,896]{1,0:T(8,128)(2,1)} %bitcast.78), custom_call_target="tpu_custom_call" | custom-call | flops 2415919104 | bytes 4718592 | tf_op jit(solution)/shard_map/pallas_call | solution.py:183
  113.9 20.2 %all-to-all-start.1 = ((bf16[32,32,128]{2,1,0:T(8,128)(2,1)}), bf16[32,32,128]{2,1,0:T(8,128)(2,1)S(1)}, u32[]{:S(2)}, u32[]{:S(2)}) async-start(bf16[32,32,128]{2,1,0:T(8,128)(2,1)} %bitcast.71), calls=%async_computation.1 | async-start | bytes 524288 | tf_op jit(solution)/shard_map/all_to_all | solution.py:304
  135.5 3.7 %collective-permute-start.11 = (bf16[2,32,3584]{2,1,0:T(8,128)(2,1)}, bf16[2,32,3584]{2,1,0:T(8,128)(2,1)S(1)}, u32[]{:S(2)}, u32[]{:S(2)}) collective-permute-start(bf16[2,32,3584]{2,1,0:T(8,128)(2,1)} %add_convert_fusion.2.rest_0_), channel_id=1, source_target_pairs={{0,6},{1,7},{2,0},{3,1},{4,2},{5,3},{6,4},{7,5},{8,14},{9,15},{10,... | collective-permute-start | bytes 1376264 | tf_op jit(solution)/shard_map/ppermute | solution.py:252
  145.5 12.2 %all-to-all-start.2 = ((bf16[32,32,128]{2,1,0:T(8,128)(2,1)}), bf16[32,32,128]{2,1,0:T(8,128)(2,1)S(1)}, u32[]{:S(2)}, u32[]{:S(2)}) async-start(bf16[32,32,128]{2,1,0:T(8,128)(2,1)} %broadcast_in_dim.73), calls=%async_computation.2 | async-start | bytes 524288 | tf_op jit(solution)/shard_map/all_to_all | solution.py:312
  165.1 3.0 %all-to-all-done.2 = bf16[32,32,128]{2,1,0:T(8,128)(2,1)S(1)} async-done(((bf16[32,32,128]{2,1,0:T(8,128)(2,1)}), bf16[32,32,128]{2,1,0:T(8,128)(2,1)S(1)}, u32[]{:S(2)}, u32[]{:S(2)}) %all-to-all-start.2) | async-done | bytes 262176 | tf_op jit(solution)/shard_map/all_to_all | solution.py:312
  168.1 5.9 %collective-permute-done.20 = bf16[2,32,3584]{2,1,0:T(8,128)(2,1)} collective-permute-done((bf16[2,32,3584]{2,1,0:T(8,128)(2,1)S(1)}, bf16[2,32,3584]{2,1,0:T(8,128)(2,1)}, u32[]{:S(2)}, u32[]{:S(2)}) %collective-permute-start.20) | collective-permute-done | bytes 458784 | tf_op jit(solution)/shard_map/ppermute | solution.py:255
  177.9 5.2 %fusion = bf16[1024,896]{1,0:T(8,128)(2,1)} fusion(bf16[16,64,896]{2,1,0:T(8,128)(2,1)} %param.10, bf16[1024,16]{0,1:T(8,128)(2,1)S(1)} %copy-done.17, bf16[1024,64]{0,1:T(8,128)(2,1)S(1)} %copy.47), kind=kOutput, calls=%fused_computation.1 | convolution fusion | flops 1881931776 | bytes 3833856 | tf_op jit(solution)/shard_map/dot_general | solution.py:328
  183.0 7.3 %all-to-all-start.3 = ((bf16[8,128,896]{2,1,0:T(8,128)(2,1)}), bf16[8,128,896]{2,1,0:T(8,128)(2,1)S(1)}, u32[]{:S(2)}, u32[]{:S(2)}) async-start(bf16[8,128,896]{2,1,0:T(8,128)(2,1)} %bitcast.19.refs_4_), calls=%async_computation.3 | async-start | bytes 3670016 | tf_op jit(solution)/shard_map/all_to_all | solution.py:340
  196.1 2.8 %collective-permute-done.17.refs_2_ = bf16[2,32,3584]{2,1,0:T(8,128)(2,1)S(1)} collective-permute-done((bf16[2,32,3584]{2,1,0:T(8,128)(2,1)}, bf16[2,32,3584]{2,1,0:T(8,128)(2,1)S(1)}, u32[]{:S(2)}, u32[]{:S(2)}) %collective-permute-start.17) | collective-permute-done | bytes 458784 | tf_op jit(solution)/shard_map/ppermute | solution.py:252
  200.8 4.2 %fusion.9 = f32[16,64,896]{2,1,0:T(8,128)} fusion(bf16[1024,896]{1,0:T(8,128)(2,1)S(1)} %copy-done.3, f32[16]{0:T(128)S(1)} %broadcast_divide_fusion, bf16[1024,64]{0,1:T(8,128)(2,1)S(1)} %copy.49, bf16[1024,16]{0,1:T(8,128)(2,1)S(1)} %copy-done.17), kind=kOutput, calls=%fused_computation.10 | convolution fusion | flops 1881014272 | bytes 5668928 | tf_op jit(solution)/shard_map/dot_general | solution.py:19
  209.5 9.5 %collective-permute-done.23.refs_1_ = bf16[2,32,3584]{2,1,0:T(8,128)(2,1)S(1)} collective-permute-done((bf16[2,32,3584]{2,1,0:T(8,128)(2,1)S(1)}, bf16[2,32,3584]{2,1,0:T(8,128)(2,1)S(1)}, u32[]{:S(2)}, u32[]{:S(2)}) %collective-permute-start.23) | collective-permute-done | bytes 458784 | tf_op jit(solution)/shard_map/ppermute | solution.py:255
  219.0 11.0 %collective-permute-done.24.refs_2_ = bf16[2,32,3584]{2,1,0:T(8,128)(2,1)S(1)} collective-permute-done((bf16[2,32,3584]{2,1,0:T(8,128)(2,1)S(1)}, bf16[2,32,3584]{2,1,0:T(8,128)(2,1)S(1)}, u32[]{:S(2)}, u32[]{:S(2)}) %collective-permute-start.24) | collective-permute-done | bytes 458784 | tf_op jit(solution)/shard_map/ppermute | solution.py:255
  230.8 5.1 %all-to-all-done.3.refs_4_ = bf16[8,128,896]{2,1,0:T(8,128)(2,1)S(1)} async-done(((bf16[8,128,896]{2,1,0:T(8,128)(2,1)}), bf16[8,128,896]{2,1,0:T(8,128)(2,1)S(1)}, u32[]{:S(2)}, u32[]{:S(2)}) %all-to-all-start.3) | async-done | bytes 1835040 | tf_op jit(solution)/shard_map/all_to_all | solution.py:340
  (132 shorter events, 65.1 us)
Async XLA Ops:
  0.6 22.7 %collective-permute-start = (bf16[128,2048]{1,0:T(8,128)(2,1)}, bf16[128,2048]{1,0:T(8,128)(2,1)S(1)}, u32[]{:S(2)}, u32[]{:S(2)}) collective-permute-start(bf16[128,2048]{1,0:T(8,128)(2,1)} %near_ref.1), channel_id=1, source_target_pairs={{0,1},{1,0},{2,3},{3,2},{4,5},{5,4},{6,7},{7,6},{8,9},{9,8},{10,11... | collective-permute-start | bytes 1572872 | tf_op jit(solution)/shard_map/ppermute | solution.py:252
  6.8 99.0 %all-to-all-start = ((bf16[8,128,896]{2,1,0:T(8,128)(2,1)}), bf16[8,128,896]{2,1,0:T(8,128)(2,1)S(1)}, u32[]{:S(2)}, u32[]{:S(2)}) async-start(bf16[8,128,896]{2,1,0:T(8,128)(2,1)} %bitcast.72), calls=%async_computation | async-start | bytes 3670016 | tf_op jit(solution)/shard_map/all_to_all | solution.py:272
  19.0 40.4 %collective-permute-start.7 = (bf16[128,2048]{1,0:T(8,128)(2,1)}, bf16[128,2048]{1,0:T(8,128)(2,1)S(1)}, u32[]{:S(2)}, u32[]{:S(2)}) collective-permute-start(bf16[128,2048]{1,0:T(8,128)(2,1)} %collective-permute-done.2.near_ref), channel_id=1, source_target_pairs={{0,2},{1,3},{2,4},{3,5},{4,6},{5,7},{6,0},{7,1},{8,10},{9,11},{10,... | collective-permute-start | bytes 1572872 | tf_op jit(solution)/shard_map/ppermute | solution.py:252
  23.3 36.1 %collective-permute-start.3 = (bf16[128,2048]{1,0:T(8,128)(2,1)}, bf16[128,2048]{1,0:T(8,128)(2,1)S(1)}, u32[]{:S(2)}, u32[]{:S(2)}) collective-permute-start(bf16[128,2048]{1,0:T(8,128)(2,1)} %collective-permute-done.2.near_ref), channel_id=1, source_target_pairs={{0,1},{1,0},{2,3},{3,2},{4,5},{5,4},{6,7},{7,6},{8,9},{9,8},{10,11... | collective-permute-start | bytes 1572872 | tf_op jit(solution)/shard_map/ppermute | solution.py:252
  34.6 35.0 %collective-permute-start.1 = (bf16[2,32,3584]{2,1,0:T(8,128)(2,1)S(1)}, bf16[2,32,3584]{2,1,0:T(8,128)(2,1)S(1)}, u32[]{:S(2)}, u32[]{:S(2)}) collective-permute-start(bf16[2,32,3584]{2,1,0:T(8,128)(2,1)S(1)} %get-tuple-element.28), channel_id=1, source_target_pairs={{0,8},{8,0},{16,24},{24,16},{1,9},{9,1},{17,25},{25,17},{2,10},{10... | collective-permute-start | bytes 1376264 | tf_op jit(solution)/shard_map/ppermute | solution.py:255
  59.4 20.0 %collective-permute-start.8 = (bf16[128,2048]{1,0:T(8,128)(2,1)S(1)}, bf16[128,2048]{1,0:T(8,128)(2,1)S(1)}, u32[]{:S(2)}, u32[]{:S(2)}) collective-permute-start(bf16[128,2048]{1,0:T(8,128)(2,1)S(1)} %collective-permute-done.7.near_ref), channel_id=1, source_target_pairs={{0,1},{1,0},{2,3},{3,2},{4,5},{5,4},{6,7},{7,6},{8,9},{9,8},{10,11... | collective-permute-start | bytes 1572872 | tf_op jit(solution)/shard_map/ppermute | solution.py:252
  66.0 25.6 %collective-permute-start.6 = (bf16[2,32,3584]{2,1,0:T(8,128)(2,1)S(1)}, bf16[2,32,3584]{2,1,0:T(8,128)(2,1)S(1)}, u32[]{:S(2)}, u32[]{:S(2)}) collective-permute-start(bf16[2,32,3584]{2,1,0:T(8,128)(2,1)S(1)} %get-tuple-element.32), channel_id=1, source_target_pairs={{0,8},{8,0},{16,24},{24,16},{1,9},{9,1},{17,25},{25,17},{2,10},{10... | collective-permute-start | bytes 1376264 | tf_op jit(solution)/shard_map/ppermute | solution.py:255
  67.6 24.6 %collective-permute-start.9 = (bf16[2,32,3584]{2,1,0:T(8,128)(2,1)S(1)}, bf16[2,32,3584]{2,1,0:T(8,128)(2,1)S(1)}, u32[]{:S(2)}, u32[]{:S(2)}) collective-permute-start(bf16[2,32,3584]{2,1,0:T(8,128)(2,1)S(1)} %get-tuple-element.34), channel_id=1, source_target_pairs={{0,16},{8,24},{16,0},{24,8},{1,17},{9,25},{17,1},{25,9},{2,18},{10... | collective-permute-start | bytes 1376264 | tf_op jit(solution)/shard_map/ppermute | solution.py:255
  69.1 23.6 %collective-permute-start.10 = (bf16[2,32,3584]{2,1,0:T(8,128)(2,1)S(1)}, bf16[2,32,3584]{2,1,0:T(8,128)(2,1)S(1)}, u32[]{:S(2)}, u32[]{:S(2)}) collective-permute-start(bf16[2,32,3584]{2,1,0:T(8,128)(2,1)S(1)} %get-tuple-element.35), channel_id=1, source_target_pairs={{0,24},{8,16},{16,8},{24,0},{1,25},{9,17},{17,9},{25,1},{2,26},{10... | collective-permute-start | bytes 1376264 | tf_op jit(solution)/shard_map/ppermute | solution.py:255
  79.5 54.6 %collective-permute-start.4 = (bf16[2,32,3584]{2,1,0:T(8,128)(2,1)}, bf16[2,32,3584]{2,1,0:T(8,128)(2,1)}, u32[]{:S(2)}, u32[]{:S(2)}) collective-permute-start(bf16[2,32,3584]{2,1,0:T(8,128)(2,1)} %get-tuple-element.30), channel_id=1, source_target_pairs={{0,16},{8,24},{16,0},{24,8},{1,17},{9,25},{17,1},{25,9},{2,18},{10... | collective-permute-start | bytes 1376264 | tf_op jit(solution)/shard_map/ppermute | solution.py:255
  89.2 44.9 %collective-permute-start.5 = (bf16[2,32,3584]{2,1,0:T(8,128)(2,1)}, bf16[2,32,3584]{2,1,0:T(8,128)(2,1)}, u32[]{:S(2)}, u32[]{:S(2)}) collective-permute-start(bf16[2,32,3584]{2,1,0:T(8,128)(2,1)} %get-tuple-element.31), channel_id=1, source_target_pairs={{0,24},{8,16},{16,8},{24,0},{1,25},{9,17},{17,9},{25,1},{2,26},{10... | collective-permute-start | bytes 1376264 | tf_op jit(solution)/shard_map/ppermute | solution.py:255
  91.6 49.8 %collective-permute-start.12 = (bf16[2,32,3584]{2,1,0:T(8,128)(2,1)}, bf16[2,32,3584]{2,1,0:T(8,128)(2,1)}, u32[]{:S(2)}, u32[]{:S(2)}) collective-permute-start(bf16[2,32,3584]{2,1,0:T(8,128)(2,1)} %get-tuple-element.36), channel_id=1, source_target_pairs={{0,8},{8,0},{16,24},{24,16},{1,9},{9,1},{17,25},{25,17},{2,10},{10... | collective-permute-start | bytes 1376264 | tf_op jit(solution)/shard_map/ppermute | solution.py:255
  92.2 65.5 %collective-permute-start.15 = (bf16[2,32,3584]{2,1,0:T(8,128)(2,1)}, bf16[2,32,3584]{2,1,0:T(8,128)(2,1)}, u32[]{:S(2)}, u32[]{:S(2)}) collective-permute-start(bf16[2,32,3584]{2,1,0:T(8,128)(2,1)} %get-tuple-element.38), channel_id=1, source_target_pairs={{0,16},{8,24},{16,0},{24,8},{1,17},{9,25},{17,1},{25,9},{2,18},{10... | collective-permute-start | bytes 1376264 | tf_op jit(solution)/shard_map/ppermute | solution.py:255
  95.0 65.4 %collective-permute-start.16 = (bf16[2,32,3584]{2,1,0:T(8,128)(2,1)}, bf16[2,32,3584]{2,1,0:T(8,128)(2,1)}, u32[]{:S(2)}, u32[]{:S(2)}) collective-permute-start(bf16[2,32,3584]{2,1,0:T(8,128)(2,1)} %get-tuple-element.39), channel_id=1, source_target_pairs={{0,24},{8,16},{16,8},{24,0},{1,25},{9,17},{17,9},{25,1},{2,26},{10... | collective-permute-start | bytes 1376264 | tf_op jit(solution)/shard_map/ppermute | solution.py:255
  113.9 30.7 %all-to-all-start.1 = ((bf16[32,32,128]{2,1,0:T(8,128)(2,1)}), bf16[32,32,128]{2,1,0:T(8,128)(2,1)S(1)}, u32[]{:S(2)}, u32[]{:S(2)}) async-start(bf16[32,32,128]{2,1,0:T(8,128)(2,1)} %bitcast.71), calls=%async_computation.1 | async-start | bytes 524288 | tf_op jit(solution)/shard_map/all_to_all | solution.py:304
  135.5 60.6 %collective-permute-start.11 = (bf16[2,32,3584]{2,1,0:T(8,128)(2,1)}, bf16[2,32,3584]{2,1,0:T(8,128)(2,1)S(1)}, u32[]{:S(2)}, u32[]{:S(2)}) collective-permute-start(bf16[2,32,3584]{2,1,0:T(8,128)(2,1)} %add_convert_fusion.2.rest_0_), channel_id=1, source_target_pairs={{0,6},{1,7},{2,0},{3,1},{4,2},{5,3},{6,4},{7,5},{8,14},{9,15},{10,... | collective-permute-start | bytes 1376264 | tf_op jit(solution)/shard_map/ppermute | solution.py:252
  140.0 25.1 %collective-permute-start.18 = (bf16[2,32,3584]{2,1,0:T(8,128)(2,1)}, bf16[2,32,3584]{2,1,0:T(8,128)(2,1)S(1)}, u32[]{:S(2)}, u32[]{:S(2)}) collective-permute-start(bf16[2,32,3584]{2,1,0:T(8,128)(2,1)} %copy-done.12), channel_id=1, source_target_pairs={{0,8},{8,0},{16,24},{24,16},{1,9},{9,1},{17,25},{25,17},{2,10},{10... | collective-permute-start | bytes 1376264 | tf_op jit(solution)/shard_map/ppermute | solution.py:255
  141.5 26.6 %collective-permute-start.19 = (bf16[2,32,3584]{2,1,0:T(8,128)(2,1)}, bf16[2,32,3584]{2,1,0:T(8,128)(2,1)}, u32[]{:S(2)}, u32[]{:S(2)}) collective-permute-start(bf16[2,32,3584]{2,1,0:T(8,128)(2,1)} %get-tuple-element.44), channel_id=1, source_target_pairs={{0,16},{8,24},{16,0},{24,8},{1,17},{9,25},{17,1},{25,9},{2,18},{10... | collective-permute-start | bytes 1376264 | tf_op jit(solution)/shard_map/ppermute | solution.py:255
  145.5 22.6 %all-to-all-start.2 = ((bf16[32,32,128]{2,1,0:T(8,128)(2,1)}), bf16[32,32,128]{2,1,0:T(8,128)(2,1)S(1)}, u32[]{:S(2)}, u32[]{:S(2)}) async-start(bf16[32,32,128]{2,1,0:T(8,128)(2,1)} %broadcast_in_dim.73), calls=%async_computation.2 | async-start | bytes 524288 | tf_op jit(solution)/shard_map/all_to_all | solution.py:312
  162.7 36.3 %collective-permute-start.17 = (bf16[2,32,3584]{2,1,0:T(8,128)(2,1)}, bf16[2,32,3584]{2,1,0:T(8,128)(2,1)S(1)}, u32[]{:S(2)}, u32[]{:S(2)}) collective-permute-start(bf16[2,32,3584]{2,1,0:T(8,128)(2,1)} %add_convert_fusion.1), channel_id=1, source_target_pairs={{0,4},{1,5},{2,6},{3,7},{4,0},{5,1},{6,2},{7,3},{8,12},{9,13},{10,... | collective-permute-start | bytes 1376264 | tf_op jit(solution)/shard_map/ppermute | solution.py:252
  176.2 22.7 %collective-permute-start.21 = (bf16[2,32,3584]{2,1,0:T(8,128)(2,1)}, bf16[2,32,3584]{2,1,0:T(8,128)(2,1)}, u32[]{:S(2)}, u32[]{:S(2)}) collective-permute-start(bf16[2,32,3584]{2,1,0:T(8,128)(2,1)} %add_convert_fusion.refs_1_), channel_id=1, source_target_pairs={{0,2},{1,3},{2,4},{3,5},{4,6},{5,7},{6,0},{7,1},{8,10},{9,11},{10,... | collective-permute-start | bytes 1376264 | tf_op jit(solution)/shard_map/ppermute | solution.py:252
  183.0 52.8 %all-to-all-start.3 = ((bf16[8,128,896]{2,1,0:T(8,128)(2,1)}), bf16[8,128,896]{2,1,0:T(8,128)(2,1)S(1)}, u32[]{:S(2)}, u32[]{:S(2)}) async-start(bf16[8,128,896]{2,1,0:T(8,128)(2,1)} %bitcast.19.refs_4_), calls=%async_computation.3 | async-start | bytes 3670016 | tf_op jit(solution)/shard_map/all_to_all | solution.py:340
  207.8 22.3 %collective-permute-start.24 = (bf16[2,32,3584]{2,1,0:T(8,128)(2,1)S(1)}, bf16[2,32,3584]{2,1,0:T(8,128)(2,1)S(1)}, u32[]{:S(2)}, u32[]{:S(2)}) collective-permute-start(bf16[2,32,3584]{2,1,0:T(8,128)(2,1)S(1)} %pad_maximum_fusion.4), channel_id=1, source_target_pairs={{0,16},{8,24},{16,0},{24,8},{1,17},{9,25},{17,1},{25,9},{2,18},{10... | collective-permute-start | bytes 1376264 | tf_op jit(solution)/shard_map/ppermute | solution.py:255
  209.3 20.7 %collective-permute-start.25 = (bf16[2,32,3584]{2,1,0:T(8,128)(2,1)S(1)}, bf16[2,32,3584]{2,1,0:T(8,128)(2,1)S(1)}, u32[]{:S(2)}, u32[]{:S(2)}) collective-permute-start(bf16[2,32,3584]{2,1,0:T(8,128)(2,1)S(1)} %pad_maximum_fusion.5), channel_id=1, source_target_pairs={{0,24},{8,16},{16,8},{24,0},{1,25},{9,17},{17,9},{25,1},{2,26},{10... | collective-permute-start | bytes 1376264 | tf_op jit(solution)/shard_map/ppermute | solution.py:255
  (26 other events, 292.4 us)

commit v10 on v1

--- a/solution.py
+++ b/solution.py
@@ -12,6 +12,7 @@
 CONTRACT_ROWS = (((0,), (0,)), ((), ()))
 CORES = 2
 MOST_ROWS = 1024
+ANYWHERE = pl.BlockSpec(memory_space=pl.ANY)
 
 
 def dot(left, right, dims):
@@ -110,6 +111,7 @@
             out_specs=pl.BlockSpec((part, each * width), lambda at, place: (place[0] ^ at, 0)),
         ),
         out_shape=jax.ShapeDtypeStruct((block, each * width), jnp.bfloat16),
+        compiler_params=pltpu.CompilerParams(vmem_limit_bytes=24 << 20),
         cost_estimate=pl.CostEstimate(
             flops=block * each * width, bytes_accessed=6 * block * each * width, transcendentals=0
         ),
@@ -118,6 +120,21 @@
 
 def add(*terms):
     return sum(term.astype(jnp.float32) for term in terms).astype(jnp.bfloat16)
+
+
+def touch_kernel(*refs):
+    pass
+
+
+def touch(values, *gates):
+    return pl.pallas_call(
+        touch_kernel,
+        in_specs=[ANYWHERE] * (len(values) + len(gates)),
+        out_specs=[ANYWHERE] * len(values),
+        out_shape=[jax.ShapeDtypeStruct(value.shape, value.dtype) for value in values],
+        input_output_aliases={at: at for at in range(len(values))},
+        compiler_params=pltpu.CompilerParams(vmem_limit_bytes=1 << 20),
+    )(*values, *gates)
 
 
 def after(value, *others):
@@ -219,7 +236,10 @@
     def total(step, seconds, *gates):
         near_kept, _, far_kept, _ = products[step]
         near_came, far_came = firsts[step]
-        near_last, far_last = lax.optimization_barrier(seconds + gates)[:2]
+        if step == last - 1:
+            near_last, far_last = touch(seconds, *gates)
+        else:
+            near_last, far_last = lax.optimization_barrier(seconds + gates)[:2]
         return (
             add(near_kept[0], near_came[0], near_last),
             add(far_kept[0], far_came[0], far_last),

time: 217 us -> 223 us (1.028)
  waiting for transfers between devices: 82.4 us -> 66.4 us
  local copies, waits for them, and re-layouts: 19.2 us -> 33.5 us
  other arithmetic: 7.19 us -> 14.5 us
    ppermute x19, waiting for transfers between devices: 27.7 us -> 17.8 us  [grp_move(): return lax.ppermute(value, 'grp', [(g, g ^ flip) for g in range(groups)])]
    convert_element_type x16, other arithmetic: 6.04 us -> 11.4 us  [add(): sum((term.astype(jnp.float32) for term in terms)).astype(jnp.bfloat16)]
    dynamic_update_slice x8, local copies, waits for them, and re-layouts: 0.09 us -> 5.05 us  [shards(): lax.dynamic_update_index_in_dim(grad_slab, columns, back + (core ^ flip), 0)]
    ppermute x14, waiting for transfers between devices: 20.3 us -> 17.1 us  [seq_move(): return lax.ppermute(value, 'seq', pairs)]
    dynamic_update_slice x8, local copies, waits for them, and re-layouts: 6.41 us -> 8.97 us  [put(): lax.dynamic_update_index_in_dim(arrived, came[flip], ahead + (core ^ flip...]
    ppermute x14, starting transfers between devices: 24.7 us -> 22.2 us  [seq_move(): return lax.ppermute(value, 'seq', pairs)]
    unnamed x24 -> x50, local copies, waits for them, and re-layouts: 5.22 us -> 7.25 us
  transfers between devices with their start and end apart: 37 -> 37, of which waited for: 16 -> 11; matrix products, arithmetic and copies ran while one was open for 18% -> 26% of each run, Pallas kernels for 10% -> 10%
where the time goes in v10:
time: 223 us; the launch traced here: 222 us
  waiting for transfers between devices  66.4 us (30%)
  starting transfers between devices  62 us (28%)
  local copies, waits for them, and re-layouts  33.5 us (15%)
  Pallas kernels  26.3 us (12%)
  matrix products  17.7 us (8%)
  other arithmetic  14.5 us (7%)
    ppermute x19, starting transfers between devices, grp_move(): return lax.ppermute(value, 'grp', [(g, g ^ flip) for g in range(groups)])  23.3 us
    pallas_call x4, Pallas kernels, chunk_product(): pl.pallas_call(functools.partial(chunk_kernel, STAGES), grid_spec=pltpu.P...  22.3 us
    ppermute x14, starting transfers between devices, seq_move(): return lax.ppermute(value, 'seq', pairs)  22.2 us
    ppermute x19, waiting for transfers between devices, grp_move(): return lax.ppermute(value, 'grp', [(g, g ^ flip) for g in range(groups)])  17.8 us
    ppermute x14, waiting for transfers between devices, seq_move(): return lax.ppermute(value, 'seq', pairs)  17.1 us
    all_to_all x1, waiting for transfers between devices, shards(): term = lax.all_to_all(term, 'seq', split_axis=0, concat_axis=0, tiled=True)  15.1 us
    dot_general x4, matrix products, dot(): lax.dot_general(left, right, dims, preferred_element_type=jnp.float32)  14.1 us
    convert_element_type x16, other arithmetic, add(): sum((term.astype(jnp.float32) for term in terms)).astype(jnp.bfloat16)  11.4 us
  transfers between devices with their start and end apart: 37, of which 11 were waited for; matrix products, arithmetic and copies ran while one was open for 26% of the time, Pallas kernels for 10%

profile of v10, /device:TPU:0, one launch (start us, length us, event | category | flops | bytes accessed | tf_op | source)
XLA Modules:
  0.0 221.7 jit_solution(15566705908929184182)
XLA Ops:
  3.8 3.0 %copy.46 = bf16[16,8,8,896]{3,2,0,1:T(8,128)(2,1)} copy(bf16[16,8,8,896]{3,2,1,0:T(8,128)(2,1)} %bitcast.138) | data formatting | bytes 3670016 | tf_op jit(solution)/shard_map/reshape | solution.py:208
  6.8 4.4 %all-to-all-start = ((bf16[8,128,896]{2,1,0:T(8,128)(2,1)}), bf16[8,128,896]{2,1,0:T(8,128)(2,1)}, u32[]{:S(2)}, u32[]{:S(2)}) async-start(bf16[8,128,896]{2,1,0:T(8,128)(2,1)} %bitcast.133), calls=%async_computation | async-start | bytes 3670016 | tf_op jit(solution)/shard_map/all_to_all | solution.py:207
  12.4 6.5 %collective-permute-done.3.near_ref = bf16[128,2048]{1,0:T(8,128)(2,1)S(1)} collective-permute-done((bf16[128,2048]{1,0:T(8,128)(2,1)}, bf16[128,2048]{1,0:T(8,128)(2,1)S(1)}, u32[]{:S(2)}, u32[]{:S(2)}) %collective-permute-start.3) | collective-permute-done | bytes 524320 | tf_op jit(solution)/shard_map/ppermute | solution.py:197
  20.4 5.2 %copy-done.1 = bf16[3584,2048]{1,0:T(8,128)(2,1)S(1)} copy-done((bf16[3584,2048]{1,0:T(8,128)(2,1)S(1)}, bf16[3584,2048]{1,0:T(8,128)(2,1)}, u32[]{:S(2)}) %copy-start.1) | copy-done | bytes 14680088
  25.6 5.4 %shard_map.94 = (bf16[2,32,3584]{2,1,0:T(8,128)(2,1)S(1)}, bf16[2,32,3584]{2,1,0:T(8,128)(2,1)S(1)}, bf16[2,32,3584]{2,1,0:T(8,128)(2,1)S(1)}, bf16[2,32,3584]{2,1,0:T(8,128)(2,1)S(1)}) custom-call(s32[1]{0:T(128)} %bitcast.place_ref, bf16[128,2048]{1,0:T(8,128)(2,1)S(1)} %copy-done.3, bf16[128,2048]{1,0:T(8,128)(2,1)S(1)} %collective-permute-done.far_ref, ...), custom_call_target="tpu_custom_call" | custom-call | flops 3758096384 | bytes 17563648 | tf_op jit(solution)/shard_map/pallas_call | solution.py:57
  34.3 4.3 %collective-permute-start.10 = (bf16[128,2048]{1,0:T(8,128)(2,1)S(1)}, bf16[128,2048]{1,0:T(8,128)(2,1)S(1)}, u32[]{:S(2)}, u32[]{:S(2)}) collective-permute-start(bf16[128,2048]{1,0:T(8,128)(2,1)S(1)} %collective-permute-done.3.near_ref), channel_id=1, source_target_pairs={{0,2},{1,3},{2,4},{3,5},{4,6},{5,7},{6,0},{7,1},{8,10},{9,11},{10,... | collective-permute-start | bytes 1572872 | tf_op jit(solution)/shard_map/ppermute | solution.py:197
  39.2 5.4 %shard_map.95 = (bf16[2,32,3584]{2,1,0:T(8,128)(2,1)S(1)}, bf16[2,32,3584]{2,1,0:T(8,128)(2,1)S(1)}, bf16[2,32,3584]{2,1,0:T(8,128)(2,1)S(1)}, bf16[2,32,3584]{2,1,0:T(8,128)(2,1)S(1)}) custom-call(s32[1]{0:T(128)} %bitcast.place_ref, bf16[128,2048]{1,0:T(8,128)(2,1)S(1)} %collective-permute-done.3.near_ref, ...), custom_call_target="tpu_custom_call" | custom-call | flops 3758096384 | bytes 17563648 | tf_op jit(solution)/shard_map/pallas_call | solution.py:57
  50.3 9.1 %collective-permute-done.10.near_ref = bf16[128,2048]{1,0:T(8,128)(2,1)S(1)} collective-permute-done((bf16[128,2048]{1,0:T(8,128)(2,1)S(1)}, bf16[128,2048]{1,0:T(8,128)(2,1)S(1)}, u32[]{:S(2)}, u32[]{:S(2)}) %collective-permute-start.10) | collective-permute-done | bytes 524320 | tf_op jit(solution)/shard_map/ppermute | solution.py:197
  60.7 8.5 %collective-permute-start.18 = (bf16[128,2048]{1,0:T(8,128)(2,1)S(1)}, bf16[128,2048]{1,0:T(8,128)(2,1)S(1)}, u32[]{:S(2)}, u32[]{:S(2)}) collective-permute-start(bf16[128,2048]{1,0:T(8,128)(2,1)S(1)} %collective-permute-done.10.near_ref), channel_id=1, source_target_pairs={{0,2},{1,3},{2,4},{3,5},{4,6},{5,7},{6,0},{7,1},{8,10},{9,11},{10,... | collective-permute-start | bytes 1572872 | tf_op jit(solution)/shard_map/ppermute | solution.py:197
  69.6 5.4 %shard_map.96 = (bf16[2,32,3584]{2,1,0:T(8,128)(2,1)S(1)}, bf16[2,32,3584]{2,1,0:T(8,128)(2,1)S(1)}, bf16[2,32,3584]{2,1,0:T(8,128)(2,1)S(1)}, bf16[2,32,3584]{2,1,0:T(8,128)(2,1)S(1)}) custom-call(s32[1]{0:T(128)} %bitcast.place_ref, bf16[128,2048]{1,0:T(8,128)(2,1)S(1)} %collective-permute-done.10.near_ref, ...), custom_call_target="tpu_custom_call" | custom-call | flops 3758096384 | bytes 17563648 | tf_op jit(solution)/shard_map/pallas_call | solution.py:57
  92.0 6.0 %shard_map.97 = (bf16[2,32,3584]{2,1,0:T(8,128)(2,1)S(1)}, bf16[2,32,3584]{2,1,0:T(8,128)(2,1)}, bf16[2,32,3584]{2,1,0:T(8,128)(2,1)S(1)}, bf16[2,32,3584]{2,1,0:T(8,128)(2,1)S(1)}) custom-call(s32[1]{0:T(128)} %bitcast.place_ref, bf16[128,2048]{1,0:T(8,128)(2,1)S(1)} %collective-permute-done.18.near_ref, ...), custom_call_target="tpu_custom_call" | custom-call | flops 3758096384 | bytes 17563648 | tf_op jit(solution)/shard_map/pallas_call | solution.py:57
  103.6 3.9 %multiply_reduce_fusion = bf16[1024,64]{0,1:T(8,128)(2,1)S(1)} fusion(f32[1024,16]{0,1:T(8,128)S(1)} %copy-done.20, bf16[16,64,896]{2,1,0:T(8,128)(2,1)S(1)} %copy-done, bf16[1024,896]{1,0:T(8,128)(2,1)} %bitcast.24), kind=kOutput, calls=%fused_computation | convolution fusion | flops 1881079808 | bytes 3866624 | tf_op jit(solution)/shard_map/dot_general | solution.py:19
  118.5 6.0 %collective-permute-done.25 = bf16[2,32,3584]{2,1,0:T(8,128)(2,1)S(1)} collective-permute-done((bf16[2,32,3584]{2,1,0:T(8,128)(2,1)}, bf16[2,32,3584]{2,1,0:T(8,128)(2,1)S(1)}, u32[]{:S(2)}, u32[]{:S(2)}) %collective-permute-start.25) | collective-permute-done | bytes 458784 | tf_op jit(solution)/shard_map/ppermute | solution.py:200
  136.8 7.1 %all-to-all-done.1 = bf16[32,32,128]{2,1,0:T(8,128)(2,1)S(1)} async-done(((bf16[32,32,128]{2,1,0:T(8,128)(2,1)}), bf16[32,32,128]{2,1,0:T(8,128)(2,1)S(1)}, u32[]{:S(2)}, u32[]{:S(2)}) %all-to-all-start.1) | async-done | bytes 262176 | tf_op jit(solution)/shard_map/all_to_all | solution.py:278
  148.5 5.2 %all-to-all-start.2 = ((bf16[32,32,128]{2,1,0:T(8,128)(2,1)}), bf16[32,32,128]{2,1,0:T(8,128)(2,1)S(1)}, u32[]{:S(2)}, u32[]{:S(2)}) async-start(bf16[32,32,128]{2,1,0:T(8,128)(2,1)} %broadcast_in_dim.110), calls=%async_computation.2 | async-start | bytes 524288 | tf_op jit(solution)/shard_map/all_to_all | solution.py:291
  156.9 9.3 %all-to-all-done.2 = bf16[32,32,128]{2,1,0:T(8,128)(2,1)S(1)} async-done(((bf16[32,32,128]{2,1,0:T(8,128)(2,1)}), bf16[32,32,128]{2,1,0:T(8,128)(2,1)S(1)}, u32[]{:S(2)}, u32[]{:S(2)}) %all-to-all-start.2) | async-done | bytes 262176 | tf_op jit(solution)/shard_map/all_to_all | solution.py:291
  166.3 3.6 %fusion = bf16[1024,896]{1,0:T(8,128)(2,1)} fusion(bf16[16,64,896]{2,1,0:T(8,128)(2,1)S(1)} %copy-done, bf16[1024,16]{0,1:T(8,128)(2,1)S(1)} %copy-done.21, bf16[1024,64]{0,1:T(8,128)(2,1)S(1)} %copy.41), kind=kOutput, calls=%fused_computation.3 | convolution fusion | flops 1881931776 | bytes 3833856 | tf_op jit(solution)/shard_map/dot_general | solution.py:307
  170.0 4.3 %all-to-all-start.3 = ((bf16[8,128,896]{2,1,0:T(8,128)(2,1)}), bf16[8,128,896]{2,1,0:T(8,128)(2,1)}, u32[]{:S(2)}, u32[]{:S(2)}) async-start(bf16[8,128,896]{2,1,0:T(8,128)(2,1)} %bitcast.139), calls=%async_computation.3 | async-start | bytes 3670016 | tf_op jit(solution)/shard_map/all_to_all | solution.py:319
  176.7 2.7 %constant_dynamic-slice_fusion = (bf16[2,32,3584]{2,1,0:T(8,128)(2,1)}, bf16[2,32,3584]{2,1,0:T(8,128)(2,1)}, bf16[2,32,3584]{2,1,0:T(8,128)(2,1)}, bf16[2,32,3584]{2,1,0:T(8,128)(2,1)S(1)}) fusion(bf16[8,32,3584]{2,1,0:T(8,128)(2,1)} %bitcast_dynamic-update-slice_fusion, s32[]{:T(128)S(6)} %select_n.141, s32[]{:T(128)S(6)} %select_n.140, s32[]{:T(128)S(6)} %select_n.139, ...), kind=kLoop, calls=%fused_computation.82 | loop fusion | bytes 3670032 | tf_op jit(solution)/shard_map/dynamic_slice | solution.py:324
  185.9 2.7 %fusion.15 = f32[16,64,256]{2,1,0:T(8,128)} fusion(bf16[1024,256,1]{1,0,2:T(8,128)(2,1)} %bitcast.51, bf16[1024,64]{0,1:T(8,128)(2,1)S(1)} %copy.43, bf16[1024,16]{0,1:T(8,128)(2,1)S(1)} %copy-done.21, f32[16]{0:T(128)S(1)} %broadcast_divide_fusion), kind=kOutput, calls=%fused_computation.15 | convolution fusion | flops 538181632 | bytes 1736768 | tf_op jit(solution)/shard_map/dot_general | solution.py:19
  188.6 5.7 %fusion.9 = f32[16,64,896]{2,1,0:T(8,128)} fusion(bf16[1024,896,1]{1,0,2:T(8,128)(2,1)} %bitcast.47, f32[16]{0:T(128)S(1)} %broadcast_divide_fusion, bf16[1024,64]{0,1:T(8,128)(2,1)S(1)} %copy.42, bf16[1024,16]{0,1:T(8,128)(2,1)S(1)} %copy-done.21), kind=kOutput, calls=%fused_computation.12 | convolution fusion | flops 1881014272 | bytes 5668928 | tf_op jit(solution)/shard_map/dot_general | solution.py:19
  194.2 8.4 %collective-permute-done.32.refs_3_ = bf16[2,32,3584]{2,1,0:T(8,128)(2,1)} collective-permute-done((bf16[2,32,3584]{2,1,0:T(8,128)(2,1)}, bf16[2,32,3584]{2,1,0:T(8,128)(2,1)}, u32[]{:S(2)}, u32[]{:S(2)}) %collective-permute-start.32) | collective-permute-done | bytes 458784 | tf_op jit(solution)/shard_map/ppermute | solution.py:200
  202.6 15.1 %all-to-all-done.3.refs_4_ = bf16[8,128,896]{2,1,0:T(8,128)(2,1)} async-done(((bf16[8,128,896]{2,1,0:T(8,128)(2,1)}), bf16[8,128,896]{2,1,0:T(8,128)(2,1)}, u32[]{:S(2)}, u32[]{:S(2)}) %all-to-all-start.3) | async-done | bytes 1835040 | tf_op jit(solution)/shard_map/all_to_all | solution.py:319
  217.7 4.0 %shard_map.99 = bf16[128,7168]{1,0:T(8,128)(2,1)} custom-call(s32[1]{0:T(128)} %bitcast.place_ref, bf16[2,32,3584]{2,1,0:T(8,128)(2,1)S(1)} %get-tuple-element.96.refs_0_, bf16[2,32,3584]{2,1,0:T(8,128)(2,1)S(1)} %collective-permute-done.30.refs_1_, bf16[2,32,3584]{2,1,0:T(8,128)(2,1)S(1)} %collective-permute-done.31.refs_2_, ...), custom_call_target="tpu_custom_call" | custom-call | flops 917504 | bytes 5505024 | tf_op jit(solution)/shard_map/pallas_call | solution.py:104
  (163 shorter events, 79.2 us)
Async XLA Ops:
  0.6 19.8 %collective-permute-start = (bf16[128,2048]{1,0:T(8,128)(2,1)}, bf16[128,2048]{1,0:T(8,128)(2,1)S(1)}, u32[]{:S(2)}, u32[]{:S(2)}) collective-permute-start(bf16[128,2048]{1,0:T(8,128)(2,1)} %near_ref.1), channel_id=1, source_target_pairs={{0,1},{1,0},{2,3},{3,2},{4,5},{5,4},{6,7},{7,6},{8,9},{9,8},{10,11... | collective-permute-start | bytes 1572872 | tf_op jit(solution)/shard_map/ppermute | solution.py:197
  1.2 17.8 %collective-permute-start.3 = (bf16[128,2048]{1,0:T(8,128)(2,1)}, bf16[128,2048]{1,0:T(8,128)(2,1)S(1)}, u32[]{:S(2)}, u32[]{:S(2)}) collective-permute-start(bf16[128,2048]{1,0:T(8,128)(2,1)} %near_ref.1), channel_id=1, source_target_pairs={{0,2},{1,3},{2,4},{3,5},{4,6},{5,7},{6,0},{7,1},{8,10},{9,11},{10,... | collective-permute-start | bytes 1572872 | tf_op jit(solution)/shard_map/ppermute | solution.py:197
  6.8 96.7 %all-to-all-start = ((bf16[8,128,896]{2,1,0:T(8,128)(2,1)}), bf16[8,128,896]{2,1,0:T(8,128)(2,1)}, u32[]{:S(2)}, u32[]{:S(2)}) async-start(bf16[8,128,896]{2,1,0:T(8,128)(2,1)} %bitcast.133), calls=%async_computation | async-start | bytes 3670016 | tf_op jit(solution)/shard_map/all_to_all | solution.py:207
  18.9 20.2 %collective-permute-start.4 = (bf16[128,2048]{1,0:T(8,128)(2,1)S(1)}, bf16[128,2048]{1,0:T(8,128)(2,1)S(1)}, u32[]{:S(2)}, u32[]{:S(2)}) collective-permute-start(bf16[128,2048]{1,0:T(8,128)(2,1)S(1)} %collective-permute-done.3.near_ref), channel_id=1, source_target_pairs={{0,1},{1,0},{2,3},{3,2},{4,5},{5,4},{6,7},{7,6},{8,9},{9,8},{10,11... | collective-permute-start | bytes 1572872 | tf_op jit(solution)/shard_map/ppermute | solution.py:197
  34.3 25.2 %collective-permute-start.10 = (bf16[128,2048]{1,0:T(8,128)(2,1)S(1)}, bf16[128,2048]{1,0:T(8,128)(2,1)S(1)}, u32[]{:S(2)}, u32[]{:S(2)}) collective-permute-start(bf16[128,2048]{1,0:T(8,128)(2,1)S(1)} %collective-permute-done.3.near_ref), channel_id=1, source_target_pairs={{0,2},{1,3},{2,4},{3,5},{4,6},{5,7},{6,0},{7,1},{8,10},{9,11},{10,... | collective-permute-start | bytes 1572872 | tf_op jit(solution)/shard_map/ppermute | solution.py:197
  47.1 22.2 %collective-permute-start.6 = (bf16[32,3584]{1,0:T(8,128)(2,1)S(1)}, bf16[32,3584]{1,0:T(8,128)(2,1)S(1)}, u32[]{:S(2)}, u32[]{:S(2)}) collective-permute-start(bf16[32,3584]{1,0:T(8,128)(2,1)S(1)} %fusion.34), channel_id=1, source_target_pairs={{0,8},{8,0},{16,24},{24,16},{1,9},{9,1},{17,25},{25,17},{2,10},{10... | collective-permute-start | bytes 688136 | tf_op jit(solution)/shard_map/ppermute | solution.py:200
  48.3 26.8 %collective-permute-start.8 = (bf16[2,32,3584]{2,1,0:T(8,128)(2,1)S(1)}, bf16[2,32,3584]{2,1,0:T(8,128)(2,1)S(1)}, u32[]{:S(2)}, u32[]{:S(2)}) collective-permute-start(bf16[2,32,3584]{2,1,0:T(8,128)(2,1)S(1)} %get-tuple-element.57), channel_id=1, source_target_pairs={{0,8},{8,0},{16,24},{24,16},{1,9},{9,1},{17,25},{25,17},{2,10},{10... | collective-permute-start | bytes 1376264 | tf_op jit(solution)/shard_map/ppermute | solution.py:200
  49.8 25.3 %collective-permute-start.9 = (bf16[2,32,3584]{2,1,0:T(8,128)(2,1)S(1)}, bf16[2,32,3584]{2,1,0:T(8,128)(2,1)S(1)}, u32[]{:S(2)}, u32[]{:S(2)}) collective-permute-start(bf16[2,32,3584]{2,1,0:T(8,128)(2,1)S(1)} %get-tuple-element.58), channel_id=1, source_target_pairs={{0,16},{8,24},{16,0},{24,8},{1,17},{9,25},{17,1},{25,9},{2,18},{10... | collective-permute-start | bytes 1376264 | tf_op jit(solution)/shard_map/ppermute | solution.py:200
  60.7 20.4 %collective-permute-start.18 = (bf16[128,2048]{1,0:T(8,128)(2,1)S(1)}, bf16[128,2048]{1,0:T(8,128)(2,1)S(1)}, u32[]{:S(2)}, u32[]{:S(2)}) collective-permute-start(bf16[128,2048]{1,0:T(8,128)(2,1)S(1)} %collective-permute-done.10.near_ref), channel_id=1, source_target_pairs={{0,2},{1,3},{2,4},{3,5},{4,6},{5,7},{6,0},{7,1},{8,10},{9,11},{10,... | collective-permute-start | bytes 1572872 | tf_op jit(solution)/shard_map/ppermute | solution.py:197
  69.3 18.8 %collective-permute-start.7 = (bf16[32,3584]{1,0:T(8,128)(2,1)S(1)}, bf16[32,3584]{1,0:T(8,128)(2,1)S(1)}, u32[]{:S(2)}, u32[]{:S(2)}) collective-permute-start(bf16[32,3584]{1,0:T(8,128)(2,1)S(1)} %fusion.31), channel_id=1, source_target_pairs={{0,1},{1,0},{2,3},{3,2},{4,5},{5,4},{6,7},{7,6},{8,9},{9,8},{10,11... | collective-permute-start | bytes 688136 | tf_op jit(solution)/shard_map/ppermute | solution.py:197
  78.5 20.3 %collective-permute-start.16 = (bf16[2,32,3584]{2,1,0:T(8,128)(2,1)S(1)}, bf16[2,32,3584]{2,1,0:T(8,128)(2,1)S(1)}, u32[]{:S(2)}, u32[]{:S(2)}) collective-permute-start(bf16[2,32,3584]{2,1,0:T(8,128)(2,1)S(1)} %get-tuple-element.67), channel_id=1, source_target_pairs={{0,8},{8,0},{16,24},{24,16},{1,9},{9,1},{17,25},{25,17},{2,10},{10... | collective-permute-start | bytes 1376264 | tf_op jit(solution)/shard_map/ppermute | solution.py:200
  81.1 17.6 %collective-permute-start.17 = (bf16[2,32,3584]{2,1,0:T(8,128)(2,1)S(1)}, bf16[2,32,3584]{2,1,0:T(8,128)(2,1)S(1)}, u32[]{:S(2)}, u32[]{:S(2)}) collective-permute-start(bf16[2,32,3584]{2,1,0:T(8,128)(2,1)S(1)} %get-tuple-element.68), channel_id=1, source_target_pairs={{0,16},{8,24},{16,0},{24,8},{1,17},{9,25},{17,1},{25,9},{2,18},{10... | collective-permute-start | bytes 1376264 | tf_op jit(solution)/shard_map/ppermute | solution.py:200
  86.1 30.6 %collective-permute-start.14 = (bf16[32,3584]{1,0:T(8,128)(2,1)}, bf16[32,3584]{1,0:T(8,128)(2,1)}, u32[]{:S(2)}, u32[]{:S(2)}) collective-permute-start(bf16[32,3584]{1,0:T(8,128)(2,1)} %fusion.30), channel_id=1, source_target_pairs={{0,6},{1,7},{2,0},{3,1},{4,2},{5,3},{6,4},{7,5},{8,14},{9,15},{10,... | collective-permute-start | bytes 688136 | tf_op jit(solution)/shard_map/ppermute | solution.py:197
  88.9 27.8 %collective-permute-start.15 = (bf16[32,3584]{1,0:T(8,128)(2,1)}, bf16[32,3584]{1,0:T(8,128)(2,1)}, u32[]{:S(2)}, u32[]{:S(2)}) collective-permute-start(bf16[32,3584]{1,0:T(8,128)(2,1)} %fusion.29), channel_id=1, source_target_pairs={{0,7},{1,6},{2,1},{3,0},{4,3},{5,2},{6,5},{7,4},{8,15},{9,14},{10,... | collective-permute-start | bytes 688136 | tf_op jit(solution)/shard_map/ppermute | solution.py:197
  102.4 16.2 %collective-permute-start.24 = (bf16[2,32,3584]{2,1,0:T(8,128)(2,1)}, bf16[2,32,3584]{2,1,0:T(8,128)(2,1)}, u32[]{:S(2)}, u32[]{:S(2)}) collective-permute-start(bf16[2,32,3584]{2,1,0:T(8,128)(2,1)} %get-tuple-element.79), channel_id=1, source_target_pairs={{0,8},{8,0},{16,24},{24,16},{1,9},{9,1},{17,25},{25,17},{2,10},{10... | collective-permute-start | bytes 1376264 | tf_op jit(solution)/shard_map/ppermute | solution.py:200
  115.6 30.4 %collective-permute-start.22 = (bf16[32,3584]{1,0:T(8,128)(2,1)}, bf16[32,3584]{1,0:T(8,128)(2,1)}, u32[]{:S(2)}, u32[]{:S(2)}) collective-permute-start(bf16[32,3584]{1,0:T(8,128)(2,1)} %fusion.28), channel_id=1, source_target_pairs={{0,4},{1,5},{2,6},{3,7},{4,0},{5,1},{6,2},{7,3},{8,12},{9,13},{10,... | collective-permute-start | bytes 688136 | tf_op jit(solution)/shard_map/ppermute | solution.py:197
  116.8 29.2 %collective-permute-start.23 = (bf16[32,3584]{1,0:T(8,128)(2,1)}, bf16[32,3584]{1,0:T(8,128)(2,1)}, u32[]{:S(2)}, u32[]{:S(2)}) collective-permute-start(bf16[32,3584]{1,0:T(8,128)(2,1)} %fusion.27), channel_id=1, source_target_pairs={{0,5},{1,4},{2,7},{3,6},{4,1},{5,0},{6,3},{7,2},{8,13},{9,12},{10,... | collective-permute-start | bytes 688136 | tf_op jit(solution)/shard_map/ppermute | solution.py:197
  126.3 17.7 %collective-permute-start.26 = (bf16[32,3584]{1,0:T(8,128)(2,1)}, bf16[32,3584]{1,0:T(8,128)(2,1)}, u32[]{:S(2)}, u32[]{:S(2)}) collective-permute-start(bf16[32,3584]{1,0:T(8,128)(2,1)} %fusion.39), channel_id=1, source_target_pairs={{0,16},{8,24},{16,0},{24,8},{1,17},{9,25},{17,1},{25,9},{2,18},{10... | collective-permute-start | bytes 688136 | tf_op jit(solution)/shard_map/ppermute | solution.py:200
  128.6 15.4 %collective-permute-start.27 = (bf16[32,3584]{1,0:T(8,128)(2,1)}, bf16[32,3584]{1,0:T(8,128)(2,1)S(1)}, u32[]{:S(2)}, u32[]{:S(2)}) collective-permute-start(bf16[32,3584]{1,0:T(8,128)(2,1)} %fusion.40), channel_id=1, source_target_pairs={{0,8},{8,0},{16,24},{24,16},{1,9},{9,1},{17,25},{25,17},{2,10},{10... | collective-permute-start | bytes 688136 | tf_op jit(solution)/shard_map/ppermute | solution.py:200
  145.1 29.1 %collective-permute-start.28 = (bf16[32,3584]{1,0:T(8,128)(2,1)S(1)}, bf16[32,3584]{1,0:T(8,128)(2,1)}, u32[]{:S(2)}, u32[]{:S(2)}) collective-permute-start(bf16[32,3584]{1,0:T(8,128)(2,1)S(1)} %fusion.26), channel_id=1, source_target_pairs={{0,2},{1,3},{2,4},{3,5},{4,6},{5,7},{6,0},{7,1},{8,10},{9,11},{10,... | collective-permute-start | bytes 688136 | tf_op jit(solution)/shard_map/ppermute | solution.py:197
  147.7 26.6 %collective-permute-start.29 = (bf16[32,3584]{1,0:T(8,128)(2,1)}, bf16[32,3584]{1,0:T(8,128)(2,1)S(1)}, u32[]{:S(2)}, u32[]{:S(2)}) collective-permute-start(bf16[32,3584]{1,0:T(8,128)(2,1)} %fusion.25), channel_id=1, source_target_pairs={{0,3},{1,2},{2,5},{3,4},{4,7},{5,6},{6,1},{7,0},{8,11},{9,10},{10,... | collective-permute-start | bytes 688136 | tf_op jit(solution)/shard_map/ppermute | solution.py:197
  148.5 17.7 %all-to-all-start.2 = ((bf16[32,32,128]{2,1,0:T(8,128)(2,1)}), bf16[32,32,128]{2,1,0:T(8,128)(2,1)S(1)}, u32[]{:S(2)}, u32[]{:S(2)}) async-start(bf16[32,32,128]{2,1,0:T(8,128)(2,1)} %broadcast_in_dim.110), calls=%async_computation.2 | async-start | bytes 524288 | tf_op jit(solution)/shard_map/all_to_all | solution.py:291
  170.0 47.8 %all-to-all-start.3 = ((bf16[8,128,896]{2,1,0:T(8,128)(2,1)}), bf16[8,128,896]{2,1,0:T(8,128)(2,1)}, u32[]{:S(2)}, u32[]{:S(2)}) async-start(bf16[8,128,896]{2,1,0:T(8,128)(2,1)} %bitcast.139), calls=%async_computation.3 | async-start | bytes 3670016 | tf_op jit(solution)/shard_map/all_to_all | solution.py:319
  181.0 21.7 %collective-permute-start.32 = (bf16[2,32,3584]{2,1,0:T(8,128)(2,1)}, bf16[2,32,3584]{2,1,0:T(8,128)(2,1)}, u32[]{:S(2)}, u32[]{:S(2)}) collective-permute-start(bf16[2,32,3584]{2,1,0:T(8,128)(2,1)} %get-tuple-element.93), channel_id=1, source_target_pairs={{0,24},{8,16},{16,8},{24,0},{1,25},{9,17},{17,9},{25,1},{2,26},{10... | collective-permute-start | bytes 1376264 | tf_op jit(solution)/shard_map/ppermute | solution.py:200
  (38 other events, 481.2 us)

commit v11 on v10

--- a/solution.py
+++ b/solution.py
@@ -282,7 +282,7 @@
         concat_axis=0,
         tiled=True,
     )
-    sums = total(last - 1, seconds, ranked)
+    sums = total(last - 1, seconds, share)
     arrived = put(arrived, last - 2, came, sums[0])
     came = hop(last - 1, sums)
     begun, seconds = second(last, sums[0])

time: 223 us -> 221 us (level)
  waiting for transfers between devices: 66.4 us -> 60.2 us
    ppermute x14, waiting for transfers between devices: 17.1 us -> 26.5 us  [seq_move(): return lax.ppermute(value, 'seq', pairs)]
    all_to_all x1, waiting for transfers between devices: 9.27 us -> 0.01 us  [shards(): lax.all_to_all(jnp.broadcast_to(share[None], (devices,) + share.shape), (...]
    ppermute x19, waiting for transfers between devices: 17.8 us -> 12.2 us  [grp_move(): return lax.ppermute(value, 'grp', [(g, g ^ flip) for g in range(groups)])]
    convert_element_type x0 -> x2, local copies, waits for them, and re-layouts: none -> 2.81 us  [project(): return jnp.concatenate(parts, axis=0).astype(jnp.bfloat16)]
    ppermute x14, starting transfers between devices: 22.2 us -> 24.6 us  [seq_move(): return lax.ppermute(value, 'seq', pairs)]
    unnamed x50 -> x38, local copies, waits for them, and re-layouts: 7.25 us -> 6.01 us
  transfers between devices with their start and end apart: 37 -> 37, of which waited for: 11 -> 10; matrix products, arithmetic and copies ran while one was open for 26% -> 28% of each run, Pallas kernels for 10% -> 10%
where the time goes in v11:
time: 221 us; the launch traced here: 220 us
  starting transfers between devices  64 us (29%)
  waiting for transfers between devices  60.2 us (27%)
  local copies, waits for them, and re-layouts  33.9 us (15%)
  Pallas kernels  25.8 us (12%)
  matrix products  19.2 us (9%)
  other arithmetic  15.3 us (7%)
    ppermute x14, waiting for transfers between devices, seq_move(): return lax.ppermute(value, 'seq', pairs)  26.5 us
    ppermute x14, starting transfers between devices, seq_move(): return lax.ppermute(value, 'seq', pairs)  24.6 us
    ppermute x19, starting transfers between devices, grp_move(): return lax.ppermute(value, 'grp', [(g, g ^ flip) for g in range(groups)])  23.2 us
    pallas_call x4, Pallas kernels, chunk_product(): pl.pallas_call(functools.partial(chunk_kernel, STAGES), grid_spec=pltpu.P...  21.8 us
    all_to_all x1, waiting for transfers between devices, shards(): term = lax.all_to_all(term, 'seq', split_axis=0, concat_axis=0, tiled=True)  15.9 us
    dot_general x4, matrix products, dot(): lax.dot_general(left, right, dims, preferred_element_type=jnp.float32)  15.6 us
    convert_element_type x16, other arithmetic, add(): sum((term.astype(jnp.float32) for term in terms)).astype(jnp.bfloat16)  12.6 us
    ppermute x19, waiting for transfers between devices, grp_move(): return lax.ppermute(value, 'grp', [(g, g ^ flip) for g in range(groups)])  12.2 us
  transfers between devices with their start and end apart: 37, of which 10 were waited for; matrix products, arithmetic and copies ran while one was open for 28% of the time, Pallas kernels for 10%

profile of v11, /device:TPU:0, one launch (start us, length us, event | category | flops | bytes accessed | tf_op | source)
XLA Modules:
  0.0 219.7 jit_solution(5594846077752180124)
XLA Ops:
  1.2 2.6 %collective-permute-start.3 = (bf16[128,2048]{1,0:T(8,128)(2,1)}, bf16[128,2048]{1,0:T(8,128)(2,1)S(1)}, u32[]{:S(2)}, u32[]{:S(2)}) collective-permute-start(bf16[128,2048]{1,0:T(8,128)(2,1)} %near_ref.1), channel_id=1, source_target_pairs={{0,2},{1,3},{2,4},{3,5},{4,6},{5,7},{6,0},{7,1},{8,10},{9,11},{10,... | collective-permute-start | bytes 1572872 | tf_op jit(solution)/shard_map/ppermute | solution.py:197
  3.8 3.0 %copy.46 = bf16[16,8,8,896]{3,2,0,1:T(8,128)(2,1)} copy(bf16[16,8,8,896]{3,2,1,0:T(8,128)(2,1)} %bitcast.136) | data formatting | bytes 3670016 | tf_op jit(solution)/shard_map/reshape | solution.py:208
  6.8 4.4 %all-to-all-start = ((bf16[8,128,896]{2,1,0:T(8,128)(2,1)}), bf16[8,128,896]{2,1,0:T(8,128)(2,1)}, u32[]{:S(2)}, u32[]{:S(2)}) async-start(bf16[8,128,896]{2,1,0:T(8,128)(2,1)} %bitcast.133), calls=%async_computation | async-start | bytes 3670016 | tf_op jit(solution)/shard_map/all_to_all | solution.py:207
  12.4 6.5 %collective-permute-done.3.near_ref = bf16[128,2048]{1,0:T(8,128)(2,1)S(1)} collective-permute-done((bf16[128,2048]{1,0:T(8,128)(2,1)}, bf16[128,2048]{1,0:T(8,128)(2,1)S(1)}, u32[]{:S(2)}, u32[]{:S(2)}) %collective-permute-start.3) | collective-permute-done | bytes 524320 | tf_op jit(solution)/shard_map/ppermute | solution.py:197
  20.4 5.2 %copy-done.1 = bf16[3584,2048]{1,0:T(8,128)(2,1)S(1)} copy-done((bf16[3584,2048]{1,0:T(8,128)(2,1)S(1)}, bf16[3584,2048]{1,0:T(8,128)(2,1)}, u32[]{:S(2)}) %copy-start.1) | copy-done | bytes 14680088
  25.6 5.4 %shard_map.94 = (bf16[2,32,3584]{2,1,0:T(8,128)(2,1)S(1)}, bf16[2,32,3584]{2,1,0:T(8,128)(2,1)S(1)}, bf16[2,32,3584]{2,1,0:T(8,128)(2,1)S(1)}, bf16[2,32,3584]{2,1,0:T(8,128)(2,1)S(1)}) custom-call(s32[1]{0:T(128)} %bitcast.place_ref, bf16[128,2048]{1,0:T(8,128)(2,1)S(1)} %copy-done.3, bf16[128,2048]{1,0:T(8,128)(2,1)S(1)} %collective-permute-done.far_ref, ...), custom_call_target="tpu_custom_call" | custom-call | flops 3758096384 | bytes 17563648 | tf_op jit(solution)/shard_map/pallas_call | solution.py:57
  34.2 4.3 %collective-permute-start.10 = (bf16[128,2048]{1,0:T(8,128)(2,1)S(1)}, bf16[128,2048]{1,0:T(8,128)(2,1)S(1)}, u32[]{:S(2)}, u32[]{:S(2)}) collective-permute-start(bf16[128,2048]{1,0:T(8,128)(2,1)S(1)} %collective-permute-done.3.near_ref), channel_id=1, source_target_pairs={{0,2},{1,3},{2,4},{3,5},{4,6},{5,7},{6,0},{7,1},{8,10},{9,11},{10,... | collective-permute-start | bytes 1572872 | tf_op jit(solution)/shard_map/ppermute | solution.py:197
  39.2 5.4 %shard_map.95 = (bf16[2,32,3584]{2,1,0:T(8,128)(2,1)S(1)}, bf16[2,32,3584]{2,1,0:T(8,128)(2,1)S(1)}, bf16[2,32,3584]{2,1,0:T(8,128)(2,1)S(1)}, bf16[2,32,3584]{2,1,0:T(8,128)(2,1)S(1)}) custom-call(s32[1]{0:T(128)} %bitcast.place_ref, bf16[128,2048]{1,0:T(8,128)(2,1)S(1)} %collective-permute-done.3.near_ref, ...), custom_call_target="tpu_custom_call" | custom-call | flops 3758096384 | bytes 17563648 | tf_op jit(solution)/shard_map/pallas_call | solution.py:57
  50.3 9.2 %collective-permute-done.10.near_ref = bf16[128,2048]{1,0:T(8,128)(2,1)S(1)} collective-permute-done((bf16[128,2048]{1,0:T(8,128)(2,1)S(1)}, bf16[128,2048]{1,0:T(8,128)(2,1)S(1)}, u32[]{:S(2)}, u32[]{:S(2)}) %collective-permute-start.10) | collective-permute-done | bytes 524320 | tf_op jit(solution)/shard_map/ppermute | solution.py:197
  60.7 8.5 %collective-permute-start.18 = (bf16[128,2048]{1,0:T(8,128)(2,1)S(1)}, bf16[128,2048]{1,0:T(8,128)(2,1)S(1)}, u32[]{:S(2)}, u32[]{:S(2)}) collective-permute-start(bf16[128,2048]{1,0:T(8,128)(2,1)S(1)} %collective-permute-done.10.near_ref), channel_id=1, source_target_pairs={{0,2},{1,3},{2,4},{3,5},{4,6},{5,7},{6,0},{7,1},{8,10},{9,11},{10,... | collective-permute-start | bytes 1572872 | tf_op jit(solution)/shard_map/ppermute | solution.py:197
  69.6 5.4 %shard_map.96 = (bf16[2,32,3584]{2,1,0:T(8,128)(2,1)S(1)}, bf16[2,32,3584]{2,1,0:T(8,128)(2,1)S(1)}, bf16[2,32,3584]{2,1,0:T(8,128)(2,1)S(1)}, bf16[2,32,3584]{2,1,0:T(8,128)(2,1)S(1)}) custom-call(s32[1]{0:T(128)} %bitcast.place_ref, bf16[128,2048]{1,0:T(8,128)(2,1)S(1)} %collective-permute-done.10.near_ref, ...), custom_call_target="tpu_custom_call" | custom-call | flops 3758096384 | bytes 17563648 | tf_op jit(solution)/shard_map/pallas_call | solution.py:57
  90.7 5.5 %shard_map.97 = (bf16[2,32,3584]{2,1,0:T(8,128)(2,1)S(1)}, bf16[2,32,3584]{2,1,0:T(8,128)(2,1)S(1)}, bf16[2,32,3584]{2,1,0:T(8,128)(2,1)S(1)}, bf16[2,32,3584]{2,1,0:T(8,128)(2,1)S(1)}) custom-call(s32[1]{0:T(128)} %bitcast.place_ref, bf16[128,2048]{1,0:T(8,128)(2,1)S(1)} %collective-permute-done.18.near_ref, ...), custom_call_target="tpu_custom_call" | custom-call | flops 3758096384 | bytes 17563648 | tf_op jit(solution)/shard_map/pallas_call | solution.py:57
  101.2 4.5 %multiply_reduce_fusion = bf16[1024,64]{0,1:T(8,128)(2,1)} fusion(f32[1024,16]{0,1:T(8,128)S(1)} %get-tuple-element.100, bf16[16,64,896]{2,1,0:T(8,128)(2,1)S(1)} %copy-done, bf16[1024,896]{1,0:T(8,128)(2,1)} %bitcast.24), kind=kOutput, calls=%fused_computation | convolution fusion | flops 1881079808 | bytes 3866624 | tf_op jit(solution)/shard_map/dot_general | solution.py:19
  106.9 2.6 %multiply_reduce_fusion.1 = bf16[1024,64]{0,1:T(8,128)(2,1)} fusion(bf16[16,64,256]{2,1,0:T(8,128)(2,1)} %param.11, f32[1024,16]{0,1:T(8,128)S(1)} %get-tuple-element.100, bf16[1024,256]{1,0:T(8,128)(2,1)} %bitcast.22), kind=kOutput, calls=%fused_computation.1 | convolution fusion | flops 538902528 | bytes 1245184 | tf_op jit(solution)/shard_map/dot_general | solution.py:19
  120.4 5.6 %all-to-all-done.1.refs_2_ = bf16[32,32,128]{2,1,0:T(8,128)(2,1)S(1)} async-done(((bf16[32,32,128]{2,1,0:T(8,128)(2,1)}), bf16[32,32,128]{2,1,0:T(8,128)(2,1)S(1)}, u32[]{:S(2)}, u32[]{:S(2)}) %all-to-all-start.1) | async-done | bytes 262176 | tf_op jit(solution)/shard_map/all_to_all | solution.py:278
  138.9 4.3 %all-to-all-start.2 = ((bf16[32,32,128]{2,1,0:T(8,128)(2,1)}), bf16[32,32,128]{2,1,0:T(8,128)(2,1)S(1)}, u32[]{:S(2)}, u32[]{:S(2)}) async-start(bf16[32,32,128]{2,1,0:T(8,128)(2,1)} %broadcast_in_dim.110), calls=%async_computation.2 | async-start | bytes 524288 | tf_op jit(solution)/shard_map/all_to_all | solution.py:291
  149.5 9.4 %collective-permute-done.23 = bf16[32,3584]{1,0:T(8,128)(2,1)} collective-permute-done((bf16[32,3584]{1,0:T(8,128)(2,1)}, bf16[32,3584]{1,0:T(8,128)(2,1)}, u32[]{:S(2)}, u32[]{:S(2)}) %collective-permute-start.23) | collective-permute-done | bytes 229408 | tf_op jit(solution)/shard_map/ppermute | solution.py:197
  163.7 3.6 %fusion = bf16[1024,896]{1,0:T(8,128)(2,1)} fusion(bf16[16,64,896]{2,1,0:T(8,128)(2,1)S(1)} %copy-done, bf16[1024,16]{0,1:T(8,128)(2,1)S(1)} %copy-done.16, bf16[1024,64]{0,1:T(8,128)(2,1)S(1)} %copy.41), kind=kOutput, calls=%fused_computation.3 | convolution fusion | flops 1881931776 | bytes 3833856 | tf_op jit(solution)/shard_map/dot_general | solution.py:307
  167.4 4.8 %all-to-all-start.3 = ((bf16[8,128,896]{2,1,0:T(8,128)(2,1)}), bf16[8,128,896]{2,1,0:T(8,128)(2,1)}, u32[]{:S(2)}, u32[]{:S(2)}) async-start(bf16[8,128,896]{2,1,0:T(8,128)(2,1)} %bitcast.137), calls=%async_computation.3 | async-start | bytes 3670016 | tf_op jit(solution)/shard_map/all_to_all | solution.py:319
  182.7 2.7 %fusion.15 = f32[16,64,256]{2,1,0:T(8,128)} fusion(bf16[1024,256,1]{1,0,2:T(8,128)(2,1)} %bitcast.51, bf16[1024,64]{0,1:T(8,128)(2,1)S(1)} %copy.43, bf16[1024,16]{0,1:T(8,128)(2,1)S(1)} %copy-done.16, f32[16]{0:T(128)S(1)} %broadcast_divide_fusion), kind=kOutput, calls=%fused_computation.15 | convolution fusion | flops 538181632 | bytes 1736768 | tf_op jit(solution)/shard_map/dot_general | solution.py:19
  185.5 5.7 %fusion.9 = f32[16,64,896]{2,1,0:T(8,128)} fusion(bf16[1024,896,1]{1,0,2:T(8,128)(2,1)} %bitcast.47, f32[16]{0:T(128)S(1)} %broadcast_divide_fusion, bf16[1024,64]{0,1:T(8,128)(2,1)S(1)} %copy.42, bf16[1024,16]{0,1:T(8,128)(2,1)S(1)} %copy-done.16), kind=kOutput, calls=%fused_computation.12 | convolution fusion | flops 1881014272 | bytes 5668928 | tf_op jit(solution)/shard_map/dot_general | solution.py:19
  191.1 8.8 %collective-permute-done.31.refs_2_ = bf16[2,32,3584]{2,1,0:T(8,128)(2,1)S(1)} collective-permute-done((bf16[2,32,3584]{2,1,0:T(8,128)(2,1)}, bf16[2,32,3584]{2,1,0:T(8,128)(2,1)S(1)}, u32[]{:S(2)}, u32[]{:S(2)}) %collective-permute-start.31) | collective-permute-done | bytes 458784 | tf_op jit(solution)/shard_map/ppermute | solution.py:200
  199.9 15.9 %all-to-all-done.3.refs_4_ = bf16[8,128,896]{2,1,0:T(8,128)(2,1)} async-done(((bf16[8,128,896]{2,1,0:T(8,128)(2,1)}), bf16[8,128,896]{2,1,0:T(8,128)(2,1)}, u32[]{:S(2)}, u32[]{:S(2)}) %all-to-all-start.3) | async-done | bytes 1835040 | tf_op jit(solution)/shard_map/all_to_all | solution.py:319
  215.7 4.0 %shard_map.99 = bf16[128,7168]{1,0:T(8,128)(2,1)} custom-call(s32[1]{0:T(128)} %bitcast.place_ref, bf16[2,32,3584]{2,1,0:T(8,128)(2,1)S(1)} %get-tuple-element.96.refs_0_, bf16[2,32,3584]{2,1,0:T(8,128)(2,1)S(1)} %collective-permute-done.30.refs_1_, bf16[2,32,3584]{2,1,0:T(8,128)(2,1)S(1)} %collective-permute-done.31.refs_2_, ...), custom_call_target="tpu_custom_call" | custom-call | flops 917504 | bytes 5505024 | tf_op jit(solution)/shard_map/pallas_call | solution.py:104
  (150 shorter events, 81.0 us)
Async XLA Ops:
  0.6 19.8 %collective-permute-start = (bf16[128,2048]{1,0:T(8,128)(2,1)}, bf16[128,2048]{1,0:T(8,128)(2,1)S(1)}, u32[]{:S(2)}, u32[]{:S(2)}) collective-permute-start(bf16[128,2048]{1,0:T(8,128)(2,1)} %near_ref.1), channel_id=1, source_target_pairs={{0,1},{1,0},{2,3},{3,2},{4,5},{5,4},{6,7},{7,6},{8,9},{9,8},{10,11... | collective-permute-start | bytes 1572872 | tf_op jit(solution)/shard_map/ppermute | solution.py:197
  1.2 17.8 %collective-permute-start.3 = (bf16[128,2048]{1,0:T(8,128)(2,1)}, bf16[128,2048]{1,0:T(8,128)(2,1)S(1)}, u32[]{:S(2)}, u32[]{:S(2)}) collective-permute-start(bf16[128,2048]{1,0:T(8,128)(2,1)} %near_ref.1), channel_id=1, source_target_pairs={{0,2},{1,3},{2,4},{3,5},{4,6},{5,7},{6,0},{7,1},{8,10},{9,11},{10,... | collective-permute-start | bytes 1572872 | tf_op jit(solution)/shard_map/ppermute | solution.py:197
  6.8 94.5 %all-to-all-start = ((bf16[8,128,896]{2,1,0:T(8,128)(2,1)}), bf16[8,128,896]{2,1,0:T(8,128)(2,1)}, u32[]{:S(2)}, u32[]{:S(2)}) async-start(bf16[8,128,896]{2,1,0:T(8,128)(2,1)} %bitcast.133), calls=%async_computation | async-start | bytes 3670016 | tf_op jit(solution)/shard_map/all_to_all | solution.py:207
  18.9 20.2 %collective-permute-start.4 = (bf16[128,2048]{1,0:T(8,128)(2,1)S(1)}, bf16[128,2048]{1,0:T(8,128)(2,1)S(1)}, u32[]{:S(2)}, u32[]{:S(2)}) collective-permute-start(bf16[128,2048]{1,0:T(8,128)(2,1)S(1)} %collective-permute-done.3.near_ref), channel_id=1, source_target_pairs={{0,1},{1,0},{2,3},{3,2},{4,5},{5,4},{6,7},{7,6},{8,9},{9,8},{10,11... | collective-permute-start | bytes 1572872 | tf_op jit(solution)/shard_map/ppermute | solution.py:197
  34.2 25.2 %collective-permute-start.10 = (bf16[128,2048]{1,0:T(8,128)(2,1)S(1)}, bf16[128,2048]{1,0:T(8,128)(2,1)S(1)}, u32[]{:S(2)}, u32[]{:S(2)}) collective-permute-start(bf16[128,2048]{1,0:T(8,128)(2,1)S(1)} %collective-permute-done.3.near_ref), channel_id=1, source_target_pairs={{0,2},{1,3},{2,4},{3,5},{4,6},{5,7},{6,0},{7,1},{8,10},{9,11},{10,... | collective-permute-start | bytes 1572872 | tf_op jit(solution)/shard_map/ppermute | solution.py:197
  45.4 15.3 %collective-permute-start.5 = (bf16[32,3584]{1,0:T(8,128)(2,1)S(1)}, bf16[32,3584]{1,0:T(8,128)(2,1)S(1)}, u32[]{:S(2)}, u32[]{:S(2)}) collective-permute-start(bf16[32,3584]{1,0:T(8,128)(2,1)S(1)} %fusion.33), channel_id=1, source_target_pairs={{0,16},{8,24},{16,0},{24,8},{1,17},{9,25},{17,1},{25,9},{2,18},{10... | collective-permute-start | bytes 688136 | tf_op jit(solution)/shard_map/ppermute | solution.py:200
  47.1 22.2 %collective-permute-start.6 = (bf16[32,3584]{1,0:T(8,128)(2,1)S(1)}, bf16[32,3584]{1,0:T(8,128)(2,1)S(1)}, u32[]{:S(2)}, u32[]{:S(2)}) collective-permute-start(bf16[32,3584]{1,0:T(8,128)(2,1)S(1)} %fusion.34), channel_id=1, source_target_pairs={{0,8},{8,0},{16,24},{24,16},{1,9},{9,1},{17,25},{25,17},{2,10},{10... | collective-permute-start | bytes 688136 | tf_op jit(solution)/shard_map/ppermute | solution.py:200
  48.3 26.8 %collective-permute-start.8 = (bf16[2,32,3584]{2,1,0:T(8,128)(2,1)S(1)}, bf16[2,32,3584]{2,1,0:T(8,128)(2,1)S(1)}, u32[]{:S(2)}, u32[]{:S(2)}) collective-permute-start(bf16[2,32,3584]{2,1,0:T(8,128)(2,1)S(1)} %get-tuple-element.57), channel_id=1, source_target_pairs={{0,8},{8,0},{16,24},{24,16},{1,9},{9,1},{17,25},{25,17},{2,10},{10... | collective-permute-start | bytes 1376264 | tf_op jit(solution)/shard_map/ppermute | solution.py:200
  49.8 25.3 %collective-permute-start.9 = (bf16[2,32,3584]{2,1,0:T(8,128)(2,1)S(1)}, bf16[2,32,3584]{2,1,0:T(8,128)(2,1)S(1)}, u32[]{:S(2)}, u32[]{:S(2)}) collective-permute-start(bf16[2,32,3584]{2,1,0:T(8,128)(2,1)S(1)} %get-tuple-element.58), channel_id=1, source_target_pairs={{0,16},{8,24},{16,0},{24,8},{1,17},{9,25},{17,1},{25,9},{2,18},{10... | collective-permute-start | bytes 1376264 | tf_op jit(solution)/shard_map/ppermute | solution.py:200
  60.7 20.4 %collective-permute-start.18 = (bf16[128,2048]{1,0:T(8,128)(2,1)S(1)}, bf16[128,2048]{1,0:T(8,128)(2,1)S(1)}, u32[]{:S(2)}, u32[]{:S(2)}) collective-permute-start(bf16[128,2048]{1,0:T(8,128)(2,1)S(1)} %collective-permute-done.10.near_ref), channel_id=1, source_target_pairs={{0,2},{1,3},{2,4},{3,5},{4,6},{5,7},{6,0},{7,1},{8,10},{9,11},{10,... | collective-permute-start | bytes 1572872 | tf_op jit(solution)/shard_map/ppermute | solution.py:197
  69.3 19.6 %collective-permute-start.7 = (bf16[32,3584]{1,0:T(8,128)(2,1)S(1)}, bf16[32,3584]{1,0:T(8,128)(2,1)S(1)}, u32[]{:S(2)}, u32[]{:S(2)}) collective-permute-start(bf16[32,3584]{1,0:T(8,128)(2,1)S(1)} %fusion.31), channel_id=1, source_target_pairs={{0,1},{1,0},{2,3},{3,2},{4,5},{5,4},{6,7},{7,6},{8,9},{9,8},{10,11... | collective-permute-start | bytes 688136 | tf_op jit(solution)/shard_map/ppermute | solution.py:197
  78.5 18.5 %collective-permute-start.16 = (bf16[2,32,3584]{2,1,0:T(8,128)(2,1)S(1)}, bf16[2,32,3584]{2,1,0:T(8,128)(2,1)S(1)}, u32[]{:S(2)}, u32[]{:S(2)}) collective-permute-start(bf16[2,32,3584]{2,1,0:T(8,128)(2,1)S(1)} %get-tuple-element.67), channel_id=1, source_target_pairs={{0,8},{8,0},{16,24},{24,16},{1,9},{9,1},{17,25},{25,17},{2,10},{10... | collective-permute-start | bytes 1376264 | tf_op jit(solution)/shard_map/ppermute | solution.py:200
  81.1 15.9 %collective-permute-start.17 = (bf16[2,32,3584]{2,1,0:T(8,128)(2,1)S(1)}, bf16[2,32,3584]{2,1,0:T(8,128)(2,1)S(1)}, u32[]{:S(2)}, u32[]{:S(2)}) collective-permute-start(bf16[2,32,3584]{2,1,0:T(8,128)(2,1)S(1)} %get-tuple-element.68), channel_id=1, source_target_pairs={{0,16},{8,24},{16,0},{24,8},{1,17},{9,25},{17,1},{25,9},{2,18},{10... | collective-permute-start | bytes 1376264 | tf_op jit(solution)/shard_map/ppermute | solution.py:200
  86.1 43.8 %collective-permute-start.14 = (bf16[32,3584]{1,0:T(8,128)(2,1)}, bf16[32,3584]{1,0:T(8,128)(2,1)}, u32[]{:S(2)}, u32[]{:S(2)}) collective-permute-start(bf16[32,3584]{1,0:T(8,128)(2,1)} %fusion.30), channel_id=1, source_target_pairs={{0,6},{1,7},{2,0},{3,1},{4,2},{5,3},{6,4},{7,5},{8,14},{9,15},{10,... | collective-permute-start | bytes 688136 | tf_op jit(solution)/shard_map/ppermute | solution.py:197
  88.9 41.0 %collective-permute-start.15 = (bf16[32,3584]{1,0:T(8,128)(2,1)}, bf16[32,3584]{1,0:T(8,128)(2,1)}, u32[]{:S(2)}, u32[]{:S(2)}) collective-permute-start(bf16[32,3584]{1,0:T(8,128)(2,1)} %fusion.29), channel_id=1, source_target_pairs={{0,7},{1,6},{2,1},{3,0},{4,3},{5,2},{6,5},{7,4},{8,15},{9,14},{10,... | collective-permute-start | bytes 688136 | tf_op jit(solution)/shard_map/ppermute | solution.py:197
  97.9 21.1 %collective-permute-start.20 = (bf16[32,3584]{1,0:T(8,128)(2,1)}, bf16[32,3584]{1,0:T(8,128)(2,1)S(1)}, u32[]{:S(2)}, u32[]{:S(2)}) collective-permute-start(bf16[32,3584]{1,0:T(8,128)(2,1)} %fusion.37), channel_id=1, source_target_pairs={{0,16},{8,24},{16,0},{24,8},{1,17},{9,25},{17,1},{25,9},{2,18},{10... | collective-permute-start | bytes 688136 | tf_op jit(solution)/shard_map/ppermute | solution.py:200
  99.1 21.3 %collective-permute-start.21 = (bf16[32,3584]{1,0:T(8,128)(2,1)}, bf16[32,3584]{1,0:T(8,128)(2,1)S(1)}, u32[]{:S(2)}, u32[]{:S(2)}) collective-permute-start(bf16[32,3584]{1,0:T(8,128)(2,1)} %fusion.38), channel_id=1, source_target_pairs={{0,8},{8,0},{16,24},{24,16},{1,9},{9,1},{17,25},{25,17},{2,10},{10... | collective-permute-start | bytes 688136 | tf_op jit(solution)/shard_map/ppermute | solution.py:200
  127.8 21.7 %collective-permute-start.22 = (bf16[32,3584]{1,0:T(8,128)(2,1)}, bf16[32,3584]{1,0:T(8,128)(2,1)}, u32[]{:S(2)}, u32[]{:S(2)}) collective-permute-start(bf16[32,3584]{1,0:T(8,128)(2,1)} %fusion.28), channel_id=1, source_target_pairs={{0,4},{1,5},{2,6},{3,7},{4,0},{5,1},{6,2},{7,3},{8,12},{9,13},{10,... | collective-permute-start | bytes 688136 | tf_op jit(solution)/shard_map/ppermute | solution.py:197
  129.9 29.0 %collective-permute-start.23 = (bf16[32,3584]{1,0:T(8,128)(2,1)}, bf16[32,3584]{1,0:T(8,128)(2,1)}, u32[]{:S(2)}, u32[]{:S(2)}) collective-permute-start(bf16[32,3584]{1,0:T(8,128)(2,1)} %fusion.27), channel_id=1, source_target_pairs={{0,5},{1,4},{2,7},{3,6},{4,1},{5,0},{6,3},{7,2},{8,13},{9,12},{10,... | collective-permute-start | bytes 688136 | tf_op jit(solution)/shard_map/ppermute | solution.py:197
  138.9 24.7 %all-to-all-start.2 = ((bf16[32,32,128]{2,1,0:T(8,128)(2,1)}), bf16[32,32,128]{2,1,0:T(8,128)(2,1)S(1)}, u32[]{:S(2)}, u32[]{:S(2)}) async-start(bf16[32,32,128]{2,1,0:T(8,128)(2,1)} %broadcast_in_dim.110), calls=%async_computation.2 | async-start | bytes 524288 | tf_op jit(solution)/shard_map/all_to_all | solution.py:291
  147.7 24.5 %collective-permute-start.28 = (bf16[32,3584]{1,0:T(8,128)(2,1)S(1)}, bf16[32,3584]{1,0:T(8,128)(2,1)S(1)}, u32[]{:S(2)}, u32[]{:S(2)}) collective-permute-start(bf16[32,3584]{1,0:T(8,128)(2,1)S(1)} %fusion.26), channel_id=1, source_target_pairs={{0,2},{1,3},{2,4},{3,5},{4,6},{5,7},{6,0},{7,1},{8,10},{9,11},{10,... | collective-permute-start | bytes 688136 | tf_op jit(solution)/shard_map/ppermute | solution.py:197
  167.4 48.4 %all-to-all-start.3 = ((bf16[8,128,896]{2,1,0:T(8,128)(2,1)}), bf16[8,128,896]{2,1,0:T(8,128)(2,1)}, u32[]{:S(2)}, u32[]{:S(2)}) async-start(bf16[8,128,896]{2,1,0:T(8,128)(2,1)} %bitcast.137), calls=%async_computation.3 | async-start | bytes 3670016 | tf_op jit(solution)/shard_map/all_to_all | solution.py:319
  177.2 22.7 %collective-permute-start.31 = (bf16[2,32,3584]{2,1,0:T(8,128)(2,1)}, bf16[2,32,3584]{2,1,0:T(8,128)(2,1)S(1)}, u32[]{:S(2)}, u32[]{:S(2)}) collective-permute-start(bf16[2,32,3584]{2,1,0:T(8,128)(2,1)} %get-tuple-element.94), channel_id=1, source_target_pairs={{0,16},{8,24},{16,0},{24,8},{1,17},{9,25},{17,1},{25,9},{2,18},{10... | collective-permute-start | bytes 1376264 | tf_op jit(solution)/shard_map/ppermute | solution.py:200
  178.1 21.8 %collective-permute-start.32 = (bf16[2,32,3584]{2,1,0:T(8,128)(2,1)}, bf16[2,32,3584]{2,1,0:T(8,128)(2,1)}, u32[]{:S(2)}, u32[]{:S(2)}) collective-permute-start(bf16[2,32,3584]{2,1,0:T(8,128)(2,1)} %get-tuple-element.93), channel_id=1, source_target_pairs={{0,24},{8,16},{16,8},{24,0},{1,25},{9,17},{17,9},{25,1},{2,26},{10... | collective-permute-start | bytes 1376264 | tf_op jit(solution)/shard_map/ppermute | solution.py:200
  (32 other events, 396.7 us)

commit v12 on v11

--- a/solution.py
+++ b/solution.py
@@ -236,7 +236,7 @@
     def total(step, seconds, *gates):
         near_kept, _, far_kept, _ = products[step]
         near_came, far_came = firsts[step]
-        if step == last - 1:
+        if step >= last - 1:
             near_last, far_last = touch(seconds, *gates)
         else:
             near_last, far_last = lax.optimization_barrier(seconds + gates)[:2]
@@ -295,9 +295,8 @@
         concat_axis=0,
         tiled=True,
     ).reshape(count * block, 2 * ranks)
-    sums = total(last, seconds, share)
-    arrived = put(arrived, last - 1, came, sums[0])
-    came = hop(last, sums)
+    sums = total(last, seconds, ranked)
+    before, came = came, hop(last, sums)
     ranked = after(ranked, *sums)
     grad_rank = ranked[:, :ranks]
 
@@ -314,7 +313,8 @@
         axis=0,
     )
     term = (term * ADAPTER_SCALE).astype(jnp.bfloat16).reshape(count, block, down_slab)
-    arrived = put(arrived, last, came, term)
+    arrived = put(arrived, last - 1, touch(before, term))
+    arrived = put(arrived, last, touch(came, term))
     rank_here = after(ranked, term)
     term = lax.all_to_all(term, "seq", split_axis=0, concat_axis=0, tiled=True)
 

time: 221 us -> 221 us (level)
    ppermute x19, waiting for transfers between devices: 12.2 us -> 22 us  [grp_move(): return lax.ppermute(value, 'grp', [(g, g ^ flip) for g in range(groups)])]
    ppermute x14, waiting for transfers between devices: 26.5 us -> 17.1 us  [seq_move(): return lax.ppermute(value, 'seq', pairs)]
    all_to_all x1, waiting for transfers between devices: 0.01 us -> 7.05 us  [shards(): lax.all_to_all(jnp.broadcast_to(share[None], (devices,) + share.shape), (...]
    all_to_all x1, waiting for transfers between devices: 15.9 us -> 10.2 us  [shards(): term = lax.all_to_all(term, 'seq', split_axis=0, concat_axis=0, tiled=True)]
    unnamed x38, local copies, waits for them, and re-layouts: 6.01 us -> 8.54 us
  transfers between devices with their start and end apart: 37 -> 37, of which waited for: 10 -> 12; matrix products, arithmetic and copies ran while one was open for 28% -> 27% of each run, Pallas kernels for 10% -> 10%
where the time goes in v12:
time: 221 us; the launch traced here: 220 us
  starting transfers between devices  62.9 us (28%)
  waiting for transfers between devices  61.9 us (28%)
  local copies, waits for them, and re-layouts  32.8 us (15%)
  Pallas kernels  25.6 us (12%)
  matrix products  19.3 us (9%)
  other arithmetic  16 us (7%)
    ppermute x19, starting transfers between devices, grp_move(): return lax.ppermute(value, 'grp', [(g, g ^ flip) for g in range(groups)])  24.4 us
    ppermute x14, starting transfers between devices, seq_move(): return lax.ppermute(value, 'seq', pairs)  22.7 us
    ppermute x19, waiting for transfers between devices, grp_move(): return lax.ppermute(value, 'grp', [(g, g ^ flip) for g in range(groups)])  22 us
    pallas_call x4, Pallas kernels, chunk_product(): pl.pallas_call(functools.partial(chunk_kernel, STAGES), grid_spec=pltpu.P...  21.8 us
    ppermute x14, waiting for transfers between devices, seq_move(): return lax.ppermute(value, 'seq', pairs)  17.1 us
    dot_general x4, matrix products, dot(): lax.dot_general(left, right, dims, preferred_element_type=jnp.float32)  15.7 us
    convert_element_type x16, other arithmetic, add(): sum((term.astype(jnp.float32) for term in terms)).astype(jnp.bfloat16)  13.3 us
    all_to_all x1, waiting for transfers between devices, shards(): term = lax.all_to_all(term, 'seq', split_axis=0, concat_axis=0, tiled=True)  10.2 us
  transfers between devices with their start and end apart: 37, of which 12 were waited for; matrix products, arithmetic and copies ran while one was open for 27% of the time, Pallas kernels for 10%

profile of v12, /device:TPU:0, one launch (start us, length us, event | category | flops | bytes accessed | tf_op | source)
XLA Modules:
  0.0 219.9 jit_solution(10754597372750116808)
XLA Ops:
  3.8 3.0 %copy.46 = bf16[16,8,8,896]{3,2,0,1:T(8,128)(2,1)} copy(bf16[16,8,8,896]{3,2,1,0:T(8,128)(2,1)} %bitcast.140) | data formatting | bytes 3670016 | tf_op jit(solution)/shard_map/reshape | solution.py:208
  6.8 4.5 %all-to-all-start = ((bf16[8,128,896]{2,1,0:T(8,128)(2,1)}), bf16[8,128,896]{2,1,0:T(8,128)(2,1)}, u32[]{:S(2)}, u32[]{:S(2)}) async-start(bf16[8,128,896]{2,1,0:T(8,128)(2,1)} %bitcast.139), calls=%async_computation | async-start | bytes 3670016 | tf_op jit(solution)/shard_map/all_to_all | solution.py:207
  12.4 6.5 %collective-permute-done.3.near_ref = bf16[128,2048]{1,0:T(8,128)(2,1)S(1)} collective-permute-done((bf16[128,2048]{1,0:T(8,128)(2,1)}, bf16[128,2048]{1,0:T(8,128)(2,1)S(1)}, u32[]{:S(2)}, u32[]{:S(2)}) %collective-permute-start.3) | collective-permute-done | bytes 524320 | tf_op jit(solution)/shard_map/ppermute | solution.py:197
  20.4 5.2 %copy-done.1 = bf16[3584,2048]{1,0:T(8,128)(2,1)S(1)} copy-done((bf16[3584,2048]{1,0:T(8,128)(2,1)S(1)}, bf16[3584,2048]{1,0:T(8,128)(2,1)}, u32[]{:S(2)}) %copy-start.1) | copy-done | bytes 14680088
  25.6 5.4 %shard_map.94 = (bf16[2,32,3584]{2,1,0:T(8,128)(2,1)S(1)}, bf16[2,32,3584]{2,1,0:T(8,128)(2,1)S(1)}, bf16[2,32,3584]{2,1,0:T(8,128)(2,1)S(1)}, bf16[2,32,3584]{2,1,0:T(8,128)(2,1)S(1)}) custom-call(s32[1]{0:T(128)} %bitcast.place_ref, bf16[128,2048]{1,0:T(8,128)(2,1)S(1)} %copy-done.5, bf16[128,2048]{1,0:T(8,128)(2,1)S(1)} %collective-permute-done.far_ref, ...), custom_call_target="tpu_custom_call" | custom-call | flops 3758096384 | bytes 17563648 | tf_op jit(solution)/shard_map/pallas_call | solution.py:57
  34.2 4.3 %collective-permute-start.10 = (bf16[128,2048]{1,0:T(8,128)(2,1)S(1)}, bf16[128,2048]{1,0:T(8,128)(2,1)S(1)}, u32[]{:S(2)}, u32[]{:S(2)}) collective-permute-start(bf16[128,2048]{1,0:T(8,128)(2,1)S(1)} %collective-permute-done.3.near_ref), channel_id=1, source_target_pairs={{0,2},{1,3},{2,4},{3,5},{4,6},{5,7},{6,0},{7,1},{8,10},{9,11},{10,... | collective-permute-start | bytes 1572872 | tf_op jit(solution)/shard_map/ppermute | solution.py:197
  39.2 5.4 %shard_map.95 = (bf16[2,32,3584]{2,1,0:T(8,128)(2,1)S(1)}, bf16[2,32,3584]{2,1,0:T(8,128)(2,1)S(1)}, bf16[2,32,3584]{2,1,0:T(8,128)(2,1)S(1)}, bf16[2,32,3584]{2,1,0:T(8,128)(2,1)S(1)}) custom-call(s32[1]{0:T(128)} %bitcast.place_ref, bf16[128,2048]{1,0:T(8,128)(2,1)S(1)} %collective-permute-done.3.near_ref, ...), custom_call_target="tpu_custom_call" | custom-call | flops 3758096384 | bytes 17563648 | tf_op jit(solution)/shard_map/pallas_call | solution.py:57
  50.3 9.1 %collective-permute-done.10.near_ref = bf16[128,2048]{1,0:T(8,128)(2,1)S(1)} collective-permute-done((bf16[128,2048]{1,0:T(8,128)(2,1)S(1)}, bf16[128,2048]{1,0:T(8,128)(2,1)S(1)}, u32[]{:S(2)}, u32[]{:S(2)}) %collective-permute-start.10) | collective-permute-done | bytes 524320 | tf_op jit(solution)/shard_map/ppermute | solution.py:197
  60.7 8.5 %collective-permute-start.18 = (bf16[128,2048]{1,0:T(8,128)(2,1)S(1)}, bf16[128,2048]{1,0:T(8,128)(2,1)S(1)}, u32[]{:S(2)}, u32[]{:S(2)}) collective-permute-start(bf16[128,2048]{1,0:T(8,128)(2,1)S(1)} %collective-permute-done.10.near_ref), channel_id=1, source_target_pairs={{0,2},{1,3},{2,4},{3,5},{4,6},{5,7},{6,0},{7,1},{8,10},{9,11},{10,... | collective-permute-start | bytes 1572872 | tf_op jit(solution)/shard_map/ppermute | solution.py:197
  69.6 5.4 %shard_map.96 = (bf16[2,32,3584]{2,1,0:T(8,128)(2,1)S(1)}, bf16[2,32,3584]{2,1,0:T(8,128)(2,1)S(1)}, bf16[2,32,3584]{2,1,0:T(8,128)(2,1)S(1)}, bf16[2,32,3584]{2,1,0:T(8,128)(2,1)S(1)}) custom-call(s32[1]{0:T(128)} %bitcast.place_ref, bf16[128,2048]{1,0:T(8,128)(2,1)S(1)} %collective-permute-done.10.near_ref, ...), custom_call_target="tpu_custom_call" | custom-call | flops 3758096384 | bytes 17563648 | tf_op jit(solution)/shard_map/pallas_call | solution.py:57
  92.6 5.4 %shard_map.97 = (bf16[2,32,3584]{2,1,0:T(8,128)(2,1)S(1)}, bf16[2,32,3584]{2,1,0:T(8,128)(2,1)S(1)}, bf16[2,32,3584]{2,1,0:T(8,128)(2,1)S(1)}, bf16[2,32,3584]{2,1,0:T(8,128)(2,1)S(1)}) custom-call(s32[1]{0:T(128)} %bitcast.place_ref, bf16[128,2048]{1,0:T(8,128)(2,1)S(1)} %collective-permute-done.18.near_ref, ...), custom_call_target="tpu_custom_call" | custom-call | flops 3758096384 | bytes 17563648 | tf_op jit(solution)/shard_map/pallas_call | solution.py:57
  102.4 4.5 %multiply_reduce_fusion = bf16[1024,64]{0,1:T(8,128)(2,1)} fusion(f32[1024,16]{0,1:T(8,128)S(1)} %get-tuple-element.100, bf16[16,64,896]{2,1,0:T(8,128)(2,1)S(1)} %copy-done, bf16[1024,896]{1,0:T(8,128)(2,1)} %bitcast.24), kind=kOutput, calls=%fused_computation | convolution fusion | flops 1881079808 | bytes 3866624 | tf_op jit(solution)/shard_map/dot_general | solution.py:19
  121.6 5.6 %all-to-all-done.1.refs_2_ = bf16[32,32,128]{2,1,0:T(8,128)(2,1)S(1)} async-done(((bf16[32,32,128]{2,1,0:T(8,128)(2,1)}), bf16[32,32,128]{2,1,0:T(8,128)(2,1)S(1)}, u32[]{:S(2)}, u32[]{:S(2)}) %all-to-all-start.1) | async-done | bytes 262176 | tf_op jit(solution)/shard_map/all_to_all | solution.py:278
  137.6 3.6 %all-to-all-start.2 = ((bf16[32,32,128]{2,1,0:T(8,128)(2,1)}), bf16[32,32,128]{2,1,0:T(8,128)(2,1)S(1)}, u32[]{:S(2)}, u32[]{:S(2)}) async-start(bf16[32,32,128]{2,1,0:T(8,128)(2,1)} %broadcast_in_dim.108), calls=%async_computation.2 | async-start | bytes 524288 | tf_op jit(solution)/shard_map/all_to_all | solution.py:291
  147.4 4.1 %collective-permute-done.27.refs_1_ = bf16[32,3584]{1,0:T(8,128)(2,1)S(1)} collective-permute-done((bf16[32,3584]{1,0:T(8,128)(2,1)S(1)}, bf16[32,3584]{1,0:T(8,128)(2,1)S(1)}, u32[]{:S(2)}, u32[]{:S(2)}) %collective-permute-start.27) | collective-permute-done | bytes 229408 | tf_op jit(solution)/shard_map/ppermute | solution.py:200
  151.5 7.0 %all-to-all-done.2 = bf16[32,32,128]{2,1,0:T(8,128)(2,1)S(1)} async-done(((bf16[32,32,128]{2,1,0:T(8,128)(2,1)}), bf16[32,32,128]{2,1,0:T(8,128)(2,1)S(1)}, u32[]{:S(2)}, u32[]{:S(2)}) %all-to-all-start.2) | async-done | bytes 262176 | tf_op jit(solution)/shard_map/all_to_all | solution.py:291
  162.4 3.6 %fusion = bf16[1024,896]{1,0:T(8,128)(2,1)} fusion(bf16[16,64,896]{2,1,0:T(8,128)(2,1)S(1)} %copy-done, bf16[1024,16]{0,1:T(8,128)(2,1)S(1)} %copy-done.16, bf16[1024,64]{0,1:T(8,128)(2,1)S(1)} %copy.41), kind=kOutput, calls=%fused_computation.3 | convolution fusion | flops 1881931776 | bytes 3833856 | tf_op jit(solution)/shard_map/dot_general | solution.py:306
  166.1 5.2 %all-to-all-start.3 = ((bf16[8,128,896]{2,1,0:T(8,128)(2,1)}), bf16[8,128,896]{2,1,0:T(8,128)(2,1)}, u32[]{:S(2)}, u32[]{:S(2)}) async-start(bf16[8,128,896]{2,1,0:T(8,128)(2,1)} %bitcast.133), calls=%async_computation.3 | async-start | bytes 3670016 | tf_op jit(solution)/shard_map/all_to_all | solution.py:319
  174.6 2.9 %fusion.15 = f32[16,64,256]{2,1,0:T(8,128)} fusion(bf16[1024,256,1]{1,0,2:T(8,128)(2,1)} %bitcast.51, bf16[1024,64]{0,1:T(8,128)(2,1)S(1)} %copy.43, bf16[1024,16]{0,1:T(8,128)(2,1)S(1)} %copy-done.16, f32[16]{0:T(128)S(1)} %broadcast_divide_fusion), kind=kOutput, calls=%fused_computation.15 | convolution fusion | flops 538181632 | bytes 1736768 | tf_op jit(solution)/shard_map/dot_general | solution.py:19
  184.0 5.7 %fusion.9 = f32[16,64,896]{2,1,0:T(8,128)} fusion(bf16[1024,896,1]{1,0,2:T(8,128)(2,1)} %bitcast.47, f32[16]{0:T(128)S(1)} %broadcast_divide_fusion, bf16[1024,64]{0,1:T(8,128)(2,1)S(1)} %copy.42, bf16[1024,16]{0,1:T(8,128)(2,1)S(1)} %copy-done.16), kind=kOutput, calls=%fused_computation.12 | convolution fusion | flops 1881014272 | bytes 5668928 | tf_op jit(solution)/shard_map/dot_general | solution.py:19
  189.7 4.2 %collective-permute-done.30.refs_1_ = bf16[2,32,3584]{2,1,0:T(8,128)(2,1)S(1)} collective-permute-done((bf16[2,32,3584]{2,1,0:T(8,128)(2,1)S(1)}, bf16[2,32,3584]{2,1,0:T(8,128)(2,1)S(1)}, u32[]{:S(2)}, u32[]{:S(2)}) %collective-permute-start.30) | collective-permute-done | bytes 458784 | tf_op jit(solution)/shard_map/ppermute | solution.py:200
  193.8 10.3 %collective-permute-done.31.refs_2_ = bf16[2,32,3584]{2,1,0:T(8,128)(2,1)S(1)} collective-permute-done((bf16[2,32,3584]{2,1,0:T(8,128)(2,1)S(1)}, bf16[2,32,3584]{2,1,0:T(8,128)(2,1)S(1)}, u32[]{:S(2)}, u32[]{:S(2)}) %collective-permute-start.31) | collective-permute-done | bytes 458784 | tf_op jit(solution)/shard_map/ppermute | solution.py:200
  204.9 10.2 %all-to-all-done.3.refs_4_ = bf16[8,128,896]{2,1,0:T(8,128)(2,1)} async-done(((bf16[8,128,896]{2,1,0:T(8,128)(2,1)}), bf16[8,128,896]{2,1,0:T(8,128)(2,1)}, u32[]{:S(2)}, u32[]{:S(2)}) %all-to-all-start.3) | async-done | bytes 1835040 | tf_op jit(solution)/shard_map/all_to_all | solution.py:319
  216.1 3.8 %shard_map.102 = bf16[128,7168]{1,0:T(8,128)(2,1)} custom-call(s32[1]{0:T(128)} %bitcast.place_ref, bf16[2,32,3584]{2,1,0:T(8,128)(2,1)S(1)} %get-tuple-element.96.refs_0_, bf16[2,32,3584]{2,1,0:T(8,128)(2,1)S(1)} %collective-permute-done.30.refs_1_, bf16[2,32,3584]{2,1,0:T(8,128)(2,1)S(1)} %collective-permute-done.31.refs_2_, ...), custom_call_target="tpu_custom_call" | custom-call | flops 917504 | bytes 5505024 | tf_op jit(solution)/shard_map/pallas_call | solution.py:104
  (153 shorter events, 85.1 us)
Async XLA Ops:
  0.6 19.8 %collective-permute-start = (bf16[128,2048]{1,0:T(8,128)(2,1)}, bf16[128,2048]{1,0:T(8,128)(2,1)S(1)}, u32[]{:S(2)}, u32[]{:S(2)}) collective-permute-start(bf16[128,2048]{1,0:T(8,128)(2,1)} %near_ref.1), channel_id=1, source_target_pairs={{0,1},{1,0},{2,3},{3,2},{4,5},{5,4},{6,7},{7,6},{8,9},{9,8},{10,11... | collective-permute-start | bytes 1572872 | tf_op jit(solution)/shard_map/ppermute | solution.py:197
  1.2 17.8 %collective-permute-start.3 = (bf16[128,2048]{1,0:T(8,128)(2,1)}, bf16[128,2048]{1,0:T(8,128)(2,1)S(1)}, u32[]{:S(2)}, u32[]{:S(2)}) collective-permute-start(bf16[128,2048]{1,0:T(8,128)(2,1)} %near_ref.1), channel_id=1, source_target_pairs={{0,2},{1,3},{2,4},{3,5},{4,6},{5,7},{6,0},{7,1},{8,10},{9,11},{10,... | collective-permute-start | bytes 1572872 | tf_op jit(solution)/shard_map/ppermute | solution.py:197
  6.8 95.6 %all-to-all-start = ((bf16[8,128,896]{2,1,0:T(8,128)(2,1)}), bf16[8,128,896]{2,1,0:T(8,128)(2,1)}, u32[]{:S(2)}, u32[]{:S(2)}) async-start(bf16[8,128,896]{2,1,0:T(8,128)(2,1)} %bitcast.139), calls=%async_computation | async-start | bytes 3670016 | tf_op jit(solution)/shard_map/all_to_all | solution.py:207
  18.9 20.2 %collective-permute-start.4 = (bf16[128,2048]{1,0:T(8,128)(2,1)S(1)}, bf16[128,2048]{1,0:T(8,128)(2,1)S(1)}, u32[]{:S(2)}, u32[]{:S(2)}) collective-permute-start(bf16[128,2048]{1,0:T(8,128)(2,1)S(1)} %collective-permute-done.3.near_ref), channel_id=1, source_target_pairs={{0,1},{1,0},{2,3},{3,2},{4,5},{5,4},{6,7},{7,6},{8,9},{9,8},{10,11... | collective-permute-start | bytes 1572872 | tf_op jit(solution)/shard_map/ppermute | solution.py:197
  34.2 25.2 %collective-permute-start.10 = (bf16[128,2048]{1,0:T(8,128)(2,1)S(1)}, bf16[128,2048]{1,0:T(8,128)(2,1)S(1)}, u32[]{:S(2)}, u32[]{:S(2)}) collective-permute-start(bf16[128,2048]{1,0:T(8,128)(2,1)S(1)} %collective-permute-done.3.near_ref), channel_id=1, source_target_pairs={{0,2},{1,3},{2,4},{3,5},{4,6},{5,7},{6,0},{7,1},{8,10},{9,11},{10,... | collective-permute-start | bytes 1572872 | tf_op jit(solution)/shard_map/ppermute | solution.py:197
  45.5 15.3 %collective-permute-start.5 = (bf16[32,3584]{1,0:T(8,128)(2,1)S(1)}, bf16[32,3584]{1,0:T(8,128)(2,1)S(1)}, u32[]{:S(2)}, u32[]{:S(2)}) collective-permute-start(bf16[32,3584]{1,0:T(8,128)(2,1)S(1)} %fusion.33), channel_id=1, source_target_pairs={{0,16},{8,24},{16,0},{24,8},{1,17},{9,25},{17,1},{25,9},{2,18},{10... | collective-permute-start | bytes 688136 | tf_op jit(solution)/shard_map/ppermute | solution.py:200
  47.1 22.2 %collective-permute-start.6 = (bf16[32,3584]{1,0:T(8,128)(2,1)S(1)}, bf16[32,3584]{1,0:T(8,128)(2,1)S(1)}, u32[]{:S(2)}, u32[]{:S(2)}) collective-permute-start(bf16[32,3584]{1,0:T(8,128)(2,1)S(1)} %fusion.34), channel_id=1, source_target_pairs={{0,8},{8,0},{16,24},{24,16},{1,9},{9,1},{17,25},{25,17},{2,10},{10... | collective-permute-start | bytes 688136 | tf_op jit(solution)/shard_map/ppermute | solution.py:200
  48.3 26.8 %collective-permute-start.8 = (bf16[2,32,3584]{2,1,0:T(8,128)(2,1)S(1)}, bf16[2,32,3584]{2,1,0:T(8,128)(2,1)S(1)}, u32[]{:S(2)}, u32[]{:S(2)}) collective-permute-start(bf16[2,32,3584]{2,1,0:T(8,128)(2,1)S(1)} %get-tuple-element.57), channel_id=1, source_target_pairs={{0,8},{8,0},{16,24},{24,16},{1,9},{9,1},{17,25},{25,17},{2,10},{10... | collective-permute-start | bytes 1376264 | tf_op jit(solution)/shard_map/ppermute | solution.py:200
  49.8 25.3 %collective-permute-start.9 = (bf16[2,32,3584]{2,1,0:T(8,128)(2,1)S(1)}, bf16[2,32,3584]{2,1,0:T(8,128)(2,1)S(1)}, u32[]{:S(2)}, u32[]{:S(2)}) collective-permute-start(bf16[2,32,3584]{2,1,0:T(8,128)(2,1)S(1)} %get-tuple-element.58), channel_id=1, source_target_pairs={{0,16},{8,24},{16,0},{24,8},{1,17},{9,25},{17,1},{25,9},{2,18},{10... | collective-permute-start | bytes 1376264 | tf_op jit(solution)/shard_map/ppermute | solution.py:200
  60.7 20.4 %collective-permute-start.18 = (bf16[128,2048]{1,0:T(8,128)(2,1)S(1)}, bf16[128,2048]{1,0:T(8,128)(2,1)S(1)}, u32[]{:S(2)}, u32[]{:S(2)}) collective-permute-start(bf16[128,2048]{1,0:T(8,128)(2,1)S(1)} %collective-permute-done.10.near_ref), channel_id=1, source_target_pairs={{0,2},{1,3},{2,4},{3,5},{4,6},{5,7},{6,0},{7,1},{8,10},{9,11},{10,... | collective-permute-start | bytes 1572872 | tf_op jit(solution)/shard_map/ppermute | solution.py:197
  69.4 19.6 %collective-permute-start.7 = (bf16[32,3584]{1,0:T(8,128)(2,1)S(1)}, bf16[32,3584]{1,0:T(8,128)(2,1)S(1)}, u32[]{:S(2)}, u32[]{:S(2)}) collective-permute-start(bf16[32,3584]{1,0:T(8,128)(2,1)S(1)} %fusion.31), channel_id=1, source_target_pairs={{0,1},{1,0},{2,3},{3,2},{4,5},{5,4},{6,7},{7,6},{8,9},{9,8},{10,11... | collective-permute-start | bytes 688136 | tf_op jit(solution)/shard_map/ppermute | solution.py:197
  78.5 19.6 %collective-permute-start.16 = (bf16[2,32,3584]{2,1,0:T(8,128)(2,1)S(1)}, bf16[2,32,3584]{2,1,0:T(8,128)(2,1)S(1)}, u32[]{:S(2)}, u32[]{:S(2)}) collective-permute-start(bf16[2,32,3584]{2,1,0:T(8,128)(2,1)S(1)} %get-tuple-element.67), channel_id=1, source_target_pairs={{0,8},{8,0},{16,24},{24,16},{1,9},{9,1},{17,25},{25,17},{2,10},{10... | collective-permute-start | bytes 1376264 | tf_op jit(solution)/shard_map/ppermute | solution.py:200
  81.1 17.0 %collective-permute-start.17 = (bf16[2,32,3584]{2,1,0:T(8,128)(2,1)S(1)}, bf16[2,32,3584]{2,1,0:T(8,128)(2,1)S(1)}, u32[]{:S(2)}, u32[]{:S(2)}) collective-permute-start(bf16[2,32,3584]{2,1,0:T(8,128)(2,1)S(1)} %get-tuple-element.68), channel_id=1, source_target_pairs={{0,16},{8,24},{16,0},{24,8},{1,17},{9,25},{17,1},{25,9},{2,18},{10... | collective-permute-start | bytes 1376264 | tf_op jit(solution)/shard_map/ppermute | solution.py:200
  86.1 45.0 %collective-permute-start.14 = (bf16[32,3584]{1,0:T(8,128)(2,1)}, bf16[32,3584]{1,0:T(8,128)(2,1)}, u32[]{:S(2)}, u32[]{:S(2)}) collective-permute-start(bf16[32,3584]{1,0:T(8,128)(2,1)} %fusion.30), channel_id=1, source_target_pairs={{0,6},{1,7},{2,0},{3,1},{4,2},{5,3},{6,4},{7,5},{8,14},{9,15},{10,... | collective-permute-start | bytes 688136 | tf_op jit(solution)/shard_map/ppermute | solution.py:197
  88.9 42.2 %collective-permute-start.15 = (bf16[32,3584]{1,0:T(8,128)(2,1)}, bf16[32,3584]{1,0:T(8,128)(2,1)}, u32[]{:S(2)}, u32[]{:S(2)}) collective-permute-start(bf16[32,3584]{1,0:T(8,128)(2,1)} %fusion.29), channel_id=1, source_target_pairs={{0,7},{1,6},{2,1},{3,0},{4,3},{5,2},{6,5},{7,4},{8,15},{9,14},{10,... | collective-permute-start | bytes 688136 | tf_op jit(solution)/shard_map/ppermute | solution.py:197
  99.0 21.1 %collective-permute-start.20 = (bf16[32,3584]{1,0:T(8,128)(2,1)}, bf16[32,3584]{1,0:T(8,128)(2,1)S(1)}, u32[]{:S(2)}, u32[]{:S(2)}) collective-permute-start(bf16[32,3584]{1,0:T(8,128)(2,1)} %fusion.37), channel_id=1, source_target_pairs={{0,16},{8,24},{16,0},{24,8},{1,17},{9,25},{17,1},{25,9},{2,18},{10... | collective-permute-start | bytes 688136 | tf_op jit(solution)/shard_map/ppermute | solution.py:200
  100.3 21.3 %collective-permute-start.21 = (bf16[32,3584]{1,0:T(8,128)(2,1)}, bf16[32,3584]{1,0:T(8,128)(2,1)S(1)}, u32[]{:S(2)}, u32[]{:S(2)}) collective-permute-start(bf16[32,3584]{1,0:T(8,128)(2,1)} %fusion.38), channel_id=1, source_target_pairs={{0,8},{8,0},{16,24},{24,16},{1,9},{9,1},{17,25},{25,17},{2,10},{10... | collective-permute-start | bytes 688136 | tf_op jit(solution)/shard_map/ppermute | solution.py:200
  129.1 42.2 %collective-permute-start.22 = (bf16[32,3584]{1,0:T(8,128)(2,1)}, bf16[32,3584]{1,0:T(8,128)(2,1)S(1)}, u32[]{:S(2)}, u32[]{:S(2)}) collective-permute-start(bf16[32,3584]{1,0:T(8,128)(2,1)} %fusion.28), channel_id=1, source_target_pairs={{0,4},{1,5},{2,6},{3,7},{4,0},{5,1},{6,2},{7,3},{8,12},{9,13},{10,... | collective-permute-start | bytes 688136 | tf_op jit(solution)/shard_map/ppermute | solution.py:197
  131.1 40.1 %collective-permute-start.23 = (bf16[32,3584]{1,0:T(8,128)(2,1)}, bf16[32,3584]{1,0:T(8,128)(2,1)S(1)}, u32[]{:S(2)}, u32[]{:S(2)}) collective-permute-start(bf16[32,3584]{1,0:T(8,128)(2,1)} %fusion.27), channel_id=1, source_target_pairs={{0,5},{1,4},{2,7},{3,6},{4,1},{5,0},{6,3},{7,2},{8,13},{9,12},{10,... | collective-permute-start | bytes 688136 | tf_op jit(solution)/shard_map/ppermute | solution.py:197
  137.6 20.9 %all-to-all-start.2 = ((bf16[32,32,128]{2,1,0:T(8,128)(2,1)}), bf16[32,32,128]{2,1,0:T(8,128)(2,1)S(1)}, u32[]{:S(2)}, u32[]{:S(2)}) async-start(bf16[32,32,128]{2,1,0:T(8,128)(2,1)} %broadcast_in_dim.108), calls=%async_computation.2 | async-start | bytes 524288 | tf_op jit(solution)/shard_map/all_to_all | solution.py:291
  160.4 17.1 %collective-permute-start.28 = (bf16[32,3584]{1,0:T(8,128)(2,1)}, bf16[32,3584]{1,0:T(8,128)(2,1)S(1)}, u32[]{:S(2)}, u32[]{:S(2)}) collective-permute-start(bf16[32,3584]{1,0:T(8,128)(2,1)} %fusion.26), channel_id=1, source_target_pairs={{0,2},{1,3},{2,4},{3,5},{4,6},{5,7},{6,0},{7,1},{8,10},{9,11},{10,... | collective-permute-start | bytes 688136 | tf_op jit(solution)/shard_map/ppermute | solution.py:197
  166.1 49.0 %all-to-all-start.3 = ((bf16[8,128,896]{2,1,0:T(8,128)(2,1)}), bf16[8,128,896]{2,1,0:T(8,128)(2,1)}, u32[]{:S(2)}, u32[]{:S(2)}) async-start(bf16[8,128,896]{2,1,0:T(8,128)(2,1)} %bitcast.133), calls=%async_computation.3 | async-start | bytes 3670016 | tf_op jit(solution)/shard_map/all_to_all | solution.py:319
  181.6 22.5 %collective-permute-start.31 = (bf16[2,32,3584]{2,1,0:T(8,128)(2,1)S(1)}, bf16[2,32,3584]{2,1,0:T(8,128)(2,1)S(1)}, u32[]{:S(2)}, u32[]{:S(2)}) collective-permute-start(bf16[2,32,3584]{2,1,0:T(8,128)(2,1)S(1)} %get-tuple-element.94), channel_id=1, source_target_pairs={{0,16},{8,24},{16,0},{24,8},{1,17},{9,25},{17,1},{25,9},{2,18},{10... | collective-permute-start | bytes 1376264 | tf_op jit(solution)/shard_map/ppermute | solution.py:200
  182.7 21.4 %collective-permute-start.32 = (bf16[2,32,3584]{2,1,0:T(8,128)(2,1)S(1)}, bf16[2,32,3584]{2,1,0:T(8,128)(2,1)S(1)}, u32[]{:S(2)}, u32[]{:S(2)}) collective-permute-start(bf16[2,32,3584]{2,1,0:T(8,128)(2,1)S(1)} %get-tuple-element.93), channel_id=1, source_target_pairs={{0,24},{8,16},{16,8},{24,0},{1,25},{9,17},{17,9},{25,1},{2,26},{10... | collective-permute-start | bytes 1376264 | tf_op jit(solution)/shard_map/ppermute | solution.py:200
  (32 other events, 376.7 us)
